TPU v7x, 256 devices: a whole 4x4x8 slice. The times are simulated.
256 devices in a mesh: section: 8 (over y, z_hi), tp: 32 (over x, z_lo, core).
Axes of the slice: x: 4, y: 4, z: 8 (z_hi: 2, z_lo: 4; z = z_hi * 4 + z_lo), core: 2. Of those that a mesh axis runs over, the one named last changes fastest.
Arguments:
- scan_input: bfloat16 [2048, 16384], P('section', 'tp'), may hold values from -6 to 6
- input_map: bfloat16 [2048, 1024], P('section'), may hold values from -0.375 to 0.375
- output_map: bfloat16 [2048, 1024], P('section'), may hold values from -0.375 to 0.375
- log_decay: float32 [2048, 256], P('section', 'tp'), may hold values from -0.6 to 0
- skip_gain: float32 [256], P('tp'), may hold values from 0.5 to 2
- query_rows: bfloat16 [2048, 8192], P('section', 'tp'), may hold values from -10 to 10
- key_rows: bfloat16 [2048, 1024], P('section'), may hold values from -10 to 10
- value_rows: bfloat16 [2048, 1024], P('section'), may hold values from -15 to 15
- out_weight: bfloat16 [8192, 8192], P(None, 'tp'), may hold values from -0.5 to 0.5
Outputs:
- ssm_out: bfloat16 [2048, 16384], P('section', 'tp')
- attn_out: bfloat16 [8192, 2048], P('tp', 'section')
All inputs are finite; a program needn't handle non-finite values.
Results may differ from a plain program's by a relative error of at most 0.0075.
Values may be sent and summed in bfloat16 or wider, within the bound.
No kernel may reach another device: no remote copies, remote signals or barrier semaphores. Data moves between devices by JAX's collectives and lax.ppermute only.
A program may use at most 64 MiB of HBM per device.

v0:
```python
import math

import jax
import jax.numpy as jnp
from jax import lax
from jax.sharding import PartitionSpec as P

SCAN_HEADS = 256
SSM_HEAD_DIM = 64
N_STATE = 128
GROUPS = 8
Q_HEADS = 64
KV_HEADS = 8
HEAD_DIM = 128
BLOCK = 128


highest = lax.Precision.HIGHEST
masked_score = -1e30


def shifted(block, axis, distance):
    devices = range(lax.axis_size(axis))
    route = [(i - distance, i) for i in devices if i - distance in devices]
    return lax.ppermute(block, axis, route)


def local_mixer(scan_input, in_rows, out_rows, log_decay, skip_gain):
    length = scan_input.shape[0]
    head_count = log_decay.shape[1]
    blocks = length // BLOCK
    inputs = scan_input.astype(jnp.float32).reshape(blocks, BLOCK, head_count, SSM_HEAD_DIM)
    in_blocks = in_rows.reshape(blocks, BLOCK, N_STATE)
    out_blocks = out_rows.reshape(blocks, BLOCK, N_STATE)
    running = jnp.cumsum(log_decay.reshape(blocks, BLOCK, head_count), axis=1)
    causal = (jnp.arange(BLOCK)[:, None] >= jnp.arange(BLOCK)[None, :])[None, :, :, None]
    affinity = jnp.einsum("bqn,bsn->bqs", out_blocks, in_blocks, preferred_element_type=jnp.float32)
    decay_gaps = running[:, :, None, :] - running[:, None, :, :]
    mixing = affinity[..., None] * jnp.exp(jnp.where(causal, decay_gaps, -jnp.inf))
    inside = jnp.einsum("bqsh,bshp->bqhp", mixing, inputs, precision=highest)
    in_wide = in_blocks.astype(jnp.float32)
    out_wide = out_blocks.astype(jnp.float32)
    block_decay = running[:, -1, :]
    tail_decay = jnp.exp(block_decay[:, None, :] - running)
    block_states = jnp.einsum(
        "bshp,bsn->bhpn", inputs * tail_decay[..., None], in_wide, precision=highest
    )

    def advance(hidden, block_item):
        contribution, decay_total = block_item
        return (jnp.exp(decay_total)[:, None, None] * hidden + contribution, hidden)

    start_state = jnp.zeros((head_count, SSM_HEAD_DIM, N_STATE), jnp.float32)
    closing, entering = lax.scan(advance, start_state, (block_states, block_decay))
    carried = jnp.exp(running)[..., None] * jnp.einsum(
        "bqn,bhpn->bqhp", out_wide, entering, precision=highest
    )
    local_out = inside + carried + skip_gain[None, None, :, None] * inputs
    offsets = jnp.cumsum(block_decay, axis=0) - block_decay
    reach_decay = jnp.exp(running + offsets[:, None, :])
    return (local_out, closing, jnp.sum(block_decay, axis=0), reach_decay, out_wide)


def on_device(
    scan_input,
    input_map,
    output_map,
    log_decay,
    skip_gain,
    query_rows,
    key_rows,
    value_rows,
    out_weight,
):
    head_count = log_decay.shape[1]
    per_group = SCAN_HEADS // GROUPS
    group_index = lax.axis_index("tp") * head_count // per_group
    in_rows = lax.dynamic_slice_in_dim(input_map, group_index * N_STATE, N_STATE, 1)
    out_rows = lax.dynamic_slice_in_dim(output_map, group_index * N_STATE, N_STATE, 1)
    local_out, closing, decay_total, reach_decay, out_wide = local_mixer(
        scan_input, in_rows, out_rows, log_decay, skip_gain
    )

    def relay_turn(turn_index, hidden):
        handed = jnp.exp(decay_total)[:, None, None] * hidden + closing
        return shifted(handed, "section", 1)

    incoming = lax.fori_loop(0, lax.axis_size("section") - 1, relay_turn, jnp.zeros_like(closing))
    correction = reach_decay[..., None] * jnp.einsum(
        "bqn,hpn->bqhp", out_wide, incoming, precision=highest
    )
    ssm_out = (local_out + correction).reshape(scan_input.shape).astype(jnp.bfloat16)
    length = query_rows.shape[0]
    query_heads = query_rows.shape[1] // HEAD_DIM
    kv_index = lax.axis_index("tp") * query_heads // (Q_HEADS // KV_HEADS)
    key_head = lax.dynamic_slice_in_dim(key_rows, kv_index * HEAD_DIM, HEAD_DIM, 1)
    value_head = lax.dynamic_slice_in_dim(value_rows, kv_index * HEAD_DIM, HEAD_DIM, 1)
    queries = query_rows.reshape(length, query_heads, HEAD_DIM)
    first_row = lax.axis_index("section") * length
    query_pos = first_row + jnp.arange(length, dtype=jnp.int32)
    scale = 1.0 / math.sqrt(HEAD_DIM)
    start_carry = (
        jnp.full((length, query_heads), masked_score, jnp.float32),
        jnp.zeros((length, query_heads), jnp.float32),
        jnp.zeros((length, query_heads, HEAD_DIM), jnp.float32),
    )
    key_part = lax.all_gather(key_head, "section", axis=0, tiled=True)
    value_part = lax.all_gather(value_head, "section", axis=0, tiled=True)

    def work(state):
        row_max, row_total, weighted = state
        scores = (
            jnp.einsum("lhd,kd->lhk", queries, key_part, preferred_element_type=jnp.float32) * scale
        )
        key_pos = jnp.arange(key_part.shape[0], dtype=jnp.int32)
        allowed = (key_pos[None, :] <= query_pos[:, None])[:, None, :]
        scores = jnp.where(allowed, scores, masked_score)
        new_max = jnp.maximum(row_max, jnp.max(scores, axis=-1))
        weights = jnp.where(allowed, jnp.exp(scores - new_max[..., None]), 0.0)
        row_total = jnp.sum(weights, axis=-1)
        weighted = jnp.einsum(
            "lhk,kd->lhd",
            weights.astype(jnp.bfloat16),
            value_part,
            preferred_element_type=jnp.float32,
        )
        return (new_max, row_total, weighted)

    def keep_carry(state):
        return state

    row_max, row_total, weighted = lax.cond(
        jnp.int32(0) <= first_row + length - 1, work, keep_carry, start_carry
    )
    attended = (
        (weighted / row_total[..., None])
        .reshape(length, query_heads * HEAD_DIM)
        .astype(jnp.bfloat16)
    )
    summed = lax.psum_scatter(
        lax.dot_general(
            out_weight, attended, (((1,), (1,)), ((), ())), preferred_element_type=jnp.float32
        ),
        "tp",
        scatter_dimension=0,
        tiled=True,
    )
    attn_out = summed.astype(jnp.bfloat16)
    return (ssm_out, attn_out)


def solution(mesh):
    placed = (
        P("section", "tp"),
        P("section", None),
        P("section", None),
        P("section", "tp"),
        P("tp"),
        P("section", "tp"),
        P("section", None),
        P("section", None),
        P(None, "tp"),
    )
    return jax.shard_map(
        on_device,
        mesh=mesh,
        in_specs=placed,
        out_specs=(P("section", "tp"), P("tp", "section")),
        check_vma=False,
    )
```

profile of v0, /device:TPU:8, one launch (start us, length us, event | category | flops | bytes accessed | tf_op | source)
XLA Modules:
  0.0 328.7 jit_solution(7200395051437499476)
XLA Ops:
  7.2 0.0 copy-start
  7.2 0.0 reduce-scatter.2.cloned.1.call-start
  7.2 1.0 copy-done
  8.2 49.6 %all_gather.6 = bf16[2048,128]{1,0:T(8,128)(2,1)S(1)} all-gather(bf16[256,128]{1,0:T(8,128)(2,1)S(1)} %constant_dynamic-slice_fusion.2), channel_id=1, replica_groups=mesh['section'=8,'tp'=32] {'section'}, dimensions={0}, use_global_device_ids=true | all-gather | bytes 589824 | tf_op jit(solution)/shard_map/all_gather | solution.py:107
  57.8 0.8 constant_dynamic-slice_fusion.1
  58.7 45.9 %all_gather.7 = bf16[2048,128]{1,0:T(8,128)(2,1)S(1)} all-gather(bf16[256,128]{1,0:T(8,128)(2,1)S(1)} %constant_dynamic-slice_fusion.1), channel_id=1, replica_groups=mesh['section'=8,'tp'=32] {'section'}, dimensions={0}, use_global_device_ids=true | all-gather | bytes 589824 | tf_op jit(solution)/shard_map/all_gather | solution.py:108
  104.6 5.0 %conditional.1 = (f32[256,2]{0,1:T(2,128)S(1)}, f32[256,2,128]{0,2,1:T(8,128)S(1)}) conditional(s32[]{:T(128)} %convert_element_type.26, () %tuple.33, (s32[]{:T(128)}, s32[256]{0:T(256)S(1)}, bf16[256,256]{1,0:T(8,128)(2,1)}, bf16[2048,128]{1,0:T(8,128)(2,1)S(1)}, bf16[2048,128]{1,0:T(8,128)(2,1)S(1)}) %tuple.34), branch_computations={%region_7.8_spmd, %region_8.11_spmd} | conditional | flops 551026432 | bytes 16137236 | solution.py:132
  104.6 0.4 iota_compare_fusion
  105.0 2.0 fusion
  107.0 1.2 fusion.3
  108.2 1.4 fusion.2
  109.7 6.7 %convolution_bitcast_fusion = f32[8192,256]{0,1:T(8,128)} fusion(bf16[256,256]{0,1:T(8,128)(2,1)S(1)} %bitcast.79, bf16[8192,256]{1,0:T(8,128)(2,1)} %param.23), kind=kOutput, calls=%fused_computation.24 | convolution fusion | flops 1073741824 | bytes 12713984 | tf_op jit(solution)/shard_map/dot_general | solution.py:141
  116.4 0.0 copy-start.2
  116.4 0.0 copy-start.1
  116.4 0.0 reduce-scatter.2.cloned.1.call-update
  116.5 0.6 copy-done.2
  117.1 0.1 copy.37
  117.2 0.2 reduce_window_sum.22
  117.4 0.1 copy.38
  117.5 0.1 fusion.34
  117.6 0.1 copy.44
  117.7 0.0 copy-done.1
  117.7 0.3 reshape.106
  117.9 0.3 copy.41
  118.3 0.1 copy.42
  118.3 0.1 copy.45
  118.5 0.9 constant_dynamic-slice_fusion.3
  119.4 0.2 fusion.36
  119.5 0.4 fusion.24
  119.9 0.3 while.26
  120.0 0.1 bitcast_add_fusion.2
  120.2 0.1 bitcast_add_fusion.2
  120.3 0.0 copy-start.3
  120.3 149.4 %while.25 = (s32[]{:T(128)}, f32[8,64,128]{2,1,0:T(8,128)S(1)}, f32[8,1,1]{0,2,1:T(1,128)S(1)}, f32[8,64,128]{2,1,0:T(8,128)S(1)}, s32[]{:T(128)}) while((s32[]{:T(128)}, f32[8,64,128]{2,1,0:T(8,128)S(1)}, f32[8,1,1]{0,2,1:T(1,128)S(1)}, f32[8,64,128]{2,1,0:T(8,128)S(1)}, s32[]{:T(128)}) %tuple.69), condition=%wide.region_6.7_spmd, body=%wide.region_5.6_spmd.sunk | while | flops 131074 | bytes 1835141 | solution.py:88
  120.3 0.1 multiply_add_fusion.2
  120.4 8.8 %collective-permute-start = (f32[8,64,128]{2,1,0:T(8,128)S(1)}, f32[8,64,128]{2,1,0:T(8,128)S(1)}, u32[]{:S(2)}, u32[]{:S(2)}) collective-permute-start(f32[8,64,128]{2,1,0:T(8,128)S(1)} %multiply_add_fusion.2), channel_id=1, source_target_pairs={{0,32},{32,64},{64,96},{96,128},{128,160},{160,192},{192,224},{1,3... | collective-permute-start | bytes 786440 | tf_op jit(solution)/shard_map/while/body/eval_jaxpr/ppermute | solution.py:25
  129.2 14.1 %collective-permute-done = f32[8,64,128]{2,1,0:T(8,128)S(1)} collective-permute-done((f32[8,64,128]{2,1,0:T(8,128)S(1)}, f32[8,64,128]{2,1,0:T(8,128)S(1)}, u32[]{:S(2)}, u32[]{:S(2)}) %collective-permute-start) | collective-permute-done | bytes 262176 | tf_op jit(solution)/shard_map/while/body/eval_jaxpr/ppermute | solution.py:25
  143.3 0.1 multiply_add_fusion.2
  143.4 8.7 %collective-permute-start = (f32[8,64,128]{2,1,0:T(8,128)S(1)}, f32[8,64,128]{2,1,0:T(8,128)S(1)}, u32[]{:S(2)}, u32[]{:S(2)}) collective-permute-start(f32[8,64,128]{2,1,0:T(8,128)S(1)} %multiply_add_fusion.2), channel_id=1, source_target_pairs={{0,32},{32,64},{64,96},{96,128},{128,160},{160,192},{192,224},{1,3... | collective-permute-start | bytes 786440 | tf_op jit(solution)/shard_map/while/body/eval_jaxpr/ppermute | solution.py:25
  152.1 11.0 %collective-permute-done = f32[8,64,128]{2,1,0:T(8,128)S(1)} collective-permute-done((f32[8,64,128]{2,1,0:T(8,128)S(1)}, f32[8,64,128]{2,1,0:T(8,128)S(1)}, u32[]{:S(2)}, u32[]{:S(2)}) %collective-permute-start) | collective-permute-done | bytes 262176 | tf_op jit(solution)/shard_map/while/body/eval_jaxpr/ppermute | solution.py:25
  163.2 0.1 multiply_add_fusion.2
  163.3 8.9 %collective-permute-start = (f32[8,64,128]{2,1,0:T(8,128)S(1)}, f32[8,64,128]{2,1,0:T(8,128)S(1)}, u32[]{:S(2)}, u32[]{:S(2)}) collective-permute-start(f32[8,64,128]{2,1,0:T(8,128)S(1)} %multiply_add_fusion.2), channel_id=1, source_target_pairs={{0,32},{32,64},{64,96},{96,128},{128,160},{160,192},{192,224},{1,3... | collective-permute-start | bytes 786440 | tf_op jit(solution)/shard_map/while/body/eval_jaxpr/ppermute | solution.py:25
  172.2 11.4 %collective-permute-done = f32[8,64,128]{2,1,0:T(8,128)S(1)} collective-permute-done((f32[8,64,128]{2,1,0:T(8,128)S(1)}, f32[8,64,128]{2,1,0:T(8,128)S(1)}, u32[]{:S(2)}, u32[]{:S(2)}) %collective-permute-start) | collective-permute-done | bytes 262176 | tf_op jit(solution)/shard_map/while/body/eval_jaxpr/ppermute | solution.py:25
  183.6 0.1 multiply_add_fusion.2
  183.7 8.8 %collective-permute-start = (f32[8,64,128]{2,1,0:T(8,128)S(1)}, f32[8,64,128]{2,1,0:T(8,128)S(1)}, u32[]{:S(2)}, u32[]{:S(2)}) collective-permute-start(f32[8,64,128]{2,1,0:T(8,128)S(1)} %multiply_add_fusion.2), channel_id=1, source_target_pairs={{0,32},{32,64},{64,96},{96,128},{128,160},{160,192},{192,224},{1,3... | collective-permute-start | bytes 786440 | tf_op jit(solution)/shard_map/while/body/eval_jaxpr/ppermute | solution.py:25
  192.5 13.7 %collective-permute-done = f32[8,64,128]{2,1,0:T(8,128)S(1)} collective-permute-done((f32[8,64,128]{2,1,0:T(8,128)S(1)}, f32[8,64,128]{2,1,0:T(8,128)S(1)}, u32[]{:S(2)}, u32[]{:S(2)}) %collective-permute-start) | collective-permute-done | bytes 262176 | tf_op jit(solution)/shard_map/while/body/eval_jaxpr/ppermute | solution.py:25
  206.2 0.1 multiply_add_fusion.2
  206.3 6.4 %collective-permute-start = (f32[8,64,128]{2,1,0:T(8,128)S(1)}, f32[8,64,128]{2,1,0:T(8,128)S(1)}, u32[]{:S(2)}, u32[]{:S(2)}) collective-permute-start(f32[8,64,128]{2,1,0:T(8,128)S(1)} %multiply_add_fusion.2), channel_id=1, source_target_pairs={{0,32},{32,64},{64,96},{96,128},{128,160},{160,192},{192,224},{1,3... | collective-permute-start | bytes 786440 | tf_op jit(solution)/shard_map/while/body/eval_jaxpr/ppermute | solution.py:25
  212.7 16.2 %collective-permute-done = f32[8,64,128]{2,1,0:T(8,128)S(1)} collective-permute-done((f32[8,64,128]{2,1,0:T(8,128)S(1)}, f32[8,64,128]{2,1,0:T(8,128)S(1)}, u32[]{:S(2)}, u32[]{:S(2)}) %collective-permute-start) | collective-permute-done | bytes 262176 | tf_op jit(solution)/shard_map/while/body/eval_jaxpr/ppermute | solution.py:25
  228.9 0.1 multiply_add_fusion.2
  229.0 5.6 %collective-permute-start = (f32[8,64,128]{2,1,0:T(8,128)S(1)}, f32[8,64,128]{2,1,0:T(8,128)S(1)}, u32[]{:S(2)}, u32[]{:S(2)}) collective-permute-start(f32[8,64,128]{2,1,0:T(8,128)S(1)} %multiply_add_fusion.2), channel_id=1, source_target_pairs={{0,32},{32,64},{64,96},{96,128},{128,160},{160,192},{192,224},{1,3... | collective-permute-start | bytes 786440 | tf_op jit(solution)/shard_map/while/body/eval_jaxpr/ppermute | solution.py:25
  234.6 16.8 %collective-permute-done = f32[8,64,128]{2,1,0:T(8,128)S(1)} collective-permute-done((f32[8,64,128]{2,1,0:T(8,128)S(1)}, f32[8,64,128]{2,1,0:T(8,128)S(1)}, u32[]{:S(2)}, u32[]{:S(2)}) %collective-permute-start) | collective-permute-done | bytes 262176 | tf_op jit(solution)/shard_map/while/body/eval_jaxpr/ppermute | solution.py:25
  251.4 0.1 multiply_add_fusion.2
  251.5 3.7 %collective-permute-start = (f32[8,64,128]{2,1,0:T(8,128)S(1)}, f32[8,64,128]{2,1,0:T(8,128)S(1)}, u32[]{:S(2)}, u32[]{:S(2)}) collective-permute-start(f32[8,64,128]{2,1,0:T(8,128)S(1)} %multiply_add_fusion.2), channel_id=1, source_target_pairs={{0,32},{32,64},{64,96},{96,128},{128,160},{160,192},{192,224},{1,3... | collective-permute-start | bytes 786440 | tf_op jit(solution)/shard_map/while/body/eval_jaxpr/ppermute | solution.py:25
  255.2 14.5 %collective-permute-done = f32[8,64,128]{2,1,0:T(8,128)S(1)} collective-permute-done((f32[8,64,128]{2,1,0:T(8,128)S(1)}, f32[8,64,128]{2,1,0:T(8,128)S(1)}, u32[]{:S(2)}, u32[]{:S(2)}) %collective-permute-start) | collective-permute-done | bytes 262176 | tf_op jit(solution)/shard_map/while/body/eval_jaxpr/ppermute | solution.py:25
  269.7 0.4 convolution_multiply_fusion
  270.1 0.4 convolution_multiply_fusion.1
  270.5 0.0 copy-done.3
  270.5 1.3 fusion.19
  271.8 0.3 copy.52
  272.1 1.0 reshape.105
  273.1 46.9 %reduce-scatter.2.cloned.1.call-done = f32[256,256]{0,1:T(8,128)} async-done(((f32[8192,256]{0,1:T(8,128)}), f32[256,256]{0,1:T(8,128)}) %reduce-scatter.2.cloned.1.call-update) | async-done | bytes 262160 | tf_op jit(solution)/shard_map/reduce_scatter | solution.py:140
  320.1 1.0 convert_element_type.29
  321.0 0.8 copy.49
  (16 shorter events, 0.2 us)
Async XLA Ops:
  7.2 1.0 copy-start
  7.2 312.9 %reduce-scatter.2.cloned.1.call-start = ((), (), s32[]{:S(2)}) async-start(), calls=%async_computation.1 | async-start | bytes 8650752 | tf_op jit(solution)/shard_map/reduce_scatter | solution.py:140
  116.4 0.7 copy-start.2
  116.4 1.2 copy-start.1
  120.3 150.2 %copy-start.3 = (f32[8]{0:T(128)S(1)}, f32[8]{0:T(128)}, u32[]{:S(2)}) copy-start(f32[8]{0:T(128)} %param.19) | copy-start | bytes 100
  120.4 22.9 %collective-permute-start = (f32[8,64,128]{2,1,0:T(8,128)S(1)}, f32[8,64,128]{2,1,0:T(8,128)S(1)}, u32[]{:S(2)}, u32[]{:S(2)}) collective-permute-start(f32[8,64,128]{2,1,0:T(8,128)S(1)} %multiply_add_fusion.2), channel_id=1, source_target_pairs={{0,32},{32,64},{64,96},{96,128},{128,160},{160,192},{192,224},{1,3... | collective-permute-start | bytes 786440 | tf_op jit(solution)/shard_map/while/body/eval_jaxpr/ppermute | solution.py:25
  143.4 19.8 %collective-permute-start = (f32[8,64,128]{2,1,0:T(8,128)S(1)}, f32[8,64,128]{2,1,0:T(8,128)S(1)}, u32[]{:S(2)}, u32[]{:S(2)}) collective-permute-start(f32[8,64,128]{2,1,0:T(8,128)S(1)} %multiply_add_fusion.2), channel_id=1, source_target_pairs={{0,32},{32,64},{64,96},{96,128},{128,160},{160,192},{192,224},{1,3... | collective-permute-start | bytes 786440 | tf_op jit(solution)/shard_map/while/body/eval_jaxpr/ppermute | solution.py:25
  163.3 20.3 %collective-permute-start = (f32[8,64,128]{2,1,0:T(8,128)S(1)}, f32[8,64,128]{2,1,0:T(8,128)S(1)}, u32[]{:S(2)}, u32[]{:S(2)}) collective-permute-start(f32[8,64,128]{2,1,0:T(8,128)S(1)} %multiply_add_fusion.2), channel_id=1, source_target_pairs={{0,32},{32,64},{64,96},{96,128},{128,160},{160,192},{192,224},{1,3... | collective-permute-start | bytes 786440 | tf_op jit(solution)/shard_map/while/body/eval_jaxpr/ppermute | solution.py:25
  183.7 22.5 %collective-permute-start = (f32[8,64,128]{2,1,0:T(8,128)S(1)}, f32[8,64,128]{2,1,0:T(8,128)S(1)}, u32[]{:S(2)}, u32[]{:S(2)}) collective-permute-start(f32[8,64,128]{2,1,0:T(8,128)S(1)} %multiply_add_fusion.2), channel_id=1, source_target_pairs={{0,32},{32,64},{64,96},{96,128},{128,160},{160,192},{192,224},{1,3... | collective-permute-start | bytes 786440 | tf_op jit(solution)/shard_map/while/body/eval_jaxpr/ppermute | solution.py:25
  206.3 22.6 %collective-permute-start = (f32[8,64,128]{2,1,0:T(8,128)S(1)}, f32[8,64,128]{2,1,0:T(8,128)S(1)}, u32[]{:S(2)}, u32[]{:S(2)}) collective-permute-start(f32[8,64,128]{2,1,0:T(8,128)S(1)} %multiply_add_fusion.2), channel_id=1, source_target_pairs={{0,32},{32,64},{64,96},{96,128},{128,160},{160,192},{192,224},{1,3... | collective-permute-start | bytes 786440 | tf_op jit(solution)/shard_map/while/body/eval_jaxpr/ppermute | solution.py:25
  229.0 22.4 %collective-permute-start = (f32[8,64,128]{2,1,0:T(8,128)S(1)}, f32[8,64,128]{2,1,0:T(8,128)S(1)}, u32[]{:S(2)}, u32[]{:S(2)}) collective-permute-start(f32[8,64,128]{2,1,0:T(8,128)S(1)} %multiply_add_fusion.2), channel_id=1, source_target_pairs={{0,32},{32,64},{64,96},{96,128},{128,160},{160,192},{192,224},{1,3... | collective-permute-start | bytes 786440 | tf_op jit(solution)/shard_map/while/body/eval_jaxpr/ppermute | solution.py:25
  251.5 18.2 %collective-permute-start = (f32[8,64,128]{2,1,0:T(8,128)S(1)}, f32[8,64,128]{2,1,0:T(8,128)S(1)}, u32[]{:S(2)}, u32[]{:S(2)}) collective-permute-start(f32[8,64,128]{2,1,0:T(8,128)S(1)} %multiply_add_fusion.2), channel_id=1, source_target_pairs={{0,32},{32,64},{64,96},{96,128},{128,160},{160,192},{192,224},{1,3... | collective-permute-start | bytes 786440 | tf_op jit(solution)/shard_map/while/body/eval_jaxpr/ppermute | solution.py:25
Sparse Core Ops, SparseCore 0:
  116.6 203.4 reduce-scatter.1
where the time goes:
time: 333 us; the launch traced here: 329 us
  waiting for transfers between devices  145 us (44%)
  blocking collectives  95.5 us (29%)
  starting transfers between devices  50.9 us (15%)
  between operations  14.2 us (4%)
  matrix products  12.6 us (4%)
  local copies, waits for them, and re-layouts  6.51 us (2%)
  other arithmetic  3.97 us (1%)
    ppermute x7, waiting for transfers between devices, shifted(): return lax.ppermute(block, axis, route)  97.8 us
    ppermute x7, starting transfers between devices, shifted(): return lax.ppermute(block, axis, route)  50.8 us
    all_gather x1, blocking collectives, on_device(): key_part = lax.all_gather(key_head, 'section', axis=0, tiled=True)  49.6 us
    reduce_scatter x1, waiting for transfers between devices, on_device(): lax.psum_scatter(lax.dot_general(out_weight, attended, (((1,), (1,)), (()...  46.9 us
    all_gather x1, blocking collectives, on_device(): value_part = lax.all_gather(value_head, 'section', axis=0, tiled=True)  45.9 us
    dot_general x1, matrix products, on_device(): lax.dot_general(out_weight, attended, (((1,), (1,)), ((), ())), preferred...  6.74 us
  transfers between devices with their start and end apart: 8, of which 8 were waited for; matrix products, arithmetic and copies ran while one was open for 2% of the time, Pallas kernels for 0%

commit v1 on v0

v1 whole, which is shorter than its diff:
```python
import math

import jax
import jax.numpy as jnp
from jax import lax
from jax.experimental import pallas as pl
from jax.experimental.pallas import tpu as pltpu
from jax.sharding import PartitionSpec as P

SCAN_HEADS = 256
SSM_HEAD_DIM = 64
N_STATE = 128
GROUPS = 8
Q_HEADS = 64
KV_HEADS = 8
HEAD_DIM = 128

SECTIONS = 8
TP = 32
ROWS = 256
CHIPS = 16
masked_score = -1e30
bf16 = jnp.bfloat16
f32 = jnp.float32
VMEM_LIMIT = 48 * 1024 * 1024


def swap_core(block):
    return lax.ppermute(block, "tp", [(t, t ^ 1) for t in range(TP)])


def swap_zh(block):
    return lax.ppermute(block, "section", [(s, s ^ 1) for s in range(SECTIONS)])


def shift_y(block, distance):
    route = [(s, (s + 2 * distance) % SECTIONS) for s in range(SECTIONS)]
    return lax.ppermute(block, "section", route)


def swap_zh_near(block):
    route = [
        (s * TP + t, (s ^ 1) * TP + (t ^ 4)) for s in range(SECTIONS) for t in range(TP)
    ]
    return lax.ppermute(block, ("section", "tp"), route)


def swap_chip(block, offset):
    return lax.ppermute(block, "tp", [(t, t ^ (2 * offset)) for t in range(TP)])


def params():
    return pltpu.CompilerParams(vmem_limit_bytes=VMEM_LIMIT)


def whole(shape):
    return pl.BlockSpec(shape, lambda i, s: (0,) * len(shape))


def call(body, scalars, in_specs, out_shapes, args, scratch=(), flops=0, moved=0):
    return pl.pallas_call(
        body,
        grid_spec=pltpu.PrefetchScalarGridSpec(
            num_scalar_prefetch=1,
            grid=(1,),
            in_specs=in_specs,
            out_specs=[whole(o.shape) for o in out_shapes],
            scratch_shapes=list(scratch),
        ),
        out_shape=out_shapes,
        compiler_params=params(),
        cost_estimate=pl.CostEstimate(flops=flops, bytes_accessed=moved, transcendentals=0),
    )(scalars, *args)


def pick_body(s, k_own, v_own, k_far, v_far, own, far):
    @pl.when(s[2] == 0)
    def _():
        own[...] = k_own[...]
        far[...] = k_far[...]

    @pl.when(s[2] != 0)
    def _():
        own[...] = v_own[...]
        far[...] = v_far[...]


def attend_body(s, q, m0, m1, m2, m3, o0, o1, o2, o3, out, scores):
    y, zh, core = s[0], s[1], s[2]
    length = q.shape[0]
    half = m0.shape[0] // 2
    me = y * 2 + zh

    def run(keys, values):
        stacked = jnp.concatenate([q[:, :HEAD_DIM], q[:, HEAD_DIM:]], axis=0)
        top = None
        for b, key in enumerate(keys):
            for part in range(2):
                got = lax.dot_general(
                    stacked,
                    key[part * half : (part + 1) * half, :],
                    (((1,), (1,)), ((), ())),
                    preferred_element_type=f32,
                ) * (1.0 / math.sqrt(HEAD_DIM))
                if b == 0 and part == 0:
                    row = lax.broadcasted_iota(jnp.int32, got.shape, 0) & (length - 1)
                    col = lax.broadcasted_iota(jnp.int32, got.shape, 1)
                    got = jnp.where(col <= row, got, masked_score)
                else:
                    owner = ((y + 4 - b) & 3) * 2 + (zh if part == 0 else 1 - zh)
                    got = jnp.where(owner < me, got, masked_score)
                at = (2 * b + part) * half
                scores[:, at : at + half] = got
                peak = jnp.max(got, axis=1, keepdims=True)
                top = peak if top is None else jnp.maximum(top, peak)
        total = jnp.zeros_like(top)
        mixed = jnp.zeros(stacked.shape, f32)
        for b, value in enumerate(values):
            weights = jnp.exp(scores[:, 2 * half * b : 2 * half * (b + 1)] - top)
            total = total + jnp.sum(weights, axis=1, keepdims=True)
            mixed = mixed + jnp.dot(weights.astype(bf16), value[...], preferred_element_type=f32)
        done = (mixed / total).astype(bf16)
        out[:, :HEAD_DIM] = done[:length]
        out[:, HEAD_DIM:] = done[length:]

    @pl.when(core == 0)
    def _():
        run((m0, m1, m2, m3), (o0, o1, o2, o3))

    @pl.when(core != 0)
    def _():
        run((o0, o1, o2, o3), (m0, m1, m2, m3))


def project_body(count):
    def body(s, *refs):
        own = refs[:count]
        got = refs[count : 2 * count]
        here, there = refs[2 * count : 2 * count + 2]
        outs = refs[2 * count + 2 :]
        contract = (((1,), (1,)), ((), ()))
        for w, v, o in zip(own, got, outs):
            o[...] = (
                lax.dot_general(w[...], here[...], contract, preferred_element_type=f32)
                + lax.dot_general(v[...], there[...], contract, preferred_element_type=f32)
            ).astype(bf16)

    return body


def running_sums(decay):
    length = decay.shape[0]
    row = lax.broadcasted_iota(jnp.int32, (length, length), 0)
    col = lax.broadcasted_iota(jnp.int32, (length, length), 1)
    lower = (col <= row).astype(f32)
    down = jnp.dot(lower, decay, precision=lax.Precision.HIGHEST, preferred_element_type=f32)
    across = lax.dot_general(
        decay,
        lower,
        (((0,), (1,)), ((), ())),
        precision=lax.Precision.HIGHEST,
        preferred_element_type=f32,
    )
    return down, across


def widen(per_head, width):
    heads = per_head.shape[1]
    row = lax.broadcasted_iota(jnp.int32, (heads, heads * width), 0)
    col = lax.broadcasted_iota(jnp.int32, (heads, heads * width), 1)
    spread = ((col // width) == row).astype(f32)
    return jnp.dot(per_head, spread, precision=lax.Precision.HIGHEST, preferred_element_type=f32)


def closing_body(s, x, in_rows, decay, out):
    heads = decay.shape[1]
    inner = heads * SSM_HEAD_DIM
    length = x.shape[0]
    down, across = running_sums(decay[...])
    tail = widen(jnp.exp(down[length - 1 :, :] - down), SSM_HEAD_DIM)
    scaled = (x[...].astype(f32) * tail).astype(bf16)
    out[:inner, :] = lax.dot_general(
        scaled, in_rows[...], (((0,), (0,)), ((), ())), preferred_element_type=f32
    ).astype(bf16)
    fade = jnp.exp(across[:, length - 1 :])
    fade = jnp.broadcast_to(fade, (heads, N_STATE))
    high = fade.astype(bf16)
    out[inner : inner + 2 * heads, :] = jnp.concatenate(
        [high.astype(f32), fade - high.astype(f32)], axis=0
    ).astype(bf16)


def fades(state, inner, heads):
    both = state[inner : inner + 2 * heads, :].astype(f32)
    return both[:heads] + both[heads:]


def head_rows(h):
    return slice(h * SSM_HEAD_DIM, (h + 1) * SSM_HEAD_DIM)


def pair_body(heads):
    inner = heads * SSM_HEAD_DIM

    def body(s, mine, partner, out):
        def run(first, second):
            fade0 = fades(first, inner, heads)
            fade1 = fades(second, inner, heads)
            for h in range(heads):
                rows = head_rows(h)
                out[rows, :] = (
                    fade1[h : h + 1] * first[rows, :].astype(f32) + second[rows, :].astype(f32)
                ).astype(bf16)
            fade = fade0 * fade1
            high = fade.astype(bf16)
            out[inner : inner + 2 * heads, :] = jnp.concatenate(
                [high.astype(f32), fade - high.astype(f32)], axis=0
            ).astype(bf16)

        @pl.when(s[1] == 0)
        def _():
            run(mine, partner)

        @pl.when(s[1] != 0)
        def _():
            run(partner, mine)

    return body


def scan_body(s, x, in_rows, out_rows, decay, gain, partner, t1, t2, t3, out, entering):
    y, zh = s[0], s[1]
    heads = decay.shape[1]
    inner = heads * SSM_HEAD_DIM
    length = x.shape[0]
    down, across = running_sums(decay[...])
    fade1 = fades(t1, inner, heads)
    fade2 = fades(t2, inner, heads)
    fade0 = fades(partner, inner, heads)
    for h in range(heads):
        rows = head_rows(h)
        third = jnp.where(y >= 3, t3[rows, :].astype(f32), 0.0)
        second = jnp.where(y >= 2, t2[rows, :].astype(f32), 0.0)
        first = jnp.where(y >= 1, t1[rows, :].astype(f32), 0.0)
        state = first + fade1[h : h + 1] * (second + fade2[h : h + 1] * third)
        later = fade0[h : h + 1] * state + partner[rows, :].astype(f32)
        entering[rows, :] = jnp.where(zh == 0, state, later).astype(bf16)
    contract = (((1,), (1,)), ((), ()))
    wide = x[...].astype(f32)
    carried = widen(jnp.exp(down), SSM_HEAD_DIM) * lax.dot_general(
        out_rows[...], entering[...], contract, preferred_element_type=f32
    )
    rest = carried + widen(gain[...], SSM_HEAD_DIM) * wide
    affinity = lax.dot_general(
        out_rows[...], in_rows[...], contract, preferred_element_type=f32
    )
    row = lax.broadcasted_iota(jnp.int32, (length, length), 0)
    col = lax.broadcasted_iota(jnp.int32, (length, length), 1)
    causal = col <= row
    for h in range(heads):
        lanes = slice(h * SSM_HEAD_DIM, (h + 1) * SSM_HEAD_DIM)
        gaps = down[:, h : h + 1] - across[h : h + 1, :]
        mixing = affinity * jnp.exp(jnp.where(causal, gaps, masked_score))
        inside = jnp.dot(mixing.astype(bf16), x[:, lanes], preferred_element_type=f32)
        out[:, lanes] = (inside + rest[:, lanes]).astype(bf16)


def sum_body(count):
    def body(s, *refs):
        total = refs[0][...].astype(f32)
        for ref in refs[1:count]:
            total = total + ref[...].astype(f32)
        refs[count][...] = total.astype(bf16)

    return body


def on_device(
    scan_input,
    input_map,
    output_map,
    log_decay,
    skip_gain,
    query_rows,
    key_rows,
    value_rows,
    out_weight,
):
    section = lax.axis_index("section")
    tp = lax.axis_index("tp")
    y, zh = section // 2, section % 2
    core, chip = tp % 2, tp // 2
    group = tp // (TP // GROUPS)
    shape = jax.ShapeDtypeStruct
    scalars = jnp.stack(
        [y, zh, core, group, group ^ 1] + [chip ^ r for r in range(CHIPS)]
    ).astype(jnp.int32)

    length = query_rows.shape[0]
    head_block = (length, HEAD_DIM)
    own_spec = pl.BlockSpec(head_block, lambda i, s: (0, s[3]))
    far_spec = pl.BlockSpec(head_block, lambda i, s: (0, s[4]))
    block = shape(head_block, bf16)
    own, far = call(
        pick_body,
        scalars,
        [own_spec, own_spec, far_spec, far_spec],
        [block, block],
        (key_rows, value_rows, key_rows, value_rows),
        moved=6 * length * HEAD_DIM * 2,
    )
    pair = jnp.concatenate([own, swap_zh_near(far)], axis=0)

    weights = out_weight.reshape(CHIPS, 2, ROWS, out_weight.shape[1])
    sent = lax.dynamic_index_in_dim(weights, 1 - core, 1, keepdims=False)
    got_weight = swap_core(sent.reshape(CHIPS * ROWS, out_weight.shape[1]))

    heads = log_decay.shape[1]
    inner = heads * SSM_HEAD_DIM
    state_shape = shape((inner + 2 * heads, N_STATE), bf16)
    x_spec = whole(scan_input.shape)
    decay_spec = whole(log_decay.shape)
    (closing,) = call(
        closing_body,
        scalars,
        [x_spec, own_spec, decay_spec],
        [state_shape],
        (scan_input, input_map, log_decay),
        flops=2 * length * inner * N_STATE,
        moved=600000,
    )

    pairs = [pair] + [shift_y(pair, d) for d in (1, 2, 3)]
    others = [swap_core(p) for p in pairs]
    (attended,) = call(
        attend_body,
        scalars,
        [whole(query_rows.shape)] + [whole(pair.shape)] * 8,
        [shape(query_rows.shape, bf16)],
        (query_rows, *pairs, *others),
        scratch=[pltpu.VMEM((2 * length, 4 * pair.shape[0]), f32)],
        flops=4 * 2 * length * 4 * pair.shape[0] * HEAD_DIM,
        moved=2000000,
    )
    attended_there = swap_core(attended)

    partner = swap_zh(closing)
    (joined,) = call(
        pair_body(heads),
        scalars,
        [whole(closing.shape)] * 2,
        [state_shape],
        (closing, partner),
        moved=400000,
    )
    earlier = [shift_y(joined, d) for d in (1, 2, 3)]

    weight_block = (ROWS, out_weight.shape[1])
    parts = []
    for start in range(0, CHIPS, 4):
        offsets = list(range(start, start + 4))
        own_specs = [
            pl.BlockSpec(weight_block, lambda i, s, r=r: (s[5 + r] * 2 + s[2], 0)) for r in offsets
        ]
        got_specs = [pl.BlockSpec(weight_block, lambda i, s, r=r: (s[5 + r], 0)) for r in offsets]
        parts += call(
            project_body(4),
            scalars,
            own_specs + got_specs + [whole(attended.shape)] * 2,
            [shape((ROWS, length), bf16)] * 4,
            [out_weight] * 4 + [got_weight] * 4 + [attended, attended_there],
            flops=4 * 2 * ROWS * 512 * length,
            moved=2000000,
        )
    arrived = [parts[0]] + [swap_chip(parts[r], r) for r in range(1, CHIPS)]
    (attn_out,) = call(
        sum_body(CHIPS),
        scalars,
        [whole((ROWS, length))] * CHIPS,
        [shape((ROWS, length), bf16)],
        arrived,
        moved=17 * ROWS * length * 2,
    )

    (ssm_out,) = call(
        scan_body,
        scalars,
        [x_spec, own_spec, own_spec, decay_spec, whole((1, heads))]
        + [whole(closing.shape)] * 4,
        [shape(scan_input.shape, bf16)],
        (
            scan_input,
            input_map,
            output_map,
            log_decay,
            skip_gain.reshape(1, heads),
            partner,
            *earlier,
        ),
        scratch=[pltpu.VMEM((inner, N_STATE), bf16)],
        flops=2 * heads * length * length * SSM_HEAD_DIM,
        moved=1500000,
    )
    return (ssm_out, attn_out)


def solution(mesh):
    placed = (
        P("section", "tp"),
        P("section", None),
        P("section", None),
        P("section", "tp"),
        P("tp"),
        P("section", "tp"),
        P("section", None),
        P("section", None),
        P(None, "tp"),
    )
    return jax.shard_map(
        on_device,
        mesh=mesh,
        in_specs=placed,
        out_specs=(P("section", "tp"), P("tp", "section")),
        check_vma=False,
    )
```

time: 333 us -> 107 us (0.32)
  the two profiles are of different devices: /device:TPU:8 before, /device:TPU:33 now
where the time goes in v1:
time: 107 us
  starting transfers between devices  50.2 us (47%)
  waiting for transfers between devices  31.2 us (29%)
  Pallas kernels  20.2 us (19%)
  local copies, waits for them, and re-layouts  4.54 us (4%)
    ppermute x15, starting transfers between devices, swap_chip(): return lax.ppermute(block, 'tp', [(t, t ^ 2 * offset) for t in range(TP)])  25.6 us
    ppermute x15, waiting for transfers between devices, swap_chip(): return lax.ppermute(block, 'tp', [(t, t ^ 2 * offset) for t in range(TP)])  22.5 us
    pallas_call x10, Pallas kernels, call(): pl.pallas_call(body, grid_spec=pltpu.PrefetchScalarGridSpec(num_scalar_pr...  20.2 us
    ppermute x6, starting transfers between devices, shift_y(): return lax.ppermute(block, 'section', route)  9.54 us
    ppermute x6, starting transfers between devices, swap_core(): return lax.ppermute(block, 'tp', [(t, t ^ 1) for t in range(TP)])  5.44 us
    ppermute x1, starting transfers between devices, swap_zh_near(): return lax.ppermute(block, ('section', 'tp'), route)  5.21 us
    ppermute x1, starting transfers between devices, swap_zh(): return lax.ppermute(block, 'section', [(s, s ^ 1) for s in range(SECTIONS)])  4.35 us
    ppermute x1, waiting for transfers between devices, swap_zh_near(): return lax.ppermute(block, ('section', 'tp'), route)  3.8 us
  transfers between devices with their start and end apart: 29, of which 11 were waited for; matrix products, arithmetic and copies ran while one was open for 0% of the time, Pallas kernels for 18%

profile of v1, /device:TPU:33, one launch (start us, length us, event | category | flops | bytes accessed | tf_op | source)
XLA Modules:
  0.0 107.0 jit_solution(3743505856785764015)
XLA Ops:
  0.7 3.2 %constant_dynamic-slice_fusion = bf16[16,1,256,256]{3,2,1,0:T(8,128)(2,1)} fusion(bf16[16,2,256,256]{3,2,1,0:T(8,128)(2,1)} %bitcast.27, s32[]{:T(128)S(6)} %select_n.30), kind=kLoop, calls=%fused_computation.2 | loop fusion | bytes 4194308 | tf_op jit(solution)/shard_map/jit(dynamic_index_in_dim)/dynamic_slice | solution.py:315
  3.9 0.7 collective-permute-start.4
  4.6 0.1 stack.87.s
  4.7 0.6 shard_map.107
  5.3 5.2 %collective-permute-start.5 = (bf16[256,128]{1,0:T(8,128)(2,1)S(1)}, bf16[256,128]{1,0:T(8,128)(2,1)S(1)}, u32[]{:S(2)}, u32[]{:S(2)}) collective-permute-start(bf16[256,128]{1,0:T(8,128)(2,1)S(1)} %get-tuple-element.21), channel_id=1, source_target_pairs={{0,36},{1,37},{2,38},{3,39},{4,32},{5,33},{6,34},{7,35},{8,44},{9,... | collective-permute-start | bytes 196616 | tf_op jit(solution)/shard_map/ppermute | solution.py:45
  10.6 3.8 %collective-permute-done.5 = bf16[256,128]{1,0:T(8,128)(2,1)S(1)} collective-permute-done((bf16[256,128]{1,0:T(8,128)(2,1)S(1)}, bf16[256,128]{1,0:T(8,128)(2,1)S(1)}, u32[]{:S(2)}, u32[]{:S(2)}) %collective-permute-start.5) | collective-permute-done | bytes 65568 | tf_op jit(solution)/shard_map/ppermute | solution.py:45
  14.4 1.4 %collective-permute-start.6 = (bf16[512,128]{1,0:T(8,128)(2,1)S(1)}, bf16[512,128]{1,0:T(8,128)(2,1)S(1)}, u32[]{:S(2)}, u32[]{:S(2)}) collective-permute-start(bf16[512,128]{1,0:T(8,128)(2,1)S(1)} %constant_dynamic-update-slice_fusion.m0), channel_id=1, source_target_pairs={{0,64},{32,96},{64,128},{96,160},{128,192},{160,224},{192,0},{224,... | collective-permute-start | bytes 393224 | tf_op jit(solution)/shard_map/ppermute | solution.py:38
  15.7 2.6 %collective-permute-start.7 = (bf16[512,128]{1,0:T(8,128)(2,1)S(1)}, bf16[512,128]{1,0:T(8,128)(2,1)S(1)}, u32[]{:S(2)}, u32[]{:S(2)}) collective-permute-start(bf16[512,128]{1,0:T(8,128)(2,1)S(1)} %constant_dynamic-update-slice_fusion.m0), channel_id=1, source_target_pairs={{0,128},{32,160},{64,192},{96,224},{128,0},{160,32},{192,64},{224,... | collective-permute-start | bytes 393224 | tf_op jit(solution)/shard_map/ppermute | solution.py:38
  18.4 1.1 collective-permute-start.8
  19.4 1.5 %collective-permute-start.9 = (bf16[512,128]{1,0:T(8,128)(2,1)S(1)}, bf16[512,128]{1,0:T(8,128)(2,1)S(1)}, u32[]{:S(2)}, u32[]{:S(2)}) collective-permute-start(bf16[512,128]{1,0:T(8,128)(2,1)S(1)} %constant_dynamic-update-slice_fusion.m0), channel_id=1, source_target_pairs={{0,1},{1,0},{2,3},{3,2},{4,5},{5,4},{6,7},{7,6},{8,9},{9,8},{10,11... | collective-permute-start | bytes 393224 | tf_op jit(solution)/shard_map/ppermute | solution.py:29
  20.9 0.0 collective-permute-done.6.m1
  20.9 0.7 collective-permute-start.10
  21.6 2.5 %collective-permute-done.7.m2 = bf16[512,128]{1,0:T(8,128)(2,1)S(1)} collective-permute-done((bf16[512,128]{1,0:T(8,128)(2,1)S(1)}, bf16[512,128]{1,0:T(8,128)(2,1)S(1)}, u32[]{:S(2)}, u32[]{:S(2)}) %collective-permute-start.7) | collective-permute-done | bytes 131104 | tf_op jit(solution)/shard_map/ppermute | solution.py:38
  24.1 1.5 %collective-permute-start.11 = (bf16[512,128]{1,0:T(8,128)(2,1)S(1)}, bf16[512,128]{1,0:T(8,128)(2,1)S(1)}, u32[]{:S(2)}, u32[]{:S(2)}) collective-permute-start(bf16[512,128]{1,0:T(8,128)(2,1)S(1)} %collective-permute-done.7.m2), channel_id=1, source_target_pairs={{0,1},{1,0},{2,3},{3,2},{4,5},{5,4},{6,7},{7,6},{8,9},{9,8},{10,11... | collective-permute-start | bytes 393224 | tf_op jit(solution)/shard_map/ppermute | solution.py:29
  25.6 0.0 collective-permute-done.8.m3
  25.6 0.0 collective-permute-start.12
  25.6 0.1 copy.12.decay
  25.8 0.0 copy-start.2
  25.8 1.0 copy-done.2
  26.8 1.9 %shard_map.104.mine = bf16[528,128]{1,0:T(8,128)(2,1)S(1)} custom-call(s32[21]{0:T(128)S(1)} %stack.87.s, bf16[256,512]{1,0:T(8,128)(2,1)S(1)} %copy-done.4, bf16[256,1024]{1,0:T(8,128)(2,1)S(1)} %copy-done.2, f32[256,8]{1,0:T(8,128)S(1)} %copy.12.decay), custom_call_target="tpu_custom_call" | custom-call | flops 33554432 | bytes 600000 | tf_op jit(solution)/shard_map/pallas_call | solution.py:61
  28.8 4.3 %collective-permute-start = (bf16[528,128]{1,0:T(8,128)(2,1)S(1)}, bf16[528,128]{1,0:T(8,128)(2,1)S(1)}, u32[]{:S(2)}, u32[]{:S(2)}) collective-permute-start(bf16[528,128]{1,0:T(8,128)(2,1)S(1)} %shard_map.104.mine), channel_id=1, source_target_pairs={{0,32},{32,0},{64,96},{96,64},{128,160},{160,128},{192,224},{224,1... | collective-permute-start | bytes 405512 | tf_op jit(solution)/shard_map/ppermute | solution.py:33
  33.1 0.0 collective-permute-done.10.o1
  33.1 0.0 collective-permute-done.11.o2
  33.1 0.0 collective-permute-done.12.o3
  33.1 4.1 %shard_map.108.refs_8_ = bf16[256,256]{1,0:T(8,128)(2,1)S(1)} custom-call(s32[21]{0:T(128)S(1)} %stack.87.s, bf16[256,256]{1,0:T(8,128)(2,1)S(1)} %copy-done.7, bf16[512,128]{1,0:T(8,128)(2,1)S(1)} %constant_dynamic-update-slice_fusion.m0, bf16[512,128]{1,0:T(8,128)(2,1)S(1)} %collective-permute-done.6.m1, bf16[512,128]{1,0:T(8,128)(2,1)S(1)} %collective-permute-done.7.m2, ...), custom_call_target="tpu_custom_call" | custom-call | flops 536870912 | bytes 2000000 | tf_op jit(solution)/shard_map/pallas_call | solution.py:61
  37.3 1.1 collective-permute-start.13
  38.3 2.4 %collective-permute-done.partner = bf16[528,128]{1,0:T(8,128)(2,1)S(1)} collective-permute-done((bf16[528,128]{1,0:T(8,128)(2,1)S(1)}, bf16[528,128]{1,0:T(8,128)(2,1)S(1)}, u32[]{:S(2)}, u32[]{:S(2)}) %collective-permute-start) | collective-permute-done | bytes 135200 | tf_op jit(solution)/shard_map/ppermute | solution.py:33
  40.7 0.6 shard_map.105
  41.3 1.1 %collective-permute-start.1 = (bf16[528,128]{1,0:T(8,128)(2,1)S(1)}, bf16[528,128]{1,0:T(8,128)(2,1)S(1)}, u32[]{:S(2)}, u32[]{:S(2)}) collective-permute-start(bf16[528,128]{1,0:T(8,128)(2,1)S(1)} %shard_map.105), channel_id=1, source_target_pairs={{0,64},{32,96},{64,128},{96,160},{128,192},{160,224},{192,0},{224,... | collective-permute-start | bytes 405512 | tf_op jit(solution)/shard_map/ppermute | solution.py:38
  42.4 2.6 %collective-permute-start.2 = (bf16[528,128]{1,0:T(8,128)(2,1)S(1)}, bf16[528,128]{1,0:T(8,128)(2,1)S(1)}, u32[]{:S(2)}, u32[]{:S(2)}) collective-permute-start(bf16[528,128]{1,0:T(8,128)(2,1)S(1)} %shard_map.105), channel_id=1, source_target_pairs={{0,128},{32,160},{64,192},{96,224},{128,0},{160,32},{192,64},{224,... | collective-permute-start | bytes 405512 | tf_op jit(solution)/shard_map/ppermute | solution.py:38
  45.0 0.8 collective-permute-start.3
  45.8 0.0 collective-permute-done.13.refs_9_
  45.8 0.0 collective-permute-done.4.refs_4_.refs_5_.refs_6_.refs_7_
  45.8 2.1 %shard_map.112 = (bf16[256,256]{1,0:T(8,128)(2,1)S(1)}, bf16[256,256]{1,0:T(8,128)(2,1)S(1)}, bf16[256,256]{1,0:T(8,128)(2,1)S(1)}, bf16[256,256]{1,0:T(8,128)(2,1)S(1)}) custom-call(s32[21]{0:T(128)S(1)} %stack.87.s, bf16[8192,256]{1,0:T(8,128)(2,1)} %refs_3_.7, bf16[8192,256]{1,0:T(8,128)(2,1)} %refs_3_.7, bf16[8192,256]{1,0:T(8,128)(2,1)} %refs_3_.7, ...), custom_call_target="tpu_custom_call" | custom-call | flops 268435456 | bytes 2000000 | tf_op jit(solution)/shard_map/pallas_call | solution.py:61
  47.9 2.6 %collective-permute-start.25 = (bf16[256,256]{1,0:T(8,128)(2,1)S(1)}, bf16[256,256]{1,0:T(8,128)(2,1)S(1)}, u32[]{:S(2)}, u32[]{:S(2)}) collective-permute-start(bf16[256,256]{1,0:T(8,128)(2,1)S(1)} %get-tuple-element.34), channel_id=1, source_target_pairs={{0,24},{1,25},{2,26},{3,27},{4,28},{5,29},{6,30},{7,31},{8,16},{9,... | collective-permute-start | bytes 393224 | tf_op jit(solution)/shard_map/ppermute | solution.py:49
  50.5 2.1 %shard_map.111 = (bf16[256,256]{1,0:T(8,128)(2,1)S(1)}, bf16[256,256]{1,0:T(8,128)(2,1)S(1)}, bf16[256,256]{1,0:T(8,128)(2,1)S(1)}, bf16[256,256]{1,0:T(8,128)(2,1)S(1)}) custom-call(s32[21]{0:T(128)S(1)} %stack.87.s, bf16[8192,256]{1,0:T(8,128)(2,1)} %refs_3_.7, bf16[8192,256]{1,0:T(8,128)(2,1)} %refs_3_.7, bf16[8192,256]{1,0:T(8,128)(2,1)} %refs_3_.7, ...), custom_call_target="tpu_custom_call" | custom-call | flops 268435456 | bytes 2000000 | tf_op jit(solution)/shard_map/pallas_call | solution.py:61
  52.6 0.0 collective-permute-done.1.t1
  52.6 4.1 %collective-permute-start.27 = (bf16[256,256]{1,0:T(8,128)(2,1)S(1)}, bf16[256,256]{1,0:T(8,128)(2,1)S(1)}, u32[]{:S(2)}, u32[]{:S(2)}) collective-permute-start(bf16[256,256]{1,0:T(8,128)(2,1)S(1)} %get-tuple-element.36), channel_id=1, source_target_pairs={{0,28},{1,29},{2,30},{3,31},{4,24},{5,25},{6,26},{7,27},{8,20},{9,... | collective-permute-start | bytes 393224 | tf_op jit(solution)/shard_map/ppermute | solution.py:49
  56.7 0.0 collective-permute-done.2.t2
  56.7 0.6 collective-permute-start.28
  57.4 0.0 collective-permute-done.3.t3
  57.4 0.3 collective-permute-start.21
  57.7 2.1 %shard_map.110 = (bf16[256,256]{1,0:T(8,128)(2,1)S(1)}, bf16[256,256]{1,0:T(8,128)(2,1)S(1)}, bf16[256,256]{1,0:T(8,128)(2,1)S(1)}, bf16[256,256]{1,0:T(8,128)(2,1)S(1)}) custom-call(s32[21]{0:T(128)S(1)} %stack.87.s, bf16[8192,256]{1,0:T(8,128)(2,1)} %refs_3_.7, bf16[8192,256]{1,0:T(8,128)(2,1)} %refs_3_.7, bf16[8192,256]{1,0:T(8,128)(2,1)} %refs_3_.7, ...), custom_call_target="tpu_custom_call" | custom-call | flops 268435456 | bytes 2000000 | tf_op jit(solution)/shard_map/pallas_call | solution.py:61
  59.8 3.5 %collective-permute-start.22 = (bf16[256,256]{1,0:T(8,128)(2,1)S(1)}, bf16[256,256]{1,0:T(8,128)(2,1)S(1)}, u32[]{:S(2)}, u32[]{:S(2)}) collective-permute-start(bf16[256,256]{1,0:T(8,128)(2,1)S(1)} %get-tuple-element.31), channel_id=1, source_target_pairs={{0,18},{1,19},{2,16},{3,17},{4,22},{5,23},{6,20},{7,21},{8,26},{9,... | collective-permute-start | bytes 393224 | tf_op jit(solution)/shard_map/ppermute | solution.py:49
  63.3 0.9 collective-permute-start.23
  64.2 1.4 %collective-permute-done.27.refs_14_ = bf16[256,256]{1,0:T(8,128)(2,1)S(1)} collective-permute-done((bf16[256,256]{1,0:T(8,128)(2,1)S(1)}, bf16[256,256]{1,0:T(8,128)(2,1)S(1)}, u32[]{:S(2)}, u32[]{:S(2)}) %collective-permute-start.27) | collective-permute-done | bytes 131104 | tf_op jit(solution)/shard_map/ppermute | solution.py:49
  65.6 1.8 %collective-permute-start.24 = (bf16[256,256]{1,0:T(8,128)(2,1)S(1)}, bf16[256,256]{1,0:T(8,128)(2,1)S(1)}, u32[]{:S(2)}, u32[]{:S(2)}) collective-permute-start(bf16[256,256]{1,0:T(8,128)(2,1)S(1)} %get-tuple-element.33), channel_id=1, source_target_pairs={{0,22},{1,23},{2,20},{3,21},{4,18},{5,19},{6,16},{7,17},{8,30},{9,... | collective-permute-start | bytes 393224 | tf_op jit(solution)/shard_map/ppermute | solution.py:49
  67.3 4.1 %collective-permute-done.28.refs_15_ = bf16[256,256]{1,0:T(8,128)(2,1)S(1)} collective-permute-done((bf16[256,256]{1,0:T(8,128)(2,1)S(1)}, bf16[256,256]{1,0:T(8,128)(2,1)S(1)}, u32[]{:S(2)}, u32[]{:S(2)}) %collective-permute-start.28) | collective-permute-done | bytes 131104 | tf_op jit(solution)/shard_map/ppermute | solution.py:49
  71.5 0.0 copy-start.6
  71.5 3.0 %collective-permute-start.18 = (bf16[256,256]{1,0:T(8,128)(2,1)S(1)}, bf16[256,256]{1,0:T(8,128)(2,1)S(1)}, u32[]{:S(2)}, u32[]{:S(2)}) collective-permute-start(bf16[256,256]{1,0:T(8,128)(2,1)S(1)} %get-tuple-element.27), channel_id=1, source_target_pairs={{0,10},{1,11},{2,8},{3,9},{4,14},{5,15},{6,12},{7,13},{8,2},{9,3},... | collective-permute-start | bytes 393224 | tf_op jit(solution)/shard_map/ppermute | solution.py:49
  74.5 2.1 %shard_map.109 = (bf16[256,256]{1,0:T(8,128)(2,1)S(1)}, bf16[256,256]{1,0:T(8,128)(2,1)S(1)}, bf16[256,256]{1,0:T(8,128)(2,1)S(1)}, bf16[256,256]{1,0:T(8,128)(2,1)S(1)}) custom-call(s32[21]{0:T(128)S(1)} %stack.87.s, bf16[8192,256]{1,0:T(8,128)(2,1)} %refs_3_.7, bf16[8192,256]{1,0:T(8,128)(2,1)} %refs_3_.7, bf16[8192,256]{1,0:T(8,128)(2,1)} %refs_3_.7, ...), custom_call_target="tpu_custom_call" | custom-call | flops 268435456 | bytes 2000000 | tf_op jit(solution)/shard_map/pallas_call | solution.py:61
  76.6 0.6 collective-permute-start.19
  77.2 0.2 collective-permute-done.23.refs_10_
  77.3 1.7 %collective-permute-start.20 = (bf16[256,256]{1,0:T(8,128)(2,1)S(1)}, bf16[256,256]{1,0:T(8,128)(2,1)S(1)}, u32[]{:S(2)}, u32[]{:S(2)}) collective-permute-start(bf16[256,256]{1,0:T(8,128)(2,1)S(1)} %get-tuple-element.29), channel_id=1, source_target_pairs={{0,14},{1,15},{2,12},{3,13},{4,10},{5,11},{6,8},{7,9},{8,6},{9,7},... | collective-permute-start | bytes 393224 | tf_op jit(solution)/shard_map/ppermute | solution.py:49
  79.0 1.1 %collective-permute-done.24.refs_11_ = bf16[256,256]{1,0:T(8,128)(2,1)S(1)} collective-permute-done((bf16[256,256]{1,0:T(8,128)(2,1)S(1)}, bf16[256,256]{1,0:T(8,128)(2,1)S(1)}, u32[]{:S(2)}, u32[]{:S(2)}) %collective-permute-start.24) | collective-permute-done | bytes 131104 | tf_op jit(solution)/shard_map/ppermute | solution.py:49
  80.2 0.9 collective-permute-start.14
  81.1 4.8 %collective-permute-start.15 = (bf16[256,256]{1,0:T(8,128)(2,1)S(1)}, bf16[256,256]{1,0:T(8,128)(2,1)S(1)}, u32[]{:S(2)}, u32[]{:S(2)}) collective-permute-start(bf16[256,256]{1,0:T(8,128)(2,1)S(1)} %get-tuple-element.24), channel_id=1, source_target_pairs={{0,4},{1,5},{2,6},{3,7},{4,0},{5,1},{6,2},{7,3},{8,12},{9,13},{10,... | collective-permute-start | bytes 393224 | tf_op jit(solution)/shard_map/ppermute | solution.py:49
  86.0 0.8 collective-permute-start.16
  86.7 3.1 %shard_map.106 = bf16[256,512]{1,0:T(8,128)(2,1)} custom-call(s32[21]{0:T(128)S(1)} %stack.87.s, bf16[256,512]{1,0:T(8,128)(2,1)S(1)} %copy-done.4, bf16[256,1024]{1,0:T(8,128)(2,1)S(1)} %copy-done.3, bf16[256,1024]{1,0:T(8,128)(2,1)S(1)} %copy-done.5, f32[256,8]{1,0:T(8,128)S(1)} %copy.12.decay, f32[1,8]{1,0:T(1,128)S(1)} %bitcast.26, ...), custom_call_target="tpu_custom_call" | custom-call | flops 67108864 | bytes 1500000 | tf_op jit(solution)/shard_map/pallas_call | solution.py:61
  89.8 1.9 %collective-permute-done.19.refs_6_ = bf16[256,256]{1,0:T(8,128)(2,1)S(1)} collective-permute-done((bf16[256,256]{1,0:T(8,128)(2,1)S(1)}, bf16[256,256]{1,0:T(8,128)(2,1)S(1)}, u32[]{:S(2)}, u32[]{:S(2)}) %collective-permute-start.19) | collective-permute-done | bytes 131104 | tf_op jit(solution)/shard_map/ppermute | solution.py:49
  91.7 6.6 %collective-permute-done.20.refs_7_ = bf16[256,256]{1,0:T(8,128)(2,1)S(1)} collective-permute-done((bf16[256,256]{1,0:T(8,128)(2,1)S(1)}, bf16[256,256]{1,0:T(8,128)(2,1)S(1)}, u32[]{:S(2)}, u32[]{:S(2)}) %collective-permute-start.20) | collective-permute-done | bytes 131104 | tf_op jit(solution)/shard_map/ppermute | solution.py:49
  98.3 2.8 %collective-permute-done.15.refs_2_ = bf16[256,256]{1,0:T(8,128)(2,1)S(1)} collective-permute-done((bf16[256,256]{1,0:T(8,128)(2,1)S(1)}, bf16[256,256]{1,0:T(8,128)(2,1)S(1)}, u32[]{:S(2)}, u32[]{:S(2)}) %collective-permute-start.15) | collective-permute-done | bytes 131104 | tf_op jit(solution)/shard_map/ppermute | solution.py:49
  101.1 4.4 %collective-permute-done.16.refs_3_ = bf16[256,256]{1,0:T(8,128)(2,1)S(1)} collective-permute-done((bf16[256,256]{1,0:T(8,128)(2,1)S(1)}, bf16[256,256]{1,0:T(8,128)(2,1)S(1)}, u32[]{:S(2)}, u32[]{:S(2)}) %collective-permute-start.16) | collective-permute-done | bytes 131104 | tf_op jit(solution)/shard_map/ppermute | solution.py:49
  105.5 1.5 %shard_map.113 = bf16[256,256]{1,0:T(8,128)(2,1)} custom-call(s32[21]{0:T(128)S(1)} %stack.87.s, bf16[256,256]{1,0:T(8,128)(2,1)S(1)} %get-tuple-element.22.refs_0_, bf16[256,256]{1,0:T(8,128)(2,1)S(1)} %collective-permute-done.14.refs_1_, bf16[256,256]{1,0:T(8,128)(2,1)S(1)} %collective-permute-done.15.refs_2_, ...), custom_call_target="tpu_custom_call" | custom-call | bytes 2228224 | tf_op jit(solution)/shard_map/pallas_call | solution.py:61
  (27 shorter events, 0.1 us)
Async XLA Ops:
  0.6 4.0 %copy-start = (bf16[256,1024]{1,0:T(8,128)(2,1)S(1)}, bf16[256,1024]{1,0:T(8,128)(2,1)}, u32[]{:S(2)}) copy-start(bf16[256,1024]{1,0:T(8,128)(2,1)} %k_far.1) | copy-start | bytes 1572868
  0.7 4.0 %copy-start.1 = (bf16[256,1024]{1,0:T(8,128)(2,1)S(1)}, bf16[256,1024]{1,0:T(8,128)(2,1)}, u32[]{:S(2)}) copy-start(bf16[256,1024]{1,0:T(8,128)(2,1)} %v_far.1) | copy-start | bytes 1572868
  3.9 21.7 %copy-start.8 = (f32[256,8]{0,1:T(8,128)S(1)}, f32[256,8]{0,1:T(8,128)}, u32[]{:S(2)}) copy-start(f32[256,8]{0,1:T(8,128)} %param.12) | copy-start | bytes 24580
  3.9 21.9 %copy-start.4 = (bf16[256,512]{1,0:T(8,128)(2,1)S(1)}, bf16[256,512]{1,0:T(8,128)(2,1)}, u32[]{:S(2)}) copy-start(bf16[256,512]{1,0:T(8,128)(2,1)} %x.3) | copy-start | bytes 786436
  3.9 29.2 %copy-start.7 = (bf16[256,256]{1,0:T(8,128)(2,1)S(1)}, bf16[256,256]{1,0:T(8,128)(2,1)}, u32[]{:S(2)}) copy-start(bf16[256,256]{1,0:T(8,128)(2,1)} %q.1) | copy-start | bytes 393220
  3.9 41.9 %collective-permute-start.4 = (bf16[4096,256]{1,0:T(8,128)(2,1)}, bf16[4096,256]{1,0:T(8,128)(2,1)S(1)}, u32[]{:S(2)}, u32[]{:S(2)}) collective-permute-start(bf16[4096,256]{1,0:T(8,128)(2,1)} %bitcast.23), channel_id=1, source_target_pairs={{0,1},{1,0},{2,3},{3,2},{4,5},{5,4},{6,7},{7,6},{8,9},{9,8},{10,11... | collective-permute-start | bytes 6291464 | tf_op jit(solution)/shard_map/ppermute | solution.py:29
  5.3 9.0 %collective-permute-start.5 = (bf16[256,128]{1,0:T(8,128)(2,1)S(1)}, bf16[256,128]{1,0:T(8,128)(2,1)S(1)}, u32[]{:S(2)}, u32[]{:S(2)}) collective-permute-start(bf16[256,128]{1,0:T(8,128)(2,1)S(1)} %get-tuple-element.21), channel_id=1, source_target_pairs={{0,36},{1,37},{2,38},{3,39},{4,32},{5,33},{6,34},{7,35},{8,44},{9,... | collective-permute-start | bytes 196616 | tf_op jit(solution)/shard_map/ppermute | solution.py:45
  14.4 6.5 %collective-permute-start.6 = (bf16[512,128]{1,0:T(8,128)(2,1)S(1)}, bf16[512,128]{1,0:T(8,128)(2,1)S(1)}, u32[]{:S(2)}, u32[]{:S(2)}) collective-permute-start(bf16[512,128]{1,0:T(8,128)(2,1)S(1)} %constant_dynamic-update-slice_fusion.m0), channel_id=1, source_target_pairs={{0,64},{32,96},{64,128},{96,160},{128,192},{160,224},{192,0},{224,... | collective-permute-start | bytes 393224 | tf_op jit(solution)/shard_map/ppermute | solution.py:38
  15.7 8.4 %collective-permute-start.7 = (bf16[512,128]{1,0:T(8,128)(2,1)S(1)}, bf16[512,128]{1,0:T(8,128)(2,1)S(1)}, u32[]{:S(2)}, u32[]{:S(2)}) collective-permute-start(bf16[512,128]{1,0:T(8,128)(2,1)S(1)} %constant_dynamic-update-slice_fusion.m0), channel_id=1, source_target_pairs={{0,128},{32,160},{64,192},{96,224},{128,0},{160,32},{192,64},{224,... | collective-permute-start | bytes 393224 | tf_op jit(solution)/shard_map/ppermute | solution.py:38
  18.4 7.3 %collective-permute-start.8 = (bf16[512,128]{1,0:T(8,128)(2,1)S(1)}, bf16[512,128]{1,0:T(8,128)(2,1)S(1)}, u32[]{:S(2)}, u32[]{:S(2)}) collective-permute-start(bf16[512,128]{1,0:T(8,128)(2,1)S(1)} %constant_dynamic-update-slice_fusion.m0), channel_id=1, source_target_pairs={{0,192},{32,224},{64,0},{96,32},{128,64},{160,96},{192,128},{224,1... | collective-permute-start | bytes 393224 | tf_op jit(solution)/shard_map/ppermute | solution.py:38
  19.4 9.3 %collective-permute-start.9 = (bf16[512,128]{1,0:T(8,128)(2,1)S(1)}, bf16[512,128]{1,0:T(8,128)(2,1)S(1)}, u32[]{:S(2)}, u32[]{:S(2)}) collective-permute-start(bf16[512,128]{1,0:T(8,128)(2,1)S(1)} %constant_dynamic-update-slice_fusion.m0), channel_id=1, source_target_pairs={{0,1},{1,0},{2,3},{3,2},{4,5},{5,4},{6,7},{7,6},{8,9},{9,8},{10,11... | collective-permute-start | bytes 393224 | tf_op jit(solution)/shard_map/ppermute | solution.py:29
  20.9 12.2 %collective-permute-start.10 = (bf16[512,128]{1,0:T(8,128)(2,1)S(1)}, bf16[512,128]{1,0:T(8,128)(2,1)S(1)}, u32[]{:S(2)}, u32[]{:S(2)}) collective-permute-start(bf16[512,128]{1,0:T(8,128)(2,1)S(1)} %collective-permute-done.6.m1), channel_id=1, source_target_pairs={{0,1},{1,0},{2,3},{3,2},{4,5},{5,4},{6,7},{7,6},{8,9},{9,8},{10,11... | collective-permute-start | bytes 393224 | tf_op jit(solution)/shard_map/ppermute | solution.py:29
  24.1 9.0 %collective-permute-start.11 = (bf16[512,128]{1,0:T(8,128)(2,1)S(1)}, bf16[512,128]{1,0:T(8,128)(2,1)S(1)}, u32[]{:S(2)}, u32[]{:S(2)}) collective-permute-start(bf16[512,128]{1,0:T(8,128)(2,1)S(1)} %collective-permute-done.7.m2), channel_id=1, source_target_pairs={{0,1},{1,0},{2,3},{3,2},{4,5},{5,4},{6,7},{7,6},{8,9},{9,8},{10,11... | collective-permute-start | bytes 393224 | tf_op jit(solution)/shard_map/ppermute | solution.py:29
  25.6 7.5 %collective-permute-start.12 = (bf16[512,128]{1,0:T(8,128)(2,1)S(1)}, bf16[512,128]{1,0:T(8,128)(2,1)}, u32[]{:S(2)}, u32[]{:S(2)}) collective-permute-start(bf16[512,128]{1,0:T(8,128)(2,1)S(1)} %collective-permute-done.8.m3), channel_id=1, source_target_pairs={{0,1},{1,0},{2,3},{3,2},{4,5},{5,4},{6,7},{7,6},{8,9},{9,8},{10,11... | collective-permute-start | bytes 393224 | tf_op jit(solution)/shard_map/ppermute | solution.py:29
  25.8 1.0 copy-start.2
  28.8 11.9 %collective-permute-start = (bf16[528,128]{1,0:T(8,128)(2,1)S(1)}, bf16[528,128]{1,0:T(8,128)(2,1)S(1)}, u32[]{:S(2)}, u32[]{:S(2)}) collective-permute-start(bf16[528,128]{1,0:T(8,128)(2,1)S(1)} %shard_map.104.mine), channel_id=1, source_target_pairs={{0,32},{32,0},{64,96},{96,64},{128,160},{160,128},{192,224},{224,1... | collective-permute-start | bytes 405512 | tf_op jit(solution)/shard_map/ppermute | solution.py:33
  37.3 8.5 %collective-permute-start.13 = (bf16[256,256]{1,0:T(8,128)(2,1)S(1)}, bf16[256,256]{1,0:T(8,128)(2,1)S(1)}, u32[]{:S(2)}, u32[]{:S(2)}) collective-permute-start(bf16[256,256]{1,0:T(8,128)(2,1)S(1)} %shard_map.108.refs_8_), channel_id=1, source_target_pairs={{0,1},{1,0},{2,3},{3,2},{4,5},{5,4},{6,7},{7,6},{8,9},{9,8},{10,11... | collective-permute-start | bytes 393224 | tf_op jit(solution)/shard_map/ppermute | solution.py:29
  41.3 11.3 %collective-permute-start.1 = (bf16[528,128]{1,0:T(8,128)(2,1)S(1)}, bf16[528,128]{1,0:T(8,128)(2,1)S(1)}, u32[]{:S(2)}, u32[]{:S(2)}) collective-permute-start(bf16[528,128]{1,0:T(8,128)(2,1)S(1)} %shard_map.105), channel_id=1, source_target_pairs={{0,64},{32,96},{64,128},{96,160},{128,192},{160,224},{192,0},{224,... | collective-permute-start | bytes 405512 | tf_op jit(solution)/shard_map/ppermute | solution.py:38
  42.4 14.3 %collective-permute-start.2 = (bf16[528,128]{1,0:T(8,128)(2,1)S(1)}, bf16[528,128]{1,0:T(8,128)(2,1)S(1)}, u32[]{:S(2)}, u32[]{:S(2)}) collective-permute-start(bf16[528,128]{1,0:T(8,128)(2,1)S(1)} %shard_map.105), channel_id=1, source_target_pairs={{0,128},{32,160},{64,192},{96,224},{128,0},{160,32},{192,64},{224,... | collective-permute-start | bytes 405512 | tf_op jit(solution)/shard_map/ppermute | solution.py:38
  45.0 12.4 %collective-permute-start.3 = (bf16[528,128]{1,0:T(8,128)(2,1)S(1)}, bf16[528,128]{1,0:T(8,128)(2,1)S(1)}, u32[]{:S(2)}, u32[]{:S(2)}) collective-permute-start(bf16[528,128]{1,0:T(8,128)(2,1)S(1)} %shard_map.105), channel_id=1, source_target_pairs={{0,192},{32,224},{64,0},{96,32},{128,64},{160,96},{192,128},{224,1... | collective-permute-start | bytes 405512 | tf_op jit(solution)/shard_map/ppermute | solution.py:38
  47.9 11.9 %collective-permute-start.25 = (bf16[256,256]{1,0:T(8,128)(2,1)S(1)}, bf16[256,256]{1,0:T(8,128)(2,1)S(1)}, u32[]{:S(2)}, u32[]{:S(2)}) collective-permute-start(bf16[256,256]{1,0:T(8,128)(2,1)S(1)} %get-tuple-element.34), channel_id=1, source_target_pairs={{0,24},{1,25},{2,26},{3,27},{4,28},{5,29},{6,30},{7,31},{8,16},{9,... | collective-permute-start | bytes 393224 | tf_op jit(solution)/shard_map/ppermute | solution.py:49
  50.5 12.8 %collective-permute-start.26 = (bf16[256,256]{1,0:T(8,128)(2,1)S(1)}, bf16[256,256]{1,0:T(8,128)(2,1)S(1)}, u32[]{:S(2)}, u32[]{:S(2)}) collective-permute-start(bf16[256,256]{1,0:T(8,128)(2,1)S(1)} %get-tuple-element.35), channel_id=1, source_target_pairs={{0,26},{1,27},{2,24},{3,25},{4,30},{5,31},{6,28},{7,29},{8,18},{9,... | collective-permute-start | bytes 393224 | tf_op jit(solution)/shard_map/ppermute | solution.py:49
  52.6 12.9 %collective-permute-start.27 = (bf16[256,256]{1,0:T(8,128)(2,1)S(1)}, bf16[256,256]{1,0:T(8,128)(2,1)S(1)}, u32[]{:S(2)}, u32[]{:S(2)}) collective-permute-start(bf16[256,256]{1,0:T(8,128)(2,1)S(1)} %get-tuple-element.36), channel_id=1, source_target_pairs={{0,28},{1,29},{2,30},{3,31},{4,24},{5,25},{6,26},{7,27},{8,20},{9,... | collective-permute-start | bytes 393224 | tf_op jit(solution)/shard_map/ppermute | solution.py:49
  56.7 14.7 %collective-permute-start.28 = (bf16[256,256]{1,0:T(8,128)(2,1)S(1)}, bf16[256,256]{1,0:T(8,128)(2,1)S(1)}, u32[]{:S(2)}, u32[]{:S(2)}) collective-permute-start(bf16[256,256]{1,0:T(8,128)(2,1)S(1)} %get-tuple-element.37), channel_id=1, source_target_pairs={{0,30},{1,31},{2,28},{3,29},{4,26},{5,27},{6,24},{7,25},{8,22},{9,... | collective-permute-start | bytes 393224 | tf_op jit(solution)/shard_map/ppermute | solution.py:49
  57.4 14.1 %collective-permute-start.21 = (bf16[256,256]{1,0:T(8,128)(2,1)S(1)}, bf16[256,256]{1,0:T(8,128)(2,1)S(1)}, u32[]{:S(2)}, u32[]{:S(2)}) collective-permute-start(bf16[256,256]{1,0:T(8,128)(2,1)S(1)} %get-tuple-element.30), channel_id=1, source_target_pairs={{0,16},{1,17},{2,18},{3,19},{4,20},{5,21},{6,22},{7,23},{8,24},{9,... | collective-permute-start | bytes 393224 | tf_op jit(solution)/shard_map/ppermute | solution.py:49
  59.8 16.8 %collective-permute-start.22 = (bf16[256,256]{1,0:T(8,128)(2,1)S(1)}, bf16[256,256]{1,0:T(8,128)(2,1)S(1)}, u32[]{:S(2)}, u32[]{:S(2)}) collective-permute-start(bf16[256,256]{1,0:T(8,128)(2,1)S(1)} %get-tuple-element.31), channel_id=1, source_target_pairs={{0,18},{1,19},{2,16},{3,17},{4,22},{5,23},{6,20},{7,21},{8,26},{9,... | collective-permute-start | bytes 393224 | tf_op jit(solution)/shard_map/ppermute | solution.py:49
  63.3 14.1 %collective-permute-start.23 = (bf16[256,256]{1,0:T(8,128)(2,1)S(1)}, bf16[256,256]{1,0:T(8,128)(2,1)S(1)}, u32[]{:S(2)}, u32[]{:S(2)}) collective-permute-start(bf16[256,256]{1,0:T(8,128)(2,1)S(1)} %get-tuple-element.32), channel_id=1, source_target_pairs={{0,20},{1,21},{2,22},{3,23},{4,16},{5,17},{6,18},{7,19},{8,28},{9,... | collective-permute-start | bytes 393224 | tf_op jit(solution)/shard_map/ppermute | solution.py:49
  65.6 14.6 %collective-permute-start.24 = (bf16[256,256]{1,0:T(8,128)(2,1)S(1)}, bf16[256,256]{1,0:T(8,128)(2,1)S(1)}, u32[]{:S(2)}, u32[]{:S(2)}) collective-permute-start(bf16[256,256]{1,0:T(8,128)(2,1)S(1)} %get-tuple-element.33), channel_id=1, source_target_pairs={{0,22},{1,23},{2,20},{3,21},{4,18},{5,19},{6,16},{7,17},{8,30},{9,... | collective-permute-start | bytes 393224 | tf_op jit(solution)/shard_map/ppermute | solution.py:49
  71.4 9.7 %collective-permute-start.17 = (bf16[256,256]{1,0:T(8,128)(2,1)S(1)}, bf16[256,256]{1,0:T(8,128)(2,1)S(1)}, u32[]{:S(2)}, u32[]{:S(2)}) collective-permute-start(bf16[256,256]{1,0:T(8,128)(2,1)S(1)} %get-tuple-element.26), channel_id=1, source_target_pairs={{0,8},{1,9},{2,10},{3,11},{4,12},{5,13},{6,14},{7,15},{8,0},{9,1},... | collective-permute-start | bytes 393224 | tf_op jit(solution)/shard_map/ppermute | solution.py:49
  71.4 15.3 %copy-start.3 = (bf16[256,1024]{1,0:T(8,128)(2,1)S(1)}, bf16[256,1024]{1,0:T(8,128)(2,1)}, u32[]{:S(2)}) copy-start(bf16[256,1024]{1,0:T(8,128)(2,1)} %in_rows.3) | copy-start | bytes 1572868
  71.4 15.3 %copy-start.5 = (bf16[256,1024]{1,0:T(8,128)(2,1)S(1)}, bf16[256,1024]{1,0:T(8,128)(2,1)}, u32[]{:S(2)}) copy-start(bf16[256,1024]{1,0:T(8,128)(2,1)} %out_rows.1) | copy-start | bytes 1572868
  71.5 15.3 %copy-start.6 = (f32[8]{0:T(128)S(1)}, f32[8]{0:T(128)}, u32[]{:S(2)}) copy-start(f32[8]{0:T(128)} %param.13) | copy-start | bytes 100
  71.5 14.5 %collective-permute-start.18 = (bf16[256,256]{1,0:T(8,128)(2,1)S(1)}, bf16[256,256]{1,0:T(8,128)(2,1)S(1)}, u32[]{:S(2)}, u32[]{:S(2)}) collective-permute-start(bf16[256,256]{1,0:T(8,128)(2,1)S(1)} %get-tuple-element.27), channel_id=1, source_target_pairs={{0,10},{1,11},{2,8},{3,9},{4,14},{5,15},{6,12},{7,13},{8,2},{9,3},... | collective-permute-start | bytes 393224 | tf_op jit(solution)/shard_map/ppermute | solution.py:49
  76.6 15.1 %collective-permute-start.19 = (bf16[256,256]{1,0:T(8,128)(2,1)S(1)}, bf16[256,256]{1,0:T(8,128)(2,1)S(1)}, u32[]{:S(2)}, u32[]{:S(2)}) collective-permute-start(bf16[256,256]{1,0:T(8,128)(2,1)S(1)} %get-tuple-element.28), channel_id=1, source_target_pairs={{0,12},{1,13},{2,14},{3,15},{4,8},{5,9},{6,10},{7,11},{8,4},{9,5},... | collective-permute-start | bytes 393224 | tf_op jit(solution)/shard_map/ppermute | solution.py:49
  77.3 21.0 %collective-permute-start.20 = (bf16[256,256]{1,0:T(8,128)(2,1)S(1)}, bf16[256,256]{1,0:T(8,128)(2,1)S(1)}, u32[]{:S(2)}, u32[]{:S(2)}) collective-permute-start(bf16[256,256]{1,0:T(8,128)(2,1)S(1)} %get-tuple-element.29), channel_id=1, source_target_pairs={{0,14},{1,15},{2,12},{3,13},{4,10},{5,11},{6,8},{7,9},{8,6},{9,7},... | collective-permute-start | bytes 393224 | tf_op jit(solution)/shard_map/ppermute | solution.py:49
  80.2 18.1 %collective-permute-start.14 = (bf16[256,256]{1,0:T(8,128)(2,1)S(1)}, bf16[256,256]{1,0:T(8,128)(2,1)S(1)}, u32[]{:S(2)}, u32[]{:S(2)}) collective-permute-start(bf16[256,256]{1,0:T(8,128)(2,1)S(1)} %get-tuple-element.23), channel_id=1, source_target_pairs={{0,2},{1,3},{2,0},{3,1},{4,6},{5,7},{6,4},{7,5},{8,10},{9,11},{10,... | collective-permute-start | bytes 393224 | tf_op jit(solution)/shard_map/ppermute | solution.py:49
  81.1 20.0 %collective-permute-start.15 = (bf16[256,256]{1,0:T(8,128)(2,1)S(1)}, bf16[256,256]{1,0:T(8,128)(2,1)S(1)}, u32[]{:S(2)}, u32[]{:S(2)}) collective-permute-start(bf16[256,256]{1,0:T(8,128)(2,1)S(1)} %get-tuple-element.24), channel_id=1, source_target_pairs={{0,4},{1,5},{2,6},{3,7},{4,0},{5,1},{6,2},{7,3},{8,12},{9,13},{10,... | collective-permute-start | bytes 393224 | tf_op jit(solution)/shard_map/ppermute | solution.py:49
  86.0 19.5 %collective-permute-start.16 = (bf16[256,256]{1,0:T(8,128)(2,1)S(1)}, bf16[256,256]{1,0:T(8,128)(2,1)S(1)}, u32[]{:S(2)}, u32[]{:S(2)}) collective-permute-start(bf16[256,256]{1,0:T(8,128)(2,1)S(1)} %get-tuple-element.25), channel_id=1, source_target_pairs={{0,6},{1,7},{2,4},{3,5},{4,2},{5,3},{6,0},{7,1},{8,14},{9,15},{10,... | collective-permute-start | bytes 393224 | tf_op jit(solution)/shard_map/ppermute | solution.py:49

commit v2 on v1

--- a/solution.py
+++ b/solution.py
@@ -22,7 +22,7 @@
 masked_score = -1e30
 bf16 = jnp.bfloat16
 f32 = jnp.float32
-VMEM_LIMIT = 48 * 1024 * 1024
+VMEM_LIMIT = 24 * 1024 * 1024
 
 
 def swap_core(block):
@@ -45,7 +45,11 @@
     return lax.ppermute(block, ("section", "tp"), route)
 
 
-def swap_chip(block, offset):
+def swap_x(block, offset):
+    return lax.ppermute(block, "tp", [(t, t ^ (8 * offset)) for t in range(TP)])
+
+
+def swap_zl(block, offset):
     return lax.ppermute(block, "tp", [(t, t ^ (2 * offset)) for t in range(TP)])
 
 
@@ -57,14 +61,14 @@
     return pl.BlockSpec(shape, lambda i, s: (0,) * len(shape))
 
 
-def call(body, scalars, in_specs, out_shapes, args, scratch=(), flops=0, moved=0):
+def call(body, scalars, in_specs, out_shapes, args, scratch=(), flops=0, moved=0, out_specs=None):
     return pl.pallas_call(
         body,
         grid_spec=pltpu.PrefetchScalarGridSpec(
             num_scalar_prefetch=1,
             grid=(1,),
             in_specs=in_specs,
-            out_specs=[whole(o.shape) for o in out_shapes],
+            out_specs=out_specs or [whole(o.shape) for o in out_shapes],
             scratch_shapes=list(scratch),
         ),
         out_shape=out_shapes,
@@ -85,43 +89,79 @@
         far[...] = v_far[...]
 
 
-def attend_body(s, q, m0, m1, m2, m3, o0, o1, o2, o3, out, scores):
+def copy_half_body(s, weights, out, sem):
+    copy = pltpu.make_async_copy(weights.at[:, 1 - s[2]], out, sem)
+    copy.start()
+    copy.wait()
+
+
+def attend_body(s, q, m0, m1, m2, m3, o0, o1, o2, o3, out, scores, top, total, mixed):
     y, zh, core = s[0], s[1], s[2]
     length = q.shape[0]
     half = m0.shape[0] // 2
     me = y * 2 + zh
+    rate = 1.0 / math.sqrt(HEAD_DIM) * math.log2(math.e)
 
     def run(keys, values):
         stacked = jnp.concatenate([q[:, :HEAD_DIM], q[:, HEAD_DIM:]], axis=0)
-        top = None
-        for b, key in enumerate(keys):
+        blocks = []
+        for b in range(4):
             for part in range(2):
-                got = lax.dot_general(
+                owner = ((y + 4 - b) & 3) * 2 + (zh if part == 0 else 1 - zh)
+                blocks.append((b, part, owner))
+        for b, part, owner in blocks:
+            rows = slice(part * half, (part + 1) * half)
+            at = (2 * b + part) * half
+
+            def score(b=b, rows=rows):
+                return lax.dot_general(
                     stacked,
-                    key[part * half : (part + 1) * half, :],
+                    keys[b][rows, :],
                     (((1,), (1,)), ((), ())),
                     preferred_element_type=f32,
-                ) * (1.0 / math.sqrt(HEAD_DIM))
-                if b == 0 and part == 0:
-                    row = lax.broadcasted_iota(jnp.int32, got.shape, 0) & (length - 1)
-                    col = lax.broadcasted_iota(jnp.int32, got.shape, 1)
-                    got = jnp.where(col <= row, got, masked_score)
-                else:
-                    owner = ((y + 4 - b) & 3) * 2 + (zh if part == 0 else 1 - zh)
-                    got = jnp.where(owner < me, got, masked_score)
-                at = (2 * b + part) * half
+                )
+
+            if b == 0 and part == 0:
+                got = score()
+                row = lax.broadcasted_iota(jnp.int32, got.shape, 0) & (length - 1)
+                col = lax.broadcasted_iota(jnp.int32, got.shape, 1)
+                got = jnp.where(col <= row, got, masked_score)
                 scores[:, at : at + half] = got
-                peak = jnp.max(got, axis=1, keepdims=True)
-                top = peak if top is None else jnp.maximum(top, peak)
-        total = jnp.zeros_like(top)
-        mixed = jnp.zeros(stacked.shape, f32)
-        for b, value in enumerate(values):
-            weights = jnp.exp(scores[:, 2 * half * b : 2 * half * (b + 1)] - top)
-            total = total + jnp.sum(weights, axis=1, keepdims=True)
-            mixed = mixed + jnp.dot(weights.astype(bf16), value[...], preferred_element_type=f32)
-        done = (mixed / total).astype(bf16)
-        out[:, :HEAD_DIM] = done[:length]
-        out[:, HEAD_DIM:] = done[length:]
+                top[...] = jnp.max(got, axis=1, keepdims=True)
+            else:
+
+                @pl.when(owner < me)
+                def _(at=at, score=score):
+                    got = score()
+                    scores[:, at : at + half] = got
+                    top[...] = jnp.maximum(top[...], jnp.max(got, axis=1, keepdims=True))
+
+        for b, part, owner in blocks:
+            rows = slice(part * half, (part + 1) * half)
+            at = (2 * b + part) * half
+
+            def weigh(b=b, rows=rows, at=at):
+                weights = jnp.exp2((scores[:, at : at + half] - top[...]) * rate)
+                return (
+                    jnp.sum(weights, axis=1, keepdims=True),
+                    jnp.dot(
+                        weights.astype(bf16), values[b][rows, :], preferred_element_type=f32
+                    ),
+                )
+
+            if b == 0 and part == 0:
+                total[...], mixed[...] = weigh()
+            else:
+
+                @pl.when(owner < me)
+                def _(weigh=weigh):
+                    more, product = weigh()
+                    total[...] += more
+                    mixed[...] += product
+
+        done = (mixed[...] / total[...]).astype(bf16).astype(f32)
+        out[:HEAD_DIM, :] = done[:length].T.astype(bf16)
+        out[HEAD_DIM:, :] = done[length:].T.astype(bf16)
 
     @pl.when(core == 0)
     def _():
@@ -132,20 +172,25 @@
         run((o0, o1, o2, o3), (m0, m1, m2, m3))
 
 
-def project_body(count):
-    def body(s, *refs):
-        own = refs[:count]
-        got = refs[count : 2 * count]
-        here, there = refs[2 * count : 2 * count + 2]
-        outs = refs[2 * count + 2 :]
-        contract = (((1,), (1,)), ((), ()))
-        for w, v, o in zip(own, got, outs):
-            o[...] = (
-                lax.dot_general(w[...], here[...], contract, preferred_element_type=f32)
-                + lax.dot_general(v[...], there[...], contract, preferred_element_type=f32)
-            ).astype(bf16)
-
-    return body
+def project_body(s, *refs):
+    count = (len(refs) - 4) // 2
+    own = refs[:count]
+    got = refs[count : 2 * count]
+    here, there = refs[2 * count : 2 * count + 2]
+    outs = refs[2 * count + 2 :]
+    each = count // len(outs)
+    for i in range(count):
+        outs[i // each][(i % each) // 2, i % 2] = (
+            jnp.dot(own[i][...], here[...], preferred_element_type=f32)
+            + jnp.dot(got[i][...], there[...], preferred_element_type=f32)
+        ).astype(bf16)
+
+
+def add_split_body(s, kept, arrived, *outs):
+    rows = kept.shape[0] // len(outs)
+    for i, out in enumerate(outs):
+        at = slice(i * rows, (i + 1) * rows)
+        out[...] = (kept[at].astype(f32) + arrived[at].astype(f32)).astype(bf16)
 
 
 def running_sums(decay):
@@ -312,7 +357,16 @@
     pair = jnp.concatenate([own, swap_zh_near(far)], axis=0)
 
     weights = out_weight.reshape(CHIPS, 2, ROWS, out_weight.shape[1])
-    sent = lax.dynamic_index_in_dim(weights, 1 - core, 1, keepdims=False)
+    (sent,) = call(
+        copy_half_body,
+        scalars,
+        [pl.BlockSpec(memory_space=pl.ANY)],
+        [shape((CHIPS, ROWS, out_weight.shape[1]), bf16)],
+        (weights,),
+        scratch=[pltpu.SemaphoreType.DMA],
+        out_specs=[pl.BlockSpec(memory_space=pl.ANY)],
+        moved=4000000,
+    )
     got_weight = swap_core(sent.reshape(CHIPS * ROWS, out_weight.shape[1]))
 
     heads = log_decay.shape[1]
@@ -338,7 +392,12 @@
         [whole(query_rows.shape)] + [whole(pair.shape)] * 8,
         [shape(query_rows.shape, bf16)],
         (query_rows, *pairs, *others),
-        scratch=[pltpu.VMEM((2 * length, 4 * pair.shape[0]), f32)],
+        scratch=[
+            pltpu.VMEM((2 * length, 4 * pair.shape[0]), f32),
+            pltpu.VMEM((2 * length, 1), f32),
+            pltpu.VMEM((2 * length, 1), f32),
+            pltpu.VMEM((2 * length, HEAD_DIM), f32),
+        ],
         flops=4 * 2 * length * 4 * pair.shape[0] * HEAD_DIM,
         moved=2000000,
     )
@@ -356,30 +415,52 @@
     earlier = [shift_y(joined, d) for d in (1, 2, 3)]
 
     weight_block = (ROWS, out_weight.shape[1])
-    parts = []
-    for start in range(0, CHIPS, 4):
-        offsets = list(range(start, start + 4))
+
+    def project(offsets):
         own_specs = [
             pl.BlockSpec(weight_block, lambda i, s, r=r: (s[5 + r] * 2 + s[2], 0)) for r in offsets
         ]
         got_specs = [pl.BlockSpec(weight_block, lambda i, s, r=r: (s[5 + r], 0)) for r in offsets]
-        parts += call(
-            project_body(4),
+        return call(
+            project_body,
             scalars,
             own_specs + got_specs + [whole(attended.shape)] * 2,
-            [shape((ROWS, length), bf16)] * 4,
-            [out_weight] * 4 + [got_weight] * 4 + [attended, attended_there],
-            flops=4 * 2 * ROWS * 512 * length,
-            moved=2000000,
+            [shape((2, 2, ROWS, length), bf16)] * 2,
+            [out_weight] * len(offsets)
+            + [got_weight] * len(offsets)
+            + [attended, attended_there],
+            flops=len(offsets) * 2 * ROWS * 512 * length,
+            moved=3000000,
         )
-    arrived = [parts[0]] + [swap_chip(parts[r], r) for r in range(1, CHIPS)]
+
+    sent1, sent2 = project([4, 5, 8, 9, 14, 15, 10, 11])
+    kept1, kept2 = project([0, 1, 12, 13, 2, 3, 6, 7])
+    arrived1, arrived2 = swap_x(sent1, 1), swap_x(sent2, 3)
+
+    def add_split(kept, arrived, parts):
+        out = shape((kept.shape[0] // parts, *kept.shape[1:]), bf16)
+        return call(
+            add_split_body,
+            scalars,
+            [whole(kept.shape)] * 2,
+            [out] * parts,
+            (kept, arrived),
+            moved=6 * kept.size,
+        )
+
+    kept1, sent1 = add_split(kept1, arrived1, 2)
+    kept2, sent2 = add_split(kept2, arrived2, 2)
+    arrived1, arrived2 = swap_x(sent1, 3), swap_x(sent2, 1)
+    z0, z1 = add_split(kept1[0], arrived1[0], 2)
+    z2, z3 = add_split(kept2[0], arrived2[0], 2)
+    arrived = [z0[0]] + [swap_zl(z[0], b) for b, z in ((1, z1), (2, z2), (3, z3))]
     (attn_out,) = call(
-        sum_body(CHIPS),
-        scalars,
-        [whole((ROWS, length))] * CHIPS,
+        sum_body(4),
+        scalars,
+        [whole((ROWS, length))] * 4,
         [shape((ROWS, length), bf16)],
         arrived,
-        moved=17 * ROWS * length * 2,
+        moved=5 * ROWS * length * 2,
     )
 
     (ssm_out,) = call(

time: 107 us -> 75.6 us (0.71)
  the two profiles are of different devices: /device:TPU:33 before, /device:TPU:8 now
where the time goes in v2:
time: 75.6 us; the launch traced here: 75.4 us
  starting transfers between devices  34.7 us (46%)
  Pallas kernels  18.7 us (25%)
  waiting for transfers between devices  16 us (21%)
  local copies, waits for them, and re-layouts  5.03 us (7%)
  between operations  0.92 us (1%)
    pallas_call x13, Pallas kernels, call(): pl.pallas_call(body, grid_spec=pltpu.PrefetchScalarGridSpec(num_scalar_pr...  18.7 us
    ppermute x6, starting transfers between devices, shift_y(): return lax.ppermute(block, 'section', route)  12.4 us
    ppermute x1, starting transfers between devices, swap_zh_near(): return lax.ppermute(block, ('section', 'tp'), route)  6.39 us
    ppermute x4, starting transfers between devices, swap_x(): return lax.ppermute(block, 'tp', [(t, t ^ 8 * offset) for t in range(TP)])  5.94 us
    ppermute x1, starting transfers between devices, swap_zh(): return lax.ppermute(block, 'section', [(s, s ^ 1) for s in range(SECTIONS)])  4.98 us
    unnamed x24, local copies, waits for them, and re-layouts  4.91 us
    ppermute x3, starting transfers between devices, swap_zl(): return lax.ppermute(block, 'tp', [(t, t ^ 2 * offset) for t in range(TP)])  4.52 us
    ppermute x6, waiting for transfers between devices, shift_y(): return lax.ppermute(block, 'section', route)  4.32 us
  transfers between devices with their start and end apart: 21, of which 10 were waited for; matrix products, arithmetic and copies ran while one was open for 0% of the time, Pallas kernels for 19%

profile of v2, /device:TPU:8, one launch (start us, length us, event | category | flops | bytes accessed | tf_op | source)
XLA Modules:
  0.0 75.4 jit_solution(12266818266311631936)
XLA Ops:
  0.7 0.1 stack.87.s
  0.8 0.0 copy-start
  0.8 2.2 %copy-done = bf16[8192,256]{1,0:T(8,128)(2,1)S(1)} copy-done((bf16[8192,256]{1,0:T(8,128)(2,1)S(1)}, bf16[8192,256]{1,0:T(8,128)(2,1)}, u32[]{:S(2)}) %copy-start) | copy-done | bytes 4194328
  3.0 0.7 shard_map.107
  3.7 0.0 copy-start.9
  3.7 0.0 copy-start.1
  3.7 0.1 collective-permute-start.4
  3.8 0.2 copy-done.3
  4.0 0.2 copy-done.4
  4.2 0.6 shard_map.108
  4.8 6.4 %collective-permute-start.5 = (bf16[256,128]{1,0:T(8,128)(2,1)S(1)}, bf16[256,128]{1,0:T(8,128)(2,1)S(1)}, u32[]{:S(2)}, u32[]{:S(2)}) collective-permute-start(bf16[256,128]{1,0:T(8,128)(2,1)S(1)} %get-tuple-element.17), channel_id=1, source_target_pairs={{0,36},{1,37},{2,38},{3,39},{4,32},{5,33},{6,34},{7,35},{8,44},{9,... | collective-permute-start | bytes 196616 | tf_op jit(solution)/shard_map/ppermute | solution.py:45
  11.2 3.1 %collective-permute-done.5 = bf16[256,128]{1,0:T(8,128)(2,1)S(1)} collective-permute-done((bf16[256,128]{1,0:T(8,128)(2,1)S(1)}, bf16[256,128]{1,0:T(8,128)(2,1)S(1)}, u32[]{:S(2)}, u32[]{:S(2)}) %collective-permute-start.5) | collective-permute-done | bytes 65568 | tf_op jit(solution)/shard_map/ppermute | solution.py:45
  14.3 1.7 %collective-permute-start.6 = (bf16[512,128]{1,0:T(8,128)(2,1)S(1)}, bf16[512,128]{1,0:T(8,128)(2,1)S(1)}, u32[]{:S(2)}, u32[]{:S(2)}) collective-permute-start(bf16[512,128]{1,0:T(8,128)(2,1)S(1)} %constant_dynamic-update-slice_fusion.m0), channel_id=1, source_target_pairs={{0,64},{32,96},{64,128},{96,160},{128,192},{160,224},{192,0},{224,... | collective-permute-start | bytes 393224 | tf_op jit(solution)/shard_map/ppermute | solution.py:38
  15.9 0.9 %collective-permute-start.7 = (bf16[512,128]{1,0:T(8,128)(2,1)S(1)}, bf16[512,128]{1,0:T(8,128)(2,1)S(1)}, u32[]{:S(2)}, u32[]{:S(2)}) collective-permute-start(bf16[512,128]{1,0:T(8,128)(2,1)S(1)} %constant_dynamic-update-slice_fusion.m0), channel_id=1, source_target_pairs={{0,128},{32,160},{64,192},{96,224},{128,0},{160,32},{192,64},{224,... | collective-permute-start | bytes 393224 | tf_op jit(solution)/shard_map/ppermute | solution.py:38
  16.9 2.4 %collective-permute-start.8 = (bf16[512,128]{1,0:T(8,128)(2,1)S(1)}, bf16[512,128]{1,0:T(8,128)(2,1)S(1)}, u32[]{:S(2)}, u32[]{:S(2)}) collective-permute-start(bf16[512,128]{1,0:T(8,128)(2,1)S(1)} %constant_dynamic-update-slice_fusion.m0), channel_id=1, source_target_pairs={{0,192},{32,224},{64,0},{96,32},{128,64},{160,96},{192,128},{224,1... | collective-permute-start | bytes 393224 | tf_op jit(solution)/shard_map/ppermute | solution.py:38
  19.3 0.0 collective-permute-start.9
  19.3 0.9 %collective-permute-done.6.m1 = bf16[512,128]{1,0:T(8,128)(2,1)S(1)} collective-permute-done((bf16[512,128]{1,0:T(8,128)(2,1)S(1)}, bf16[512,128]{1,0:T(8,128)(2,1)S(1)}, u32[]{:S(2)}, u32[]{:S(2)}) %collective-permute-start.6) | collective-permute-done | bytes 131104 | tf_op jit(solution)/shard_map/ppermute | solution.py:38
  20.2 0.0 collective-permute-start.10
  20.2 2.8 %collective-permute-done.7.m2 = bf16[512,128]{1,0:T(8,128)(2,1)S(1)} collective-permute-done((bf16[512,128]{1,0:T(8,128)(2,1)S(1)}, bf16[512,128]{1,0:T(8,128)(2,1)S(1)}, u32[]{:S(2)}, u32[]{:S(2)}) %collective-permute-start.7) | collective-permute-done | bytes 131104 | tf_op jit(solution)/shard_map/ppermute | solution.py:38
  23.1 0.0 collective-permute-start.11
  23.1 0.6 collective-permute-done.8.m3
  23.6 0.0 collective-permute-start.12
  23.6 0.0 collective-permute-done.9.o0
  23.6 0.8 %collective-permute-done.11.o2 = bf16[512,128]{1,0:T(8,128)(2,1)S(1)} collective-permute-done((bf16[512,128]{1,0:T(8,128)(2,1)S(1)}, bf16[512,128]{1,0:T(8,128)(2,1)S(1)}, u32[]{:S(2)}, u32[]{:S(2)}) %collective-permute-start.11) | collective-permute-done | bytes 131104 | tf_op jit(solution)/shard_map/ppermute | solution.py:29
  24.4 0.6 collective-permute-done.12.o3
  25.0 2.6 %shard_map.109.refs_16_ = bf16[256,256]{1,0:T(8,128)(2,1)S(1)} custom-call(s32[21]{0:T(128)S(1)} %stack.87.s, bf16[256,256]{1,0:T(8,128)(2,1)S(1)} %copy-done.9, bf16[512,128]{1,0:T(8,128)(2,1)S(1)} %constant_dynamic-update-slice_fusion.m0, bf16[512,128]{1,0:T(8,128)(2,1)S(1)} %collective-permute-done.6.m1, bf16[512,128]{1,0:T(8,128)(2,1)S(1)} %collective-permute-done.7.m2, ...), custom_call_target="tpu_custom_call" | custom-call | flops 536870912 | bytes 2000000 | tf_op jit(solution)/shard_map/pallas_call | solution.py:65
  27.6 0.0 copy-start.10
  27.6 0.0 copy-start.5
  27.6 0.0 copy-start.6
  27.6 0.4 collective-permute-start.13
  28.0 1.2 %collective-permute-done.13.refs_17_ = bf16[256,256]{1,0:T(8,128)(2,1)S(1)} collective-permute-done((bf16[256,256]{1,0:T(8,128)(2,1)S(1)}, bf16[256,256]{1,0:T(8,128)(2,1)S(1)}, u32[]{:S(2)}, u32[]{:S(2)}) %collective-permute-start.13) | collective-permute-done | bytes 131104 | tf_op jit(solution)/shard_map/ppermute | solution.py:29
  29.2 0.0 collective-permute-done.4.refs_8_.refs_9_.refs_10_.refs_11_.refs_12_.refs_13_.refs_14_.refs_15_
  29.2 2.1 %shard_map.111 = (bf16[2,2,256,256]{3,2,1,0:T(8,128)(2,1)}, bf16[2,2,256,256]{3,2,1,0:T(8,128)(2,1)}) custom-call(s32[21]{0:T(128)S(1)} %stack.87.s, bf16[8192,256]{1,0:T(8,128)(2,1)S(1)} %copy-done.1, bf16[8192,256]{1,0:T(8,128)(2,1)S(1)} %copy-done.1, bf16[8192,256]{1,0:T(8,128)(2,1)S(1)} %copy-done.1, bf16[8192,256]{1,0:T(8,128)(2,1)S(1)} %copy-done.1, ...), custom_call_target="tpu_custom_call" | custom-call | flops 536870912 | bytes 3000000 | tf_op jit(solution)/shard_map/pallas_call | solution.py:65
  31.3 2.8 %collective-permute-start.17 = (bf16[2,2,256,256]{3,2,1,0:T(8,128)(2,1)}, bf16[2,2,256,256]{3,2,1,0:T(8,128)(2,1)}, u32[]{:S(2)}, u32[]{:S(2)}) collective-permute-start(bf16[2,2,256,256]{3,2,1,0:T(8,128)(2,1)} %get-tuple-element.25), channel_id=1, source_target_pairs={{0,24},{1,25},{2,26},{3,27},{4,28},{5,29},{6,30},{7,31},{8,16},{9,... | collective-permute-start | bytes 1572872 | tf_op jit(solution)/shard_map/ppermute | solution.py:49
  34.0 0.2 collective-permute-start.14
  34.3 0.1 copy.12.decay
  34.4 1.9 %shard_map.104.mine = bf16[528,128]{1,0:T(8,128)(2,1)S(1)} custom-call(s32[21]{0:T(128)S(1)} %stack.87.s, bf16[256,512]{1,0:T(8,128)(2,1)S(1)} %copy-done.6, bf16[256,1024]{1,0:T(8,128)(2,1)S(1)} %copy-done.5, f32[256,8]{1,0:T(8,128)S(1)} %copy.12.decay), custom_call_target="tpu_custom_call" | custom-call | flops 33554432 | bytes 600000 | tf_op jit(solution)/shard_map/pallas_call | solution.py:65
  36.4 5.0 %collective-permute-start = (bf16[528,128]{1,0:T(8,128)(2,1)S(1)}, bf16[528,128]{1,0:T(8,128)(2,1)S(1)}, u32[]{:S(2)}, u32[]{:S(2)}) collective-permute-start(bf16[528,128]{1,0:T(8,128)(2,1)S(1)} %shard_map.104.mine), channel_id=1, source_target_pairs={{0,32},{32,0},{64,96},{96,64},{128,160},{160,128},{192,224},{224,1... | collective-permute-start | bytes 405512 | tf_op jit(solution)/shard_map/ppermute | solution.py:33
  41.3 2.2 %copy-done.2 = bf16[8192,256]{1,0:T(8,128)(2,1)S(1)} copy-done((bf16[8192,256]{1,0:T(8,128)(2,1)S(1)}, bf16[8192,256]{1,0:T(8,128)(2,1)}, u32[]{:S(2)}) %copy-start.2) | copy-done | bytes 4194328
  43.5 1.2 %shard_map.110 = (bf16[2,2,256,256]{3,2,1,0:T(8,128)(2,1)S(1)}, bf16[2,2,256,256]{3,2,1,0:T(8,128)(2,1)S(1)}) custom-call(s32[21]{0:T(128)S(1)} %stack.87.s, bf16[8192,256]{1,0:T(8,128)(2,1)S(1)} %copy-done.2, bf16[8192,256]{1,0:T(8,128)(2,1)S(1)} %copy-done.2, bf16[8192,256]{1,0:T(8,128)(2,1)S(1)} %copy-done.2, bf16[8192,256]{1,0:T(8,128)(2,1)S(1)} %copy-done.2, ...), custom_call_target="tpu_custom_call" | custom-call | flops 536870912 | bytes 3000000 | tf_op jit(solution)/shard_map/pallas_call | solution.py:65
  44.8 0.0 copy-start.7
  44.8 0.0 copy-start.8
  44.8 2.0 %collective-permute-done.17.arrived = bf16[2,2,256,256]{3,2,1,0:T(8,128)(2,1)} collective-permute-done((bf16[2,2,256,256]{3,2,1,0:T(8,128)(2,1)}, bf16[2,2,256,256]{3,2,1,0:T(8,128)(2,1)}, u32[]{:S(2)}, u32[]{:S(2)}) %collective-permute-start.17) | collective-permute-done | bytes 524320 | tf_op jit(solution)/shard_map/ppermute | solution.py:49
  46.8 1.7 %shard_map.114 = (bf16[1,2,256,256]{3,2,1,0:T(8,128)(2,1)S(1)}, bf16[1,2,256,256]{3,2,1,0:T(8,128)(2,1)S(1)}) custom-call(s32[21]{0:T(128)S(1)} %stack.87.s, bf16[2,2,256,256]{3,2,1,0:T(8,128)(2,1)S(1)} %get-tuple-element.24.kept, bf16[2,2,256,256]{3,2,1,0:T(8,128)(2,1)} %collective-permute-done.17.arrived), custom_call_target="tpu_custom_call" | custom-call | bytes 1572864 | tf_op jit(solution)/shard_map/pallas_call | solution.py:65
  48.5 0.4 collective-permute-start.18
  48.9 0.0 collective-permute-done.14.arrived
  48.9 1.7 %shard_map.112 = (bf16[1,2,256,256]{3,2,1,0:T(8,128)(2,1)S(1)}, bf16[1,2,256,256]{3,2,1,0:T(8,128)(2,1)S(1)}) custom-call(s32[21]{0:T(128)S(1)} %stack.87.s, bf16[2,2,256,256]{3,2,1,0:T(8,128)(2,1)S(1)} %get-tuple-element.18.kept, bf16[2,2,256,256]{3,2,1,0:T(8,128)(2,1)} %collective-permute-done.14.arrived), custom_call_target="tpu_custom_call" | custom-call | bytes 1572864 | tf_op jit(solution)/shard_map/pallas_call | solution.py:65
  50.6 2.6 %collective-permute-start.15 = (bf16[1,2,256,256]{3,2,1,0:T(8,128)(2,1)S(1)}, bf16[1,2,256,256]{3,2,1,0:T(8,128)(2,1)S(1)}, u32[]{:S(2)}, u32[]{:S(2)}) collective-permute-start(bf16[1,2,256,256]{3,2,1,0:T(8,128)(2,1)S(1)} %get-tuple-element.21), channel_id=1, source_target_pairs={{0,24},{1,25},{2,26},{3,27},{4,28},{5,29},{6,30},{7,31},{8,16},{9,... | collective-permute-start | bytes 786440 | tf_op jit(solution)/shard_map/ppermute | solution.py:49
  53.2 0.0 collective-permute-done.partner
  53.2 0.6 shard_map.105
  53.8 2.5 %collective-permute-start.1 = (bf16[528,128]{1,0:T(8,128)(2,1)S(1)}, bf16[528,128]{1,0:T(8,128)(2,1)S(1)}, u32[]{:S(2)}, u32[]{:S(2)}) collective-permute-start(bf16[528,128]{1,0:T(8,128)(2,1)S(1)} %shard_map.105), channel_id=1, source_target_pairs={{0,64},{32,96},{64,128},{96,160},{128,192},{160,224},{192,0},{224,... | collective-permute-start | bytes 405512 | tf_op jit(solution)/shard_map/ppermute | solution.py:38
  56.3 2.3 %collective-permute-start.2 = (bf16[528,128]{1,0:T(8,128)(2,1)S(1)}, bf16[528,128]{1,0:T(8,128)(2,1)S(1)}, u32[]{:S(2)}, u32[]{:S(2)}) collective-permute-start(bf16[528,128]{1,0:T(8,128)(2,1)S(1)} %shard_map.105), channel_id=1, source_target_pairs={{0,128},{32,160},{64,192},{96,224},{128,0},{160,32},{192,64},{224,... | collective-permute-start | bytes 405512 | tf_op jit(solution)/shard_map/ppermute | solution.py:38
  58.6 2.5 %collective-permute-start.3 = (bf16[528,128]{1,0:T(8,128)(2,1)S(1)}, bf16[528,128]{1,0:T(8,128)(2,1)S(1)}, u32[]{:S(2)}, u32[]{:S(2)}) collective-permute-start(bf16[528,128]{1,0:T(8,128)(2,1)S(1)} %shard_map.105), channel_id=1, source_target_pairs={{0,192},{32,224},{64,0},{96,32},{128,64},{160,96},{192,128},{224,1... | collective-permute-start | bytes 405512 | tf_op jit(solution)/shard_map/ppermute | solution.py:38
  61.2 0.0 collective-permute-done.18
  61.2 0.6 shard_map.115
  61.8 2.5 %collective-permute-start.19 = (bf16[256,256]{1,0:T(8,128)(2,1)S(1)}, bf16[256,256]{1,0:T(8,128)(2,1)S(1)}, u32[]{:S(2)}, u32[]{:S(2)}) collective-permute-start(bf16[256,256]{1,0:T(8,128)(2,1)S(1)} %bitcast.41), channel_id=1, source_target_pairs={{0,4},{1,5},{2,6},{3,7},{4,0},{5,1},{6,2},{7,3},{8,12},{9,13},{10,... | collective-permute-start | bytes 393224 | tf_op jit(solution)/shard_map/ppermute | solution.py:53
  64.2 0.0 collective-permute-done.15
  64.3 2.0 %collective-permute-start.20 = (bf16[256,256]{1,0:T(8,128)(2,1)S(1)}, bf16[256,256]{1,0:T(8,128)(2,1)S(1)}, u32[]{:S(2)}, u32[]{:S(2)}) collective-permute-start(bf16[256,256]{1,0:T(8,128)(2,1)S(1)} %bitcast.40), channel_id=1, source_target_pairs={{0,6},{1,7},{2,4},{3,5},{4,2},{5,3},{6,0},{7,1},{8,14},{9,15},{10,... | collective-permute-start | bytes 393224 | tf_op jit(solution)/shard_map/ppermute | solution.py:53
  66.2 0.6 shard_map.113
  66.8 0.1 collective-permute-start.16
  67.0 3.1 %shard_map.106 = bf16[256,512]{1,0:T(8,128)(2,1)} custom-call(s32[21]{0:T(128)S(1)} %stack.87.s, bf16[256,512]{1,0:T(8,128)(2,1)S(1)} %copy-done.6, bf16[256,1024]{1,0:T(8,128)(2,1)S(1)} %copy-done.5, bf16[256,1024]{1,0:T(8,128)(2,1)S(1)} %copy-done.7, f32[256,8]{1,0:T(8,128)S(1)} %copy.12.decay, f32[1,8]{1,0:T(1,128)S(1)} %bitcast.39, ...), custom_call_target="tpu_custom_call" | custom-call | flops 67108864 | bytes 1500000 | tf_op jit(solution)/shard_map/pallas_call | solution.py:65
  70.0 3.4 %collective-permute-done.19.refs_2_ = bf16[256,256]{1,0:T(8,128)(2,1)S(1)} collective-permute-done((bf16[256,256]{1,0:T(8,128)(2,1)S(1)}, bf16[256,256]{1,0:T(8,128)(2,1)S(1)}, u32[]{:S(2)}, u32[]{:S(2)}) %collective-permute-start.19) | collective-permute-done | bytes 131104 | tf_op jit(solution)/shard_map/ppermute | solution.py:53
  73.4 0.7 collective-permute-done.16.refs_1_
  74.1 1.3 %shard_map.116 = bf16[256,256]{1,0:T(8,128)(2,1)} custom-call(s32[21]{0:T(128)S(1)} %stack.87.s, bf16[256,256]{1,0:T(8,128)(2,1)S(1)} %bitcast.38, bf16[256,256]{1,0:T(8,128)(2,1)S(1)} %collective-permute-done.16.refs_1_, bf16[256,256]{1,0:T(8,128)(2,1)S(1)} %collective-permute-done.19.refs_2_, bf16[256,256]{1,0:T(8,128)(2,1)S(1)} %collective-permute-done.20.refs_3_), custom_call_target="tpu_custom_call" | custom-call | bytes 655360 | tf_op jit(solution)/shard_map/pallas_call | solution.py:65
  (17 shorter events, 0.1 us)
Async XLA Ops:
  0.8 2.2 %copy-start = (bf16[8192,256]{1,0:T(8,128)(2,1)S(1)}, bf16[8192,256]{1,0:T(8,128)(2,1)}, u32[]{:S(2)}) copy-start(bf16[8192,256]{1,0:T(8,128)(2,1)} %refs_7_.3) | copy-start | bytes 12582916
  3.0 1.0 %copy-start.3 = (bf16[256,1024]{1,0:T(8,128)(2,1)S(1)}, bf16[256,1024]{1,0:T(8,128)(2,1)}, u32[]{:S(2)}) copy-start(bf16[256,1024]{1,0:T(8,128)(2,1)} %k_far.1) | copy-start | bytes 1572868
  3.0 1.2 %copy-start.4 = (bf16[256,1024]{1,0:T(8,128)(2,1)S(1)}, bf16[256,1024]{1,0:T(8,128)(2,1)}, u32[]{:S(2)}) copy-start(bf16[256,1024]{1,0:T(8,128)(2,1)} %v_far.1) | copy-start | bytes 1572868
  3.7 21.3 %copy-start.9 = (bf16[256,256]{1,0:T(8,128)(2,1)S(1)}, bf16[256,256]{1,0:T(8,128)(2,1)}, u32[]{:S(2)}) copy-start(bf16[256,256]{1,0:T(8,128)(2,1)} %q.1) | copy-start | bytes 393220
  3.7 25.5 %copy-start.1 = (bf16[8192,256]{1,0:T(8,128)(2,1)S(1)}, bf16[8192,256]{1,0:T(8,128)(2,1)}, u32[]{:S(2)}) copy-start(bf16[8192,256]{1,0:T(8,128)(2,1)} %refs_7_.3) | copy-start | bytes 12582916
  3.7 25.5 %collective-permute-start.4 = (bf16[4096,256]{1,0:T(8,128)(2,1)S(1)}, bf16[4096,256]{1,0:T(8,128)(2,1)S(1)}, u32[]{:S(2)}, u32[]{:S(2)}) collective-permute-start(bf16[4096,256]{1,0:T(8,128)(2,1)S(1)} %bitcast.33), channel_id=1, source_target_pairs={{0,1},{1,0},{2,3},{3,2},{4,5},{5,4},{6,7},{7,6},{8,9},{9,8},{10,11... | collective-permute-start | bytes 6291464 | tf_op jit(solution)/shard_map/ppermute | solution.py:29
  4.8 9.5 %collective-permute-start.5 = (bf16[256,128]{1,0:T(8,128)(2,1)S(1)}, bf16[256,128]{1,0:T(8,128)(2,1)S(1)}, u32[]{:S(2)}, u32[]{:S(2)}) collective-permute-start(bf16[256,128]{1,0:T(8,128)(2,1)S(1)} %get-tuple-element.17), channel_id=1, source_target_pairs={{0,36},{1,37},{2,38},{3,39},{4,32},{5,33},{6,34},{7,35},{8,44},{9,... | collective-permute-start | bytes 196616 | tf_op jit(solution)/shard_map/ppermute | solution.py:45
  14.3 5.9 %collective-permute-start.6 = (bf16[512,128]{1,0:T(8,128)(2,1)S(1)}, bf16[512,128]{1,0:T(8,128)(2,1)S(1)}, u32[]{:S(2)}, u32[]{:S(2)}) collective-permute-start(bf16[512,128]{1,0:T(8,128)(2,1)S(1)} %constant_dynamic-update-slice_fusion.m0), channel_id=1, source_target_pairs={{0,64},{32,96},{64,128},{96,160},{128,192},{160,224},{192,0},{224,... | collective-permute-start | bytes 393224 | tf_op jit(solution)/shard_map/ppermute | solution.py:38
  15.9 7.1 %collective-permute-start.7 = (bf16[512,128]{1,0:T(8,128)(2,1)S(1)}, bf16[512,128]{1,0:T(8,128)(2,1)S(1)}, u32[]{:S(2)}, u32[]{:S(2)}) collective-permute-start(bf16[512,128]{1,0:T(8,128)(2,1)S(1)} %constant_dynamic-update-slice_fusion.m0), channel_id=1, source_target_pairs={{0,128},{32,160},{64,192},{96,224},{128,0},{160,32},{192,64},{224,... | collective-permute-start | bytes 393224 | tf_op jit(solution)/shard_map/ppermute | solution.py:38
  16.9 6.7 %collective-permute-start.8 = (bf16[512,128]{1,0:T(8,128)(2,1)S(1)}, bf16[512,128]{1,0:T(8,128)(2,1)S(1)}, u32[]{:S(2)}, u32[]{:S(2)}) collective-permute-start(bf16[512,128]{1,0:T(8,128)(2,1)S(1)} %constant_dynamic-update-slice_fusion.m0), channel_id=1, source_target_pairs={{0,192},{32,224},{64,0},{96,32},{128,64},{160,96},{192,128},{224,1... | collective-permute-start | bytes 393224 | tf_op jit(solution)/shard_map/ppermute | solution.py:38
  19.3 4.3 %collective-permute-start.9 = (bf16[512,128]{1,0:T(8,128)(2,1)S(1)}, bf16[512,128]{1,0:T(8,128)(2,1)S(1)}, u32[]{:S(2)}, u32[]{:S(2)}) collective-permute-start(bf16[512,128]{1,0:T(8,128)(2,1)S(1)} %constant_dynamic-update-slice_fusion.m0), channel_id=1, source_target_pairs={{0,1},{1,0},{2,3},{3,2},{4,5},{5,4},{6,7},{7,6},{8,9},{9,8},{10,11... | collective-permute-start | bytes 393224 | tf_op jit(solution)/shard_map/ppermute | solution.py:29
  20.2 3.4 %collective-permute-start.10 = (bf16[512,128]{1,0:T(8,128)(2,1)S(1)}, bf16[512,128]{1,0:T(8,128)(2,1)S(1)}, u32[]{:S(2)}, u32[]{:S(2)}) collective-permute-start(bf16[512,128]{1,0:T(8,128)(2,1)S(1)} %collective-permute-done.6.m1), channel_id=1, source_target_pairs={{0,1},{1,0},{2,3},{3,2},{4,5},{5,4},{6,7},{7,6},{8,9},{9,8},{10,11... | collective-permute-start | bytes 393224 | tf_op jit(solution)/shard_map/ppermute | solution.py:29
  23.1 1.3 %collective-permute-start.11 = (bf16[512,128]{1,0:T(8,128)(2,1)S(1)}, bf16[512,128]{1,0:T(8,128)(2,1)S(1)}, u32[]{:S(2)}, u32[]{:S(2)}) collective-permute-start(bf16[512,128]{1,0:T(8,128)(2,1)S(1)} %collective-permute-done.7.m2), channel_id=1, source_target_pairs={{0,1},{1,0},{2,3},{3,2},{4,5},{5,4},{6,7},{7,6},{8,9},{9,8},{10,11... | collective-permute-start | bytes 393224 | tf_op jit(solution)/shard_map/ppermute | solution.py:29
  23.6 1.3 %collective-permute-start.12 = (bf16[512,128]{1,0:T(8,128)(2,1)S(1)}, bf16[512,128]{1,0:T(8,128)(2,1)S(1)}, u32[]{:S(2)}, u32[]{:S(2)}) collective-permute-start(bf16[512,128]{1,0:T(8,128)(2,1)S(1)} %collective-permute-done.8.m3), channel_id=1, source_target_pairs={{0,1},{1,0},{2,3},{3,2},{4,5},{5,4},{6,7},{7,6},{8,9},{9,8},{10,11... | collective-permute-start | bytes 393224 | tf_op jit(solution)/shard_map/ppermute | solution.py:29
  27.6 6.7 %copy-start.10 = (f32[256,8]{0,1:T(8,128)S(1)}, f32[256,8]{0,1:T(8,128)}, u32[]{:S(2)}) copy-start(f32[256,8]{0,1:T(8,128)} %param.12) | copy-start | bytes 24580
  27.6 6.8 %copy-start.5 = (bf16[256,1024]{1,0:T(8,128)(2,1)S(1)}, bf16[256,1024]{1,0:T(8,128)(2,1)}, u32[]{:S(2)}) copy-start(bf16[256,1024]{1,0:T(8,128)(2,1)} %in_rows.3) | copy-start | bytes 1572868
  27.6 6.8 %copy-start.6 = (bf16[256,512]{1,0:T(8,128)(2,1)S(1)}, bf16[256,512]{1,0:T(8,128)(2,1)}, u32[]{:S(2)}) copy-start(bf16[256,512]{1,0:T(8,128)(2,1)} %x.3) | copy-start | bytes 786436
  27.6 1.6 %collective-permute-start.13 = (bf16[256,256]{1,0:T(8,128)(2,1)S(1)}, bf16[256,256]{1,0:T(8,128)(2,1)S(1)}, u32[]{:S(2)}, u32[]{:S(2)}) collective-permute-start(bf16[256,256]{1,0:T(8,128)(2,1)S(1)} %shard_map.109.refs_16_), channel_id=1, source_target_pairs={{0,1},{1,0},{2,3},{3,2},{4,5},{5,4},{6,7},{7,6},{8,9},{9,8},{10,11... | collective-permute-start | bytes 393224 | tf_op jit(solution)/shard_map/ppermute | solution.py:29
  31.3 15.5 %collective-permute-start.17 = (bf16[2,2,256,256]{3,2,1,0:T(8,128)(2,1)}, bf16[2,2,256,256]{3,2,1,0:T(8,128)(2,1)}, u32[]{:S(2)}, u32[]{:S(2)}) collective-permute-start(bf16[2,2,256,256]{3,2,1,0:T(8,128)(2,1)} %get-tuple-element.25), channel_id=1, source_target_pairs={{0,24},{1,25},{2,26},{3,27},{4,28},{5,29},{6,30},{7,31},{8,16},{9,... | collective-permute-start | bytes 1572872 | tf_op jit(solution)/shard_map/ppermute | solution.py:49
  34.0 14.8 %collective-permute-start.14 = (bf16[2,2,256,256]{3,2,1,0:T(8,128)(2,1)}, bf16[2,2,256,256]{3,2,1,0:T(8,128)(2,1)}, u32[]{:S(2)}, u32[]{:S(2)}) collective-permute-start(bf16[2,2,256,256]{3,2,1,0:T(8,128)(2,1)} %get-tuple-element.19), channel_id=1, source_target_pairs={{0,8},{1,9},{2,10},{3,11},{4,12},{5,13},{6,14},{7,15},{8,0},{9,1},... | collective-permute-start | bytes 1572872 | tf_op jit(solution)/shard_map/ppermute | solution.py:49
  36.4 16.8 %collective-permute-start = (bf16[528,128]{1,0:T(8,128)(2,1)S(1)}, bf16[528,128]{1,0:T(8,128)(2,1)S(1)}, u32[]{:S(2)}, u32[]{:S(2)}) collective-permute-start(bf16[528,128]{1,0:T(8,128)(2,1)S(1)} %shard_map.104.mine), channel_id=1, source_target_pairs={{0,32},{32,0},{64,96},{96,64},{128,160},{160,128},{192,224},{224,1... | collective-permute-start | bytes 405512 | tf_op jit(solution)/shard_map/ppermute | solution.py:33
  41.3 2.2 %copy-start.2 = (bf16[8192,256]{1,0:T(8,128)(2,1)S(1)}, bf16[8192,256]{1,0:T(8,128)(2,1)}, u32[]{:S(2)}) copy-start(bf16[8192,256]{1,0:T(8,128)(2,1)} %refs_7_.3) | copy-start | bytes 12582916
  44.8 22.2 %copy-start.7 = (bf16[256,1024]{1,0:T(8,128)(2,1)S(1)}, bf16[256,1024]{1,0:T(8,128)(2,1)}, u32[]{:S(2)}) copy-start(bf16[256,1024]{1,0:T(8,128)(2,1)} %out_rows.1) | copy-start | bytes 1572868
  44.8 22.2 %copy-start.8 = (f32[8]{0:T(128)S(1)}, f32[8]{0:T(128)}, u32[]{:S(2)}) copy-start(f32[8]{0:T(128)} %param.13) | copy-start | bytes 100
  48.5 12.7 %collective-permute-start.18 = (bf16[1,2,256,256]{3,2,1,0:T(8,128)(2,1)S(1)}, bf16[1,2,256,256]{3,2,1,0:T(8,128)(2,1)S(1)}, u32[]{:S(2)}, u32[]{:S(2)}) collective-permute-start(bf16[1,2,256,256]{3,2,1,0:T(8,128)(2,1)S(1)} %get-tuple-element.27), channel_id=1, source_target_pairs={{0,8},{1,9},{2,10},{3,11},{4,12},{5,13},{6,14},{7,15},{8,0},{9,1},... | collective-permute-start | bytes 786440 | tf_op jit(solution)/shard_map/ppermute | solution.py:49
  50.6 13.7 %collective-permute-start.15 = (bf16[1,2,256,256]{3,2,1,0:T(8,128)(2,1)S(1)}, bf16[1,2,256,256]{3,2,1,0:T(8,128)(2,1)S(1)}, u32[]{:S(2)}, u32[]{:S(2)}) collective-permute-start(bf16[1,2,256,256]{3,2,1,0:T(8,128)(2,1)S(1)} %get-tuple-element.21), channel_id=1, source_target_pairs={{0,24},{1,25},{2,26},{3,27},{4,28},{5,29},{6,30},{7,31},{8,16},{9,... | collective-permute-start | bytes 786440 | tf_op jit(solution)/shard_map/ppermute | solution.py:49
  53.8 13.0 %collective-permute-start.1 = (bf16[528,128]{1,0:T(8,128)(2,1)S(1)}, bf16[528,128]{1,0:T(8,128)(2,1)S(1)}, u32[]{:S(2)}, u32[]{:S(2)}) collective-permute-start(bf16[528,128]{1,0:T(8,128)(2,1)S(1)} %shard_map.105), channel_id=1, source_target_pairs={{0,64},{32,96},{64,128},{96,160},{128,192},{160,224},{192,0},{224,... | collective-permute-start | bytes 405512 | tf_op jit(solution)/shard_map/ppermute | solution.py:38
  56.3 10.6 %collective-permute-start.2 = (bf16[528,128]{1,0:T(8,128)(2,1)S(1)}, bf16[528,128]{1,0:T(8,128)(2,1)S(1)}, u32[]{:S(2)}, u32[]{:S(2)}) collective-permute-start(bf16[528,128]{1,0:T(8,128)(2,1)S(1)} %shard_map.105), channel_id=1, source_target_pairs={{0,128},{32,160},{64,192},{96,224},{128,0},{160,32},{192,64},{224,... | collective-permute-start | bytes 405512 | tf_op jit(solution)/shard_map/ppermute | solution.py:38
  58.6 8.3 %collective-permute-start.3 = (bf16[528,128]{1,0:T(8,128)(2,1)S(1)}, bf16[528,128]{1,0:T(8,128)(2,1)S(1)}, u32[]{:S(2)}, u32[]{:S(2)}) collective-permute-start(bf16[528,128]{1,0:T(8,128)(2,1)S(1)} %shard_map.105), channel_id=1, source_target_pairs={{0,192},{32,224},{64,0},{96,32},{128,64},{160,96},{192,128},{224,1... | collective-permute-start | bytes 405512 | tf_op jit(solution)/shard_map/ppermute | solution.py:38
  61.8 11.6 %collective-permute-start.19 = (bf16[256,256]{1,0:T(8,128)(2,1)S(1)}, bf16[256,256]{1,0:T(8,128)(2,1)S(1)}, u32[]{:S(2)}, u32[]{:S(2)}) collective-permute-start(bf16[256,256]{1,0:T(8,128)(2,1)S(1)} %bitcast.41), channel_id=1, source_target_pairs={{0,4},{1,5},{2,6},{3,7},{4,0},{5,1},{6,2},{7,3},{8,12},{9,13},{10,... | collective-permute-start | bytes 393224 | tf_op jit(solution)/shard_map/ppermute | solution.py:53
  64.3 9.2 %collective-permute-start.20 = (bf16[256,256]{1,0:T(8,128)(2,1)S(1)}, bf16[256,256]{1,0:T(8,128)(2,1)S(1)}, u32[]{:S(2)}, u32[]{:S(2)}) collective-permute-start(bf16[256,256]{1,0:T(8,128)(2,1)S(1)} %bitcast.40), channel_id=1, source_target_pairs={{0,6},{1,7},{2,4},{3,5},{4,2},{5,3},{6,0},{7,1},{8,14},{9,15},{10,... | collective-permute-start | bytes 393224 | tf_op jit(solution)/shard_map/ppermute | solution.py:53
  66.8 7.3 %collective-permute-start.16 = (bf16[256,256]{1,0:T(8,128)(2,1)S(1)}, bf16[256,256]{1,0:T(8,128)(2,1)S(1)}, u32[]{:S(2)}, u32[]{:S(2)}) collective-permute-start(bf16[256,256]{1,0:T(8,128)(2,1)S(1)} %bitcast.42), channel_id=1, source_target_pairs={{0,2},{1,3},{2,0},{3,1},{4,6},{5,7},{6,4},{7,5},{8,10},{9,11},{10,... | collective-permute-start | bytes 393224 | tf_op jit(solution)/shard_map/ppermute | solution.py:53

commit v3 on v1

--- a/solution.py
+++ b/solution.py
@@ -45,7 +45,15 @@
     return lax.ppermute(block, ("section", "tp"), route)
 
 
-def swap_chip(block, offset):
+def swap_x(block, offset):
+    return lax.ppermute(block, "tp", [(t, t ^ (8 * offset)) for t in range(TP)])
+
+
+def swap_x_cross(block, offset):
+    return lax.ppermute(block, "tp", [(t, t ^ (8 * offset) ^ 1) for t in range(TP)])
+
+
+def swap_zl(block, offset):
     return lax.ppermute(block, "tp", [(t, t ^ (2 * offset)) for t in range(TP)])
 
 
@@ -57,14 +65,14 @@
     return pl.BlockSpec(shape, lambda i, s: (0,) * len(shape))
 
 
-def call(body, scalars, in_specs, out_shapes, args, scratch=(), flops=0, moved=0):
+def call(body, scalars, in_specs, out_shapes, args, scratch=(), flops=0, moved=0, out_specs=None):
     return pl.pallas_call(
         body,
         grid_spec=pltpu.PrefetchScalarGridSpec(
             num_scalar_prefetch=1,
             grid=(1,),
             in_specs=in_specs,
-            out_specs=[whole(o.shape) for o in out_shapes],
+            out_specs=out_specs or [whole(o.shape) for o in out_shapes],
             scratch_shapes=list(scratch),
         ),
         out_shape=out_shapes,
@@ -85,67 +93,112 @@
         far[...] = v_far[...]
 
 
-def attend_body(s, q, m0, m1, m2, m3, o0, o1, o2, o3, out, scores):
+def copy_blocks_body(offsets):
+    def body(s, weights, after, *refs):
+        outs, sems = refs[: len(offsets)], refs[len(offsets)]
+        copies = []
+        for k, (out, blocks) in enumerate(zip(outs, offsets)):
+            for i, (r, flip) in enumerate(blocks):
+                core = 1 - s[2] if flip else s[2]
+                copies.append(
+                    pltpu.make_async_copy(
+                        weights.at[s[5 + r] * 2 + core], out.at[i], sems.at[len(copies)]
+                    )
+                )
+        for copy in copies:
+            copy.start()
+        for copy in copies:
+            copy.wait()
+
+    return body
+
+
+def fold(op, block, into=None):
+    for at in range(0, block.shape[1], 128):
+        part = block[:, at : at + 128]
+        into = part if into is None else op(into, part)
+    return into
+
+
+def attend_body(s, q, mine, other, mine_far, other_far, out, scores):
     y, zh, core = s[0], s[1], s[2]
     length = q.shape[0]
-    half = m0.shape[0] // 2
     me = y * 2 + zh
-
-    def run(keys, values):
+    rate = 1.0 / math.sqrt(HEAD_DIM) * math.log2(math.e)
+
+    def run(near_keys, far_keys, near_values, far_values):
         stacked = jnp.concatenate([q[:, :HEAD_DIM], q[:, HEAD_DIM:]], axis=0)
         top = None
-        for b, key in enumerate(keys):
-            for part in range(2):
-                got = lax.dot_general(
-                    stacked,
-                    key[part * half : (part + 1) * half, :],
-                    (((1,), (1,)), ((), ())),
-                    preferred_element_type=f32,
-                ) * (1.0 / math.sqrt(HEAD_DIM))
-                if b == 0 and part == 0:
-                    row = lax.broadcasted_iota(jnp.int32, got.shape, 0) & (length - 1)
-                    col = lax.broadcasted_iota(jnp.int32, got.shape, 1)
-                    got = jnp.where(col <= row, got, masked_score)
-                else:
-                    owner = ((y + 4 - b) & 3) * 2 + (zh if part == 0 else 1 - zh)
-                    got = jnp.where(owner < me, got, masked_score)
-                at = (2 * b + part) * half
-                scores[:, at : at + half] = got
-                peak = jnp.max(got, axis=1, keepdims=True)
-                top = peak if top is None else jnp.maximum(top, peak)
-        total = jnp.zeros_like(top)
+        for block in range(8):
+            b, part = block // 2, block % 2
+            keys, row = (near_keys, block) if b == 0 else (far_keys, block - 2)
+            got = lax.dot_general(
+                stacked,
+                keys[row * length : (row + 1) * length, :],
+                (((1,), (1,)), ((), ())),
+                preferred_element_type=f32,
+            )
+            if block == 0:
+                row = lax.broadcasted_iota(jnp.int32, got.shape, 0) & (length - 1)
+                col = lax.broadcasted_iota(jnp.int32, got.shape, 1)
+                got = jnp.where(col <= row, got, masked_score)
+            else:
+                owner = ((y + 4 - b) & 3) * 2 + (zh if part == 0 else 1 - zh)
+                got = got + jnp.where(owner < me, 0.0, masked_score).astype(f32)
+            scores[:, block * length : (block + 1) * length] = got
+            top = fold(jnp.maximum, got, top)
+        top = jnp.max(top, axis=1, keepdims=True) * rate
+        total = None
         mixed = jnp.zeros(stacked.shape, f32)
-        for b, value in enumerate(values):
-            weights = jnp.exp(scores[:, 2 * half * b : 2 * half * (b + 1)] - top)
-            total = total + jnp.sum(weights, axis=1, keepdims=True)
-            mixed = mixed + jnp.dot(weights.astype(bf16), value[...], preferred_element_type=f32)
-        done = (mixed / total).astype(bf16)
-        out[:, :HEAD_DIM] = done[:length]
-        out[:, HEAD_DIM:] = done[length:]
+        for b in range(4):
+            at = slice(2 * length * b, 2 * length * (b + 1))
+            weights = jnp.exp2(scores[:, at] * rate - top)
+            total = fold(jnp.add, weights, total)
+            value = near_values[...] if b == 0 else far_values[
+                2 * length * (b - 1) : 2 * length * b, :
+            ]
+            mixed = mixed + jnp.dot(weights.astype(bf16), value, preferred_element_type=f32)
+        done = mixed / jnp.sum(total, axis=1, keepdims=True)
+        done = done.astype(bf16).astype(f32)
+        out[:HEAD_DIM, :] = done[:length].T.astype(bf16)
+        out[HEAD_DIM:, :] = done[length:].T.astype(bf16)
 
     @pl.when(core == 0)
     def _():
-        run((m0, m1, m2, m3), (o0, o1, o2, o3))
+        run(mine, mine_far, other, other_far)
 
     @pl.when(core != 0)
     def _():
-        run((o0, o1, o2, o3), (m0, m1, m2, m3))
-
-
-def project_body(count):
-    def body(s, *refs):
-        own = refs[:count]
-        got = refs[count : 2 * count]
-        here, there = refs[2 * count : 2 * count + 2]
-        outs = refs[2 * count + 2 :]
-        contract = (((1,), (1,)), ((), ()))
-        for w, v, o in zip(own, got, outs):
-            o[...] = (
-                lax.dot_general(w[...], here[...], contract, preferred_element_type=f32)
-                + lax.dot_general(v[...], there[...], contract, preferred_element_type=f32)
-            ).astype(bf16)
-
-    return body
+        run(other, other_far, mine, mine_far)
+
+
+def project_body(s, own0, own1, own2, own3, mate, s1, x1, s2, x2, a0, ac, a1, a1c, a3, a3c, out1, out2):
+    own = (own0, own1, own2, own3)
+    here, near = a0[...], ac[...]
+    for i in range(4):
+        first = i < 2
+        same, cross = (s1, x1) if first else (s2, x2)
+        there, far = (a1, a1c) if first else (a3, a3c)
+        out = out1 if first else out2
+        out[i % 2] = (
+            jnp.dot(own[i][...], here, preferred_element_type=f32)
+            + jnp.dot(mate[i // 2, 0, i % 2], near, preferred_element_type=f32)
+            + jnp.dot(same[i % 2], there[...], preferred_element_type=f32)
+            + jnp.dot(cross[i % 2], far[...], preferred_element_type=f32)
+        ).astype(bf16)
+
+
+def gather_body(s, *refs):
+    rows = refs[0].shape[0]
+    for i, ref in enumerate(refs[:-1]):
+        refs[-1][i * rows : (i + 1) * rows, :] = ref[...]
+
+
+def add_split_body(s, kept, arrived, *outs):
+    rows = kept.shape[0] // len(outs)
+    for i, out in enumerate(outs):
+        at = slice(i * rows, (i + 1) * rows)
+        out[...] = (kept[at].astype(f32) + arrived[at].astype(f32)).astype(bf16)
 
 
 def running_sums(decay):
@@ -228,21 +281,32 @@
     return body
 
 
-def scan_body(s, x, in_rows, out_rows, decay, gain, partner, t1, t2, t3, out, entering):
+def chain_body(heads):
+    inner = heads * SSM_HEAD_DIM
+
+    def body(s, joined, near, out):
+        fade = fades(joined, inner, heads)
+        for h in range(heads):
+            rows = head_rows(h)
+            before = jnp.where(s[0] >= 1, near[rows, :].astype(f32), 0.0)
+            out[rows, :] = (fade[h : h + 1] * before + joined[rows, :].astype(f32)).astype(bf16)
+
+    return body
+
+
+def scan_body(s, x, in_rows, out_rows, decay, gain, partner, near, far, out, entering):
     y, zh = s[0], s[1]
     heads = decay.shape[1]
     inner = heads * SSM_HEAD_DIM
     length = x.shape[0]
     down, across = running_sums(decay[...])
-    fade1 = fades(t1, inner, heads)
-    fade2 = fades(t2, inner, heads)
+    fade1 = fades(near, inner, heads)
     fade0 = fades(partner, inner, heads)
     for h in range(heads):
         rows = head_rows(h)
-        third = jnp.where(y >= 3, t3[rows, :].astype(f32), 0.0)
-        second = jnp.where(y >= 2, t2[rows, :].astype(f32), 0.0)
-        first = jnp.where(y >= 1, t1[rows, :].astype(f32), 0.0)
-        state = first + fade1[h : h + 1] * (second + fade2[h : h + 1] * third)
+        second = jnp.where(y >= 2, far[rows, :].astype(f32), 0.0)
+        first = jnp.where(y >= 1, near[rows, :].astype(f32), 0.0)
+        state = first + fade1[h : h + 1] * second
         later = fade0[h : h + 1] * state + partner[rows, :].astype(f32)
         entering[rows, :] = jnp.where(zh == 0, state, later).astype(bf16)
     contract = (((1,), (1,)), ((), ()))
@@ -301,6 +365,19 @@
     own_spec = pl.BlockSpec(head_block, lambda i, s: (0, s[3]))
     far_spec = pl.BlockSpec(head_block, lambda i, s: (0, s[4]))
     block = shape(head_block, bf16)
+
+    def gather(blocks):
+        rows, lanes = blocks[0].shape
+        (out,) = call(
+            gather_body,
+            scalars,
+            [whole(blocks[0].shape)] * len(blocks),
+            [shape((rows * len(blocks), lanes), bf16)],
+            blocks,
+            moved=4 * len(blocks) * rows * lanes,
+        )
+        return out
+
     own, far = call(
         pick_body,
         scalars,
@@ -309,11 +386,30 @@
         (key_rows, value_rows, key_rows, value_rows),
         moved=6 * length * HEAD_DIM * 2,
     )
-    pair = jnp.concatenate([own, swap_zh_near(far)], axis=0)
-
-    weights = out_weight.reshape(CHIPS, 2, ROWS, out_weight.shape[1])
-    sent = lax.dynamic_index_in_dim(weights, 1 - core, 1, keepdims=False)
-    got_weight = swap_core(sent.reshape(CHIPS * ROWS, out_weight.shape[1]))
+    arrived_far = swap_zh_near(far)
+
+    weights = out_weight.reshape(2 * CHIPS, ROWS, out_weight.shape[1])
+    any_spec = pl.BlockSpec(memory_space=pl.ANY)
+
+    def copy_blocks(offsets, after):
+        return call(
+            copy_blocks_body(offsets),
+            scalars,
+            [any_spec] * 2,
+            [shape((len(o), *weights.shape[1:]), bf16) for o in offsets],
+            (weights, after),
+            scratch=[pltpu.SemaphoreType.DMA((sum(len(o) for o in offsets),))],
+            out_specs=[any_spec] * len(offsets),
+            moved=4000000,
+        )
+
+    to1, to3 = (4, 5, 8, 9), (14, 15, 10, 11)
+    sent = copy_blocks([[(r, flip) for r in to] for to in (to1, to3) for flip in (0, 1)], far)
+    same1, cross1 = swap_x(sent[0], 1), swap_x_cross(sent[1], 1)
+    same3, cross3 = swap_x(sent[2], 3), swap_x_cross(sent[3], 3)
+    (sent_mate,) = copy_blocks([[(r, 1) for r in (0, 1, 12, 13, 2, 3, 6, 7)]], sent[0])
+    mate = swap_core(sent_mate)
+    pair = gather([own, arrived_far])
 
     heads = log_decay.shape[1]
     inner = heads * SSM_HEAD_DIM
@@ -330,19 +426,28 @@
         moved=600000,
     )
 
-    pairs = [pair] + [shift_y(pair, d) for d in (1, 2, 3)]
-    others = [swap_core(p) for p in pairs]
+    pair_other = swap_core(pair)
+    fetched = gather([shift_y(pair, d) for d in (1, 2, 3)])
+    fetched_other = swap_core(fetched)
     (attended,) = call(
         attend_body,
         scalars,
-        [whole(query_rows.shape)] + [whole(pair.shape)] * 8,
-        [shape(query_rows.shape, bf16)],
-        (query_rows, *pairs, *others),
+        [whole(query_rows.shape)] + [whole(pair.shape)] * 2 + [whole(fetched.shape)] * 2,
+        [shape((query_rows.shape[1], length), bf16)],
+        (query_rows, pair, pair_other, fetched, fetched_other),
         scratch=[pltpu.VMEM((2 * length, 4 * pair.shape[0]), f32)],
         flops=4 * 2 * length * 4 * pair.shape[0] * HEAD_DIM,
         moved=2000000,
     )
-    attended_there = swap_core(attended)
+    attended1, attended3 = swap_x(attended, 1), swap_x(attended, 3)
+    heard = [
+        attended,
+        swap_core(attended),
+        attended1,
+        swap_core(attended1),
+        attended3,
+        swap_core(attended3),
+    ]
 
     partner = swap_zh(closing)
     (joined,) = call(
@@ -353,40 +458,71 @@
         (closing, partner),
         moved=400000,
     )
-    earlier = [shift_y(joined, d) for d in (1, 2, 3)]
+    near = shift_y(joined, 1)
+    (chained,) = call(
+        chain_body(heads),
+        scalars,
+        [whole(closing.shape)] * 2,
+        [shape((inner, N_STATE), bf16)],
+        (joined, near),
+        moved=400000,
+    )
+    further = shift_y(chained, 2)
 
     weight_block = (ROWS, out_weight.shape[1])
-    parts = []
-    for start in range(0, CHIPS, 4):
-        offsets = list(range(start, start + 4))
+    part = shape((2, ROWS, length), bf16)
+
+    def project(offsets, half):
         own_specs = [
             pl.BlockSpec(weight_block, lambda i, s, r=r: (s[5 + r] * 2 + s[2], 0)) for r in offsets
         ]
-        got_specs = [pl.BlockSpec(weight_block, lambda i, s, r=r: (s[5 + r], 0)) for r in offsets]
-        parts += call(
-            project_body(4),
+        mate_spec = pl.BlockSpec((2, 1, 2, *weight_block), lambda i, s: (0, half, 0, 0, 0))
+        slab_spec = pl.BlockSpec((2, *weight_block), lambda i, s: (half, 0, 0))
+        return call(
+            project_body,
             scalars,
-            own_specs + got_specs + [whole(attended.shape)] * 2,
-            [shape((ROWS, length), bf16)] * 4,
-            [out_weight] * 4 + [got_weight] * 4 + [attended, attended_there],
-            flops=4 * 2 * ROWS * 512 * length,
-            moved=2000000,
+            own_specs + [mate_spec] + [slab_spec] * 4 + [whole(attended.shape)] * 6,
+            [part] * 2,
+            [out_weight] * 4
+            + [mate.reshape(2, 2, 2, *weight_block), same1, cross1, same3, cross3]
+            + heard,
+            flops=4 * 2 * ROWS * 1024 * length,
+            moved=3000000,
         )
-    arrived = [parts[0]] + [swap_chip(parts[r], r) for r in range(1, CHIPS)]
+
+    sent1, sent2 = project([12, 13, 6, 7], 1)
+    kept1, kept2 = project([0, 1, 2, 3], 0)
+    arrived1, arrived2 = swap_x(sent1, 3), swap_x(sent2, 1)
+
+    def add_split(kept, arrived):
+        out = shape((1, ROWS, length), bf16)
+        return call(
+            add_split_body,
+            scalars,
+            [whole(kept.shape)] * 2,
+            [out] * 2,
+            (kept, arrived),
+            moved=6 * kept.size,
+        )
+
+    z0, z1 = add_split(kept1, arrived1)
+    z2, z3 = add_split(kept2, arrived2)
+    arrived = [z0[0]] + [swap_zl(z[0], b) for b, z in ((2, z2), (3, z3), (1, z1))]
     (attn_out,) = call(
-        sum_body(CHIPS),
-        scalars,
-        [whole((ROWS, length))] * CHIPS,
+        sum_body(4),
+        scalars,
+        [whole((ROWS, length))] * 4,
         [shape((ROWS, length), bf16)],
         arrived,
-        moved=17 * ROWS * length * 2,
+        moved=5 * ROWS * length * 2,
     )
 
     (ssm_out,) = call(
         scan_body,
         scalars,
         [x_spec, own_spec, own_spec, decay_spec, whole((1, heads))]
-        + [whole(closing.shape)] * 4,
+        + [whole(closing.shape)] * 2
+        + [whole(further.shape)],
         [shape(scan_input.shape, bf16)],
         (
             scan_input,
@@ -395,7 +531,8 @@
             log_decay,
             skip_gain.reshape(1, heads),
             partner,
-            *earlier,
+            near,
+            further,
         ),
         scratch=[pltpu.VMEM((inner, N_STATE), bf16)],
         flops=2 * heads * length * length * SSM_HEAD_DIM,

time: 107 us -> 114 us (1.065)
  the two profiles are of different devices: /device:TPU:33 before, /device:TPU:8 now
where the time goes in v3:
time: 114 us; the launch traced here: 112 us
  Pallas kernels  39 us (34%)
  starting transfers between devices  37.4 us (33%)
  waiting for transfers between devices  31.5 us (28%)
  local copies, waits for them, and re-layouts  3.38 us (3%)
    pallas_call x15, Pallas kernels, call(): pl.pallas_call(body, grid_spec=pltpu.PrefetchScalarGridSpec(num_scalar_pr...  39 us
    ppermute x6, starting transfers between devices, swap_x(): return lax.ppermute(block, 'tp', [(t, t ^ 8 * offset) for t in range(TP)])  11.4 us
    ppermute x6, waiting for transfers between devices, swap_x(): return lax.ppermute(block, 'tp', [(t, t ^ 8 * offset) for t in range(TP)])  9.85 us
    ppermute x2, waiting for transfers between devices, swap_x_cross(): lax.ppermute(block, 'tp', [(t, t ^ 8 * offset ^ 1) for t in range(TP)])  8.8 us
    ppermute x3, starting transfers between devices, swap_zl(): return lax.ppermute(block, 'tp', [(t, t ^ 2 * offset) for t in range(TP)])  6.83 us
    ppermute x1, starting transfers between devices, swap_zh_near(): return lax.ppermute(block, ('section', 'tp'), route)  6.39 us
    ppermute x5, starting transfers between devices, shift_y(): return lax.ppermute(block, 'section', route)  6.11 us
    ppermute x5, waiting for transfers between devices, shift_y(): return lax.ppermute(block, 'section', route)  5.36 us
  transfers between devices with their start and end apart: 24, of which 8 were waited for; matrix products, arithmetic and copies ran while one was open for 0% of the time, Pallas kernels for 33%

profile of v3, /device:TPU:8, one launch (start us, length us, event | category | flops | bytes accessed | tf_op | source)
XLA Modules:
  0.0 112.3 jit_solution(7952152901518844415)
XLA Ops:
  0.7 0.1 stack.87.s
  0.8 0.0 copy-start.1
  0.8 1.0 copy-done.1
  1.8 1.0 copy-done.2
  2.9 0.6 shard_map.108
  3.5 6.4 %collective-permute-start.8 = (bf16[256,128]{1,0:T(8,128)(2,1)S(1)}, bf16[256,128]{1,0:T(8,128)(2,1)S(1)}, u32[]{:S(2)}, u32[]{:S(2)}) collective-permute-start(bf16[256,128]{1,0:T(8,128)(2,1)S(1)} %get-tuple-element.16.after), channel_id=1, source_target_pairs={{0,36},{1,37},{2,38},{3,39},{4,32},{5,33},{6,34},{7,35},{8,44},{9,... | collective-permute-start | bytes 196616 | tf_op jit(solution)/shard_map/ppermute | solution.py:45
  9.9 2.8 %collective-permute-done.8.refs_1_ = bf16[256,128]{1,0:T(8,128)(2,1)S(1)} collective-permute-done((bf16[256,128]{1,0:T(8,128)(2,1)S(1)}, bf16[256,128]{1,0:T(8,128)(2,1)S(1)}, u32[]{:S(2)}, u32[]{:S(2)}) %collective-permute-start.8) | collective-permute-done | bytes 65568 | tf_op jit(solution)/shard_map/ppermute | solution.py:45
  12.7 0.5 shard_map.111.mine
  13.2 1.7 %collective-permute-start.10 = (bf16[512,128]{1,0:T(8,128)(2,1)S(1)}, bf16[512,128]{1,0:T(8,128)(2,1)S(1)}, u32[]{:S(2)}, u32[]{:S(2)}) collective-permute-start(bf16[512,128]{1,0:T(8,128)(2,1)S(1)} %shard_map.111.mine), channel_id=1, source_target_pairs={{0,64},{32,96},{64,128},{96,160},{128,192},{160,224},{192,0},{224,... | collective-permute-start | bytes 393224 | tf_op jit(solution)/shard_map/ppermute | solution.py:38
  14.9 0.9 collective-permute-start.11
  15.8 2.4 %collective-permute-start.12 = (bf16[512,128]{1,0:T(8,128)(2,1)S(1)}, bf16[512,128]{1,0:T(8,128)(2,1)S(1)}, u32[]{:S(2)}, u32[]{:S(2)}) collective-permute-start(bf16[512,128]{1,0:T(8,128)(2,1)S(1)} %shard_map.111.mine), channel_id=1, source_target_pairs={{0,192},{32,224},{64,0},{96,32},{128,64},{160,96},{192,128},{224,1... | collective-permute-start | bytes 393224 | tf_op jit(solution)/shard_map/ppermute | solution.py:38
  18.2 17.7 %shard_map.109 = (bf16[4,256,256]{2,1,0:T(8,128)(2,1)S(1)}, bf16[4,256,256]{2,1,0:T(8,128)(2,1)S(1)}, bf16[4,256,256]{2,1,0:T(8,128)(2,1)S(1)}, bf16[4,256,256]{2,1,0:T(8,128)(2,1)}) custom-call(s32[21]{0:T(128)S(1)} %stack.87.s, bf16[32,256,256]{2,1,0:T(8,128)(2,1)} %bitcast.28, bf16[256,128]{1,0:T(8,128)(2,1)S(1)} %get-tuple-element.16.after), custom_call_target="tpu_custom_call" | custom-call | bytes 4000000 | tf_op jit(solution)/shard_map/pallas_call | solution.py:69
  35.9 0.0 copy-start.8
  36.0 0.0 copy-start.9
  36.0 0.0 copy-start.5
  36.0 1.6 %shard_map.110 = bf16[8,256,256]{2,1,0:T(8,128)(2,1)} custom-call(s32[21]{0:T(128)S(1)} %stack.87.s, bf16[32,256,256]{2,1,0:T(8,128)(2,1)S(1)} %bitcast.29, bf16[4,256,256]{2,1,0:T(8,128)(2,1)S(1)} %get-tuple-element.17.after), custom_call_target="tpu_custom_call" | custom-call | bytes 4000000 | tf_op jit(solution)/shard_map/pallas_call | solution.py:69
  37.6 0.1 collective-permute-start.3
  37.7 0.0 collective-permute-done.10.refs_0_
  37.7 0.6 shard_map.112.mine_far
  38.3 0.6 collective-permute-start.13
  38.9 0.1 collective-permute-start.9
  39.0 1.5 %collective-permute-start.4 = (bf16[4,256,256]{2,1,0:T(8,128)(2,1)S(1)}, bf16[4,256,256]{2,1,0:T(8,128)(2,1)S(1)}, u32[]{:S(2)}, u32[]{:S(2)}) collective-permute-start(bf16[4,256,256]{2,1,0:T(8,128)(2,1)S(1)} %get-tuple-element.17.after), channel_id=1, source_target_pairs={{0,8},{1,9},{2,10},{3,11},{4,12},{5,13},{6,14},{7,15},{8,0},{9,1},... | collective-permute-start | bytes 1572872 | tf_op jit(solution)/shard_map/ppermute | solution.py:49
  40.5 0.3 collective-permute-start.5
  40.7 0.3 collective-permute-done.9.other
  41.1 2.8 %collective-permute-start.6 = (bf16[4,256,256]{2,1,0:T(8,128)(2,1)S(1)}, bf16[4,256,256]{2,1,0:T(8,128)(2,1)S(1)}, u32[]{:S(2)}, u32[]{:S(2)}) collective-permute-start(bf16[4,256,256]{2,1,0:T(8,128)(2,1)S(1)} %get-tuple-element.19), channel_id=1, source_target_pairs={{0,24},{1,25},{2,26},{3,27},{4,28},{5,29},{6,30},{7,31},{8,16},{9,... | collective-permute-start | bytes 1572872 | tf_op jit(solution)/shard_map/ppermute | solution.py:49
  43.8 0.0 collective-permute-done.13.other_far
  43.9 0.0 collective-permute-start.7
  43.9 4.2 %shard_map.113.a0 = bf16[256,256]{1,0:T(8,128)(2,1)} custom-call(s32[21]{0:T(128)S(1)} %stack.87.s, bf16[256,256]{1,0:T(8,128)(2,1)S(1)} %copy-done.8, bf16[512,128]{1,0:T(8,128)(2,1)S(1)} %shard_map.111.mine, bf16[512,128]{1,0:T(8,128)(2,1)S(1)} %collective-permute-done.9.other, bf16[1536,128]{1,0:T(8,128)(2,1)S(1)} %shard_map.112.mine_far, ...), custom_call_target="tpu_custom_call" | custom-call | flops 536870912 | bytes 2000000 | tf_op jit(solution)/shard_map/pallas_call | solution.py:69
  48.0 5.7 %collective-permute-done.4.s1 = bf16[4,256,256]{2,1,0:T(8,128)(2,1)S(1)} collective-permute-done((bf16[4,256,256]{2,1,0:T(8,128)(2,1)S(1)}, bf16[4,256,256]{2,1,0:T(8,128)(2,1)S(1)}, u32[]{:S(2)}, u32[]{:S(2)}) %collective-permute-start.4) | collective-permute-done | bytes 524320 | tf_op jit(solution)/shard_map/ppermute | solution.py:49
  53.7 1.5 %collective-permute-start.15 = (bf16[256,256]{1,0:T(8,128)(2,1)}, bf16[256,256]{1,0:T(8,128)(2,1)}, u32[]{:S(2)}, u32[]{:S(2)}) collective-permute-start(bf16[256,256]{1,0:T(8,128)(2,1)} %shard_map.113.a0), channel_id=1, source_target_pairs={{0,8},{1,9},{2,10},{3,11},{4,12},{5,13},{6,14},{7,15},{8,0},{9,1},... | collective-permute-start | bytes 393224 | tf_op jit(solution)/shard_map/ppermute | solution.py:49
  55.2 8.8 %collective-permute-done.5.x1 = bf16[4,256,256]{2,1,0:T(8,128)(2,1)S(1)} collective-permute-done((bf16[4,256,256]{2,1,0:T(8,128)(2,1)S(1)}, bf16[4,256,256]{2,1,0:T(8,128)(2,1)S(1)}, u32[]{:S(2)}, u32[]{:S(2)}) %collective-permute-start.5) | collective-permute-done | bytes 524320 | tf_op jit(solution)/shard_map/ppermute | solution.py:53
  64.0 2.8 %collective-permute-start.17 = (bf16[256,256]{1,0:T(8,128)(2,1)}, bf16[256,256]{1,0:T(8,128)(2,1)}, u32[]{:S(2)}, u32[]{:S(2)}) collective-permute-start(bf16[256,256]{1,0:T(8,128)(2,1)} %shard_map.113.a0), channel_id=1, source_target_pairs={{0,24},{1,25},{2,26},{3,27},{4,28},{5,29},{6,30},{7,31},{8,16},{9,... | collective-permute-start | bytes 393224 | tf_op jit(solution)/shard_map/ppermute | solution.py:49
  66.7 0.0 collective-permute-done.6.s2
  66.7 0.8 collective-permute-start.14
  67.5 0.0 collective-permute-done.15.a1
  67.5 0.1 collective-permute-start.16
  67.6 4.2 %collective-permute-done.17.a3 = bf16[256,256]{1,0:T(8,128)(2,1)} collective-permute-done((bf16[256,256]{1,0:T(8,128)(2,1)}, bf16[256,256]{1,0:T(8,128)(2,1)}, u32[]{:S(2)}, u32[]{:S(2)}) %collective-permute-start.17) | collective-permute-done | bytes 131104 | tf_op jit(solution)/shard_map/ppermute | solution.py:49
  71.8 0.1 collective-permute-start.18
  71.9 0.1 copy.12.decay
  72.0 0.0 copy-start.3
  72.1 1.0 copy-done.3
  73.1 1.9 %shard_map.104.mine = bf16[528,128]{1,0:T(8,128)(2,1)S(1)} custom-call(s32[21]{0:T(128)S(1)} %stack.87.s, bf16[256,512]{1,0:T(8,128)(2,1)S(1)} %copy-done.5, bf16[256,1024]{1,0:T(8,128)(2,1)S(1)} %copy-done.3, f32[256,8]{1,0:T(8,128)S(1)} %copy.12.decay), custom_call_target="tpu_custom_call" | custom-call | flops 33554432 | bytes 600000 | tf_op jit(solution)/shard_map/pallas_call | solution.py:69
  75.0 4.6 %collective-permute-start = (bf16[528,128]{1,0:T(8,128)(2,1)S(1)}, bf16[528,128]{1,0:T(8,128)(2,1)S(1)}, u32[]{:S(2)}, u32[]{:S(2)}) collective-permute-start(bf16[528,128]{1,0:T(8,128)(2,1)S(1)} %shard_map.104.mine), channel_id=1, source_target_pairs={{0,32},{32,0},{64,96},{96,64},{128,160},{160,128},{192,224},{224,1... | collective-permute-start | bytes 405512 | tf_op jit(solution)/shard_map/ppermute | solution.py:33
  79.7 2.6 %shard_map.115 = (bf16[2,256,256]{2,1,0:T(8,128)(2,1)S(1)}, bf16[2,256,256]{2,1,0:T(8,128)(2,1)S(1)}) custom-call(s32[21]{0:T(128)S(1)} %stack.87.s, bf16[8192,256]{1,0:T(8,128)(2,1)} %own3.3, bf16[8192,256]{1,0:T(8,128)(2,1)} %own3.3, bf16[8192,256]{1,0:T(8,128)(2,1)} %own3.3, bf16[8192,256]{1,0:T(8,128)(2,1)} %own3.3, ...), custom_call_target="tpu_custom_call" | custom-call | flops 536870912 | bytes 3000000 | tf_op jit(solution)/shard_map/pallas_call | solution.py:69
  82.3 0.4 collective-permute-start.20
  82.7 2.5 %collective-permute-start.19 = (bf16[2,256,256]{2,1,0:T(8,128)(2,1)S(1)}, bf16[2,256,256]{2,1,0:T(8,128)(2,1)S(1)}, u32[]{:S(2)}, u32[]{:S(2)}) collective-permute-start(bf16[2,256,256]{2,1,0:T(8,128)(2,1)S(1)} %get-tuple-element.23), channel_id=1, source_target_pairs={{0,24},{1,25},{2,26},{3,27},{4,28},{5,29},{6,30},{7,31},{8,16},{9,... | collective-permute-start | bytes 786440 | tf_op jit(solution)/shard_map/ppermute | solution.py:49
  85.2 0.6 shard_map.105.joined
  85.8 0.1 collective-permute-start.1
  85.9 5.3 %collective-permute-done.1.near = bf16[528,128]{1,0:T(8,128)(2,1)S(1)} collective-permute-done((bf16[528,128]{1,0:T(8,128)(2,1)S(1)}, bf16[528,128]{1,0:T(8,128)(2,1)S(1)}, u32[]{:S(2)}, u32[]{:S(2)}) %collective-permute-start.1) | collective-permute-done | bytes 135200 | tf_op jit(solution)/shard_map/ppermute | solution.py:38
  91.2 0.6 shard_map.106
  91.8 0.0 copy-start.4
  91.9 0.0 copy-start.6
  91.9 0.0 copy-start.7
  91.9 1.0 collective-permute-start.2
  92.9 2.6 %shard_map.114 = (bf16[2,256,256]{2,1,0:T(8,128)(2,1)S(1)}, bf16[2,256,256]{2,1,0:T(8,128)(2,1)S(1)}) custom-call(s32[21]{0:T(128)S(1)} %stack.87.s, bf16[8192,256]{1,0:T(8,128)(2,1)} %own3.3, bf16[8192,256]{1,0:T(8,128)(2,1)} %own3.3, bf16[8192,256]{1,0:T(8,128)(2,1)} %own3.3, bf16[8192,256]{1,0:T(8,128)(2,1)} %own3.3, ...), custom_call_target="tpu_custom_call" | custom-call | flops 536870912 | bytes 3000000 | tf_op jit(solution)/shard_map/pallas_call | solution.py:69
  95.5 0.6 shard_map.117
  96.1 4.8 %collective-permute-start.21 = (bf16[256,256]{1,0:T(8,128)(2,1)S(1)}, bf16[256,256]{1,0:T(8,128)(2,1)S(1)}, u32[]{:S(2)}, u32[]{:S(2)}) collective-permute-start(bf16[256,256]{1,0:T(8,128)(2,1)S(1)} %bitcast.35), channel_id=1, source_target_pairs={{0,4},{1,5},{2,6},{3,7},{4,0},{5,1},{6,2},{7,3},{8,12},{9,13},{10,... | collective-permute-start | bytes 393224 | tf_op jit(solution)/shard_map/ppermute | solution.py:57
  101.0 1.9 %collective-permute-start.22 = (bf16[256,256]{1,0:T(8,128)(2,1)S(1)}, bf16[256,256]{1,0:T(8,128)(2,1)S(1)}, u32[]{:S(2)}, u32[]{:S(2)}) collective-permute-start(bf16[256,256]{1,0:T(8,128)(2,1)S(1)} %bitcast.34), channel_id=1, source_target_pairs={{0,6},{1,7},{2,4},{3,5},{4,2},{5,3},{6,0},{7,1},{8,14},{9,15},{10,... | collective-permute-start | bytes 393224 | tf_op jit(solution)/shard_map/ppermute | solution.py:57
  102.9 0.6 shard_map.116
  103.5 0.1 collective-permute-start.23
  103.6 3.0 %shard_map.107 = bf16[256,512]{1,0:T(8,128)(2,1)} custom-call(s32[21]{0:T(128)S(1)} %stack.87.s, bf16[256,512]{1,0:T(8,128)(2,1)S(1)} %copy-done.5, bf16[256,1024]{1,0:T(8,128)(2,1)S(1)} %copy-done.4, bf16[256,1024]{1,0:T(8,128)(2,1)S(1)} %copy-done.6, f32[256,8]{1,0:T(8,128)S(1)} %copy.12.decay, f32[1,8]{1,0:T(1,128)S(1)} %bitcast.33, ...), custom_call_target="tpu_custom_call" | custom-call | flops 67108864 | bytes 1500000 | tf_op jit(solution)/shard_map/pallas_call | solution.py:69
  106.7 3.7 %collective-permute-done.21.refs_1_ = bf16[256,256]{1,0:T(8,128)(2,1)S(1)} collective-permute-done((bf16[256,256]{1,0:T(8,128)(2,1)S(1)}, bf16[256,256]{1,0:T(8,128)(2,1)S(1)}, u32[]{:S(2)}, u32[]{:S(2)}) %collective-permute-start.21) | collective-permute-done | bytes 131104 | tf_op jit(solution)/shard_map/ppermute | solution.py:57
  110.4 0.7 collective-permute-done.23.refs_3_
  111.0 1.3 %shard_map.118 = bf16[256,256]{1,0:T(8,128)(2,1)} custom-call(s32[21]{0:T(128)S(1)} %stack.87.s, bf16[256,256]{1,0:T(8,128)(2,1)S(1)} %bitcast.32, bf16[256,256]{1,0:T(8,128)(2,1)S(1)} %collective-permute-done.21.refs_1_, bf16[256,256]{1,0:T(8,128)(2,1)S(1)} %collective-permute-done.22.refs_2_, bf16[256,256]{1,0:T(8,128)(2,1)S(1)} %collective-permute-done.23.refs_3_), custom_call_target="tpu_custom_call" | custom-call | bytes 655360 | tf_op jit(solution)/shard_map/pallas_call | solution.py:69
  (21 shorter events, 0.0 us)
Async XLA Ops:
  0.8 1.0 copy-start.1
  1.8 1.0 copy-start.2
  2.9 33.1 %copy-start = (bf16[8192,256]{1,0:T(8,128)(2,1)S(1)}, bf16[8192,256]{1,0:T(8,128)(2,1)}, u32[]{:S(2)}) copy-start(bf16[8192,256]{1,0:T(8,128)(2,1)} %own3.3) | copy-start | bytes 12582916
  3.5 9.2 %collective-permute-start.8 = (bf16[256,128]{1,0:T(8,128)(2,1)S(1)}, bf16[256,128]{1,0:T(8,128)(2,1)S(1)}, u32[]{:S(2)}, u32[]{:S(2)}) collective-permute-start(bf16[256,128]{1,0:T(8,128)(2,1)S(1)} %get-tuple-element.16.after), channel_id=1, source_target_pairs={{0,36},{1,37},{2,38},{3,39},{4,32},{5,33},{6,34},{7,35},{8,44},{9,... | collective-permute-start | bytes 196616 | tf_op jit(solution)/shard_map/ppermute | solution.py:45
  13.2 24.5 %collective-permute-start.10 = (bf16[512,128]{1,0:T(8,128)(2,1)S(1)}, bf16[512,128]{1,0:T(8,128)(2,1)S(1)}, u32[]{:S(2)}, u32[]{:S(2)}) collective-permute-start(bf16[512,128]{1,0:T(8,128)(2,1)S(1)} %shard_map.111.mine), channel_id=1, source_target_pairs={{0,64},{32,96},{64,128},{96,160},{128,192},{160,224},{192,0},{224,... | collective-permute-start | bytes 393224 | tf_op jit(solution)/shard_map/ppermute | solution.py:38
  14.9 22.8 %collective-permute-start.11 = (bf16[512,128]{1,0:T(8,128)(2,1)S(1)}, bf16[512,128]{1,0:T(8,128)(2,1)S(1)}, u32[]{:S(2)}, u32[]{:S(2)}) collective-permute-start(bf16[512,128]{1,0:T(8,128)(2,1)S(1)} %shard_map.111.mine), channel_id=1, source_target_pairs={{0,128},{32,160},{64,192},{96,224},{128,0},{160,32},{192,64},{224,... | collective-permute-start | bytes 393224 | tf_op jit(solution)/shard_map/ppermute | solution.py:38
  15.8 21.9 %collective-permute-start.12 = (bf16[512,128]{1,0:T(8,128)(2,1)S(1)}, bf16[512,128]{1,0:T(8,128)(2,1)S(1)}, u32[]{:S(2)}, u32[]{:S(2)}) collective-permute-start(bf16[512,128]{1,0:T(8,128)(2,1)S(1)} %shard_map.111.mine), channel_id=1, source_target_pairs={{0,192},{32,224},{64,0},{96,32},{128,64},{160,96},{192,128},{224,1... | collective-permute-start | bytes 393224 | tf_op jit(solution)/shard_map/ppermute | solution.py:38
  35.9 7.9 %copy-start.8 = (bf16[256,256]{1,0:T(8,128)(2,1)S(1)}, bf16[256,256]{1,0:T(8,128)(2,1)}, u32[]{:S(2)}) copy-start(bf16[256,256]{1,0:T(8,128)(2,1)} %q.1) | copy-start | bytes 393220
  36.0 35.9 %copy-start.9 = (f32[256,8]{0,1:T(8,128)S(1)}, f32[256,8]{0,1:T(8,128)}, u32[]{:S(2)}) copy-start(f32[256,8]{0,1:T(8,128)} %param.12) | copy-start | bytes 24580
  36.0 36.1 %copy-start.5 = (bf16[256,512]{1,0:T(8,128)(2,1)S(1)}, bf16[256,512]{1,0:T(8,128)(2,1)}, u32[]{:S(2)}) copy-start(bf16[256,512]{1,0:T(8,128)(2,1)} %x.3) | copy-start | bytes 786436
  37.6 42.1 %collective-permute-start.3 = (bf16[8,256,256]{2,1,0:T(8,128)(2,1)}, bf16[8,256,256]{2,1,0:T(8,128)(2,1)S(1)}, u32[]{:S(2)}, u32[]{:S(2)}) collective-permute-start(bf16[8,256,256]{2,1,0:T(8,128)(2,1)} %shard_map.110), channel_id=1, source_target_pairs={{0,1},{1,0},{2,3},{3,2},{4,5},{5,4},{6,7},{7,6},{8,9},{9,8},{10,11... | collective-permute-start | bytes 3145736 | tf_op jit(solution)/shard_map/ppermute | solution.py:29
  38.3 5.6 %collective-permute-start.13 = (bf16[1536,128]{1,0:T(8,128)(2,1)S(1)}, bf16[1536,128]{1,0:T(8,128)(2,1)S(1)}, u32[]{:S(2)}, u32[]{:S(2)}) collective-permute-start(bf16[1536,128]{1,0:T(8,128)(2,1)S(1)} %shard_map.112.mine_far), channel_id=1, source_target_pairs={{0,1},{1,0},{2,3},{3,2},{4,5},{5,4},{6,7},{7,6},{8,9},{9,8},{10,11... | collective-permute-start | bytes 1179656 | tf_op jit(solution)/shard_map/ppermute | solution.py:29
  38.9 2.2 %collective-permute-start.9 = (bf16[512,128]{1,0:T(8,128)(2,1)S(1)}, bf16[512,128]{1,0:T(8,128)(2,1)S(1)}, u32[]{:S(2)}, u32[]{:S(2)}) collective-permute-start(bf16[512,128]{1,0:T(8,128)(2,1)S(1)} %shard_map.111.mine), channel_id=1, source_target_pairs={{0,1},{1,0},{2,3},{3,2},{4,5},{5,4},{6,7},{7,6},{8,9},{9,8},{10,11... | collective-permute-start | bytes 393224 | tf_op jit(solution)/shard_map/ppermute | solution.py:29
  39.0 14.7 %collective-permute-start.4 = (bf16[4,256,256]{2,1,0:T(8,128)(2,1)S(1)}, bf16[4,256,256]{2,1,0:T(8,128)(2,1)S(1)}, u32[]{:S(2)}, u32[]{:S(2)}) collective-permute-start(bf16[4,256,256]{2,1,0:T(8,128)(2,1)S(1)} %get-tuple-element.17.after), channel_id=1, source_target_pairs={{0,8},{1,9},{2,10},{3,11},{4,12},{5,13},{6,14},{7,15},{8,0},{9,1},... | collective-permute-start | bytes 1572872 | tf_op jit(solution)/shard_map/ppermute | solution.py:49
  40.5 23.5 %collective-permute-start.5 = (bf16[4,256,256]{2,1,0:T(8,128)(2,1)S(1)}, bf16[4,256,256]{2,1,0:T(8,128)(2,1)S(1)}, u32[]{:S(2)}, u32[]{:S(2)}) collective-permute-start(bf16[4,256,256]{2,1,0:T(8,128)(2,1)S(1)} %get-tuple-element.18), channel_id=1, source_target_pairs={{0,9},{1,8},{2,11},{3,10},{4,13},{5,12},{6,15},{7,14},{8,1},{9,0},... | collective-permute-start | bytes 1572872 | tf_op jit(solution)/shard_map/ppermute | solution.py:53
  41.1 25.7 %collective-permute-start.6 = (bf16[4,256,256]{2,1,0:T(8,128)(2,1)S(1)}, bf16[4,256,256]{2,1,0:T(8,128)(2,1)S(1)}, u32[]{:S(2)}, u32[]{:S(2)}) collective-permute-start(bf16[4,256,256]{2,1,0:T(8,128)(2,1)S(1)} %get-tuple-element.19), channel_id=1, source_target_pairs={{0,24},{1,25},{2,26},{3,27},{4,28},{5,29},{6,30},{7,31},{8,16},{9,... | collective-permute-start | bytes 1572872 | tf_op jit(solution)/shard_map/ppermute | solution.py:49
  43.9 31.2 %collective-permute-start.7 = (bf16[4,256,256]{2,1,0:T(8,128)(2,1)}, bf16[4,256,256]{2,1,0:T(8,128)(2,1)S(1)}, u32[]{:S(2)}, u32[]{:S(2)}) collective-permute-start(bf16[4,256,256]{2,1,0:T(8,128)(2,1)} %get-tuple-element.20), channel_id=1, source_target_pairs={{0,25},{1,24},{2,27},{3,26},{4,29},{5,28},{6,31},{7,30},{8,17},{9,... | collective-permute-start | bytes 1572872 | tf_op jit(solution)/shard_map/ppermute | solution.py:53
  53.7 13.8 %collective-permute-start.15 = (bf16[256,256]{1,0:T(8,128)(2,1)}, bf16[256,256]{1,0:T(8,128)(2,1)}, u32[]{:S(2)}, u32[]{:S(2)}) collective-permute-start(bf16[256,256]{1,0:T(8,128)(2,1)} %shard_map.113.a0), channel_id=1, source_target_pairs={{0,8},{1,9},{2,10},{3,11},{4,12},{5,13},{6,14},{7,15},{8,0},{9,1},... | collective-permute-start | bytes 393224 | tf_op jit(solution)/shard_map/ppermute | solution.py:49
  64.0 7.8 %collective-permute-start.17 = (bf16[256,256]{1,0:T(8,128)(2,1)}, bf16[256,256]{1,0:T(8,128)(2,1)}, u32[]{:S(2)}, u32[]{:S(2)}) collective-permute-start(bf16[256,256]{1,0:T(8,128)(2,1)} %shard_map.113.a0), channel_id=1, source_target_pairs={{0,24},{1,25},{2,26},{3,27},{4,28},{5,29},{6,30},{7,31},{8,16},{9,... | collective-permute-start | bytes 393224 | tf_op jit(solution)/shard_map/ppermute | solution.py:49
  66.7 12.9 %collective-permute-start.14 = (bf16[256,256]{1,0:T(8,128)(2,1)}, bf16[256,256]{1,0:T(8,128)(2,1)}, u32[]{:S(2)}, u32[]{:S(2)}) collective-permute-start(bf16[256,256]{1,0:T(8,128)(2,1)} %shard_map.113.a0), channel_id=1, source_target_pairs={{0,1},{1,0},{2,3},{3,2},{4,5},{5,4},{6,7},{7,6},{8,9},{9,8},{10,11... | collective-permute-start | bytes 393224 | tf_op jit(solution)/shard_map/ppermute | solution.py:29
  67.5 12.1 %collective-permute-start.16 = (bf16[256,256]{1,0:T(8,128)(2,1)}, bf16[256,256]{1,0:T(8,128)(2,1)}, u32[]{:S(2)}, u32[]{:S(2)}) collective-permute-start(bf16[256,256]{1,0:T(8,128)(2,1)} %collective-permute-done.15.a1), channel_id=1, source_target_pairs={{0,1},{1,0},{2,3},{3,2},{4,5},{5,4},{6,7},{7,6},{8,9},{9,8},{10,11... | collective-permute-start | bytes 393224 | tf_op jit(solution)/shard_map/ppermute | solution.py:29
  71.8 7.9 %collective-permute-start.18 = (bf16[256,256]{1,0:T(8,128)(2,1)}, bf16[256,256]{1,0:T(8,128)(2,1)}, u32[]{:S(2)}, u32[]{:S(2)}) collective-permute-start(bf16[256,256]{1,0:T(8,128)(2,1)} %collective-permute-done.17.a3), channel_id=1, source_target_pairs={{0,1},{1,0},{2,3},{3,2},{4,5},{5,4},{6,7},{7,6},{8,9},{9,8},{10,11... | collective-permute-start | bytes 393224 | tf_op jit(solution)/shard_map/ppermute | solution.py:29
  72.0 1.0 copy-start.3
  75.0 10.2 %collective-permute-start = (bf16[528,128]{1,0:T(8,128)(2,1)S(1)}, bf16[528,128]{1,0:T(8,128)(2,1)S(1)}, u32[]{:S(2)}, u32[]{:S(2)}) collective-permute-start(bf16[528,128]{1,0:T(8,128)(2,1)S(1)} %shard_map.104.mine), channel_id=1, source_target_pairs={{0,32},{32,0},{64,96},{96,64},{128,160},{160,128},{192,224},{224,1... | collective-permute-start | bytes 405512 | tf_op jit(solution)/shard_map/ppermute | solution.py:33
  82.3 13.2 %collective-permute-start.20 = (bf16[2,256,256]{2,1,0:T(8,128)(2,1)S(1)}, bf16[2,256,256]{2,1,0:T(8,128)(2,1)S(1)}, u32[]{:S(2)}, u32[]{:S(2)}) collective-permute-start(bf16[2,256,256]{2,1,0:T(8,128)(2,1)S(1)} %get-tuple-element.26), channel_id=1, source_target_pairs={{0,8},{1,9},{2,10},{3,11},{4,12},{5,13},{6,14},{7,15},{8,0},{9,1},... | collective-permute-start | bytes 786440 | tf_op jit(solution)/shard_map/ppermute | solution.py:49
  82.7 20.2 %collective-permute-start.19 = (bf16[2,256,256]{2,1,0:T(8,128)(2,1)S(1)}, bf16[2,256,256]{2,1,0:T(8,128)(2,1)S(1)}, u32[]{:S(2)}, u32[]{:S(2)}) collective-permute-start(bf16[2,256,256]{2,1,0:T(8,128)(2,1)S(1)} %get-tuple-element.23), channel_id=1, source_target_pairs={{0,24},{1,25},{2,26},{3,27},{4,28},{5,29},{6,30},{7,31},{8,16},{9,... | collective-permute-start | bytes 786440 | tf_op jit(solution)/shard_map/ppermute | solution.py:49
  85.8 5.4 %collective-permute-start.1 = (bf16[528,128]{1,0:T(8,128)(2,1)S(1)}, bf16[528,128]{1,0:T(8,128)(2,1)S(1)}, u32[]{:S(2)}, u32[]{:S(2)}) collective-permute-start(bf16[528,128]{1,0:T(8,128)(2,1)S(1)} %shard_map.105.joined), channel_id=1, source_target_pairs={{0,64},{32,96},{64,128},{96,160},{128,192},{160,224},{192,0},{224,... | collective-permute-start | bytes 405512 | tf_op jit(solution)/shard_map/ppermute | solution.py:38
  91.8 11.8 %copy-start.4 = (bf16[256,1024]{1,0:T(8,128)(2,1)S(1)}, bf16[256,1024]{1,0:T(8,128)(2,1)}, u32[]{:S(2)}) copy-start(bf16[256,1024]{1,0:T(8,128)(2,1)} %in_rows.3) | copy-start | bytes 1572868
  91.9 11.8 %copy-start.6 = (bf16[256,1024]{1,0:T(8,128)(2,1)S(1)}, bf16[256,1024]{1,0:T(8,128)(2,1)}, u32[]{:S(2)}) copy-start(bf16[256,1024]{1,0:T(8,128)(2,1)} %out_rows.1) | copy-start | bytes 1572868
  91.9 11.8 %copy-start.7 = (f32[8]{0:T(128)S(1)}, f32[8]{0:T(128)}, u32[]{:S(2)}) copy-start(f32[8]{0:T(128)} %param.13) | copy-start | bytes 100
  91.9 11.7 %collective-permute-start.2 = (bf16[512,128]{1,0:T(8,128)(2,1)S(1)}, bf16[512,128]{1,0:T(8,128)(2,1)S(1)}, u32[]{:S(2)}, u32[]{:S(2)}) collective-permute-start(bf16[512,128]{1,0:T(8,128)(2,1)S(1)} %shard_map.106), channel_id=1, source_target_pairs={{0,128},{32,160},{64,192},{96,224},{128,0},{160,32},{192,64},{224,... | collective-permute-start | bytes 393224 | tf_op jit(solution)/shard_map/ppermute | solution.py:38
  96.1 14.2 %collective-permute-start.21 = (bf16[256,256]{1,0:T(8,128)(2,1)S(1)}, bf16[256,256]{1,0:T(8,128)(2,1)S(1)}, u32[]{:S(2)}, u32[]{:S(2)}) collective-permute-start(bf16[256,256]{1,0:T(8,128)(2,1)S(1)} %bitcast.35), channel_id=1, source_target_pairs={{0,4},{1,5},{2,6},{3,7},{4,0},{5,1},{6,2},{7,3},{8,12},{9,13},{10,... | collective-permute-start | bytes 393224 | tf_op jit(solution)/shard_map/ppermute | solution.py:57
  101.0 9.4 %collective-permute-start.22 = (bf16[256,256]{1,0:T(8,128)(2,1)S(1)}, bf16[256,256]{1,0:T(8,128)(2,1)S(1)}, u32[]{:S(2)}, u32[]{:S(2)}) collective-permute-start(bf16[256,256]{1,0:T(8,128)(2,1)S(1)} %bitcast.34), channel_id=1, source_target_pairs={{0,6},{1,7},{2,4},{3,5},{4,2},{5,3},{6,0},{7,1},{8,14},{9,15},{10,... | collective-permute-start | bytes 393224 | tf_op jit(solution)/shard_map/ppermute | solution.py:57
  103.5 7.5 %collective-permute-start.23 = (bf16[256,256]{1,0:T(8,128)(2,1)S(1)}, bf16[256,256]{1,0:T(8,128)(2,1)S(1)}, u32[]{:S(2)}, u32[]{:S(2)}) collective-permute-start(bf16[256,256]{1,0:T(8,128)(2,1)S(1)} %bitcast.36), channel_id=1, source_target_pairs={{0,2},{1,3},{2,0},{3,1},{4,6},{5,7},{6,4},{7,5},{8,10},{9,11},{10,... | collective-permute-start | bytes 393224 | tf_op jit(solution)/shard_map/ppermute | solution.py:57

commit v4 on v3

v4 whole, which is shorter than its diff:
```python
import math

import jax
import jax.numpy as jnp
from jax import lax
from jax.experimental import pallas as pl
from jax.experimental.pallas import tpu as pltpu
from jax.sharding import PartitionSpec as P

SCAN_HEADS = 256
SSM_HEAD_DIM = 64
N_STATE = 128
GROUPS = 8
Q_HEADS = 64
KV_HEADS = 8
HEAD_DIM = 128

SECTIONS = 8
TP = 32
ROWS = 256
CHIPS = 16
masked_score = -1e30
bf16 = jnp.bfloat16
f32 = jnp.float32


def swap_core(block):
    return lax.ppermute(block, "tp", [(t, t ^ 1) for t in range(TP)])


def swap_zh(block):
    return lax.ppermute(block, "section", [(s, s ^ 1) for s in range(SECTIONS)])


def shift_y(block, distance):
    route = [(s, (s + 2 * distance) % SECTIONS) for s in range(SECTIONS)]
    return lax.ppermute(block, "section", route)


def swap_zh_near(block):
    route = [
        (s * TP + t, (s ^ 1) * TP + (t ^ 4)) for s in range(SECTIONS) for t in range(TP)
    ]
    return lax.ppermute(block, ("section", "tp"), route)


def swap_x(block, offset):
    return lax.ppermute(block, "tp", [(t, t ^ (8 * offset)) for t in range(TP)])


def swap_zl(block, offset):
    return lax.ppermute(block, "tp", [(t, t ^ (2 * offset)) for t in range(TP)])


def whole(shape):
    return pl.BlockSpec(shape, lambda i, s: (0,) * len(shape))


def call(
    body, scalars, in_specs, out_shapes, args, scratch=(), limit=16, after=(), us=0.5, out_specs=None
):
    first, count = 1 + len(in_specs), len(after)

    def ordered(*refs):
        body(*refs[:first], *refs[first + count :])

    return pl.pallas_call(
        ordered,
        grid_spec=pltpu.PrefetchScalarGridSpec(
            num_scalar_prefetch=1,
            grid=(1,),
            in_specs=list(in_specs) + [pl.BlockSpec(memory_space=pl.ANY)] * count,
            out_specs=out_specs or [whole(o.shape) for o in out_shapes],
            scratch_shapes=list(scratch),
        ),
        out_shape=out_shapes,
        compiler_params=pltpu.CompilerParams(vmem_limit_bytes=limit * 1024 * 1024),
        cost_estimate=pl.CostEstimate(
            flops=int(us * 1e9), bytes_accessed=int(us * 3.5e6), transcendentals=0
        ),
    )(scalars, *args, *after)


def copy_body(s, weights, mate, own, sems):
    copies = [
        pltpu.make_async_copy(weights.at[:, 1 - s[2]], mate, sems.at[0]),
        pltpu.make_async_copy(weights.at[:, s[2]], own, sems.at[1]),
    ]
    for copy in copies:
        copy.start()
    for copy in copies:
        copy.wait()


def join_body(s, *refs):
    rows = refs[0].shape[0]
    for i, ref in enumerate(refs[:-1]):
        refs[-1][i * rows : (i + 1) * rows, :] = ref[...]


def fold(op, block, into=None):
    for at in range(0, block.shape[1], 128):
        part = block[:, at : at + 128]
        into = part if into is None else op(into, part)
    return into


def attend(s, q, keys, values, first, scores):
    y, zh = s[0], s[1]
    length = q.shape[0]
    me = y * 2 + zh
    rate = 1.0 / math.sqrt(HEAD_DIM) * math.log2(math.e)
    stacked = jnp.concatenate([q[:, :HEAD_DIM], q[:, HEAD_DIM:]], axis=0)
    top = None
    for b, key in enumerate(keys):
        for part in range(2):
            got = lax.dot_general(
                stacked,
                key[part * length : (part + 1) * length, :],
                (((1,), (1,)), ((), ())),
                preferred_element_type=f32,
            )
            if first + b == 0 and part == 0:
                row = lax.broadcasted_iota(jnp.int32, got.shape, 0) & (length - 1)
                col = lax.broadcasted_iota(jnp.int32, got.shape, 1)
                got = jnp.where(col <= row, got, masked_score)
            else:
                owner = ((y + 4 - first - b) & 3) * 2 + (zh if part == 0 else 1 - zh)
                got = got + jnp.where(owner < me, 0.0, masked_score).astype(f32)
            scores[:, (2 * b + part) * length : (2 * b + part + 1) * length] = got
            top = fold(jnp.maximum, got, top)
    top = jnp.max(top, axis=1, keepdims=True) * rate
    total = None
    mixed = jnp.zeros(stacked.shape, f32)
    for b, value in enumerate(values):
        weights = jnp.exp2(scores[:, 2 * length * b : 2 * length * (b + 1)] * rate - top)
        total = fold(jnp.add, weights, total)
        mixed = mixed + jnp.dot(weights.astype(bf16), value[...], preferred_element_type=f32)
    return top, total, mixed


def attend_near_body(s, q, mine, other, tops, totals, mixeds, scores):
    def run(keys, values):
        top, total, mixed = attend(s, q, [keys], [values], 0, scores)
        tops[...] = jnp.broadcast_to(top, tops.shape)
        totals[...] = total
        mixeds[...] = mixed

    @pl.when(s[2] == 0)
    def _():
        run(mine, other)

    @pl.when(s[2] != 0)
    def _():
        run(other, mine)


def attend_far_body(s, q, mine, other, tops, totals, mixeds, out, scores):
    length = q.shape[0]

    def run(keys, values):
        parts = [slice(2 * length * b, 2 * length * (b + 1)) for b in range(3)]
        far_top, far_total, far_mixed = attend(
            s, q, [keys[at, :] for at in parts], [values[at, :] for at in parts], 1, scores
        )
        near_top = tops[...][:, :1]
        top = jnp.maximum(near_top, far_top)
        near, far = jnp.exp2(near_top - top), jnp.exp2(far_top - top)
        total = jnp.sum(totals[...] * near + far_total * far, axis=1, keepdims=True)
        done = (mixeds[...] * near + far_mixed * far) / total
        out[:HEAD_DIM, :] = done[:length].T.astype(bf16)
        out[HEAD_DIM:, :] = done[length:].T.astype(bf16)

    @pl.when(s[2] == 0)
    def _():
        run(mine, other)

    @pl.when(s[2] != 0)
    def _():
        run(other, mine)


def project_body(s, *refs):
    count = (len(refs) - 4) // 2
    own = refs[:count]
    got = refs[count : 2 * count]
    here, there = refs[2 * count : 2 * count + 2]
    outs = refs[2 * count + 2 :]
    each = count // len(outs)
    for i in range(count):
        outs[i // each][(i % each) // 2, i % 2] = (
            jnp.dot(own[i][0], here[...], preferred_element_type=f32)
            + jnp.dot(got[i][0], there[...], preferred_element_type=f32)
        ).astype(bf16)


def add_split_body(s, kept, arrived, *outs):
    rows = kept.shape[0] // len(outs)
    for i, out in enumerate(outs):
        at = slice(i * rows, (i + 1) * rows)
        out[...] = (kept[at].astype(f32) + arrived[at].astype(f32)).astype(bf16)


def running_sums(decay):
    length = decay.shape[0]
    row = lax.broadcasted_iota(jnp.int32, (length, length), 0)
    col = lax.broadcasted_iota(jnp.int32, (length, length), 1)
    lower = (col <= row).astype(f32)
    down = jnp.dot(lower, decay, precision=lax.Precision.HIGHEST, preferred_element_type=f32)
    across = lax.dot_general(
        decay,
        lower,
        (((0,), (1,)), ((), ())),
        precision=lax.Precision.HIGHEST,
        preferred_element_type=f32,
    )
    return down, across


def widen(per_head, width):
    heads = per_head.shape[1]
    row = lax.broadcasted_iota(jnp.int32, (heads, heads * width), 0)
    col = lax.broadcasted_iota(jnp.int32, (heads, heads * width), 1)
    spread = ((col // width) == row).astype(f32)
    return jnp.dot(per_head, spread, precision=lax.Precision.HIGHEST, preferred_element_type=f32)


def closing_body(s, x, in_rows, decay, out):
    heads = decay.shape[1]
    inner = heads * SSM_HEAD_DIM
    length = x.shape[0]
    down, across = running_sums(decay[...])
    tail = widen(jnp.exp(down[length - 1 :, :] - down), SSM_HEAD_DIM)
    scaled = (x[...].astype(f32) * tail).astype(bf16)
    out[:inner, :] = lax.dot_general(
        scaled, in_rows[...], (((0,), (0,)), ((), ())), preferred_element_type=f32
    ).astype(bf16)
    fade = jnp.exp(across[:, length - 1 :])
    fade = jnp.broadcast_to(fade, (heads, N_STATE))
    high = fade.astype(bf16)
    out[inner : inner + 2 * heads, :] = jnp.concatenate(
        [high.astype(f32), fade - high.astype(f32)], axis=0
    ).astype(bf16)


def fades(state, inner, heads):
    both = state[inner : inner + 2 * heads, :].astype(f32)
    return both[:heads] + both[heads:]


def head_rows(h):
    return slice(h * SSM_HEAD_DIM, (h + 1) * SSM_HEAD_DIM)


def pair_body(heads):
    inner = heads * SSM_HEAD_DIM

    def body(s, mine, partner, out):
        def run(first, second):
            fade0 = fades(first, inner, heads)
            fade1 = fades(second, inner, heads)
            for h in range(heads):
                rows = head_rows(h)
                out[rows, :] = (
                    fade1[h : h + 1] * first[rows, :].astype(f32) + second[rows, :].astype(f32)
                ).astype(bf16)
            fade = fade0 * fade1
            high = fade.astype(bf16)
            out[inner : inner + 2 * heads, :] = jnp.concatenate(
                [high.astype(f32), fade - high.astype(f32)], axis=0
            ).astype(bf16)

        @pl.when(s[1] == 0)
        def _():
            run(mine, partner)

        @pl.when(s[1] != 0)
        def _():
            run(partner, mine)

    return body


def chain_body(heads):
    inner = heads * SSM_HEAD_DIM

    def body(s, joined, near, out):
        fade = fades(joined, inner, heads)
        for h in range(heads):
            rows = head_rows(h)
            before = jnp.where(s[0] >= 1, near[rows, :].astype(f32), 0.0)
            out[rows, :] = (fade[h : h + 1] * before + joined[rows, :].astype(f32)).astype(bf16)

    return body


def scan_body(s, x, in_rows, out_rows, decay, gain, partner, near, far, out, entering):
    y, zh = s[0], s[1]
    heads = decay.shape[1]
    inner = heads * SSM_HEAD_DIM
    length = x.shape[0]
    down, across = running_sums(decay[...])
    fade1 = fades(near, inner, heads)
    fade0 = fades(partner, inner, heads)
    for h in range(heads):
        rows = head_rows(h)
        second = jnp.where(y >= 2, far[rows, :].astype(f32), 0.0)
        first = jnp.where(y >= 1, near[rows, :].astype(f32), 0.0)
        state = first + fade1[h : h + 1] * second
        later = fade0[h : h + 1] * state + partner[rows, :].astype(f32)
        entering[rows, :] = jnp.where(zh == 0, state, later).astype(bf16)
    contract = (((1,), (1,)), ((), ()))
    wide = x[...].astype(f32)
    carried = widen(jnp.exp(down), SSM_HEAD_DIM) * lax.dot_general(
        out_rows[...], entering[...], contract, preferred_element_type=f32
    )
    rest = carried + widen(gain[...], SSM_HEAD_DIM) * wide
    affinity = lax.dot_general(
        out_rows[...], in_rows[...], contract, preferred_element_type=f32
    )
    row = lax.broadcasted_iota(jnp.int32, (length, length), 0)
    col = lax.broadcasted_iota(jnp.int32, (length, length), 1)
    causal = col <= row
    for h in range(heads):
        lanes = slice(h * SSM_HEAD_DIM, (h + 1) * SSM_HEAD_DIM)
        gaps = down[:, h : h + 1] - across[h : h + 1, :]
        mixing = affinity * jnp.exp(jnp.where(causal, gaps, masked_score))
        inside = jnp.dot(mixing.astype(bf16), x[:, lanes], preferred_element_type=f32)
        out[:, lanes] = (inside + rest[:, lanes]).astype(bf16)


def sum_body(count):
    def body(s, *refs):
        total = refs[0][...].astype(f32)
        for ref in refs[1:count]:
            total = total + ref[...].astype(f32)
        refs[count][...] = total.astype(bf16)

    return body


def on_device(
    scan_input,
    input_map,
    output_map,
    log_decay,
    skip_gain,
    query_rows,
    key_rows,
    value_rows,
    out_weight,
):
    section = lax.axis_index("section")
    tp = lax.axis_index("tp")
    y, zh = section // 2, section % 2
    core, chip = tp % 2, tp // 2
    group = tp // (TP // GROUPS)
    shape = jax.ShapeDtypeStruct
    scalars = jnp.stack(
        [y, zh, core, group, group ^ 1] + [chip ^ r for r in range(CHIPS)]
    ).astype(jnp.int32)

    length = query_rows.shape[0]
    head_block = (length, HEAD_DIM)

    def columns(array, index):
        return lax.dynamic_slice_in_dim(array, index * HEAD_DIM, HEAD_DIM, 1)

    first = core == 0
    sent = jnp.where(first, columns(key_rows, group ^ 1), columns(value_rows, group ^ 1))
    arrived_pair = swap_zh_near(sent)
    own = jnp.where(first, columns(key_rows, group), columns(value_rows, group))
    in_rows, out_rows = columns(input_map, group), columns(output_map, group)

    (pair,) = call(
        join_body,
        scalars,
        [whole(head_block)] * 2,
        [shape((2 * length, HEAD_DIM), bf16)],
        (own, arrived_pair),
    )
    fetched = [shift_y(pair, d) for d in (2, 1, 3)]
    pair_other = swap_core(pair)

    weight_block = (ROWS, out_weight.shape[1])
    sent_mate, own_weight = call(
        copy_body,
        scalars,
        [pl.BlockSpec(memory_space=pl.ANY)],
        [shape((CHIPS, *weight_block), bf16)] * 2,
        [out_weight.reshape(CHIPS, 2, *weight_block)],
        scratch=[pltpu.SemaphoreType.DMA((2,))],
        out_specs=[pl.BlockSpec(memory_space=pl.ANY)] * 2,
        after=[sent],
    )
    mate = swap_core(sent_mate)
    heads = log_decay.shape[1]
    inner = heads * SSM_HEAD_DIM
    state_shape = shape((inner + 2 * heads, N_STATE), bf16)
    x_spec = whole(scan_input.shape)
    decay_spec = whole(log_decay.shape)
    (closing,) = call(
        closing_body,
        scalars,
        [x_spec, whole(head_block), decay_spec],
        [state_shape],
        (scan_input, in_rows, log_decay),
        us=2,
    )

    stat = shape((2 * length, HEAD_DIM), f32)
    q_spec = whole(query_rows.shape)
    near_part = call(
        attend_near_body,
        scalars,
        [q_spec] + [whole(pair.shape)] * 2,
        [stat] * 3,
        (query_rows, pair, pair_other),
        scratch=[pltpu.VMEM((2 * length, 2 * length), f32)],
        us=2.2,
    )
    (others,) = call(
        join_body,
        scalars,
        [whole(pair.shape)] * 3,
        [shape((6 * length, HEAD_DIM), bf16)],
        (fetched[1], fetched[0], fetched[2]),
        after=[closing, near_part[0]],
    )
    others_there = swap_core(others)
    (attended,) = call(
        attend_far_body,
        scalars,
        [q_spec] + [whole(others.shape)] * 2 + [whole(stat.shape)] * 3,
        [shape((query_rows.shape[1], length), bf16)],
        (query_rows, others, others_there, *near_part),
        scratch=[pltpu.VMEM((2 * length, 6 * length), f32)],
        us=40,
    )
    attended_there = swap_core(attended)

    partner = swap_zh(closing)
    def project(offsets, after=()):
        return call(
            project_body,
            scalars,
            [
                pl.BlockSpec((1, *weight_block), lambda i, s, r=r: (s[5 + r], 0, 0))
                for r in offsets * 2
            ]
            + [whole(attended.shape)] * 2,
            [shape((2, 2, ROWS, length), bf16)] * 2,
            [own_weight] * len(offsets)
            + [mate] * len(offsets)
            + [attended, attended_there],
            after=after,
            us=1.3,
        )

    sent1, sent2 = project([4, 5, 8, 9, 14, 15, 10, 11])
    (joined,) = call(
        pair_body(heads),
        scalars,
        [whole(closing.shape)] * 2,
        [state_shape],
        (closing, partner),
        after=[sent1],
    )
    near = shift_y(joined, 1)
    (chained,) = call(
        chain_body(heads),
        scalars,
        [whole(closing.shape)] * 2,
        [shape((inner, N_STATE), bf16)],
        (joined, near),
    )
    further = shift_y(chained, 2)

    kept1, kept2 = project([0, 1, 12, 13, 2, 3, 6, 7], [sent1])
    arrived1, arrived2 = swap_x(sent1, 1), swap_x(sent2, 3)

    def add_split(kept, arrived, after=()):
        out = shape((kept.shape[0] // 2, *kept.shape[1:]), bf16)
        return call(add_split_body, scalars, [whole(kept.shape)] * 2, [out] * 2, (kept, arrived), after=after)

    kept1, sent1 = add_split(kept1, arrived1, [joined])
    kept2, sent2 = add_split(kept2, arrived2)
    arrived1, arrived2 = swap_x(sent1, 3), swap_x(sent2, 1)
    z0, z1 = add_split(kept1[0], arrived1[0], [chained])
    z2, z3 = add_split(kept2[0], arrived2[0])
    arrived = [z0[0]] + [swap_zl(z[0], b) for b, z in ((2, z2), (3, z3), (1, z1))]
    (attn_out,) = call(
        sum_body(4),
        scalars,
        [whole((ROWS, length))] * 4,
        [shape((ROWS, length), bf16)],
        arrived,
        us=1.3,
    )

    (ssm_out,) = call(
        scan_body,
        scalars,
        [x_spec, whole(head_block), whole(head_block), decay_spec, whole((1, heads))]
        + [whole(closing.shape)] * 2
        + [whole(further.shape)],
        [shape(scan_input.shape, bf16)],
        (
            scan_input,
            in_rows,
            out_rows,
            log_decay,
            skip_gain.reshape(1, heads),
            partner,
            near,
            further,
        ),
        scratch=[pltpu.VMEM((inner, N_STATE), bf16)],
        us=3,
    )
    return (ssm_out, attn_out)


def solution(mesh):
    placed = (
        P("section", "tp"),
        P("section", None),
        P("section", None),
        P("section", "tp"),
        P("tp"),
        P("section", "tp"),
        P("section", None),
        P("section", None),
        P(None, "tp"),
    )
    return jax.shard_map(
        on_device,
        mesh=mesh,
        in_specs=placed,
        out_specs=(P("section", "tp"), P("tp", "section")),
        check_vma=False,
    )
```

time: 114 us -> 74 us (0.65)
  Pallas kernels: 39 us -> 18.4 us
  waiting for transfers between devices: 31.5 us -> 17.1 us
  starting transfers between devices: 37.4 us -> 34 us
  local copies, waits for them, and re-layouts: 3.38 us -> 1.82 us
    pallas_call x15 -> x16, Pallas kernels: 39 us -> 18.4 us  [call(): pl.pallas_call(ordered, grid_spec=pltpu.PrefetchScalarGridSpec(num_scalar...]
    ppermute x6 -> x4, waiting for transfers between devices: 9.85 us -> 0.67 us  [swap_x(): return lax.ppermute(block, 'tp', [(t, t ^ 8 * offset) for t in range(TP)])]
    ppermute x2 -> x0, waiting for transfers between devices: 8.8 us -> none  [swap_x_cross(): lax.ppermute(block, 'tp', [(t, t ^ 8 * offset ^ 1) for t in range(TP)])]
    ppermute x6 -> x4, starting transfers between devices: 11.4 us -> 6.02 us  [swap_x(): return lax.ppermute(block, 'tp', [(t, t ^ 8 * offset) for t in range(TP)])]
    ppermute x1, waiting for transfers between devices: 0.01 us -> 4.66 us  [swap_zh(): return lax.ppermute(block, 'section', [(s, s ^ 1) for s in range(SECTIONS)])]
    unnamed x21 -> x11, local copies, waits for them, and re-layouts: 3.28 us -> 0.85 us
    ppermute x5, starting transfers between devices: 6.11 us -> 8.25 us  [shift_y(): return lax.ppermute(block, 'section', route)]
  transfers between devices with their start and end apart: 24 -> 18, of which waited for: 8 -> 9; matrix products, arithmetic and copies ran while one was open for 0% -> 2% of each run, Pallas kernels for 33% -> 20%
where the time goes in v4:
time: 74 us; the launch traced here: 73.3 us
  starting transfers between devices  34 us (46%)
  Pallas kernels  18.4 us (25%)
  waiting for transfers between devices  17.1 us (23%)
  local copies, waits for them, and re-layouts  1.82 us (2%)
  other arithmetic  1.05 us (1%)
  between operations  0.91 us (1%)
    pallas_call x16, Pallas kernels, call(): pl.pallas_call(ordered, grid_spec=pltpu.PrefetchScalarGridSpec(num_scalar...  18.4 us
    ppermute x5, starting transfers between devices, shift_y(): return lax.ppermute(block, 'section', route)  8.25 us
    ppermute x3, starting transfers between devices, swap_zl(): return lax.ppermute(block, 'tp', [(t, t ^ 2 * offset) for t in range(TP)])  7.84 us
    ppermute x1, starting transfers between devices, swap_zh_near(): return lax.ppermute(block, ('section', 'tp'), route)  6.39 us
    ppermute x4, starting transfers between devices, swap_x(): return lax.ppermute(block, 'tp', [(t, t ^ 8 * offset) for t in range(TP)])  6.02 us
    ppermute x1, waiting for transfers between devices, swap_zh(): return lax.ppermute(block, 'section', [(s, s ^ 1) for s in range(SECTIONS)])  4.66 us
    ppermute x5, waiting for transfers between devices, shift_y(): return lax.ppermute(block, 'section', route)  4.53 us
    ppermute x1, starting transfers between devices, swap_zh(): return lax.ppermute(block, 'section', [(s, s ^ 1) for s in range(SECTIONS)])  4.48 us
  transfers between devices with their start and end apart: 18, of which 9 were waited for; matrix products, arithmetic and copies ran while one was open for 2% of the time, Pallas kernels for 20%

profile of v4, /device:TPU:8, one launch (start us, length us, event | category | flops | bytes accessed | tf_op | source)
XLA Modules:
  0.0 73.3 jit_solution(1852844569017711630)
XLA Ops:
  0.6 0.0 copy-start
  0.6 0.0 copy-start.2
  0.7 1.0 %dynamic-slice_select_fusion = (bf16[256,128]{1,0:T(8,128)(2,1)S(1)}, bf16[256,128]{1,0:T(8,128)(2,1)S(1)}) fusion(bf16[256,1024]{1,0:T(8,128)(2,1)} %param.16, s32[]{:T(128)S(6)} %select_n.48, bf16[256,1024]{1,0:T(8,128)(2,1)} %param.15, pred[]{:T(512)S(6)} %eq.6, s32[]{:T(128)S(6)} %select_n.50), kind=kLoop, calls=%fused_computation | loop fusion | flops 65536 | bytes 393225 | tf_op jit(solution)/shard_map/jit(_where)/select_n | solution.py:372
  1.7 6.4 %collective-permute-start.2 = (bf16[256,128]{1,0:T(8,128)(2,1)S(1)}, bf16[256,128]{1,0:T(8,128)(2,1)S(1)}, u32[]{:S(2)}, u32[]{:S(2)}) collective-permute-start(bf16[256,128]{1,0:T(8,128)(2,1)S(1)} %get-tuple-element.37.refs_2_), channel_id=1, source_target_pairs={{0,36},{1,37},{2,38},{3,39},{4,32},{5,33},{6,34},{7,35},{8,44},{9,... | collective-permute-start | bytes 196616 | tf_op jit(solution)/shard_map/ppermute | solution.py:44
  8.1 0.8 %copy.12.refs_3_.refs_4_ = f32[256,8]{1,0:T(8,128)S(1)} copy(f32[256,8]{0,1:T(8,128)} %param.12) | data formatting | bytes 16384 | tf_op args[3]
  9.0 0.1 stack.87.refs_0_
  9.1 0.0 copy-done
  9.1 1.8 %collective-permute-done.2.refs_2_ = bf16[256,128]{1,0:T(8,128)(2,1)S(1)} collective-permute-done((bf16[256,128]{1,0:T(8,128)(2,1)S(1)}, bf16[256,128]{1,0:T(8,128)(2,1)S(1)}, u32[]{:S(2)}, u32[]{:S(2)}) %collective-permute-start.2) | collective-permute-done | bytes 65568 | tf_op jit(solution)/shard_map/ppermute | solution.py:44
  10.9 0.5 shard_map.106.refs_2_
  11.5 0.0 copy-start.3
  11.5 0.1 collective-permute-start.6
  11.6 0.0 copy-done.2
  11.6 1.9 %shard_map.104.refs_4_.refs_1_ = bf16[528,128]{1,0:T(8,128)(2,1)S(1)} custom-call(s32[21]{0:T(128)S(1)} %stack.87.refs_0_, bf16[256,512]{1,0:T(8,128)(2,1)S(1)} %copy-done.2, bf16[256,128]{1,0:T(8,128)(2,1)S(1)} %constant_dynamic-slice_fusion.1.refs_2_, f32[256,8]{1,0:T(8,128)S(1)} %copy.12.refs_3_.refs_4_), custom_call_target="tpu_custom_call" | custom-call | flops 2000000000 | bytes 7000000 | tf_op jit(solution)/shard_map/pallas_call | solution.py:67
  13.5 1.7 %collective-permute-start.3 = (bf16[512,128]{1,0:T(8,128)(2,1)S(1)}, bf16[512,128]{1,0:T(8,128)(2,1)S(1)}, u32[]{:S(2)}, u32[]{:S(2)}) collective-permute-start(bf16[512,128]{1,0:T(8,128)(2,1)S(1)} %shard_map.106.refs_2_), channel_id=1, source_target_pairs={{0,64},{32,96},{64,128},{96,160},{128,192},{160,224},{192,0},{224,... | collective-permute-start | bytes 393224 | tf_op jit(solution)/shard_map/ppermute | solution.py:37
  15.2 1.0 %collective-permute-start.4 = (bf16[512,128]{1,0:T(8,128)(2,1)S(1)}, bf16[512,128]{1,0:T(8,128)(2,1)S(1)}, u32[]{:S(2)}, u32[]{:S(2)}) collective-permute-start(bf16[512,128]{1,0:T(8,128)(2,1)S(1)} %shard_map.106.refs_2_), channel_id=1, source_target_pairs={{0,128},{32,160},{64,192},{96,224},{128,0},{160,32},{192,64},{224,... | collective-permute-start | bytes 393224 | tf_op jit(solution)/shard_map/ppermute | solution.py:37
  16.1 2.4 %collective-permute-start.5 = (bf16[512,128]{1,0:T(8,128)(2,1)S(1)}, bf16[512,128]{1,0:T(8,128)(2,1)S(1)}, u32[]{:S(2)}, u32[]{:S(2)}) collective-permute-start(bf16[512,128]{1,0:T(8,128)(2,1)S(1)} %shard_map.106.refs_2_), channel_id=1, source_target_pairs={{0,192},{32,224},{64,0},{96,32},{128,64},{160,96},{192,128},{224,1... | collective-permute-start | bytes 393224 | tf_op jit(solution)/shard_map/ppermute | solution.py:37
  18.5 0.0 collective-permute-done.6.refs_3_
  18.5 0.0 copy-done.3
  18.5 1.3 %shard_map.107 = (f32[512,128]{1,0:T(8,128)S(1)}, f32[512,128]{1,0:T(8,128)S(1)}, f32[512,128]{1,0:T(8,128)S(1)}) custom-call(s32[21]{0:T(128)S(1)} %stack.87.refs_0_, bf16[256,256]{1,0:T(8,128)(2,1)S(1)} %copy-done.3, bf16[512,128]{1,0:T(8,128)(2,1)S(1)} %shard_map.106.refs_2_, bf16[512,128]{1,0:T(8,128)(2,1)S(1)} %collective-permute-done.6.refs_3_), custom_call_target="tpu_custom_call" | custom-call | flops 2200000000 | bytes 7700000 | tf_op jit(solution)/shard_map/pallas_call | solution.py:67
  19.9 0.0 collective-permute-done.3.refs_1_
  19.9 3.2 %collective-permute-done.4.refs_2_ = bf16[512,128]{1,0:T(8,128)(2,1)S(1)} collective-permute-done((bf16[512,128]{1,0:T(8,128)(2,1)S(1)}, bf16[512,128]{1,0:T(8,128)(2,1)S(1)}, u32[]{:S(2)}, u32[]{:S(2)}) %collective-permute-start.4) | collective-permute-done | bytes 131104 | tf_op jit(solution)/shard_map/ppermute | solution.py:37
  23.1 1.3 %collective-permute-done.5.refs_3_ = bf16[512,128]{1,0:T(8,128)(2,1)S(1)} collective-permute-done((bf16[512,128]{1,0:T(8,128)(2,1)S(1)}, bf16[512,128]{1,0:T(8,128)(2,1)S(1)}, u32[]{:S(2)}, u32[]{:S(2)}) %collective-permute-start.5) | collective-permute-done | bytes 131104 | tf_op jit(solution)/shard_map/ppermute | solution.py:37
  24.4 0.6 shard_map.108.refs_2_
  25.0 0.1 collective-permute-start.7
  25.1 0.0 copy-done.1
  25.1 0.8 %shard_map.105 = (bf16[16,256,256]{2,1,0:T(8,128)(2,1)S(1)}, bf16[16,256,256]{2,1,0:T(8,128)(2,1)S(1)}) custom-call(s32[21]{0:T(128)S(1)} %stack.87.refs_0_, bf16[16,2,256,256]{3,2,1,0:T(8,128)(2,1)S(1)} %bitcast.31, bf16[256,128]{1,0:T(8,128)(2,1)S(1)} %get-tuple-element.37.refs_2_), custom_call_target="tpu_custom_call" | custom-call | flops 500000000 | bytes 1750000 | tf_op jit(solution)/shard_map/pallas_call | solution.py:67
  26.0 0.6 collective-permute-start.1
  26.5 0.3 collective-permute-done.7.refs_3_
  26.8 2.6 %shard_map.109.refs_17_ = bf16[256,256]{1,0:T(8,128)(2,1)S(1)} custom-call(s32[21]{0:T(128)S(1)} %stack.87.refs_0_, bf16[256,256]{1,0:T(8,128)(2,1)S(1)} %copy-done.3, bf16[1536,128]{1,0:T(8,128)(2,1)S(1)} %shard_map.108.refs_2_, bf16[1536,128]{1,0:T(8,128)(2,1)S(1)} %collective-permute-done.7.refs_3_, f32[512,128]{1,0:T(8,128)S(1)} %get-tuple-element.21.refs_5_.refs_4_, ...), custom_call_target="tpu_custom_call" | custom-call | flops 40000000000 | bytes 140000000 | tf_op jit(solution)/shard_map/pallas_call | solution.py:67
  29.4 0.2 collective-permute-start.8
  29.7 1.2 %collective-permute-done.8.refs_18_ = bf16[256,256]{1,0:T(8,128)(2,1)S(1)} collective-permute-done((bf16[256,256]{1,0:T(8,128)(2,1)S(1)}, bf16[256,256]{1,0:T(8,128)(2,1)S(1)}, u32[]{:S(2)}, u32[]{:S(2)}) %collective-permute-start.8) | collective-permute-done | bytes 131104 | tf_op jit(solution)/shard_map/ppermute | solution.py:28
  30.9 0.0 collective-permute-done.1.refs_9_.refs_10_.refs_11_.refs_12_.refs_13_.refs_14_.refs_15_.refs_16_
  30.9 1.2 %shard_map.110 = (bf16[2,2,256,256]{3,2,1,0:T(8,128)(2,1)S(1)}, bf16[2,2,256,256]{3,2,1,0:T(8,128)(2,1)S(1)}) custom-call(s32[21]{0:T(128)S(1)} %stack.87.refs_0_, bf16[16,256,256]{2,1,0:T(8,128)(2,1)S(1)} %get-tuple-element.19.refs_1_.refs_2_.refs_3_.refs_4_.refs_5_.refs_6_.refs_7_.refs_8_, ...), custom_call_target="tpu_custom_call" | custom-call | flops 1300000000 | bytes 4550000 | tf_op jit(solution)/shard_map/pallas_call | solution.py:67
  32.1 3.0 %collective-permute-start.13 = (bf16[2,2,256,256]{3,2,1,0:T(8,128)(2,1)S(1)}, bf16[2,2,256,256]{3,2,1,0:T(8,128)(2,1)S(1)}, u32[]{:S(2)}, u32[]{:S(2)}) collective-permute-start(bf16[2,2,256,256]{3,2,1,0:T(8,128)(2,1)S(1)} %get-tuple-element.30), channel_id=1, source_target_pairs={{0,24},{1,25},{2,26},{3,27},{4,28},{5,29},{6,30},{7,31},{8,16},{9,... | collective-permute-start | bytes 1572872 | tf_op jit(solution)/shard_map/ppermute | solution.py:48
  35.2 0.2 collective-permute-start.11
  35.4 4.5 %collective-permute-start = (bf16[528,128]{1,0:T(8,128)(2,1)S(1)}, bf16[528,128]{1,0:T(8,128)(2,1)S(1)}, u32[]{:S(2)}, u32[]{:S(2)}) collective-permute-start(bf16[528,128]{1,0:T(8,128)(2,1)S(1)} %shard_map.104.refs_4_.refs_1_), channel_id=1, source_target_pairs={{0,32},{32,0},{64,96},{96,64},{128,160},{160,128},{192,224},{224,1... | collective-permute-start | bytes 405512 | tf_op jit(solution)/shard_map/ppermute | solution.py:32
  39.9 4.7 %collective-permute-done.refs_2_.refs_6_ = bf16[528,128]{1,0:T(8,128)(2,1)S(1)} collective-permute-done((bf16[528,128]{1,0:T(8,128)(2,1)S(1)}, bf16[528,128]{1,0:T(8,128)(2,1)S(1)}, u32[]{:S(2)}, u32[]{:S(2)}) %collective-permute-start) | collective-permute-done | bytes 135200 | tf_op jit(solution)/shard_map/ppermute | solution.py:32
  44.5 0.6 shard_map.111.refs_1_.refs_3_
  45.1 1.4 %collective-permute-start.9 = (bf16[528,128]{1,0:T(8,128)(2,1)S(1)}, bf16[528,128]{1,0:T(8,128)(2,1)S(1)}, u32[]{:S(2)}, u32[]{:S(2)}) collective-permute-start(bf16[528,128]{1,0:T(8,128)(2,1)S(1)} %shard_map.111.refs_1_.refs_3_), channel_id=1, source_target_pairs={{0,64},{32,96},{64,128},{96,160},{128,192},{160,224},{192,0},{224,... | collective-permute-start | bytes 405512 | tf_op jit(solution)/shard_map/ppermute | solution.py:37
  46.5 1.2 %shard_map.114 = (bf16[2,2,256,256]{3,2,1,0:T(8,128)(2,1)S(1)}, bf16[2,2,256,256]{3,2,1,0:T(8,128)(2,1)S(1)}) custom-call(s32[21]{0:T(128)S(1)} %stack.87.refs_0_, bf16[16,256,256]{2,1,0:T(8,128)(2,1)S(1)} %get-tuple-element.19.refs_1_.refs_2_.refs_3_.refs_4_.refs_5_.refs_6_.refs_7_.refs_8_, ...), custom_call_target="tpu_custom_call" | custom-call | flops 1300000000 | bytes 4550000 | tf_op jit(solution)/shard_map/pallas_call | solution.py:67
  47.8 0.0 collective-permute-done.13.refs_2_
  47.8 0.7 shard_map.117
  48.4 1.8 %collective-permute-start.14 = (bf16[1,2,256,256]{3,2,1,0:T(8,128)(2,1)S(1)}, bf16[1,2,256,256]{3,2,1,0:T(8,128)(2,1)S(1)}, u32[]{:S(2)}, u32[]{:S(2)}) collective-permute-start(bf16[1,2,256,256]{3,2,1,0:T(8,128)(2,1)S(1)} %get-tuple-element.32), channel_id=1, source_target_pairs={{0,8},{1,9},{2,10},{3,11},{4,12},{5,13},{6,14},{7,15},{8,0},{9,1},... | collective-permute-start | bytes 786440 | tf_op jit(solution)/shard_map/ppermute | solution.py:48
  50.3 0.0 collective-permute-done.11.refs_2_
  50.3 0.7 shard_map.115
  50.9 0.9 %collective-permute-start.12 = (bf16[1,2,256,256]{3,2,1,0:T(8,128)(2,1)S(1)}, bf16[1,2,256,256]{3,2,1,0:T(8,128)(2,1)S(1)}, u32[]{:S(2)}, u32[]{:S(2)}) collective-permute-start(bf16[1,2,256,256]{3,2,1,0:T(8,128)(2,1)S(1)} %get-tuple-element.27), channel_id=1, source_target_pairs={{0,24},{1,25},{2,26},{3,27},{4,28},{5,29},{6,30},{7,31},{8,16},{9,... | collective-permute-start | bytes 786440 | tf_op jit(solution)/shard_map/ppermute | solution.py:48
  51.9 0.0 collective-permute-done.9.refs_2_.refs_7_
  51.9 0.6 shard_map.112.refs_3_
  52.5 0.0 copy-start.4
  52.5 1.9 %collective-permute-start.10 = (bf16[512,128]{1,0:T(8,128)(2,1)S(1)}, bf16[512,128]{1,0:T(8,128)(2,1)S(1)}, u32[]{:S(2)}, u32[]{:S(2)}) collective-permute-start(bf16[512,128]{1,0:T(8,128)(2,1)S(1)} %shard_map.112.refs_3_), channel_id=1, source_target_pairs={{0,128},{32,160},{64,192},{96,224},{128,0},{160,32},{192,64},{224,... | collective-permute-start | bytes 393224 | tf_op jit(solution)/shard_map/ppermute | solution.py:37
  54.4 0.8 %constant_dynamic-slice_fusion.refs_3_ = bf16[256,128]{1,0:T(8,128)(2,1)S(1)} fusion(bf16[256,1024]{1,0:T(8,128)(2,1)} %param.11, s32[]{:T(128)S(6)} %select_n.48), kind=kLoop, calls=%fused_computation.2 | loop fusion | bytes 131076 | tf_op jit(solution)/shard_map/dynamic_slice | solution.py:367
  55.2 0.7 collective-permute-done.14
  55.9 0.6 shard_map.118
  56.5 5.5 %collective-permute-start.15 = (bf16[256,256]{1,0:T(8,128)(2,1)S(1)}, bf16[256,256]{1,0:T(8,128)(2,1)S(1)}, u32[]{:S(2)}, u32[]{:S(2)}) collective-permute-start(bf16[256,256]{1,0:T(8,128)(2,1)S(1)} %bitcast.35), channel_id=1, source_target_pairs={{0,4},{1,5},{2,6},{3,7},{4,0},{5,1},{6,2},{7,3},{8,12},{9,13},{10,... | collective-permute-start | bytes 393224 | tf_op jit(solution)/shard_map/ppermute | solution.py:52
  62.0 1.9 %collective-permute-start.16 = (bf16[256,256]{1,0:T(8,128)(2,1)S(1)}, bf16[256,256]{1,0:T(8,128)(2,1)S(1)}, u32[]{:S(2)}, u32[]{:S(2)}) collective-permute-start(bf16[256,256]{1,0:T(8,128)(2,1)S(1)} %bitcast.34), channel_id=1, source_target_pairs={{0,6},{1,7},{2,4},{3,5},{4,2},{5,3},{6,0},{7,1},{8,14},{9,15},{10,... | collective-permute-start | bytes 393224 | tf_op jit(solution)/shard_map/ppermute | solution.py:52
  63.9 0.0 collective-permute-done.12
  63.9 0.6 shard_map.116
  64.5 0.5 collective-permute-start.17
  64.9 0.0 collective-permute-done.10.refs_8_
  64.9 3.0 %shard_map.113 = bf16[256,512]{1,0:T(8,128)(2,1)} custom-call(s32[21]{0:T(128)S(1)} %stack.87.refs_0_, bf16[256,512]{1,0:T(8,128)(2,1)S(1)} %copy-done.2, bf16[256,128]{1,0:T(8,128)(2,1)S(1)} %constant_dynamic-slice_fusion.1.refs_2_, bf16[256,128]{1,0:T(8,128)(2,1)S(1)} %constant_dynamic-slice_fusion.refs_3_, f32[256,8]{1,0:T(8,128)S(1)} %copy.12.refs_3_.refs_4_, ...), custom_call_target="tpu_custom_call" | custom-call | flops 3000000000 | bytes 10500000 | tf_op jit(solution)/shard_map/pallas_call | solution.py:67
  68.0 3.3 %collective-permute-done.15.refs_2_ = bf16[256,256]{1,0:T(8,128)(2,1)S(1)} collective-permute-done((bf16[256,256]{1,0:T(8,128)(2,1)S(1)}, bf16[256,256]{1,0:T(8,128)(2,1)S(1)}, u32[]{:S(2)}, u32[]{:S(2)}) %collective-permute-start.15) | collective-permute-done | bytes 131104 | tf_op jit(solution)/shard_map/ppermute | solution.py:52
  71.3 0.0 collective-permute-done.16.refs_3_
  71.3 0.7 collective-permute-done.17.refs_4_
  72.0 1.3 %shard_map.119 = bf16[256,256]{1,0:T(8,128)(2,1)} custom-call(s32[21]{0:T(128)S(1)} %stack.87.refs_0_, bf16[256,256]{1,0:T(8,128)(2,1)S(1)} %bitcast.40, bf16[256,256]{1,0:T(8,128)(2,1)S(1)} %collective-permute-done.15.refs_2_, bf16[256,256]{1,0:T(8,128)(2,1)S(1)} %collective-permute-done.16.refs_3_, bf16[256,256]{1,0:T(8,128)(2,1)S(1)} %collective-permute-done.17.refs_4_), custom_call_target="tpu_custom_call" | custom-call | flops 1300000000 | bytes 4550000 | tf_op jit(solution)/shard_map/pallas_call | solution.py:67
  (3 shorter events, 0.0 us)
Async XLA Ops:
  0.6 8.4 %copy-start = (bf16[256,1024]{1,0:T(8,128)(2,1)S(1)}, bf16[256,1024]{1,0:T(8,128)(2,1)}, u32[]{:S(2)}) copy-start(bf16[256,1024]{1,0:T(8,128)(2,1)} %param.10) | copy-start | bytes 1572868
  0.6 10.9 %copy-start.2 = (bf16[256,512]{1,0:T(8,128)(2,1)S(1)}, bf16[256,512]{1,0:T(8,128)(2,1)}, u32[]{:S(2)}) copy-start(bf16[256,512]{1,0:T(8,128)(2,1)} %refs_1_.7) | copy-start | bytes 786436
  1.7 9.2 %collective-permute-start.2 = (bf16[256,128]{1,0:T(8,128)(2,1)S(1)}, bf16[256,128]{1,0:T(8,128)(2,1)S(1)}, u32[]{:S(2)}, u32[]{:S(2)}) collective-permute-start(bf16[256,128]{1,0:T(8,128)(2,1)S(1)} %get-tuple-element.37.refs_2_), channel_id=1, source_target_pairs={{0,36},{1,37},{2,38},{3,39},{4,32},{5,33},{6,34},{7,35},{8,44},{9,... | collective-permute-start | bytes 196616 | tf_op jit(solution)/shard_map/ppermute | solution.py:44
  11.5 7.1 %copy-start.3 = (bf16[256,256]{1,0:T(8,128)(2,1)S(1)}, bf16[256,256]{1,0:T(8,128)(2,1)}, u32[]{:S(2)}) copy-start(bf16[256,256]{1,0:T(8,128)(2,1)} %refs_1_.6) | copy-start | bytes 393220
  11.5 7.1 %collective-permute-start.6 = (bf16[512,128]{1,0:T(8,128)(2,1)S(1)}, bf16[512,128]{1,0:T(8,128)(2,1)S(1)}, u32[]{:S(2)}, u32[]{:S(2)}) collective-permute-start(bf16[512,128]{1,0:T(8,128)(2,1)S(1)} %shard_map.106.refs_2_), channel_id=1, source_target_pairs={{0,1},{1,0},{2,3},{3,2},{4,5},{5,4},{6,7},{7,6},{8,9},{9,8},{10,11... | collective-permute-start | bytes 393224 | tf_op jit(solution)/shard_map/ppermute | solution.py:28
  13.5 6.4 %collective-permute-start.3 = (bf16[512,128]{1,0:T(8,128)(2,1)S(1)}, bf16[512,128]{1,0:T(8,128)(2,1)S(1)}, u32[]{:S(2)}, u32[]{:S(2)}) collective-permute-start(bf16[512,128]{1,0:T(8,128)(2,1)S(1)} %shard_map.106.refs_2_), channel_id=1, source_target_pairs={{0,64},{32,96},{64,128},{96,160},{128,192},{160,224},{192,0},{224,... | collective-permute-start | bytes 393224 | tf_op jit(solution)/shard_map/ppermute | solution.py:37
  15.2 7.9 %collective-permute-start.4 = (bf16[512,128]{1,0:T(8,128)(2,1)S(1)}, bf16[512,128]{1,0:T(8,128)(2,1)S(1)}, u32[]{:S(2)}, u32[]{:S(2)}) collective-permute-start(bf16[512,128]{1,0:T(8,128)(2,1)S(1)} %shard_map.106.refs_2_), channel_id=1, source_target_pairs={{0,128},{32,160},{64,192},{96,224},{128,0},{160,32},{192,64},{224,... | collective-permute-start | bytes 393224 | tf_op jit(solution)/shard_map/ppermute | solution.py:37
  16.1 8.3 %collective-permute-start.5 = (bf16[512,128]{1,0:T(8,128)(2,1)S(1)}, bf16[512,128]{1,0:T(8,128)(2,1)S(1)}, u32[]{:S(2)}, u32[]{:S(2)}) collective-permute-start(bf16[512,128]{1,0:T(8,128)(2,1)S(1)} %shard_map.106.refs_2_), channel_id=1, source_target_pairs={{0,192},{32,224},{64,0},{96,32},{128,64},{160,96},{192,128},{224,1... | collective-permute-start | bytes 393224 | tf_op jit(solution)/shard_map/ppermute | solution.py:37
  18.5 6.6 %copy-start.1 = (bf16[8192,256]{1,0:T(8,128)(2,1)S(1)}, bf16[8192,256]{1,0:T(8,128)(2,1)}, u32[]{:S(2)}) copy-start(bf16[8192,256]{1,0:T(8,128)(2,1)} %param.17) | copy-start | bytes 12582916
  25.0 1.8 %collective-permute-start.7 = (bf16[1536,128]{1,0:T(8,128)(2,1)S(1)}, bf16[1536,128]{1,0:T(8,128)(2,1)S(1)}, u32[]{:S(2)}, u32[]{:S(2)}) collective-permute-start(bf16[1536,128]{1,0:T(8,128)(2,1)S(1)} %shard_map.108.refs_2_), channel_id=1, source_target_pairs={{0,1},{1,0},{2,3},{3,2},{4,5},{5,4},{6,7},{7,6},{8,9},{9,8},{10,11... | collective-permute-start | bytes 1179656 | tf_op jit(solution)/shard_map/ppermute | solution.py:28
  26.0 4.9 %collective-permute-start.1 = (bf16[16,256,256]{2,1,0:T(8,128)(2,1)S(1)}, bf16[16,256,256]{2,1,0:T(8,128)(2,1)S(1)}, u32[]{:S(2)}, u32[]{:S(2)}) collective-permute-start(bf16[16,256,256]{2,1,0:T(8,128)(2,1)S(1)} %get-tuple-element.20), channel_id=1, source_target_pairs={{0,1},{1,0},{2,3},{3,2},{4,5},{5,4},{6,7},{7,6},{8,9},{9,8},{10,11... | collective-permute-start | bytes 6291464 | tf_op jit(solution)/shard_map/ppermute | solution.py:28
  29.4 1.4 %collective-permute-start.8 = (bf16[256,256]{1,0:T(8,128)(2,1)S(1)}, bf16[256,256]{1,0:T(8,128)(2,1)S(1)}, u32[]{:S(2)}, u32[]{:S(2)}) collective-permute-start(bf16[256,256]{1,0:T(8,128)(2,1)S(1)} %shard_map.109.refs_17_), channel_id=1, source_target_pairs={{0,1},{1,0},{2,3},{3,2},{4,5},{5,4},{6,7},{7,6},{8,9},{9,8},{10,11... | collective-permute-start | bytes 393224 | tf_op jit(solution)/shard_map/ppermute | solution.py:28
  32.1 15.6 %collective-permute-start.13 = (bf16[2,2,256,256]{3,2,1,0:T(8,128)(2,1)S(1)}, bf16[2,2,256,256]{3,2,1,0:T(8,128)(2,1)S(1)}, u32[]{:S(2)}, u32[]{:S(2)}) collective-permute-start(bf16[2,2,256,256]{3,2,1,0:T(8,128)(2,1)S(1)} %get-tuple-element.30), channel_id=1, source_target_pairs={{0,24},{1,25},{2,26},{3,27},{4,28},{5,29},{6,30},{7,31},{8,16},{9,... | collective-permute-start | bytes 1572872 | tf_op jit(solution)/shard_map/ppermute | solution.py:48
  35.2 15.1 %collective-permute-start.11 = (bf16[2,2,256,256]{3,2,1,0:T(8,128)(2,1)S(1)}, bf16[2,2,256,256]{3,2,1,0:T(8,128)(2,1)S(1)}, u32[]{:S(2)}, u32[]{:S(2)}) collective-permute-start(bf16[2,2,256,256]{3,2,1,0:T(8,128)(2,1)S(1)} %get-tuple-element.24.refs_3_.refs_19_), channel_id=1, source_target_pairs={{0,8},{1,9},{2,10},{3,11},{4,12},{5,13},{6,14},{7,15},{8,0},{9,1},... | collective-permute-start | bytes 1572872 | tf_op jit(solution)/shard_map/ppermute | solution.py:48
  35.4 9.1 %collective-permute-start = (bf16[528,128]{1,0:T(8,128)(2,1)S(1)}, bf16[528,128]{1,0:T(8,128)(2,1)S(1)}, u32[]{:S(2)}, u32[]{:S(2)}) collective-permute-start(bf16[528,128]{1,0:T(8,128)(2,1)S(1)} %shard_map.104.refs_4_.refs_1_), channel_id=1, source_target_pairs={{0,32},{32,0},{64,96},{96,64},{128,160},{160,128},{192,224},{224,1... | collective-permute-start | bytes 405512 | tf_op jit(solution)/shard_map/ppermute | solution.py:32
  45.1 6.7 %collective-permute-start.9 = (bf16[528,128]{1,0:T(8,128)(2,1)S(1)}, bf16[528,128]{1,0:T(8,128)(2,1)S(1)}, u32[]{:S(2)}, u32[]{:S(2)}) collective-permute-start(bf16[528,128]{1,0:T(8,128)(2,1)S(1)} %shard_map.111.refs_1_.refs_3_), channel_id=1, source_target_pairs={{0,64},{32,96},{64,128},{96,160},{128,192},{160,224},{192,0},{224,... | collective-permute-start | bytes 405512 | tf_op jit(solution)/shard_map/ppermute | solution.py:37
  48.4 7.4 %collective-permute-start.14 = (bf16[1,2,256,256]{3,2,1,0:T(8,128)(2,1)S(1)}, bf16[1,2,256,256]{3,2,1,0:T(8,128)(2,1)S(1)}, u32[]{:S(2)}, u32[]{:S(2)}) collective-permute-start(bf16[1,2,256,256]{3,2,1,0:T(8,128)(2,1)S(1)} %get-tuple-element.32), channel_id=1, source_target_pairs={{0,8},{1,9},{2,10},{3,11},{4,12},{5,13},{6,14},{7,15},{8,0},{9,1},... | collective-permute-start | bytes 786440 | tf_op jit(solution)/shard_map/ppermute | solution.py:48
  50.9 12.9 %collective-permute-start.12 = (bf16[1,2,256,256]{3,2,1,0:T(8,128)(2,1)S(1)}, bf16[1,2,256,256]{3,2,1,0:T(8,128)(2,1)S(1)}, u32[]{:S(2)}, u32[]{:S(2)}) collective-permute-start(bf16[1,2,256,256]{3,2,1,0:T(8,128)(2,1)S(1)} %get-tuple-element.27), channel_id=1, source_target_pairs={{0,24},{1,25},{2,26},{3,27},{4,28},{5,29},{6,30},{7,31},{8,16},{9,... | collective-permute-start | bytes 786440 | tf_op jit(solution)/shard_map/ppermute | solution.py:48
  52.5 12.5 %copy-start.4 = (f32[8]{0:T(128)S(1)}, f32[8]{0:T(128)}, u32[]{:S(2)}) copy-start(f32[8]{0:T(128)} %param.13) | copy-start | bytes 100
  52.5 12.4 %collective-permute-start.10 = (bf16[512,128]{1,0:T(8,128)(2,1)S(1)}, bf16[512,128]{1,0:T(8,128)(2,1)S(1)}, u32[]{:S(2)}, u32[]{:S(2)}) collective-permute-start(bf16[512,128]{1,0:T(8,128)(2,1)S(1)} %shard_map.112.refs_3_), channel_id=1, source_target_pairs={{0,128},{32,160},{64,192},{96,224},{128,0},{160,32},{192,64},{224,... | collective-permute-start | bytes 393224 | tf_op jit(solution)/shard_map/ppermute | solution.py:37
  56.5 14.8 %collective-permute-start.15 = (bf16[256,256]{1,0:T(8,128)(2,1)S(1)}, bf16[256,256]{1,0:T(8,128)(2,1)S(1)}, u32[]{:S(2)}, u32[]{:S(2)}) collective-permute-start(bf16[256,256]{1,0:T(8,128)(2,1)S(1)} %bitcast.35), channel_id=1, source_target_pairs={{0,4},{1,5},{2,6},{3,7},{4,0},{5,1},{6,2},{7,3},{8,12},{9,13},{10,... | collective-permute-start | bytes 393224 | tf_op jit(solution)/shard_map/ppermute | solution.py:52
  62.0 9.4 %collective-permute-start.16 = (bf16[256,256]{1,0:T(8,128)(2,1)S(1)}, bf16[256,256]{1,0:T(8,128)(2,1)S(1)}, u32[]{:S(2)}, u32[]{:S(2)}) collective-permute-start(bf16[256,256]{1,0:T(8,128)(2,1)S(1)} %bitcast.34), channel_id=1, source_target_pairs={{0,6},{1,7},{2,4},{3,5},{4,2},{5,3},{6,0},{7,1},{8,14},{9,15},{10,... | collective-permute-start | bytes 393224 | tf_op jit(solution)/shard_map/ppermute | solution.py:52
  64.5 7.5 %collective-permute-start.17 = (bf16[256,256]{1,0:T(8,128)(2,1)S(1)}, bf16[256,256]{1,0:T(8,128)(2,1)S(1)}, u32[]{:S(2)}, u32[]{:S(2)}) collective-permute-start(bf16[256,256]{1,0:T(8,128)(2,1)S(1)} %bitcast.36), channel_id=1, source_target_pairs={{0,2},{1,3},{2,0},{3,1},{4,6},{5,7},{6,4},{7,5},{8,10},{9,11},{10,... | collective-permute-start | bytes 393224 | tf_op jit(solution)/shard_map/ppermute | solution.py:52

commit v5 on v4

--- a/solution.py
+++ b/solution.py
@@ -93,9 +93,10 @@
 
 
 def join_body(s, *refs):
-    rows = refs[0].shape[0]
-    for i, ref in enumerate(refs[:-1]):
-        refs[-1][i * rows : (i + 1) * rows, :] = ref[...]
+    at = 0
+    for ref in refs[:-1]:
+        refs[-1][at : at + ref.shape[0], :] = ref[...]
+        at += ref.shape[0]
 
 
 def fold(op, block, into=None):
@@ -105,64 +106,55 @@
     return into
 
 
-def attend(s, q, keys, values, first, scores):
-    y, zh = s[0], s[1]
+def attend(s, q, keys, values, owners, scores):
     length = q.shape[0]
-    me = y * 2 + zh
+    me = s[0] * 2 + s[1]
     rate = 1.0 / math.sqrt(HEAD_DIM) * math.log2(math.e)
     stacked = jnp.concatenate([q[:, :HEAD_DIM], q[:, HEAD_DIM:]], axis=0)
     top = None
-    for b, key in enumerate(keys):
-        for part in range(2):
-            got = lax.dot_general(
-                stacked,
-                key[part * length : (part + 1) * length, :],
-                (((1,), (1,)), ((), ())),
-                preferred_element_type=f32,
-            )
-            if first + b == 0 and part == 0:
-                row = lax.broadcasted_iota(jnp.int32, got.shape, 0) & (length - 1)
-                col = lax.broadcasted_iota(jnp.int32, got.shape, 1)
-                got = jnp.where(col <= row, got, masked_score)
-            else:
-                owner = ((y + 4 - first - b) & 3) * 2 + (zh if part == 0 else 1 - zh)
-                got = got + jnp.where(owner < me, 0.0, masked_score).astype(f32)
-            scores[:, (2 * b + part) * length : (2 * b + part + 1) * length] = got
-            top = fold(jnp.maximum, got, top)
+    for b, owner in enumerate(owners):
+        at = slice(b * length, (b + 1) * length)
+        got = lax.dot_general(
+            stacked, keys[at, :], (((1,), (1,)), ((), ())), preferred_element_type=f32
+        )
+        if owner is None:
+            row = lax.broadcasted_iota(jnp.int32, got.shape, 0) & (length - 1)
+            col = lax.broadcasted_iota(jnp.int32, got.shape, 1)
+            got = jnp.where(col <= row, got, masked_score)
+        else:
+            got = got + jnp.where(owner < me, 0.0, masked_score).astype(f32)
+        scores[:, at] = got
+        top = fold(jnp.maximum, got, top)
     top = jnp.max(top, axis=1, keepdims=True) * rate
     total = None
     mixed = jnp.zeros(stacked.shape, f32)
-    for b, value in enumerate(values):
-        weights = jnp.exp2(scores[:, 2 * length * b : 2 * length * (b + 1)] * rate - top)
+    for b in range(len(owners)):
+        at = slice(b * length, (b + 1) * length)
+        weights = jnp.exp2(scores[:, at] * rate - top)
         total = fold(jnp.add, weights, total)
-        mixed = mixed + jnp.dot(weights.astype(bf16), value[...], preferred_element_type=f32)
+        mixed = mixed + jnp.dot(
+            weights.astype(bf16), values[at, :], preferred_element_type=f32
+        )
     return top, total, mixed
 
 
-def attend_near_body(s, q, mine, other, tops, totals, mixeds, scores):
+def attend_near_body(s, q, keys, values, tops, totals, mixeds, scores):
+    top, total, mixed = attend(s, q, keys, values, [None], scores)
+    tops[...] = jnp.broadcast_to(top, tops.shape)
+    totals[...] = total
+    mixeds[...] = mixed
+
+
+def attend_far_body(s, q, mine, other, tops, totals, mixeds, out, scores):
+    y, zh = s[0], s[1]
+    length = q.shape[0]
+    owners = [y * 2 + 1 - zh]
+    for b in range(1, 4):
+        there = ((y + 4 - b) & 3) * 2
+        owners += [there + zh, there + 1 - zh]
+
     def run(keys, values):
-        top, total, mixed = attend(s, q, [keys], [values], 0, scores)
-        tops[...] = jnp.broadcast_to(top, tops.shape)
-        totals[...] = total
-        mixeds[...] = mixed
-
-    @pl.when(s[2] == 0)
-    def _():
-        run(mine, other)
-
-    @pl.when(s[2] != 0)
-    def _():
-        run(other, mine)
-
-
-def attend_far_body(s, q, mine, other, tops, totals, mixeds, out, scores):
-    length = q.shape[0]
-
-    def run(keys, values):
-        parts = [slice(2 * length * b, 2 * length * (b + 1)) for b in range(3)]
-        far_top, far_total, far_mixed = attend(
-            s, q, [keys[at, :] for at in parts], [values[at, :] for at in parts], 1, scores
-        )
+        far_top, far_total, far_mixed = attend(s, q, keys, values, owners, scores)
         near_top = tops[...][:, :1]
         top = jnp.maximum(near_top, far_top)
         near, far = jnp.exp2(near_top - top), jnp.exp2(far_top - top)
@@ -369,7 +361,8 @@
     first = core == 0
     sent = jnp.where(first, columns(key_rows, group ^ 1), columns(value_rows, group ^ 1))
     arrived_pair = swap_zh_near(sent)
-    own = jnp.where(first, columns(key_rows, group), columns(value_rows, group))
+    own_keys, own_values = columns(key_rows, group), columns(value_rows, group)
+    own = jnp.where(first, own_keys, own_values)
     in_rows, out_rows = columns(input_map, group), columns(output_map, group)
 
     (pair,) = call(
@@ -380,7 +373,6 @@
         (own, arrived_pair),
     )
     fetched = [shift_y(pair, d) for d in (2, 1, 3)]
-    pair_other = swap_core(pair)
 
     weight_block = (ROWS, out_weight.shape[1])
     sent_mate, own_weight = call(
@@ -405,7 +397,7 @@
         [x_spec, whole(head_block), decay_spec],
         [state_shape],
         (scan_input, in_rows, log_decay),
-        us=2,
+        us=0.3,
     )
 
     stat = shape((2 * length, HEAD_DIM), f32)
@@ -413,18 +405,18 @@
     near_part = call(
         attend_near_body,
         scalars,
-        [q_spec] + [whole(pair.shape)] * 2,
+        [q_spec] + [whole(head_block)] * 2,
         [stat] * 3,
-        (query_rows, pair, pair_other),
-        scratch=[pltpu.VMEM((2 * length, 2 * length), f32)],
-        us=2.2,
+        (query_rows, own_keys, own_values),
+        scratch=[pltpu.VMEM((2 * length, length), f32)],
+        us=0.3,
     )
     (others,) = call(
         join_body,
         scalars,
-        [whole(pair.shape)] * 3,
-        [shape((6 * length, HEAD_DIM), bf16)],
-        (fetched[1], fetched[0], fetched[2]),
+        [whole(head_block)] + [whole(pair.shape)] * 3,
+        [shape((7 * length, HEAD_DIM), bf16)],
+        (arrived_pair, fetched[1], fetched[0], fetched[2]),
         after=[closing, near_part[0]],
     )
     others_there = swap_core(others)
@@ -434,7 +426,7 @@
         [q_spec] + [whole(others.shape)] * 2 + [whole(stat.shape)] * 3,
         [shape((query_rows.shape[1], length), bf16)],
         (query_rows, others, others_there, *near_part),
-        scratch=[pltpu.VMEM((2 * length, 6 * length), f32)],
+        scratch=[pltpu.VMEM((2 * length, 7 * length), f32)],
         us=40,
     )
     attended_there = swap_core(attended)

time: 74 us -> 70.7 us (0.955)
  waiting for transfers between devices: 17.1 us -> 14 us
  starting transfers between devices: 34 us -> 32.8 us
  local copies, waits for them, and re-layouts: 1.82 us -> 2.72 us
    ppermute x1, waiting for transfers between devices: 1.8 us -> 0.01 us  [swap_zh_near(): return lax.ppermute(block, ('section', 'tp'), route)]
    ppermute x5, waiting for transfers between devices: 4.53 us -> 2.99 us  [shift_y(): return lax.ppermute(block, 'section', route)]
    unnamed x11 -> x13, local copies, waits for them, and re-layouts: 0.85 us -> 1.75 us
    ppermute x1, waiting for transfers between devices: 4.66 us -> 5.54 us  [swap_zh(): return lax.ppermute(block, 'section', [(s, s ^ 1) for s in range(SECTIONS)])]
    ppermute x1, starting transfers between devices: 4.48 us -> 3.61 us  [swap_zh(): return lax.ppermute(block, 'section', [(s, s ^ 1) for s in range(SECTIONS)])]
    ppermute x4 -> x3, waiting for transfers between devices: 1.49 us -> 1.58 us  [swap_core(): return lax.ppermute(block, 'tp', [(t, t ^ 1) for t in range(TP)])]
  transfers between devices with their start and end apart: 18 -> 17, of which waited for: 9 -> 8; matrix products, arithmetic and copies ran while one was open for 2% -> 3% of each run, Pallas kernels for 20% -> 21%
where the time goes in v5:
time: 70.7 us; the launch traced here: 69.9 us
  starting transfers between devices  32.8 us (46%)
  Pallas kernels  18.4 us (26%)
  waiting for transfers between devices  14 us (20%)
  local copies, waits for them, and re-layouts  2.72 us (4%)
  other arithmetic  1.05 us (1%)
  between operations  0.92 us (1%)
    pallas_call x16, Pallas kernels, call(): pl.pallas_call(ordered, grid_spec=pltpu.PrefetchScalarGridSpec(num_scalar...  18.4 us
    ppermute x5, starting transfers between devices, shift_y(): return lax.ppermute(block, 'section', route)  8.37 us
    ppermute x3, starting transfers between devices, swap_zl(): return lax.ppermute(block, 'tp', [(t, t ^ 2 * offset) for t in range(TP)])  7.71 us
    ppermute x1, starting transfers between devices, swap_zh_near(): return lax.ppermute(block, ('section', 'tp'), route)  6.39 us
    ppermute x4, starting transfers between devices, swap_x(): return lax.ppermute(block, 'tp', [(t, t ^ 8 * offset) for t in range(TP)])  5.84 us
    ppermute x1, waiting for transfers between devices, swap_zh(): return lax.ppermute(block, 'section', [(s, s ^ 1) for s in range(SECTIONS)])  5.54 us
    ppermute x1, starting transfers between devices, swap_zh(): return lax.ppermute(block, 'section', [(s, s ^ 1) for s in range(SECTIONS)])  3.61 us
    ppermute x3, waiting for transfers between devices, swap_zl(): return lax.ppermute(block, 'tp', [(t, t ^ 2 * offset) for t in range(TP)])  3.39 us
  transfers between devices with their start and end apart: 17, of which 8 were waited for; matrix products, arithmetic and copies ran while one was open for 3% of the time, Pallas kernels for 21%

profile of v5, /device:TPU:8, one launch (start us, length us, event | category | flops | bytes accessed | tf_op | source)
XLA Modules:
  0.0 69.9 jit_solution(16137517035857580291)
XLA Ops:
  0.6 0.0 copy-start
  0.6 0.0 copy-start.2
  0.7 1.1 %broadcast_select_fusion = (bf16[256,128]{1,0:T(8,128)(2,1)S(1)}, bf16[256,128]{1,0:T(8,128)(2,1)S(1)}, bf16[256,128]{1,0:T(8,128)(2,1)S(1)}, bf16[256,128]{1,0:T(8,128)(2,1)S(1)}) fusion(pred[]{:T(512)S(6)} %eq.6, bf16[256,1024]{1,0:T(8,128)(2,1)} %param.16, s32[]{:T(128)S(6)} %select_n.48, bf16[256,1024]{1,0:T(8,128)(2,1)} %param.15, s32[]{:T(128)S(6)} %select_n.50), kind=kLoop, calls=%fused_computation.1 | loop fusion | flops 65536 | bytes 524297 | tf_op jit(solution)/shard_map/jit(_where)/select_n | solution.py:365
  1.8 6.4 %collective-permute-start.2 = (bf16[256,128]{1,0:T(8,128)(2,1)S(1)}, bf16[256,128]{1,0:T(8,128)(2,1)S(1)}, u32[]{:S(2)}, u32[]{:S(2)}) collective-permute-start(bf16[256,128]{1,0:T(8,128)(2,1)S(1)} %get-tuple-element.39.refs_2_), channel_id=1, source_target_pairs={{0,36},{1,37},{2,38},{3,39},{4,32},{5,33},{6,34},{7,35},{8,44},{9,... | collective-permute-start | bytes 196616 | tf_op jit(solution)/shard_map/ppermute | solution.py:44
  8.1 0.8 %copy.12.refs_3_.refs_4_ = f32[256,8]{1,0:T(8,128)S(1)} copy(f32[256,8]{0,1:T(8,128)} %param.12) | data formatting | bytes 16384 | tf_op args[3]
  9.0 0.1 stack.87.refs_0_
  9.1 0.0 copy-start.3
  9.1 0.9 %copy-done.3 = bf16[256,256]{1,0:T(8,128)(2,1)S(1)} copy-done((bf16[256,256]{1,0:T(8,128)(2,1)S(1)}, bf16[256,256]{1,0:T(8,128)(2,1)}, u32[]{:S(2)}) %copy-start.3) | copy-done | bytes 131096
  10.0 1.0 %shard_map.107 = (f32[512,128]{1,0:T(8,128)S(1)}, f32[512,128]{1,0:T(8,128)S(1)}, f32[512,128]{1,0:T(8,128)S(1)}) custom-call(s32[21]{0:T(128)S(1)} %stack.87.refs_0_, bf16[256,256]{1,0:T(8,128)(2,1)S(1)} %copy-done.3, bf16[256,128]{1,0:T(8,128)(2,1)S(1)} %get-tuple-element.38.refs_2_, bf16[256,128]{1,0:T(8,128)(2,1)S(1)} %get-tuple-element.37.refs_3_), custom_call_target="tpu_custom_call" | custom-call | flops 300000000 | bytes 1050000 | tf_op jit(solution)/shard_map/pallas_call | solution.py:67
  11.0 0.0 collective-permute-done.2.refs_2_.refs_1_
  11.0 0.0 copy-start.1
  11.0 0.6 shard_map.106
  11.6 1.7 %collective-permute-start.3 = (bf16[512,128]{1,0:T(8,128)(2,1)S(1)}, bf16[512,128]{1,0:T(8,128)(2,1)S(1)}, u32[]{:S(2)}, u32[]{:S(2)}) collective-permute-start(bf16[512,128]{1,0:T(8,128)(2,1)S(1)} %shard_map.106), channel_id=1, source_target_pairs={{0,64},{32,96},{64,128},{96,160},{128,192},{160,224},{192,0},{224,... | collective-permute-start | bytes 393224 | tf_op jit(solution)/shard_map/ppermute | solution.py:37
  13.2 0.9 %collective-permute-start.4 = (bf16[512,128]{1,0:T(8,128)(2,1)S(1)}, bf16[512,128]{1,0:T(8,128)(2,1)S(1)}, u32[]{:S(2)}, u32[]{:S(2)}) collective-permute-start(bf16[512,128]{1,0:T(8,128)(2,1)S(1)} %shard_map.106), channel_id=1, source_target_pairs={{0,128},{32,160},{64,192},{96,224},{128,0},{160,32},{192,64},{224,... | collective-permute-start | bytes 393224 | tf_op jit(solution)/shard_map/ppermute | solution.py:37
  14.2 2.4 %collective-permute-start.5 = (bf16[512,128]{1,0:T(8,128)(2,1)S(1)}, bf16[512,128]{1,0:T(8,128)(2,1)S(1)}, u32[]{:S(2)}, u32[]{:S(2)}) collective-permute-start(bf16[512,128]{1,0:T(8,128)(2,1)S(1)} %shard_map.106), channel_id=1, source_target_pairs={{0,192},{32,224},{64,0},{96,32},{128,64},{160,96},{192,128},{224,1... | collective-permute-start | bytes 393224 | tf_op jit(solution)/shard_map/ppermute | solution.py:37
  16.6 0.0 copy-done
  16.6 0.0 copy-done.2
  16.6 1.9 %shard_map.104.refs_5_.refs_1_ = bf16[528,128]{1,0:T(8,128)(2,1)S(1)} custom-call(s32[21]{0:T(128)S(1)} %stack.87.refs_0_, bf16[256,512]{1,0:T(8,128)(2,1)S(1)} %copy-done.2, bf16[256,128]{1,0:T(8,128)(2,1)S(1)} %constant_dynamic-slice_fusion.3.refs_2_, f32[256,8]{1,0:T(8,128)S(1)} %copy.12.refs_3_.refs_4_), custom_call_target="tpu_custom_call" | custom-call | flops 300000000 | bytes 1050000 | tf_op jit(solution)/shard_map/pallas_call | solution.py:67
  18.6 0.0 collective-permute-done.3.refs_2_
  18.6 2.3 %collective-permute-done.4.refs_3_ = bf16[512,128]{1,0:T(8,128)(2,1)S(1)} collective-permute-done((bf16[512,128]{1,0:T(8,128)(2,1)S(1)}, bf16[512,128]{1,0:T(8,128)(2,1)S(1)}, u32[]{:S(2)}, u32[]{:S(2)}) %collective-permute-start.4) | collective-permute-done | bytes 131104 | tf_op jit(solution)/shard_map/ppermute | solution.py:37
  20.9 0.6 collective-permute-done.5.refs_4_
  21.6 0.6 shard_map.108.refs_2_
  22.1 0.1 collective-permute-start.6
  22.2 0.0 copy-done.1
  22.2 0.0 copy-start.4
  22.3 0.8 %shard_map.105 = (bf16[16,256,256]{2,1,0:T(8,128)(2,1)S(1)}, bf16[16,256,256]{2,1,0:T(8,128)(2,1)S(1)}) custom-call(s32[21]{0:T(128)S(1)} %stack.87.refs_0_, bf16[16,2,256,256]{3,2,1,0:T(8,128)(2,1)S(1)} %bitcast.31, bf16[256,128]{1,0:T(8,128)(2,1)S(1)} %get-tuple-element.39.refs_2_), custom_call_target="tpu_custom_call" | custom-call | flops 500000000 | bytes 1750000 | tf_op jit(solution)/shard_map/pallas_call | solution.py:67
  23.1 0.6 collective-permute-start.1
  23.7 0.4 collective-permute-done.6.refs_3_
  24.0 3.0 %shard_map.109.refs_17_ = bf16[256,256]{1,0:T(8,128)(2,1)S(1)} custom-call(s32[21]{0:T(128)S(1)} %stack.87.refs_0_, bf16[256,256]{1,0:T(8,128)(2,1)S(1)} %copy-done.4, bf16[1792,128]{1,0:T(8,128)(2,1)S(1)} %shard_map.108.refs_2_, bf16[1792,128]{1,0:T(8,128)(2,1)S(1)} %collective-permute-done.6.refs_3_, f32[512,128]{1,0:T(8,128)S(1)} %get-tuple-element.21.refs_6_.refs_4_, ...), custom_call_target="tpu_custom_call" | custom-call | flops 40000000000 | bytes 140000000 | tf_op jit(solution)/shard_map/pallas_call | solution.py:67
  27.0 0.2 collective-permute-start.7
  27.2 1.2 %collective-permute-done.7.refs_18_ = bf16[256,256]{1,0:T(8,128)(2,1)S(1)} collective-permute-done((bf16[256,256]{1,0:T(8,128)(2,1)S(1)}, bf16[256,256]{1,0:T(8,128)(2,1)S(1)}, u32[]{:S(2)}, u32[]{:S(2)}) %collective-permute-start.7) | collective-permute-done | bytes 131104 | tf_op jit(solution)/shard_map/ppermute | solution.py:28
  28.5 0.0 collective-permute-done.1.refs_9_.refs_10_.refs_11_.refs_12_.refs_13_.refs_14_.refs_15_.refs_16_
  28.5 1.2 %shard_map.110 = (bf16[2,2,256,256]{3,2,1,0:T(8,128)(2,1)S(1)}, bf16[2,2,256,256]{3,2,1,0:T(8,128)(2,1)S(1)}) custom-call(s32[21]{0:T(128)S(1)} %stack.87.refs_0_, bf16[16,256,256]{2,1,0:T(8,128)(2,1)S(1)} %get-tuple-element.19.refs_1_.refs_2_.refs_3_.refs_4_.refs_5_.refs_6_.refs_7_.refs_8_, ...), custom_call_target="tpu_custom_call" | custom-call | flops 1300000000 | bytes 4550000 | tf_op jit(solution)/shard_map/pallas_call | solution.py:67
  29.7 2.8 %collective-permute-start.12 = (bf16[2,2,256,256]{3,2,1,0:T(8,128)(2,1)S(1)}, bf16[2,2,256,256]{3,2,1,0:T(8,128)(2,1)S(1)}, u32[]{:S(2)}, u32[]{:S(2)}) collective-permute-start(bf16[2,2,256,256]{3,2,1,0:T(8,128)(2,1)S(1)} %get-tuple-element.30), channel_id=1, source_target_pairs={{0,24},{1,25},{2,26},{3,27},{4,28},{5,29},{6,30},{7,31},{8,16},{9,... | collective-permute-start | bytes 1572872 | tf_op jit(solution)/shard_map/ppermute | solution.py:48
  32.6 0.2 collective-permute-start.10
  32.8 3.6 %collective-permute-start = (bf16[528,128]{1,0:T(8,128)(2,1)S(1)}, bf16[528,128]{1,0:T(8,128)(2,1)S(1)}, u32[]{:S(2)}, u32[]{:S(2)}) collective-permute-start(bf16[528,128]{1,0:T(8,128)(2,1)S(1)} %shard_map.104.refs_5_.refs_1_), channel_id=1, source_target_pairs={{0,32},{32,0},{64,96},{96,64},{128,160},{160,128},{192,224},{224,1... | collective-permute-start | bytes 405512 | tf_op jit(solution)/shard_map/ppermute | solution.py:32
  36.4 5.5 %collective-permute-done.refs_2_.refs_6_ = bf16[528,128]{1,0:T(8,128)(2,1)S(1)} collective-permute-done((bf16[528,128]{1,0:T(8,128)(2,1)S(1)}, bf16[528,128]{1,0:T(8,128)(2,1)S(1)}, u32[]{:S(2)}, u32[]{:S(2)}) %collective-permute-start) | collective-permute-done | bytes 135200 | tf_op jit(solution)/shard_map/ppermute | solution.py:32
  41.9 0.6 shard_map.111.refs_1_.refs_3_
  42.5 1.4 %collective-permute-start.8 = (bf16[528,128]{1,0:T(8,128)(2,1)S(1)}, bf16[528,128]{1,0:T(8,128)(2,1)S(1)}, u32[]{:S(2)}, u32[]{:S(2)}) collective-permute-start(bf16[528,128]{1,0:T(8,128)(2,1)S(1)} %shard_map.111.refs_1_.refs_3_), channel_id=1, source_target_pairs={{0,64},{32,96},{64,128},{96,160},{128,192},{160,224},{192,0},{224,... | collective-permute-start | bytes 405512 | tf_op jit(solution)/shard_map/ppermute | solution.py:37
  43.9 1.2 %shard_map.114 = (bf16[2,2,256,256]{3,2,1,0:T(8,128)(2,1)S(1)}, bf16[2,2,256,256]{3,2,1,0:T(8,128)(2,1)S(1)}) custom-call(s32[21]{0:T(128)S(1)} %stack.87.refs_0_, bf16[16,256,256]{2,1,0:T(8,128)(2,1)S(1)} %get-tuple-element.19.refs_1_.refs_2_.refs_3_.refs_4_.refs_5_.refs_6_.refs_7_.refs_8_, ...), custom_call_target="tpu_custom_call" | custom-call | flops 1300000000 | bytes 4550000 | tf_op jit(solution)/shard_map/pallas_call | solution.py:67
  45.2 0.0 collective-permute-done.12.refs_2_
  45.2 0.7 shard_map.117
  45.8 1.8 %collective-permute-start.13 = (bf16[1,2,256,256]{3,2,1,0:T(8,128)(2,1)S(1)}, bf16[1,2,256,256]{3,2,1,0:T(8,128)(2,1)S(1)}, u32[]{:S(2)}, u32[]{:S(2)}) collective-permute-start(bf16[1,2,256,256]{3,2,1,0:T(8,128)(2,1)S(1)} %get-tuple-element.32), channel_id=1, source_target_pairs={{0,8},{1,9},{2,10},{3,11},{4,12},{5,13},{6,14},{7,15},{8,0},{9,1},... | collective-permute-start | bytes 786440 | tf_op jit(solution)/shard_map/ppermute | solution.py:48
  47.7 0.0 collective-permute-done.10.refs_2_
  47.7 0.7 shard_map.115
  48.3 0.9 %collective-permute-start.11 = (bf16[1,2,256,256]{3,2,1,0:T(8,128)(2,1)S(1)}, bf16[1,2,256,256]{3,2,1,0:T(8,128)(2,1)S(1)}, u32[]{:S(2)}, u32[]{:S(2)}) collective-permute-start(bf16[1,2,256,256]{3,2,1,0:T(8,128)(2,1)S(1)} %get-tuple-element.27), channel_id=1, source_target_pairs={{0,24},{1,25},{2,26},{3,27},{4,28},{5,29},{6,30},{7,31},{8,16},{9,... | collective-permute-start | bytes 786440 | tf_op jit(solution)/shard_map/ppermute | solution.py:48
  49.3 0.0 collective-permute-done.8.refs_2_.refs_7_
  49.3 0.6 shard_map.112.refs_3_
  49.9 0.0 copy-start.5
  49.9 2.0 %collective-permute-start.9 = (bf16[512,128]{1,0:T(8,128)(2,1)S(1)}, bf16[512,128]{1,0:T(8,128)(2,1)S(1)}, u32[]{:S(2)}, u32[]{:S(2)}) collective-permute-start(bf16[512,128]{1,0:T(8,128)(2,1)S(1)} %shard_map.112.refs_3_), channel_id=1, source_target_pairs={{0,128},{32,160},{64,192},{96,224},{128,0},{160,32},{192,64},{224,... | collective-permute-start | bytes 393224 | tf_op jit(solution)/shard_map/ppermute | solution.py:37
  51.9 0.8 %constant_dynamic-slice_fusion.2.refs_3_ = bf16[256,128]{1,0:T(8,128)(2,1)S(1)} fusion(bf16[256,1024]{1,0:T(8,128)(2,1)} %param.11, s32[]{:T(128)S(6)} %select_n.48), kind=kLoop, calls=%fused_computation.4 | loop fusion | bytes 131076 | tf_op jit(solution)/shard_map/dynamic_slice | solution.py:359
  52.7 0.5 collective-permute-done.13
  53.3 0.6 shard_map.118
  53.9 4.0 %collective-permute-start.14 = (bf16[256,256]{1,0:T(8,128)(2,1)S(1)}, bf16[256,256]{1,0:T(8,128)(2,1)S(1)}, u32[]{:S(2)}, u32[]{:S(2)}) collective-permute-start(bf16[256,256]{1,0:T(8,128)(2,1)S(1)} %bitcast.35), channel_id=1, source_target_pairs={{0,4},{1,5},{2,6},{3,7},{4,0},{5,1},{6,2},{7,3},{8,12},{9,13},{10,... | collective-permute-start | bytes 393224 | tf_op jit(solution)/shard_map/ppermute | solution.py:52
  57.9 3.3 %collective-permute-start.15 = (bf16[256,256]{1,0:T(8,128)(2,1)S(1)}, bf16[256,256]{1,0:T(8,128)(2,1)S(1)}, u32[]{:S(2)}, u32[]{:S(2)}) collective-permute-start(bf16[256,256]{1,0:T(8,128)(2,1)S(1)} %bitcast.34), channel_id=1, source_target_pairs={{0,6},{1,7},{2,4},{3,5},{4,2},{5,3},{6,0},{7,1},{8,14},{9,15},{10,... | collective-permute-start | bytes 393224 | tf_op jit(solution)/shard_map/ppermute | solution.py:52
  61.1 0.0 collective-permute-done.11
  61.1 0.6 shard_map.116
  61.7 0.5 collective-permute-start.16
  62.2 0.0 collective-permute-done.9.refs_8_
  62.2 3.0 %shard_map.113 = bf16[256,512]{1,0:T(8,128)(2,1)} custom-call(s32[21]{0:T(128)S(1)} %stack.87.refs_0_, bf16[256,512]{1,0:T(8,128)(2,1)S(1)} %copy-done.2, bf16[256,128]{1,0:T(8,128)(2,1)S(1)} %constant_dynamic-slice_fusion.3.refs_2_, bf16[256,128]{1,0:T(8,128)(2,1)S(1)} %constant_dynamic-slice_fusion.2.refs_3_, f32[256,8]{1,0:T(8,128)S(1)} %copy.12.refs_3_.refs_4_, ...), custom_call_target="tpu_custom_call" | custom-call | flops 3000000000 | bytes 10500000 | tf_op jit(solution)/shard_map/pallas_call | solution.py:67
  65.2 2.5 %collective-permute-done.14.refs_2_ = bf16[256,256]{1,0:T(8,128)(2,1)S(1)} collective-permute-done((bf16[256,256]{1,0:T(8,128)(2,1)S(1)}, bf16[256,256]{1,0:T(8,128)(2,1)S(1)}, u32[]{:S(2)}, u32[]{:S(2)}) %collective-permute-start.14) | collective-permute-done | bytes 131104 | tf_op jit(solution)/shard_map/ppermute | solution.py:52
  67.8 0.0 collective-permute-done.15.refs_3_
  67.8 0.9 %collective-permute-done.16.refs_4_ = bf16[256,256]{1,0:T(8,128)(2,1)S(1)} collective-permute-done((bf16[256,256]{1,0:T(8,128)(2,1)S(1)}, bf16[256,256]{1,0:T(8,128)(2,1)S(1)}, u32[]{:S(2)}, u32[]{:S(2)}) %collective-permute-start.16) | collective-permute-done | bytes 131104 | tf_op jit(solution)/shard_map/ppermute | solution.py:52
  68.6 1.3 %shard_map.119 = bf16[256,256]{1,0:T(8,128)(2,1)} custom-call(s32[21]{0:T(128)S(1)} %stack.87.refs_0_, bf16[256,256]{1,0:T(8,128)(2,1)S(1)} %bitcast.40, bf16[256,256]{1,0:T(8,128)(2,1)S(1)} %collective-permute-done.14.refs_2_, bf16[256,256]{1,0:T(8,128)(2,1)S(1)} %collective-permute-done.15.refs_3_, bf16[256,256]{1,0:T(8,128)(2,1)S(1)} %collective-permute-done.16.refs_4_), custom_call_target="tpu_custom_call" | custom-call | flops 1300000000 | bytes 4550000 | tf_op jit(solution)/shard_map/pallas_call | solution.py:67
  (3 shorter events, 0.0 us)
Async XLA Ops:
  0.6 16.0 %copy-start = (bf16[256,1024]{1,0:T(8,128)(2,1)S(1)}, bf16[256,1024]{1,0:T(8,128)(2,1)}, u32[]{:S(2)}) copy-start(bf16[256,1024]{1,0:T(8,128)(2,1)} %param.10) | copy-start | bytes 1572868
  0.6 16.0 %copy-start.2 = (bf16[256,512]{1,0:T(8,128)(2,1)S(1)}, bf16[256,512]{1,0:T(8,128)(2,1)}, u32[]{:S(2)}) copy-start(bf16[256,512]{1,0:T(8,128)(2,1)} %refs_1_.7) | copy-start | bytes 786436
  1.8 9.3 %collective-permute-start.2 = (bf16[256,128]{1,0:T(8,128)(2,1)S(1)}, bf16[256,128]{1,0:T(8,128)(2,1)S(1)}, u32[]{:S(2)}, u32[]{:S(2)}) collective-permute-start(bf16[256,128]{1,0:T(8,128)(2,1)S(1)} %get-tuple-element.39.refs_2_), channel_id=1, source_target_pairs={{0,36},{1,37},{2,38},{3,39},{4,32},{5,33},{6,34},{7,35},{8,44},{9,... | collective-permute-start | bytes 196616 | tf_op jit(solution)/shard_map/ppermute | solution.py:44
  9.1 0.9 %copy-start.3 = (bf16[256,256]{1,0:T(8,128)(2,1)S(1)}, bf16[256,256]{1,0:T(8,128)(2,1)}, u32[]{:S(2)}) copy-start(bf16[256,256]{1,0:T(8,128)(2,1)} %refs_1_.6) | copy-start | bytes 393220
  11.0 11.2 %copy-start.1 = (bf16[8192,256]{1,0:T(8,128)(2,1)S(1)}, bf16[8192,256]{1,0:T(8,128)(2,1)}, u32[]{:S(2)}) copy-start(bf16[8192,256]{1,0:T(8,128)(2,1)} %param.17) | copy-start | bytes 12582916
  11.6 7.0 %collective-permute-start.3 = (bf16[512,128]{1,0:T(8,128)(2,1)S(1)}, bf16[512,128]{1,0:T(8,128)(2,1)S(1)}, u32[]{:S(2)}, u32[]{:S(2)}) collective-permute-start(bf16[512,128]{1,0:T(8,128)(2,1)S(1)} %shard_map.106), channel_id=1, source_target_pairs={{0,64},{32,96},{64,128},{96,160},{128,192},{160,224},{192,0},{224,... | collective-permute-start | bytes 393224 | tf_op jit(solution)/shard_map/ppermute | solution.py:37
  13.2 7.7 %collective-permute-start.4 = (bf16[512,128]{1,0:T(8,128)(2,1)S(1)}, bf16[512,128]{1,0:T(8,128)(2,1)S(1)}, u32[]{:S(2)}, u32[]{:S(2)}) collective-permute-start(bf16[512,128]{1,0:T(8,128)(2,1)S(1)} %shard_map.106), channel_id=1, source_target_pairs={{0,128},{32,160},{64,192},{96,224},{128,0},{160,32},{192,64},{224,... | collective-permute-start | bytes 393224 | tf_op jit(solution)/shard_map/ppermute | solution.py:37
  14.2 7.4 %collective-permute-start.5 = (bf16[512,128]{1,0:T(8,128)(2,1)S(1)}, bf16[512,128]{1,0:T(8,128)(2,1)S(1)}, u32[]{:S(2)}, u32[]{:S(2)}) collective-permute-start(bf16[512,128]{1,0:T(8,128)(2,1)S(1)} %shard_map.106), channel_id=1, source_target_pairs={{0,192},{32,224},{64,0},{96,32},{128,64},{160,96},{192,128},{224,1... | collective-permute-start | bytes 393224 | tf_op jit(solution)/shard_map/ppermute | solution.py:37
  22.1 1.9 %collective-permute-start.6 = (bf16[1792,128]{1,0:T(8,128)(2,1)S(1)}, bf16[1792,128]{1,0:T(8,128)(2,1)S(1)}, u32[]{:S(2)}, u32[]{:S(2)}) collective-permute-start(bf16[1792,128]{1,0:T(8,128)(2,1)S(1)} %shard_map.108.refs_2_), channel_id=1, source_target_pairs={{0,1},{1,0},{2,3},{3,2},{4,5},{5,4},{6,7},{7,6},{8,9},{9,8},{10,11... | collective-permute-start | bytes 1376264 | tf_op jit(solution)/shard_map/ppermute | solution.py:28
  22.2 1.8 %copy-start.4 = (bf16[256,256]{1,0:T(8,128)(2,1)S(1)}, bf16[256,256]{1,0:T(8,128)(2,1)}, u32[]{:S(2)}) copy-start(bf16[256,256]{1,0:T(8,128)(2,1)} %refs_1_.6) | copy-start | bytes 393220
  23.1 5.3 %collective-permute-start.1 = (bf16[16,256,256]{2,1,0:T(8,128)(2,1)S(1)}, bf16[16,256,256]{2,1,0:T(8,128)(2,1)S(1)}, u32[]{:S(2)}, u32[]{:S(2)}) collective-permute-start(bf16[16,256,256]{2,1,0:T(8,128)(2,1)S(1)} %get-tuple-element.20), channel_id=1, source_target_pairs={{0,1},{1,0},{2,3},{3,2},{4,5},{5,4},{6,7},{7,6},{8,9},{9,8},{10,11... | collective-permute-start | bytes 6291464 | tf_op jit(solution)/shard_map/ppermute | solution.py:28
  27.0 1.4 %collective-permute-start.7 = (bf16[256,256]{1,0:T(8,128)(2,1)S(1)}, bf16[256,256]{1,0:T(8,128)(2,1)S(1)}, u32[]{:S(2)}, u32[]{:S(2)}) collective-permute-start(bf16[256,256]{1,0:T(8,128)(2,1)S(1)} %shard_map.109.refs_17_), channel_id=1, source_target_pairs={{0,1},{1,0},{2,3},{3,2},{4,5},{5,4},{6,7},{7,6},{8,9},{9,8},{10,11... | collective-permute-start | bytes 393224 | tf_op jit(solution)/shard_map/ppermute | solution.py:28
  29.7 15.4 %collective-permute-start.12 = (bf16[2,2,256,256]{3,2,1,0:T(8,128)(2,1)S(1)}, bf16[2,2,256,256]{3,2,1,0:T(8,128)(2,1)S(1)}, u32[]{:S(2)}, u32[]{:S(2)}) collective-permute-start(bf16[2,2,256,256]{3,2,1,0:T(8,128)(2,1)S(1)} %get-tuple-element.30), channel_id=1, source_target_pairs={{0,24},{1,25},{2,26},{3,27},{4,28},{5,29},{6,30},{7,31},{8,16},{9,... | collective-permute-start | bytes 1572872 | tf_op jit(solution)/shard_map/ppermute | solution.py:48
  32.6 15.1 %collective-permute-start.10 = (bf16[2,2,256,256]{3,2,1,0:T(8,128)(2,1)S(1)}, bf16[2,2,256,256]{3,2,1,0:T(8,128)(2,1)S(1)}, u32[]{:S(2)}, u32[]{:S(2)}) collective-permute-start(bf16[2,2,256,256]{3,2,1,0:T(8,128)(2,1)S(1)} %get-tuple-element.24.refs_3_.refs_19_), channel_id=1, source_target_pairs={{0,8},{1,9},{2,10},{3,11},{4,12},{5,13},{6,14},{7,15},{8,0},{9,1},... | collective-permute-start | bytes 1572872 | tf_op jit(solution)/shard_map/ppermute | solution.py:48
  32.8 9.1 %collective-permute-start = (bf16[528,128]{1,0:T(8,128)(2,1)S(1)}, bf16[528,128]{1,0:T(8,128)(2,1)S(1)}, u32[]{:S(2)}, u32[]{:S(2)}) collective-permute-start(bf16[528,128]{1,0:T(8,128)(2,1)S(1)} %shard_map.104.refs_5_.refs_1_), channel_id=1, source_target_pairs={{0,32},{32,0},{64,96},{96,64},{128,160},{160,128},{192,224},{224,1... | collective-permute-start | bytes 405512 | tf_op jit(solution)/shard_map/ppermute | solution.py:32
  42.5 6.8 %collective-permute-start.8 = (bf16[528,128]{1,0:T(8,128)(2,1)S(1)}, bf16[528,128]{1,0:T(8,128)(2,1)S(1)}, u32[]{:S(2)}, u32[]{:S(2)}) collective-permute-start(bf16[528,128]{1,0:T(8,128)(2,1)S(1)} %shard_map.111.refs_1_.refs_3_), channel_id=1, source_target_pairs={{0,64},{32,96},{64,128},{96,160},{128,192},{160,224},{192,0},{224,... | collective-permute-start | bytes 405512 | tf_op jit(solution)/shard_map/ppermute | solution.py:37
  45.8 7.4 %collective-permute-start.13 = (bf16[1,2,256,256]{3,2,1,0:T(8,128)(2,1)S(1)}, bf16[1,2,256,256]{3,2,1,0:T(8,128)(2,1)S(1)}, u32[]{:S(2)}, u32[]{:S(2)}) collective-permute-start(bf16[1,2,256,256]{3,2,1,0:T(8,128)(2,1)S(1)} %get-tuple-element.32), channel_id=1, source_target_pairs={{0,8},{1,9},{2,10},{3,11},{4,12},{5,13},{6,14},{7,15},{8,0},{9,1},... | collective-permute-start | bytes 786440 | tf_op jit(solution)/shard_map/ppermute | solution.py:48
  48.3 12.8 %collective-permute-start.11 = (bf16[1,2,256,256]{3,2,1,0:T(8,128)(2,1)S(1)}, bf16[1,2,256,256]{3,2,1,0:T(8,128)(2,1)S(1)}, u32[]{:S(2)}, u32[]{:S(2)}) collective-permute-start(bf16[1,2,256,256]{3,2,1,0:T(8,128)(2,1)S(1)} %get-tuple-element.27), channel_id=1, source_target_pairs={{0,24},{1,25},{2,26},{3,27},{4,28},{5,29},{6,30},{7,31},{8,16},{9,... | collective-permute-start | bytes 786440 | tf_op jit(solution)/shard_map/ppermute | solution.py:48
  49.9 12.3 %copy-start.5 = (f32[8]{0:T(128)S(1)}, f32[8]{0:T(128)}, u32[]{:S(2)}) copy-start(f32[8]{0:T(128)} %param.13) | copy-start | bytes 100
  49.9 12.3 %collective-permute-start.9 = (bf16[512,128]{1,0:T(8,128)(2,1)S(1)}, bf16[512,128]{1,0:T(8,128)(2,1)S(1)}, u32[]{:S(2)}, u32[]{:S(2)}) collective-permute-start(bf16[512,128]{1,0:T(8,128)(2,1)S(1)} %shard_map.112.refs_3_), channel_id=1, source_target_pairs={{0,128},{32,160},{64,192},{96,224},{128,0},{160,32},{192,64},{224,... | collective-permute-start | bytes 393224 | tf_op jit(solution)/shard_map/ppermute | solution.py:37
  53.9 13.9 %collective-permute-start.14 = (bf16[256,256]{1,0:T(8,128)(2,1)S(1)}, bf16[256,256]{1,0:T(8,128)(2,1)S(1)}, u32[]{:S(2)}, u32[]{:S(2)}) collective-permute-start(bf16[256,256]{1,0:T(8,128)(2,1)S(1)} %bitcast.35), channel_id=1, source_target_pairs={{0,4},{1,5},{2,6},{3,7},{4,0},{5,1},{6,2},{7,3},{8,12},{9,13},{10,... | collective-permute-start | bytes 393224 | tf_op jit(solution)/shard_map/ppermute | solution.py:52
  57.9 9.9 %collective-permute-start.15 = (bf16[256,256]{1,0:T(8,128)(2,1)S(1)}, bf16[256,256]{1,0:T(8,128)(2,1)S(1)}, u32[]{:S(2)}, u32[]{:S(2)}) collective-permute-start(bf16[256,256]{1,0:T(8,128)(2,1)S(1)} %bitcast.34), channel_id=1, source_target_pairs={{0,6},{1,7},{2,4},{3,5},{4,2},{5,3},{6,0},{7,1},{8,14},{9,15},{10,... | collective-permute-start | bytes 393224 | tf_op jit(solution)/shard_map/ppermute | solution.py:52
  61.7 6.9 %collective-permute-start.16 = (bf16[256,256]{1,0:T(8,128)(2,1)S(1)}, bf16[256,256]{1,0:T(8,128)(2,1)S(1)}, u32[]{:S(2)}, u32[]{:S(2)}) collective-permute-start(bf16[256,256]{1,0:T(8,128)(2,1)S(1)} %bitcast.36), channel_id=1, source_target_pairs={{0,2},{1,3},{2,0},{3,1},{4,6},{5,7},{6,4},{7,5},{8,10},{9,11},{10,... | collective-permute-start | bytes 393224 | tf_op jit(solution)/shard_map/ppermute | solution.py:52

commit v6 on v5

--- a/solution.py
+++ b/solution.py
@@ -121,7 +121,7 @@
             row = lax.broadcasted_iota(jnp.int32, got.shape, 0) & (length - 1)
             col = lax.broadcasted_iota(jnp.int32, got.shape, 1)
             got = jnp.where(col <= row, got, masked_score)
-        else:
+        elif not isinstance(owner, int):
             got = got + jnp.where(owner < me, 0.0, masked_score).astype(f32)
         scores[:, at] = got
         top = fold(jnp.maximum, got, top)
@@ -148,12 +148,9 @@
 def attend_far_body(s, q, mine, other, tops, totals, mixeds, out, scores):
     y, zh = s[0], s[1]
     length = q.shape[0]
-    owners = [y * 2 + 1 - zh]
-    for b in range(1, 4):
-        there = ((y + 4 - b) & 3) * 2
-        owners += [there + zh, there + 1 - zh]
-
-    def run(keys, values):
+
+    def run(keys, values, count):
+        owners = [y * 2 + 1 - zh] + [-1] * (count - 1)
         far_top, far_total, far_mixed = attend(s, q, keys, values, owners, scores)
         near_top = tops[...][:, :1]
         top = jnp.maximum(near_top, far_top)
@@ -163,13 +160,13 @@
         out[:HEAD_DIM, :] = done[:length].T.astype(bf16)
         out[HEAD_DIM:, :] = done[length:].T.astype(bf16)
 
-    @pl.when(s[2] == 0)
-    def _():
-        run(mine, other)
-
-    @pl.when(s[2] != 0)
-    def _():
-        run(other, mine)
+    for rank in range(SECTIONS // 2):
+        for core in range(2):
+
+            @pl.when((y == rank) & (s[2] == core))
+            def _(rank=rank, core=core):
+                keys, values = (mine, other) if core == 0 else (other, mine)
+                run(keys, values, 1 + 2 * rank)
 
 
 def project_body(s, *refs):
@@ -273,32 +270,21 @@
     return body
 
 
-def chain_body(heads):
-    inner = heads * SSM_HEAD_DIM
-
-    def body(s, joined, near, out):
-        fade = fades(joined, inner, heads)
-        for h in range(heads):
-            rows = head_rows(h)
-            before = jnp.where(s[0] >= 1, near[rows, :].astype(f32), 0.0)
-            out[rows, :] = (fade[h : h + 1] * before + joined[rows, :].astype(f32)).astype(bf16)
-
-    return body
-
-
-def scan_body(s, x, in_rows, out_rows, decay, gain, partner, near, far, out, entering):
+def scan_body(s, x, in_rows, out_rows, decay, gain, partner, t1, t2, t3, out, entering):
     y, zh = s[0], s[1]
     heads = decay.shape[1]
     inner = heads * SSM_HEAD_DIM
     length = x.shape[0]
     down, across = running_sums(decay[...])
-    fade1 = fades(near, inner, heads)
+    fade1 = fades(t1, inner, heads)
+    fade2 = fades(t2, inner, heads)
     fade0 = fades(partner, inner, heads)
     for h in range(heads):
         rows = head_rows(h)
-        second = jnp.where(y >= 2, far[rows, :].astype(f32), 0.0)
-        first = jnp.where(y >= 1, near[rows, :].astype(f32), 0.0)
-        state = first + fade1[h : h + 1] * second
+        third = jnp.where(y >= 3, t3[rows, :].astype(f32), 0.0)
+        second = jnp.where(y >= 2, t2[rows, :].astype(f32), 0.0)
+        first = jnp.where(y >= 1, t1[rows, :].astype(f32), 0.0)
+        state = first + fade1[h : h + 1] * (second + fade2[h : h + 1] * third)
         later = fade0[h : h + 1] * state + partner[rows, :].astype(f32)
         entering[rows, :] = jnp.where(zh == 0, state, later).astype(bf16)
     contract = (((1,), (1,)), ((), ()))
@@ -450,35 +436,26 @@
         )
 
     sent1, sent2 = project([4, 5, 8, 9, 14, 15, 10, 11])
+    kept1, kept2 = project([0, 1, 12, 13, 2, 3, 6, 7], [sent1])
+    arrived1, arrived2 = swap_x(sent1, 1), swap_x(sent2, 3)
+
+    def add_split(kept, arrived):
+        out = shape((kept.shape[0] // 2, *kept.shape[1:]), bf16)
+        return call(add_split_body, scalars, [whole(kept.shape)] * 2, [out] * 2, (kept, arrived))
+
+    kept1, sent1 = add_split(kept1, arrived1)
+    kept2, sent2 = add_split(kept2, arrived2)
+    arrived1, arrived2 = swap_x(sent1, 3), swap_x(sent2, 1)
     (joined,) = call(
         pair_body(heads),
         scalars,
         [whole(closing.shape)] * 2,
         [state_shape],
         (closing, partner),
-        after=[sent1],
-    )
-    near = shift_y(joined, 1)
-    (chained,) = call(
-        chain_body(heads),
-        scalars,
-        [whole(closing.shape)] * 2,
-        [shape((inner, N_STATE), bf16)],
-        (joined, near),
-    )
-    further = shift_y(chained, 2)
-
-    kept1, kept2 = project([0, 1, 12, 13, 2, 3, 6, 7], [sent1])
-    arrived1, arrived2 = swap_x(sent1, 1), swap_x(sent2, 3)
-
-    def add_split(kept, arrived, after=()):
-        out = shape((kept.shape[0] // 2, *kept.shape[1:]), bf16)
-        return call(add_split_body, scalars, [whole(kept.shape)] * 2, [out] * 2, (kept, arrived), after=after)
-
-    kept1, sent1 = add_split(kept1, arrived1, [joined])
-    kept2, sent2 = add_split(kept2, arrived2)
-    arrived1, arrived2 = swap_x(sent1, 3), swap_x(sent2, 1)
-    z0, z1 = add_split(kept1[0], arrived1[0], [chained])
+        after=[sent1, sent2],
+    )
+    earlier = [shift_y(joined, d) for d in (2, 1, 3)]
+    z0, z1 = add_split(kept1[0], arrived1[0])
     z2, z3 = add_split(kept2[0], arrived2[0])
     arrived = [z0[0]] + [swap_zl(z[0], b) for b, z in ((2, z2), (3, z3), (1, z1))]
     (attn_out,) = call(
@@ -494,8 +471,7 @@
         scan_body,
         scalars,
         [x_spec, whole(head_block), whole(head_block), decay_spec, whole((1, heads))]
-        + [whole(closing.shape)] * 2
-        + [whole(further.shape)],
+        + [whole(closing.shape)] * 4,
         [shape(scan_input.shape, bf16)],
         (
             scan_input,
@@ -504,10 +480,12 @@
             log_decay,
             skip_gain.reshape(1, heads),
             partner,
-            near,
-            further,
+            earlier[1],
+            earlier[0],
+            earlier[2],
         ),
         scratch=[pltpu.VMEM((inner, N_STATE), bf16)],
+        after=[z1, z3],
         us=3,
     )
     return (ssm_out, attn_out)

time: 70.7 us -> 69.8 us (0.987)
  waiting for transfers between devices: 14 us -> 16.2 us
  starting transfers between devices: 32.8 us -> 31.3 us
  Pallas kernels: 18.4 us -> 17.3 us
    ppermute x4, waiting for transfers between devices: 0.54 us -> 7.58 us  [swap_x(): return lax.ppermute(block, 'tp', [(t, t ^ 8 * offset) for t in range(TP)])]
    ppermute x1, waiting for transfers between devices: 5.54 us -> 0.01 us  [swap_zh(): return lax.ppermute(block, 'section', [(s, s ^ 1) for s in range(SECTIONS)])]
    ppermute x3, starting transfers between devices: 7.71 us -> 4.16 us  [swap_zl(): return lax.ppermute(block, 'tp', [(t, t ^ 2 * offset) for t in range(TP)])]
    ppermute x5 -> x6, starting transfers between devices: 8.37 us -> 10.4 us  [shift_y(): return lax.ppermute(block, 'section', route)]
    pallas_call x16 -> x15, Pallas kernels: 18.4 us -> 17.3 us  [call(): pl.pallas_call(ordered, grid_spec=pltpu.PrefetchScalarGridSpec(num_scalar...]
    ppermute x5 -> x6, waiting for transfers between devices: 2.99 us -> 2.99 us  [shift_y(): return lax.ppermute(block, 'section', route)]
  transfers between devices with their start and end apart: 17 -> 18, of which waited for: 8 -> 8; matrix products, arithmetic and copies ran while one was open for 3% -> 3% of each run, Pallas kernels for 21% -> 20%
where the time goes in v6:
time: 69.8 us; the launch traced here: 69.4 us
  starting transfers between devices  31.3 us (45%)
  Pallas kernels  17.3 us (25%)
  waiting for transfers between devices  16.2 us (23%)
  local copies, waits for them, and re-layouts  2.72 us (4%)
  other arithmetic  1.05 us (2%)
  between operations  0.94 us (1%)
    pallas_call x15, Pallas kernels, call(): pl.pallas_call(ordered, grid_spec=pltpu.PrefetchScalarGridSpec(num_scalar...  17.3 us
    ppermute x6, starting transfers between devices, shift_y(): return lax.ppermute(block, 'section', route)  10.4 us
    ppermute x4, waiting for transfers between devices, swap_x(): return lax.ppermute(block, 'tp', [(t, t ^ 8 * offset) for t in range(TP)])  7.58 us
    ppermute x1, starting transfers between devices, swap_zh_near(): return lax.ppermute(block, ('section', 'tp'), route)  6.39 us
    ppermute x4, starting transfers between devices, swap_x(): return lax.ppermute(block, 'tp', [(t, t ^ 8 * offset) for t in range(TP)])  5.8 us
    ppermute x3, starting transfers between devices, swap_zl(): return lax.ppermute(block, 'tp', [(t, t ^ 2 * offset) for t in range(TP)])  4.16 us
    ppermute x3, waiting for transfers between devices, swap_zl(): return lax.ppermute(block, 'tp', [(t, t ^ 2 * offset) for t in range(TP)])  4.04 us
    ppermute x1, starting transfers between devices, swap_zh(): return lax.ppermute(block, 'section', [(s, s ^ 1) for s in range(SECTIONS)])  3.61 us
  transfers between devices with their start and end apart: 18, of which 8 were waited for; matrix products, arithmetic and copies ran while one was open for 3% of the time, Pallas kernels for 20%

profile of v6, /device:TPU:8, one launch (start us, length us, event | category | flops | bytes accessed | tf_op | source)
XLA Modules:
  0.0 69.4 jit_solution(2548796601063405093)
XLA Ops:
  0.6 0.0 copy-start
  0.6 0.0 copy-start.2
  0.7 1.1 %broadcast_select_fusion = (bf16[256,128]{1,0:T(8,128)(2,1)S(1)}, bf16[256,128]{1,0:T(8,128)(2,1)S(1)}, bf16[256,128]{1,0:T(8,128)(2,1)S(1)}, bf16[256,128]{1,0:T(8,128)(2,1)S(1)}) fusion(pred[]{:T(512)S(6)} %eq.6, bf16[256,1024]{1,0:T(8,128)(2,1)} %param.16, s32[]{:T(128)S(6)} %select_n.48, bf16[256,1024]{1,0:T(8,128)(2,1)} %param.15, s32[]{:T(128)S(6)} %select_n.50), kind=kLoop, calls=%fused_computation.1 | loop fusion | flops 65536 | bytes 524297 | tf_op jit(solution)/shard_map/jit(_where)/select_n | solution.py:351
  1.8 6.4 %collective-permute-start.2 = (bf16[256,128]{1,0:T(8,128)(2,1)S(1)}, bf16[256,128]{1,0:T(8,128)(2,1)S(1)}, u32[]{:S(2)}, u32[]{:S(2)}) collective-permute-start(bf16[256,128]{1,0:T(8,128)(2,1)S(1)} %get-tuple-element.39.refs_2_), channel_id=1, source_target_pairs={{0,36},{1,37},{2,38},{3,39},{4,32},{5,33},{6,34},{7,35},{8,44},{9,... | collective-permute-start | bytes 196616 | tf_op jit(solution)/shard_map/ppermute | solution.py:44
  8.1 0.8 %copy.12.refs_3_.refs_4_ = f32[256,8]{1,0:T(8,128)S(1)} copy(f32[256,8]{0,1:T(8,128)} %param.12) | data formatting | bytes 16384 | tf_op args[3]
  9.0 0.1 stack.87.refs_0_
  9.1 0.0 copy-start.3
  9.1 0.9 %copy-done.3 = bf16[256,256]{1,0:T(8,128)(2,1)S(1)} copy-done((bf16[256,256]{1,0:T(8,128)(2,1)S(1)}, bf16[256,256]{1,0:T(8,128)(2,1)}, u32[]{:S(2)}) %copy-start.3) | copy-done | bytes 131096
  10.0 1.0 %shard_map.107 = (f32[512,128]{1,0:T(8,128)S(1)}, f32[512,128]{1,0:T(8,128)S(1)}, f32[512,128]{1,0:T(8,128)S(1)}) custom-call(s32[21]{0:T(128)S(1)} %stack.87.refs_0_, bf16[256,256]{1,0:T(8,128)(2,1)S(1)} %copy-done.3, bf16[256,128]{1,0:T(8,128)(2,1)S(1)} %get-tuple-element.38.refs_2_, bf16[256,128]{1,0:T(8,128)(2,1)S(1)} %get-tuple-element.37.refs_3_), custom_call_target="tpu_custom_call" | custom-call | flops 300000000 | bytes 1050000 | tf_op jit(solution)/shard_map/pallas_call | solution.py:67
  11.0 0.0 collective-permute-done.2.refs_2_.refs_1_
  11.0 0.0 copy-start.1
  11.0 0.6 shard_map.106
  11.6 1.7 %collective-permute-start.3 = (bf16[512,128]{1,0:T(8,128)(2,1)S(1)}, bf16[512,128]{1,0:T(8,128)(2,1)S(1)}, u32[]{:S(2)}, u32[]{:S(2)}) collective-permute-start(bf16[512,128]{1,0:T(8,128)(2,1)S(1)} %shard_map.106), channel_id=1, source_target_pairs={{0,64},{32,96},{64,128},{96,160},{128,192},{160,224},{192,0},{224,... | collective-permute-start | bytes 393224 | tf_op jit(solution)/shard_map/ppermute | solution.py:37
  13.2 0.9 %collective-permute-start.4 = (bf16[512,128]{1,0:T(8,128)(2,1)S(1)}, bf16[512,128]{1,0:T(8,128)(2,1)S(1)}, u32[]{:S(2)}, u32[]{:S(2)}) collective-permute-start(bf16[512,128]{1,0:T(8,128)(2,1)S(1)} %shard_map.106), channel_id=1, source_target_pairs={{0,128},{32,160},{64,192},{96,224},{128,0},{160,32},{192,64},{224,... | collective-permute-start | bytes 393224 | tf_op jit(solution)/shard_map/ppermute | solution.py:37
  14.2 2.4 %collective-permute-start.5 = (bf16[512,128]{1,0:T(8,128)(2,1)S(1)}, bf16[512,128]{1,0:T(8,128)(2,1)S(1)}, u32[]{:S(2)}, u32[]{:S(2)}) collective-permute-start(bf16[512,128]{1,0:T(8,128)(2,1)S(1)} %shard_map.106), channel_id=1, source_target_pairs={{0,192},{32,224},{64,0},{96,32},{128,64},{160,96},{192,128},{224,1... | collective-permute-start | bytes 393224 | tf_op jit(solution)/shard_map/ppermute | solution.py:37
  16.6 0.0 copy-done
  16.6 0.0 copy-done.2
  16.6 1.9 %shard_map.104.refs_5_.refs_1_ = bf16[528,128]{1,0:T(8,128)(2,1)S(1)} custom-call(s32[21]{0:T(128)S(1)} %stack.87.refs_0_, bf16[256,512]{1,0:T(8,128)(2,1)S(1)} %copy-done.2, bf16[256,128]{1,0:T(8,128)(2,1)S(1)} %constant_dynamic-slice_fusion.3.refs_2_, f32[256,8]{1,0:T(8,128)S(1)} %copy.12.refs_3_.refs_4_), custom_call_target="tpu_custom_call" | custom-call | flops 300000000 | bytes 1050000 | tf_op jit(solution)/shard_map/pallas_call | solution.py:67
  18.6 0.0 collective-permute-done.3.refs_2_
  18.6 2.3 %collective-permute-done.4.refs_3_ = bf16[512,128]{1,0:T(8,128)(2,1)S(1)} collective-permute-done((bf16[512,128]{1,0:T(8,128)(2,1)S(1)}, bf16[512,128]{1,0:T(8,128)(2,1)S(1)}, u32[]{:S(2)}, u32[]{:S(2)}) %collective-permute-start.4) | collective-permute-done | bytes 131104 | tf_op jit(solution)/shard_map/ppermute | solution.py:37
  20.9 0.6 collective-permute-done.5.refs_4_
  21.6 0.6 shard_map.108.refs_2_
  22.1 0.1 collective-permute-start.6
  22.2 0.0 copy-start.4
  22.3 0.8 %shard_map.105 = (bf16[16,256,256]{2,1,0:T(8,128)(2,1)S(1)}, bf16[16,256,256]{2,1,0:T(8,128)(2,1)S(1)}) custom-call(s32[21]{0:T(128)S(1)} %stack.87.refs_0_, bf16[16,2,256,256]{3,2,1,0:T(8,128)(2,1)S(1)} %bitcast.31, bf16[256,128]{1,0:T(8,128)(2,1)S(1)} %get-tuple-element.39.refs_2_), custom_call_target="tpu_custom_call" | custom-call | flops 500000000 | bytes 1750000 | tf_op jit(solution)/shard_map/pallas_call | solution.py:67
  23.1 0.6 collective-permute-start.1
  23.7 0.4 collective-permute-done.6.refs_3_
  24.0 2.4 %shard_map.109.refs_17_ = bf16[256,256]{1,0:T(8,128)(2,1)S(1)} custom-call(s32[21]{0:T(128)S(1)} %stack.87.refs_0_, bf16[256,256]{1,0:T(8,128)(2,1)S(1)} %copy-done.4, bf16[1792,128]{1,0:T(8,128)(2,1)S(1)} %shard_map.108.refs_2_, bf16[1792,128]{1,0:T(8,128)(2,1)S(1)} %collective-permute-done.6.refs_3_, f32[512,128]{1,0:T(8,128)S(1)} %get-tuple-element.21.refs_6_.refs_4_, ...), custom_call_target="tpu_custom_call" | custom-call | flops 40000000000 | bytes 140000000 | tf_op jit(solution)/shard_map/pallas_call | solution.py:67
  26.4 0.2 collective-permute-start.7
  26.7 1.2 %collective-permute-done.7.refs_18_ = bf16[256,256]{1,0:T(8,128)(2,1)S(1)} collective-permute-done((bf16[256,256]{1,0:T(8,128)(2,1)S(1)}, bf16[256,256]{1,0:T(8,128)(2,1)S(1)}, u32[]{:S(2)}, u32[]{:S(2)}) %collective-permute-start.7) | collective-permute-done | bytes 131104 | tf_op jit(solution)/shard_map/ppermute | solution.py:28
  27.9 0.0 collective-permute-done.1.refs_9_.refs_10_.refs_11_.refs_12_.refs_13_.refs_14_.refs_15_.refs_16_
  27.9 1.2 %shard_map.110 = (bf16[2,2,256,256]{3,2,1,0:T(8,128)(2,1)S(1)}, bf16[2,2,256,256]{3,2,1,0:T(8,128)(2,1)S(1)}) custom-call(s32[21]{0:T(128)S(1)} %stack.87.refs_0_, bf16[16,256,256]{2,1,0:T(8,128)(2,1)S(1)} %get-tuple-element.19.refs_1_.refs_2_.refs_3_.refs_4_.refs_5_.refs_6_.refs_7_.refs_8_, ...), custom_call_target="tpu_custom_call" | custom-call | flops 1300000000 | bytes 4550000 | tf_op jit(solution)/shard_map/pallas_call | solution.py:67
  29.1 2.8 %collective-permute-start.9 = (bf16[2,2,256,256]{3,2,1,0:T(8,128)(2,1)S(1)}, bf16[2,2,256,256]{3,2,1,0:T(8,128)(2,1)S(1)}, u32[]{:S(2)}, u32[]{:S(2)}) collective-permute-start(bf16[2,2,256,256]{3,2,1,0:T(8,128)(2,1)S(1)} %get-tuple-element.28), channel_id=1, source_target_pairs={{0,24},{1,25},{2,26},{3,27},{4,28},{5,29},{6,30},{7,31},{8,16},{9,... | collective-permute-start | bytes 1572872 | tf_op jit(solution)/shard_map/ppermute | solution.py:48
  32.0 0.2 collective-permute-start.8
  32.2 3.6 %collective-permute-start = (bf16[528,128]{1,0:T(8,128)(2,1)S(1)}, bf16[528,128]{1,0:T(8,128)(2,1)S(1)}, u32[]{:S(2)}, u32[]{:S(2)}) collective-permute-start(bf16[528,128]{1,0:T(8,128)(2,1)S(1)} %shard_map.104.refs_5_.refs_1_), channel_id=1, source_target_pairs={{0,32},{32,0},{64,96},{96,64},{128,160},{160,128},{192,224},{224,1... | collective-permute-start | bytes 405512 | tf_op jit(solution)/shard_map/ppermute | solution.py:32
  35.8 1.2 %shard_map.111 = (bf16[2,2,256,256]{3,2,1,0:T(8,128)(2,1)S(1)}, bf16[2,2,256,256]{3,2,1,0:T(8,128)(2,1)S(1)}) custom-call(s32[21]{0:T(128)S(1)} %stack.87.refs_0_, bf16[16,256,256]{2,1,0:T(8,128)(2,1)S(1)} %get-tuple-element.19.refs_1_.refs_2_.refs_3_.refs_4_.refs_5_.refs_6_.refs_7_.refs_8_, ...), custom_call_target="tpu_custom_call" | custom-call | flops 1300000000 | bytes 4550000 | tf_op jit(solution)/shard_map/pallas_call | solution.py:67
  37.0 7.4 %collective-permute-done.9.refs_2_ = bf16[2,2,256,256]{3,2,1,0:T(8,128)(2,1)S(1)} collective-permute-done((bf16[2,2,256,256]{3,2,1,0:T(8,128)(2,1)S(1)}, bf16[2,2,256,256]{3,2,1,0:T(8,128)(2,1)S(1)}, u32[]{:S(2)}, u32[]{:S(2)}) %collective-permute-start.9) | collective-permute-done | bytes 524320 | tf_op jit(solution)/shard_map/ppermute | solution.py:48
  44.4 0.7 shard_map.113
  45.1 0.4 collective-permute-start.14
  45.4 0.2 collective-permute-done.8.refs_2_
  45.7 0.7 shard_map.112
  46.3 2.4 %collective-permute-start.13 = (bf16[1,2,256,256]{3,2,1,0:T(8,128)(2,1)S(1)}, bf16[1,2,256,256]{3,2,1,0:T(8,128)(2,1)S(1)}, u32[]{:S(2)}, u32[]{:S(2)}) collective-permute-start(bf16[1,2,256,256]{3,2,1,0:T(8,128)(2,1)S(1)} %get-tuple-element.26.refs_3_), channel_id=1, source_target_pairs={{0,24},{1,25},{2,26},{3,27},{4,28},{5,29},{6,30},{7,31},{8,16},{9,... | collective-permute-start | bytes 786440 | tf_op jit(solution)/shard_map/ppermute | solution.py:48
  48.7 0.0 collective-permute-done.refs_2_.refs_6_
  48.7 0.6 shard_map.114
  49.3 0.0 copy-start.5
  49.3 1.5 %collective-permute-start.10 = (bf16[528,128]{1,0:T(8,128)(2,1)S(1)}, bf16[528,128]{1,0:T(8,128)(2,1)S(1)}, u32[]{:S(2)}, u32[]{:S(2)}) collective-permute-start(bf16[528,128]{1,0:T(8,128)(2,1)S(1)} %shard_map.114), channel_id=1, source_target_pairs={{0,64},{32,96},{64,128},{96,160},{128,192},{160,224},{192,0},{224,... | collective-permute-start | bytes 405512 | tf_op jit(solution)/shard_map/ppermute | solution.py:37
  50.9 1.4 %collective-permute-start.11 = (bf16[528,128]{1,0:T(8,128)(2,1)S(1)}, bf16[528,128]{1,0:T(8,128)(2,1)S(1)}, u32[]{:S(2)}, u32[]{:S(2)}) collective-permute-start(bf16[528,128]{1,0:T(8,128)(2,1)S(1)} %shard_map.114), channel_id=1, source_target_pairs={{0,128},{32,160},{64,192},{96,224},{128,0},{160,32},{192,64},{224,... | collective-permute-start | bytes 405512 | tf_op jit(solution)/shard_map/ppermute | solution.py:37
  52.3 2.5 %collective-permute-start.12 = (bf16[528,128]{1,0:T(8,128)(2,1)S(1)}, bf16[528,128]{1,0:T(8,128)(2,1)S(1)}, u32[]{:S(2)}, u32[]{:S(2)}) collective-permute-start(bf16[528,128]{1,0:T(8,128)(2,1)S(1)} %shard_map.114), channel_id=1, source_target_pairs={{0,192},{32,224},{64,0},{96,32},{128,64},{160,96},{192,128},{224,1... | collective-permute-start | bytes 405512 | tf_op jit(solution)/shard_map/ppermute | solution.py:37
  54.8 0.8 %constant_dynamic-slice_fusion.2.refs_3_ = bf16[256,128]{1,0:T(8,128)(2,1)S(1)} fusion(bf16[256,1024]{1,0:T(8,128)(2,1)} %param.11, s32[]{:T(128)S(6)} %select_n.48), kind=kLoop, calls=%fused_computation.4 | loop fusion | bytes 131076 | tf_op jit(solution)/shard_map/dynamic_slice | solution.py:345
  55.6 0.0 collective-permute-done.14
  55.6 0.6 shard_map.116
  56.2 1.9 %collective-permute-start.15 = (bf16[256,256]{1,0:T(8,128)(2,1)S(1)}, bf16[256,256]{1,0:T(8,128)(2,1)S(1)}, u32[]{:S(2)}, u32[]{:S(2)}) collective-permute-start(bf16[256,256]{1,0:T(8,128)(2,1)S(1)} %bitcast.35), channel_id=1, source_target_pairs={{0,4},{1,5},{2,6},{3,7},{4,0},{5,1},{6,2},{7,3},{8,12},{9,13},{10,... | collective-permute-start | bytes 393224 | tf_op jit(solution)/shard_map/ppermute | solution.py:52
  58.1 0.0 collective-permute-done.13
  58.1 2.2 %collective-permute-start.16 = (bf16[256,256]{1,0:T(8,128)(2,1)S(1)}, bf16[256,256]{1,0:T(8,128)(2,1)S(1)}, u32[]{:S(2)}, u32[]{:S(2)}) collective-permute-start(bf16[256,256]{1,0:T(8,128)(2,1)S(1)} %bitcast.34), channel_id=1, source_target_pairs={{0,6},{1,7},{2,4},{3,5},{4,2},{5,3},{6,0},{7,1},{8,14},{9,15},{10,... | collective-permute-start | bytes 393224 | tf_op jit(solution)/shard_map/ppermute | solution.py:52
  60.3 0.6 shard_map.115
  60.9 0.0 collective-permute-done.10.refs_7_
  60.9 0.1 collective-permute-start.17
  61.0 0.0 collective-permute-done.11.refs_8_
  61.0 0.0 collective-permute-done.12.refs_9_
  61.0 3.1 %shard_map.117 = bf16[256,512]{1,0:T(8,128)(2,1)} custom-call(s32[21]{0:T(128)S(1)} %stack.87.refs_0_, bf16[256,512]{1,0:T(8,128)(2,1)S(1)} %copy-done.2, bf16[256,128]{1,0:T(8,128)(2,1)S(1)} %constant_dynamic-slice_fusion.3.refs_2_, bf16[256,128]{1,0:T(8,128)(2,1)S(1)} %constant_dynamic-slice_fusion.2.refs_3_, f32[256,8]{1,0:T(8,128)S(1)} %copy.12.refs_3_.refs_4_, ...), custom_call_target="tpu_custom_call" | custom-call | flops 3000000000 | bytes 10500000 | tf_op jit(solution)/shard_map/pallas_call | solution.py:67
  64.1 3.5 %collective-permute-done.15.refs_2_ = bf16[256,256]{1,0:T(8,128)(2,1)S(1)} collective-permute-done((bf16[256,256]{1,0:T(8,128)(2,1)S(1)}, bf16[256,256]{1,0:T(8,128)(2,1)S(1)}, u32[]{:S(2)}, u32[]{:S(2)}) %collective-permute-start.15) | collective-permute-done | bytes 131104 | tf_op jit(solution)/shard_map/ppermute | solution.py:52
  67.6 0.0 collective-permute-done.16.refs_3_
  67.6 0.5 collective-permute-done.17.refs_4_
  68.2 1.3 %shard_map.118 = bf16[256,256]{1,0:T(8,128)(2,1)} custom-call(s32[21]{0:T(128)S(1)} %stack.87.refs_0_, bf16[256,256]{1,0:T(8,128)(2,1)S(1)} %bitcast.40, bf16[256,256]{1,0:T(8,128)(2,1)S(1)} %collective-permute-done.15.refs_2_, bf16[256,256]{1,0:T(8,128)(2,1)S(1)} %collective-permute-done.16.refs_3_, bf16[256,256]{1,0:T(8,128)(2,1)S(1)} %collective-permute-done.17.refs_4_), custom_call_target="tpu_custom_call" | custom-call | flops 1300000000 | bytes 4550000 | tf_op jit(solution)/shard_map/pallas_call | solution.py:67
  (4 shorter events, 0.0 us)
Async XLA Ops:
  0.6 16.0 %copy-start = (bf16[256,1024]{1,0:T(8,128)(2,1)S(1)}, bf16[256,1024]{1,0:T(8,128)(2,1)}, u32[]{:S(2)}) copy-start(bf16[256,1024]{1,0:T(8,128)(2,1)} %param.10) | copy-start | bytes 1572868
  0.6 16.0 %copy-start.2 = (bf16[256,512]{1,0:T(8,128)(2,1)S(1)}, bf16[256,512]{1,0:T(8,128)(2,1)}, u32[]{:S(2)}) copy-start(bf16[256,512]{1,0:T(8,128)(2,1)} %refs_1_.7) | copy-start | bytes 786436
  1.8 9.3 %collective-permute-start.2 = (bf16[256,128]{1,0:T(8,128)(2,1)S(1)}, bf16[256,128]{1,0:T(8,128)(2,1)S(1)}, u32[]{:S(2)}, u32[]{:S(2)}) collective-permute-start(bf16[256,128]{1,0:T(8,128)(2,1)S(1)} %get-tuple-element.39.refs_2_), channel_id=1, source_target_pairs={{0,36},{1,37},{2,38},{3,39},{4,32},{5,33},{6,34},{7,35},{8,44},{9,... | collective-permute-start | bytes 196616 | tf_op jit(solution)/shard_map/ppermute | solution.py:44
  9.1 0.9 %copy-start.3 = (bf16[256,256]{1,0:T(8,128)(2,1)S(1)}, bf16[256,256]{1,0:T(8,128)(2,1)}, u32[]{:S(2)}) copy-start(bf16[256,256]{1,0:T(8,128)(2,1)} %refs_1_.6) | copy-start | bytes 393220
  11.0 11.2 %copy-start.1 = (bf16[8192,256]{1,0:T(8,128)(2,1)S(1)}, bf16[8192,256]{1,0:T(8,128)(2,1)}, u32[]{:S(2)}) copy-start(bf16[8192,256]{1,0:T(8,128)(2,1)} %param.17) | copy-start | bytes 12582916
  11.6 7.0 %collective-permute-start.3 = (bf16[512,128]{1,0:T(8,128)(2,1)S(1)}, bf16[512,128]{1,0:T(8,128)(2,1)S(1)}, u32[]{:S(2)}, u32[]{:S(2)}) collective-permute-start(bf16[512,128]{1,0:T(8,128)(2,1)S(1)} %shard_map.106), channel_id=1, source_target_pairs={{0,64},{32,96},{64,128},{96,160},{128,192},{160,224},{192,0},{224,... | collective-permute-start | bytes 393224 | tf_op jit(solution)/shard_map/ppermute | solution.py:37
  13.2 7.7 %collective-permute-start.4 = (bf16[512,128]{1,0:T(8,128)(2,1)S(1)}, bf16[512,128]{1,0:T(8,128)(2,1)S(1)}, u32[]{:S(2)}, u32[]{:S(2)}) collective-permute-start(bf16[512,128]{1,0:T(8,128)(2,1)S(1)} %shard_map.106), channel_id=1, source_target_pairs={{0,128},{32,160},{64,192},{96,224},{128,0},{160,32},{192,64},{224,... | collective-permute-start | bytes 393224 | tf_op jit(solution)/shard_map/ppermute | solution.py:37
  14.2 7.4 %collective-permute-start.5 = (bf16[512,128]{1,0:T(8,128)(2,1)S(1)}, bf16[512,128]{1,0:T(8,128)(2,1)S(1)}, u32[]{:S(2)}, u32[]{:S(2)}) collective-permute-start(bf16[512,128]{1,0:T(8,128)(2,1)S(1)} %shard_map.106), channel_id=1, source_target_pairs={{0,192},{32,224},{64,0},{96,32},{128,64},{160,96},{192,128},{224,1... | collective-permute-start | bytes 393224 | tf_op jit(solution)/shard_map/ppermute | solution.py:37
  22.1 1.9 %collective-permute-start.6 = (bf16[1792,128]{1,0:T(8,128)(2,1)S(1)}, bf16[1792,128]{1,0:T(8,128)(2,1)S(1)}, u32[]{:S(2)}, u32[]{:S(2)}) collective-permute-start(bf16[1792,128]{1,0:T(8,128)(2,1)S(1)} %shard_map.108.refs_2_), channel_id=1, source_target_pairs={{0,1},{1,0},{2,3},{3,2},{4,5},{5,4},{6,7},{7,6},{8,9},{9,8},{10,11... | collective-permute-start | bytes 1376264 | tf_op jit(solution)/shard_map/ppermute | solution.py:28
  22.2 1.8 %copy-start.4 = (bf16[256,256]{1,0:T(8,128)(2,1)S(1)}, bf16[256,256]{1,0:T(8,128)(2,1)}, u32[]{:S(2)}) copy-start(bf16[256,256]{1,0:T(8,128)(2,1)} %refs_1_.6) | copy-start | bytes 393220
  23.1 4.8 %collective-permute-start.1 = (bf16[16,256,256]{2,1,0:T(8,128)(2,1)S(1)}, bf16[16,256,256]{2,1,0:T(8,128)(2,1)S(1)}, u32[]{:S(2)}, u32[]{:S(2)}) collective-permute-start(bf16[16,256,256]{2,1,0:T(8,128)(2,1)S(1)} %get-tuple-element.20), channel_id=1, source_target_pairs={{0,1},{1,0},{2,3},{3,2},{4,5},{5,4},{6,7},{7,6},{8,9},{9,8},{10,11... | collective-permute-start | bytes 6291464 | tf_op jit(solution)/shard_map/ppermute | solution.py:28
  26.4 1.4 %collective-permute-start.7 = (bf16[256,256]{1,0:T(8,128)(2,1)S(1)}, bf16[256,256]{1,0:T(8,128)(2,1)S(1)}, u32[]{:S(2)}, u32[]{:S(2)}) collective-permute-start(bf16[256,256]{1,0:T(8,128)(2,1)S(1)} %shard_map.109.refs_17_), channel_id=1, source_target_pairs={{0,1},{1,0},{2,3},{3,2},{4,5},{5,4},{6,7},{7,6},{8,9},{9,8},{10,11... | collective-permute-start | bytes 393224 | tf_op jit(solution)/shard_map/ppermute | solution.py:28
  29.1 15.3 %collective-permute-start.9 = (bf16[2,2,256,256]{3,2,1,0:T(8,128)(2,1)S(1)}, bf16[2,2,256,256]{3,2,1,0:T(8,128)(2,1)S(1)}, u32[]{:S(2)}, u32[]{:S(2)}) collective-permute-start(bf16[2,2,256,256]{3,2,1,0:T(8,128)(2,1)S(1)} %get-tuple-element.28), channel_id=1, source_target_pairs={{0,24},{1,25},{2,26},{3,27},{4,28},{5,29},{6,30},{7,31},{8,16},{9,... | collective-permute-start | bytes 1572872 | tf_op jit(solution)/shard_map/ppermute | solution.py:48
  32.0 13.7 %collective-permute-start.8 = (bf16[2,2,256,256]{3,2,1,0:T(8,128)(2,1)S(1)}, bf16[2,2,256,256]{3,2,1,0:T(8,128)(2,1)S(1)}, u32[]{:S(2)}, u32[]{:S(2)}) collective-permute-start(bf16[2,2,256,256]{3,2,1,0:T(8,128)(2,1)S(1)} %get-tuple-element.24.refs_19_), channel_id=1, source_target_pairs={{0,8},{1,9},{2,10},{3,11},{4,12},{5,13},{6,14},{7,15},{8,0},{9,1},... | collective-permute-start | bytes 1572872 | tf_op jit(solution)/shard_map/ppermute | solution.py:48
  32.2 16.5 %collective-permute-start = (bf16[528,128]{1,0:T(8,128)(2,1)S(1)}, bf16[528,128]{1,0:T(8,128)(2,1)S(1)}, u32[]{:S(2)}, u32[]{:S(2)}) collective-permute-start(bf16[528,128]{1,0:T(8,128)(2,1)S(1)} %shard_map.104.refs_5_.refs_1_), channel_id=1, source_target_pairs={{0,32},{32,0},{64,96},{96,64},{128,160},{160,128},{192,224},{224,1... | collective-permute-start | bytes 405512 | tf_op jit(solution)/shard_map/ppermute | solution.py:32
  45.1 10.5 %collective-permute-start.14 = (bf16[1,2,256,256]{3,2,1,0:T(8,128)(2,1)S(1)}, bf16[1,2,256,256]{3,2,1,0:T(8,128)(2,1)S(1)}, u32[]{:S(2)}, u32[]{:S(2)}) collective-permute-start(bf16[1,2,256,256]{3,2,1,0:T(8,128)(2,1)S(1)} %get-tuple-element.29.refs_4_), channel_id=1, source_target_pairs={{0,8},{1,9},{2,10},{3,11},{4,12},{5,13},{6,14},{7,15},{8,0},{9,1},... | collective-permute-start | bytes 786440 | tf_op jit(solution)/shard_map/ppermute | solution.py:48
  46.3 11.8 %collective-permute-start.13 = (bf16[1,2,256,256]{3,2,1,0:T(8,128)(2,1)S(1)}, bf16[1,2,256,256]{3,2,1,0:T(8,128)(2,1)S(1)}, u32[]{:S(2)}, u32[]{:S(2)}) collective-permute-start(bf16[1,2,256,256]{3,2,1,0:T(8,128)(2,1)S(1)} %get-tuple-element.26.refs_3_), channel_id=1, source_target_pairs={{0,24},{1,25},{2,26},{3,27},{4,28},{5,29},{6,30},{7,31},{8,16},{9,... | collective-permute-start | bytes 786440 | tf_op jit(solution)/shard_map/ppermute | solution.py:48
  49.3 11.7 %copy-start.5 = (f32[8]{0:T(128)S(1)}, f32[8]{0:T(128)}, u32[]{:S(2)}) copy-start(f32[8]{0:T(128)} %param.13) | copy-start | bytes 100
  49.3 11.6 %collective-permute-start.10 = (bf16[528,128]{1,0:T(8,128)(2,1)S(1)}, bf16[528,128]{1,0:T(8,128)(2,1)S(1)}, u32[]{:S(2)}, u32[]{:S(2)}) collective-permute-start(bf16[528,128]{1,0:T(8,128)(2,1)S(1)} %shard_map.114), channel_id=1, source_target_pairs={{0,64},{32,96},{64,128},{96,160},{128,192},{160,224},{192,0},{224,... | collective-permute-start | bytes 405512 | tf_op jit(solution)/shard_map/ppermute | solution.py:37
  50.9 10.1 %collective-permute-start.11 = (bf16[528,128]{1,0:T(8,128)(2,1)S(1)}, bf16[528,128]{1,0:T(8,128)(2,1)S(1)}, u32[]{:S(2)}, u32[]{:S(2)}) collective-permute-start(bf16[528,128]{1,0:T(8,128)(2,1)S(1)} %shard_map.114), channel_id=1, source_target_pairs={{0,128},{32,160},{64,192},{96,224},{128,0},{160,32},{192,64},{224,... | collective-permute-start | bytes 405512 | tf_op jit(solution)/shard_map/ppermute | solution.py:37
  52.3 8.8 %collective-permute-start.12 = (bf16[528,128]{1,0:T(8,128)(2,1)S(1)}, bf16[528,128]{1,0:T(8,128)(2,1)S(1)}, u32[]{:S(2)}, u32[]{:S(2)}) collective-permute-start(bf16[528,128]{1,0:T(8,128)(2,1)S(1)} %shard_map.114), channel_id=1, source_target_pairs={{0,192},{32,224},{64,0},{96,32},{128,64},{160,96},{192,128},{224,1... | collective-permute-start | bytes 405512 | tf_op jit(solution)/shard_map/ppermute | solution.py:37
  56.2 11.4 %collective-permute-start.15 = (bf16[256,256]{1,0:T(8,128)(2,1)S(1)}, bf16[256,256]{1,0:T(8,128)(2,1)S(1)}, u32[]{:S(2)}, u32[]{:S(2)}) collective-permute-start(bf16[256,256]{1,0:T(8,128)(2,1)S(1)} %bitcast.35), channel_id=1, source_target_pairs={{0,4},{1,5},{2,6},{3,7},{4,0},{5,1},{6,2},{7,3},{8,12},{9,13},{10,... | collective-permute-start | bytes 393224 | tf_op jit(solution)/shard_map/ppermute | solution.py:52
  58.1 9.5 %collective-permute-start.16 = (bf16[256,256]{1,0:T(8,128)(2,1)S(1)}, bf16[256,256]{1,0:T(8,128)(2,1)S(1)}, u32[]{:S(2)}, u32[]{:S(2)}) collective-permute-start(bf16[256,256]{1,0:T(8,128)(2,1)S(1)} %bitcast.34), channel_id=1, source_target_pairs={{0,6},{1,7},{2,4},{3,5},{4,2},{5,3},{6,0},{7,1},{8,14},{9,15},{10,... | collective-permute-start | bytes 393224 | tf_op jit(solution)/shard_map/ppermute | solution.py:52
  60.9 7.3 %collective-permute-start.17 = (bf16[256,256]{1,0:T(8,128)(2,1)S(1)}, bf16[256,256]{1,0:T(8,128)(2,1)S(1)}, u32[]{:S(2)}, u32[]{:S(2)}) collective-permute-start(bf16[256,256]{1,0:T(8,128)(2,1)S(1)} %bitcast.36), channel_id=1, source_target_pairs={{0,2},{1,3},{2,0},{3,1},{4,6},{5,7},{6,4},{7,5},{8,10},{9,11},{10,... | collective-permute-start | bytes 393224 | tf_op jit(solution)/shard_map/ppermute | solution.py:52

commit v7 on v6

--- a/solution.py
+++ b/solution.py
@@ -53,32 +53,37 @@
 
 
 def whole(shape):
-    return pl.BlockSpec(shape, lambda i, s: (0,) * len(shape))
+    return pl.BlockSpec(memory_space=pltpu.VMEM)
+
+
+class Place:
+    def __getitem__(self, item):
+        if item < 2:
+            section = lax.axis_index("section")
+            return section >> 1 if item == 0 else section & 1
+        tp = lax.axis_index("tp")
+        return tp & 1 if item == 2 else (tp >> 1) ^ (item - 5)
 
 
 def call(
-    body, scalars, in_specs, out_shapes, args, scratch=(), limit=16, after=(), us=0.5, out_specs=None
+    body, in_specs, out_shapes, args, scratch=(), limit=16, after=(), us=0.5, out_specs=None
 ):
-    first, count = 1 + len(in_specs), len(after)
+    first, count = len(in_specs), len(after)
 
     def ordered(*refs):
-        body(*refs[:first], *refs[first + count :])
+        body(Place(), *refs[:first], *refs[first + count :])
 
     return pl.pallas_call(
         ordered,
-        grid_spec=pltpu.PrefetchScalarGridSpec(
-            num_scalar_prefetch=1,
-            grid=(1,),
-            in_specs=list(in_specs) + [pl.BlockSpec(memory_space=pl.ANY)] * count,
-            out_specs=out_specs or [whole(o.shape) for o in out_shapes],
-            scratch_shapes=list(scratch),
-        ),
+        in_specs=list(in_specs) + [pl.BlockSpec(memory_space=pl.ANY)] * count,
+        out_specs=out_specs or [whole(o.shape) for o in out_shapes],
+        scratch_shapes=list(scratch),
         out_shape=out_shapes,
         compiler_params=pltpu.CompilerParams(vmem_limit_bytes=limit * 1024 * 1024),
         cost_estimate=pl.CostEstimate(
             flops=int(us * 1e9), bytes_accessed=int(us * 3.5e6), transcendentals=0
         ),
-    )(scalars, *args, *after)
+    )(*args, *after)
 
 
 def copy_body(s, weights, mate, own, sems):
@@ -169,25 +174,26 @@
                 run(keys, values, 1 + 2 * rank)
 
 
-def project_body(s, *refs):
-    count = (len(refs) - 4) // 2
-    own = refs[:count]
-    got = refs[count : 2 * count]
-    here, there = refs[2 * count : 2 * count + 2]
-    outs = refs[2 * count + 2 :]
-    each = count // len(outs)
-    for i in range(count):
-        outs[i // each][(i % each) // 2, i % 2] = (
-            jnp.dot(own[i][0], here[...], preferred_element_type=f32)
-            + jnp.dot(got[i][0], there[...], preferred_element_type=f32)
-        ).astype(bf16)
-
-
-def add_split_body(s, kept, arrived, *outs):
-    rows = kept.shape[0] // len(outs)
-    for i, out in enumerate(outs):
-        at = slice(i * rows, (i + 1) * rows)
-        out[...] = (kept[at].astype(f32) + arrived[at].astype(f32)).astype(bf16)
+def project_body(offsets):
+    def body(s, own, mate, here, there, *outs):
+        each = len(offsets) // len(outs)
+        for i, r in enumerate(offsets):
+            outs[i // each][(i % each) // 2, i % 2] = (
+                jnp.dot(own[s[5 + r]], here[...], preferred_element_type=f32)
+                + jnp.dot(mate[s[5 + r]], there[...], preferred_element_type=f32)
+            ).astype(bf16)
+
+    return body
+
+
+def add_split_body(s, kept1, arrived1, kept2, arrived2, *outs):
+    half = len(outs) // 2
+    for kept, arrived, pieces in (
+        (kept1, arrived1, outs[:half]),
+        (kept2, arrived2, outs[half:]),
+    ):
+        for i, out in enumerate(pieces):
+            out[...] = (kept[i].astype(f32) + arrived[i].astype(f32)).astype(bf16)
 
 
 def running_sums(decay):
@@ -328,16 +334,10 @@
     value_rows,
     out_weight,
 ):
-    section = lax.axis_index("section")
     tp = lax.axis_index("tp")
-    y, zh = section // 2, section % 2
-    core, chip = tp % 2, tp // 2
+    core = tp % 2
     group = tp // (TP // GROUPS)
     shape = jax.ShapeDtypeStruct
-    scalars = jnp.stack(
-        [y, zh, core, group, group ^ 1] + [chip ^ r for r in range(CHIPS)]
-    ).astype(jnp.int32)
-
     length = query_rows.shape[0]
     head_block = (length, HEAD_DIM)
 
@@ -353,7 +353,6 @@
 
     (pair,) = call(
         join_body,
-        scalars,
         [whole(head_block)] * 2,
         [shape((2 * length, HEAD_DIM), bf16)],
         (own, arrived_pair),
@@ -363,7 +362,6 @@
     weight_block = (ROWS, out_weight.shape[1])
     sent_mate, own_weight = call(
         copy_body,
-        scalars,
         [pl.BlockSpec(memory_space=pl.ANY)],
         [shape((CHIPS, *weight_block), bf16)] * 2,
         [out_weight.reshape(CHIPS, 2, *weight_block)],
@@ -379,7 +377,6 @@
     decay_spec = whole(log_decay.shape)
     (closing,) = call(
         closing_body,
-        scalars,
         [x_spec, whole(head_block), decay_spec],
         [state_shape],
         (scan_input, in_rows, log_decay),
@@ -390,7 +387,6 @@
     q_spec = whole(query_rows.shape)
     near_part = call(
         attend_near_body,
-        scalars,
         [q_spec] + [whole(head_block)] * 2,
         [stat] * 3,
         (query_rows, own_keys, own_values),
@@ -399,7 +395,6 @@
     )
     (others,) = call(
         join_body,
-        scalars,
         [whole(head_block)] + [whole(pair.shape)] * 3,
         [shape((7 * length, HEAD_DIM), bf16)],
         (arrived_pair, fetched[1], fetched[0], fetched[2]),
@@ -408,7 +403,6 @@
     others_there = swap_core(others)
     (attended,) = call(
         attend_far_body,
-        scalars,
         [q_spec] + [whole(others.shape)] * 2 + [whole(stat.shape)] * 3,
         [shape((query_rows.shape[1], length), bf16)],
         (query_rows, others, others_there, *near_part),
@@ -420,47 +414,38 @@
     partner = swap_zh(closing)
     def project(offsets, after=()):
         return call(
-            project_body,
-            scalars,
-            [
-                pl.BlockSpec((1, *weight_block), lambda i, s, r=r: (s[5 + r], 0, 0))
-                for r in offsets * 2
-            ]
-            + [whole(attended.shape)] * 2,
+            project_body(offsets),
+            [whole(mate.shape)] * 2 + [whole(attended.shape)] * 2,
             [shape((2, 2, ROWS, length), bf16)] * 2,
-            [own_weight] * len(offsets)
-            + [mate] * len(offsets)
-            + [attended, attended_there],
+            [own_weight, mate, attended, attended_there],
             after=after,
             us=1.3,
         )
 
     sent1, sent2 = project([4, 5, 8, 9, 14, 15, 10, 11])
-    kept1, kept2 = project([0, 1, 12, 13, 2, 3, 6, 7], [sent1])
+    kept1, kept2 = project([0, 1, 12, 13, 2, 3, 6, 7], [sent1, out_rows])
     arrived1, arrived2 = swap_x(sent1, 1), swap_x(sent2, 3)
 
-    def add_split(kept, arrived):
-        out = shape((kept.shape[0] // 2, *kept.shape[1:]), bf16)
-        return call(add_split_body, scalars, [whole(kept.shape)] * 2, [out] * 2, (kept, arrived))
-
-    kept1, sent1 = add_split(kept1, arrived1)
-    kept2, sent2 = add_split(kept2, arrived2)
+    def add_split(blocks, out):
+        return call(
+            add_split_body, [whole(block.shape) for block in blocks], [out] * 4, blocks
+        )
+
+    pair_rows = shape((2, ROWS, length), bf16)
+    kept1, sent1, kept2, sent2 = add_split((kept1, arrived1, kept2, arrived2), pair_rows)
     arrived1, arrived2 = swap_x(sent1, 3), swap_x(sent2, 1)
     (joined,) = call(
         pair_body(heads),
-        scalars,
         [whole(closing.shape)] * 2,
         [state_shape],
         (closing, partner),
         after=[sent1, sent2],
     )
     earlier = [shift_y(joined, d) for d in (2, 1, 3)]
-    z0, z1 = add_split(kept1[0], arrived1[0])
-    z2, z3 = add_split(kept2[0], arrived2[0])
-    arrived = [z0[0]] + [swap_zl(z[0], b) for b, z in ((2, z2), (3, z3), (1, z1))]
+    z0, z1, z2, z3 = add_split((kept1, arrived1, kept2, arrived2), shape((ROWS, length), bf16))
+    arrived = [z0] + [swap_zl(z, b) for b, z in ((2, z2), (3, z3), (1, z1))]
     (attn_out,) = call(
         sum_body(4),
-        scalars,
         [whole((ROWS, length))] * 4,
         [shape((ROWS, length), bf16)],
         arrived,
@@ -469,7 +454,6 @@
 
     (ssm_out,) = call(
         scan_body,
-        scalars,
         [x_spec, whole(head_block), whole(head_block), decay_spec, whole((1, heads))]
         + [whole(closing.shape)] * 4,
         [shape(scan_input.shape, bf16)],

time: 69.8 us -> 65.3 us (0.936)
  Pallas kernels: 17.3 us -> 9.06 us
  waiting for transfers between devices: 16.2 us -> 18.8 us
  starting transfers between devices: 31.3 us -> 32.6 us
    pallas_call x15 -> x13, Pallas kernels: 17.3 us -> 9.06 us  [call(): pl.pallas_call(ordered, in_specs=list(in_specs) + [pl.BlockSpec(memory_sp...]
    ppermute x4, waiting for transfers between devices: 7.58 us -> 8.49 us  [swap_x(): return lax.ppermute(block, 'tp', [(t, t ^ 8 * offset) for t in range(TP)])]
  transfers between devices with their start and end apart: 18 -> 18, of which waited for: 8 -> 11; matrix products, arithmetic and copies ran while one was open for 3% -> 3% of each run, Pallas kernels for 20% -> 12%
where the time goes in v7:
time: 65.3 us; the launch traced here: 65 us
  starting transfers between devices  32.6 us (50%)
  waiting for transfers between devices  18.8 us (29%)
  Pallas kernels  9.06 us (14%)
  local copies, waits for them, and re-layouts  2.61 us (4%)
  other arithmetic  1.05 us (2%)
  between operations  0.85 us (1%)
    ppermute x6, starting transfers between devices, shift_y(): return lax.ppermute(block, 'section', route)  10.5 us
    pallas_call x13, Pallas kernels, call(): pl.pallas_call(ordered, in_specs=list(in_specs) + [pl.BlockSpec(memory_sp...  9.06 us
    ppermute x4, waiting for transfers between devices, swap_x(): return lax.ppermute(block, 'tp', [(t, t ^ 8 * offset) for t in range(TP)])  8.49 us
    ppermute x1, starting transfers between devices, swap_zh_near(): return lax.ppermute(block, ('section', 'tp'), route)  6.39 us
    ppermute x4, starting transfers between devices, swap_x(): return lax.ppermute(block, 'tp', [(t, t ^ 8 * offset) for t in range(TP)])  5.86 us
    ppermute x3, starting transfers between devices, swap_zl(): return lax.ppermute(block, 'tp', [(t, t ^ 2 * offset) for t in range(TP)])  4.76 us
    ppermute x3, waiting for transfers between devices, swap_zl(): return lax.ppermute(block, 'tp', [(t, t ^ 2 * offset) for t in range(TP)])  4.65 us
    ppermute x1, starting transfers between devices, swap_zh(): return lax.ppermute(block, 'section', [(s, s ^ 1) for s in range(SECTIONS)])  4.26 us
  transfers between devices with their start and end apart: 18, of which 11 were waited for; matrix products, arithmetic and copies ran while one was open for 3% of the time, Pallas kernels for 12%

profile of v7, /device:TPU:8, one launch (start us, length us, event | category | flops | bytes accessed | tf_op | source)
XLA Modules:
  0.0 65.0 jit_solution(589976858578127194)
XLA Ops:
  0.6 0.0 copy-start
  0.6 0.0 copy-start.2
  0.7 1.1 %broadcast_select_fusion = (bf16[256,128]{1,0:T(8,128)(2,1)S(1)}, bf16[256,128]{1,0:T(8,128)(2,1)S(1)}, bf16[256,128]{1,0:T(8,128)(2,1)S(1)}, bf16[256,128]{1,0:T(8,128)(2,1)S(1)}) fusion(pred[]{:T(512)S(6)} %eq.5, bf16[256,1024]{1,0:T(8,128)(2,1)} %param.16, s32[]{:T(128)S(6)} %select_n.34, bf16[256,1024]{1,0:T(8,128)(2,1)} %param.15, s32[]{:T(128)S(6)} %select_n.37), kind=kLoop, calls=%fused_computation.1 | loop fusion | flops 65536 | bytes 524297 | tf_op jit(solution)/shard_map/jit(_where)/select_n | solution.py:351
  1.7 6.4 %collective-permute-start.2 = (bf16[256,128]{1,0:T(8,128)(2,1)S(1)}, bf16[256,128]{1,0:T(8,128)(2,1)S(1)}, u32[]{:S(2)}, u32[]{:S(2)}) collective-permute-start(bf16[256,128]{1,0:T(8,128)(2,1)S(1)} %get-tuple-element.39.refs_1_), channel_id=1, source_target_pairs={{0,36},{1,37},{2,38},{3,39},{4,32},{5,33},{6,34},{7,35},{8,44},{9,... | collective-permute-start | bytes 196616 | tf_op jit(solution)/shard_map/ppermute | solution.py:44
  8.1 0.8 %copy.12.refs_2_.refs_3_ = f32[256,8]{1,0:T(8,128)S(1)} copy(f32[256,8]{0,1:T(8,128)} %param.12) | data formatting | bytes 16384 | tf_op args[3]
  9.0 0.0 copy-start.3
  9.0 0.9 %copy-done.3 = bf16[256,256]{1,0:T(8,128)(2,1)S(1)} copy-done((bf16[256,256]{1,0:T(8,128)(2,1)S(1)}, bf16[256,256]{1,0:T(8,128)(2,1)}, u32[]{:S(2)}) %copy-start.3) | copy-done | bytes 131096
  9.9 0.5 shard_map.107
  10.4 0.6 collective-permute-done.2.refs_1_.refs_0_
  10.9 0.0 copy-start.1
  10.9 1.7 %collective-permute-start.3 = (bf16[512,128]{1,0:T(8,128)(2,1)S(1)}, bf16[512,128]{1,0:T(8,128)(2,1)S(1)}, u32[]{:S(2)}, u32[]{:S(2)}) collective-permute-start(bf16[512,128]{1,0:T(8,128)(2,1)S(1)} %shard_map.106), channel_id=1, source_target_pairs={{0,64},{32,96},{64,128},{96,160},{128,192},{160,224},{192,0},{224,... | collective-permute-start | bytes 393224 | tf_op jit(solution)/shard_map/ppermute | solution.py:37
  12.6 0.9 %collective-permute-start.4 = (bf16[512,128]{1,0:T(8,128)(2,1)S(1)}, bf16[512,128]{1,0:T(8,128)(2,1)S(1)}, u32[]{:S(2)}, u32[]{:S(2)}) collective-permute-start(bf16[512,128]{1,0:T(8,128)(2,1)S(1)} %shard_map.106), channel_id=1, source_target_pairs={{0,128},{32,160},{64,192},{96,224},{128,0},{160,32},{192,64},{224,... | collective-permute-start | bytes 393224 | tf_op jit(solution)/shard_map/ppermute | solution.py:37
  13.5 2.4 %collective-permute-start.5 = (bf16[512,128]{1,0:T(8,128)(2,1)S(1)}, bf16[512,128]{1,0:T(8,128)(2,1)S(1)}, u32[]{:S(2)}, u32[]{:S(2)}) collective-permute-start(bf16[512,128]{1,0:T(8,128)(2,1)S(1)} %shard_map.106), channel_id=1, source_target_pairs={{0,192},{32,224},{64,0},{96,32},{128,64},{160,96},{192,128},{224,1... | collective-permute-start | bytes 393224 | tf_op jit(solution)/shard_map/ppermute | solution.py:37
  15.9 0.0 copy-done
  16.0 0.0 copy-done.2
  16.0 1.4 %shard_map.104.refs_4_.refs_0_ = bf16[528,128]{1,0:T(8,128)(2,1)S(1)} custom-call(bf16[256,512]{1,0:T(8,128)(2,1)S(1)} %copy-done.2, bf16[256,128]{1,0:T(8,128)(2,1)S(1)} %constant_dynamic-slice_fusion.3.refs_1_, f32[256,8]{1,0:T(8,128)S(1)} %copy.12.refs_2_.refs_3_), custom_call_target="tpu_custom_call" | custom-call | flops 300000000 | bytes 1050000 | tf_op jit(solution)/shard_map/pallas_call | solution.py:76
  17.4 0.0 collective-permute-done.3.refs_1_
  17.4 2.4 %collective-permute-done.4.refs_2_ = bf16[512,128]{1,0:T(8,128)(2,1)S(1)} collective-permute-done((bf16[512,128]{1,0:T(8,128)(2,1)S(1)}, bf16[512,128]{1,0:T(8,128)(2,1)S(1)}, u32[]{:S(2)}, u32[]{:S(2)}) %collective-permute-start.4) | collective-permute-done | bytes 131104 | tf_op jit(solution)/shard_map/ppermute | solution.py:37
  19.8 0.6 collective-permute-done.5.refs_3_
  20.4 0.1 collective-permute-start.6
  20.5 0.0 copy-done.1
  20.5 0.0 copy-start.4
  20.5 0.3 shard_map.105
  20.8 0.6 collective-permute-start.1
  21.4 0.9 %collective-permute-done.6.refs_2_ = bf16[1792,128]{1,0:T(8,128)(2,1)S(1)} collective-permute-done((bf16[1792,128]{1,0:T(8,128)(2,1)S(1)}, bf16[1792,128]{1,0:T(8,128)(2,1)S(1)}, u32[]{:S(2)}, u32[]{:S(2)}) %collective-permute-start.6) | collective-permute-done | bytes 458784 | tf_op jit(solution)/shard_map/ppermute | solution.py:28
  22.3 0.0 copy-done.4
  22.3 1.8 %shard_map.109.refs_2_ = bf16[256,256]{1,0:T(8,128)(2,1)S(1)} custom-call(bf16[256,256]{1,0:T(8,128)(2,1)S(1)} %copy-done.4, bf16[1792,128]{1,0:T(8,128)(2,1)S(1)} %shard_map.108.refs_1_, bf16[1792,128]{1,0:T(8,128)(2,1)S(1)} %collective-permute-done.6.refs_2_, f32[512,128]{1,0:T(8,128)S(1)} %get-tuple-element.21.refs_5_.refs_3_, ...), custom_call_target="tpu_custom_call" | custom-call | flops 40000000000 | bytes 140000000 | tf_op jit(solution)/shard_map/pallas_call | solution.py:76
  24.1 0.2 collective-permute-start.7
  24.3 1.2 %collective-permute-done.7.refs_3_ = bf16[256,256]{1,0:T(8,128)(2,1)S(1)} collective-permute-done((bf16[256,256]{1,0:T(8,128)(2,1)S(1)}, bf16[256,256]{1,0:T(8,128)(2,1)S(1)}, u32[]{:S(2)}, u32[]{:S(2)}) %collective-permute-start.7) | collective-permute-done | bytes 131104 | tf_op jit(solution)/shard_map/ppermute | solution.py:28
  25.5 0.0 collective-permute-done.1.refs_1_
  25.5 0.7 %shard_map.110 = (bf16[2,2,256,256]{3,2,1,0:T(8,128)(2,1)S(1)}, bf16[2,2,256,256]{3,2,1,0:T(8,128)(2,1)S(1)}) custom-call(bf16[16,256,256]{2,1,0:T(8,128)(2,1)S(1)} %get-tuple-element.19.refs_0_, bf16[16,256,256]{2,1,0:T(8,128)(2,1)S(1)} %collective-permute-done.1.refs_1_, bf16[256,256]{1,0:T(8,128)(2,1)S(1)} %shard_map.109.refs_2_, ...), custom_call_target="tpu_custom_call" | custom-call | flops 1300000000 | bytes 4550000 | tf_op jit(solution)/shard_map/pallas_call | solution.py:76
  26.2 1.6 %collective-permute-start.8 = (bf16[2,2,256,256]{3,2,1,0:T(8,128)(2,1)S(1)}, bf16[2,2,256,256]{3,2,1,0:T(8,128)(2,1)S(1)}, u32[]{:S(2)}, u32[]{:S(2)}) collective-permute-start(bf16[2,2,256,256]{3,2,1,0:T(8,128)(2,1)S(1)} %get-tuple-element.24.refs_4_), channel_id=1, source_target_pairs={{0,8},{1,9},{2,10},{3,11},{4,12},{5,13},{6,14},{7,15},{8,0},{9,1},... | collective-permute-start | bytes 1572872 | tf_op jit(solution)/shard_map/ppermute | solution.py:48
  27.8 2.1 %collective-permute-start.9 = (bf16[2,2,256,256]{3,2,1,0:T(8,128)(2,1)S(1)}, bf16[2,2,256,256]{3,2,1,0:T(8,128)(2,1)S(1)}, u32[]{:S(2)}, u32[]{:S(2)}) collective-permute-start(bf16[2,2,256,256]{3,2,1,0:T(8,128)(2,1)S(1)} %get-tuple-element.27), channel_id=1, source_target_pairs={{0,24},{1,25},{2,26},{3,27},{4,28},{5,29},{6,30},{7,31},{8,16},{9,... | collective-permute-start | bytes 1572872 | tf_op jit(solution)/shard_map/ppermute | solution.py:48
  29.9 4.3 %collective-permute-start = (bf16[528,128]{1,0:T(8,128)(2,1)S(1)}, bf16[528,128]{1,0:T(8,128)(2,1)S(1)}, u32[]{:S(2)}, u32[]{:S(2)}) collective-permute-start(bf16[528,128]{1,0:T(8,128)(2,1)S(1)} %shard_map.104.refs_4_.refs_0_), channel_id=1, source_target_pairs={{0,32},{32,0},{64,96},{96,64},{128,160},{160,128},{192,224},{224,1... | collective-permute-start | bytes 405512 | tf_op jit(solution)/shard_map/ppermute | solution.py:32
  34.2 0.8 %constant_dynamic-slice_fusion.2.refs_5_.refs_2_ = bf16[256,128]{1,0:T(8,128)(2,1)S(1)} fusion(bf16[256,1024]{1,0:T(8,128)(2,1)} %param.11, s32[]{:T(128)S(6)} %select_n.34), kind=kLoop, calls=%fused_computation.4 | loop fusion | bytes 131076 | tf_op jit(solution)/shard_map/dynamic_slice | solution.py:345
  35.0 0.7 %shard_map.111 = (bf16[2,2,256,256]{3,2,1,0:T(8,128)(2,1)S(1)}, bf16[2,2,256,256]{3,2,1,0:T(8,128)(2,1)S(1)}) custom-call(bf16[16,256,256]{2,1,0:T(8,128)(2,1)S(1)} %get-tuple-element.19.refs_0_, bf16[16,256,256]{2,1,0:T(8,128)(2,1)S(1)} %collective-permute-done.1.refs_1_, bf16[256,256]{1,0:T(8,128)(2,1)S(1)} %shard_map.109.refs_2_, ...), custom_call_target="tpu_custom_call" | custom-call | flops 1300000000 | bytes 4550000 | tf_op jit(solution)/shard_map/pallas_call | solution.py:76
  35.7 4.6 %collective-permute-done.8.refs_1_ = bf16[2,2,256,256]{3,2,1,0:T(8,128)(2,1)S(1)} collective-permute-done((bf16[2,2,256,256]{3,2,1,0:T(8,128)(2,1)S(1)}, bf16[2,2,256,256]{3,2,1,0:T(8,128)(2,1)S(1)}, u32[]{:S(2)}, u32[]{:S(2)}) %collective-permute-start.8) | collective-permute-done | bytes 524320 | tf_op jit(solution)/shard_map/ppermute | solution.py:48
  40.4 2.4 %collective-permute-done.9.refs_3_ = bf16[2,2,256,256]{3,2,1,0:T(8,128)(2,1)S(1)} collective-permute-done((bf16[2,2,256,256]{3,2,1,0:T(8,128)(2,1)S(1)}, bf16[2,2,256,256]{3,2,1,0:T(8,128)(2,1)S(1)}, u32[]{:S(2)}, u32[]{:S(2)}) %collective-permute-start.9) | collective-permute-done | bytes 524320 | tf_op jit(solution)/shard_map/ppermute | solution.py:48
  42.8 0.2 shard_map.112
  43.0 0.0 copy-start.5
  43.0 2.2 %collective-permute-start.13 = (bf16[2,256,256]{2,1,0:T(8,128)(2,1)S(1)}, bf16[2,256,256]{2,1,0:T(8,128)(2,1)S(1)}, u32[]{:S(2)}, u32[]{:S(2)}) collective-permute-start(bf16[2,256,256]{2,1,0:T(8,128)(2,1)S(1)} %get-tuple-element.28.refs_2_), channel_id=1, source_target_pairs={{0,24},{1,25},{2,26},{3,27},{4,28},{5,29},{6,30},{7,31},{8,16},{9,... | collective-permute-start | bytes 786440 | tf_op jit(solution)/shard_map/ppermute | solution.py:48
  45.2 0.0 collective-permute-start.14
  45.2 0.0 collective-permute-done.refs_1_.refs_5_
  45.3 1.5 %collective-permute-start.10 = (bf16[528,128]{1,0:T(8,128)(2,1)S(1)}, bf16[528,128]{1,0:T(8,128)(2,1)S(1)}, u32[]{:S(2)}, u32[]{:S(2)}) collective-permute-start(bf16[528,128]{1,0:T(8,128)(2,1)S(1)} %shard_map.113), channel_id=1, source_target_pairs={{0,64},{32,96},{64,128},{96,160},{128,192},{160,224},{192,0},{224,... | collective-permute-start | bytes 405512 | tf_op jit(solution)/shard_map/ppermute | solution.py:37
  46.7 1.5 %collective-permute-start.11 = (bf16[528,128]{1,0:T(8,128)(2,1)S(1)}, bf16[528,128]{1,0:T(8,128)(2,1)S(1)}, u32[]{:S(2)}, u32[]{:S(2)}) collective-permute-start(bf16[528,128]{1,0:T(8,128)(2,1)S(1)} %shard_map.113), channel_id=1, source_target_pairs={{0,128},{32,160},{64,192},{96,224},{128,0},{160,32},{192,64},{224,... | collective-permute-start | bytes 405512 | tf_op jit(solution)/shard_map/ppermute | solution.py:37
  48.3 2.5 %collective-permute-start.12 = (bf16[528,128]{1,0:T(8,128)(2,1)S(1)}, bf16[528,128]{1,0:T(8,128)(2,1)S(1)}, u32[]{:S(2)}, u32[]{:S(2)}) collective-permute-start(bf16[528,128]{1,0:T(8,128)(2,1)S(1)} %shard_map.113), channel_id=1, source_target_pairs={{0,192},{32,224},{64,0},{96,32},{128,64},{160,96},{192,128},{224,1... | collective-permute-start | bytes 405512 | tf_op jit(solution)/shard_map/ppermute | solution.py:37
  50.8 0.8 %collective-permute-done.13.refs_1_ = bf16[2,256,256]{2,1,0:T(8,128)(2,1)S(1)} collective-permute-done((bf16[2,256,256]{2,1,0:T(8,128)(2,1)S(1)}, bf16[2,256,256]{2,1,0:T(8,128)(2,1)S(1)}, u32[]{:S(2)}, u32[]{:S(2)}) %collective-permute-start.13) | collective-permute-done | bytes 262176 | tf_op jit(solution)/shard_map/ppermute | solution.py:48
  51.6 0.6 collective-permute-done.14.refs_3_
  52.2 0.1 shard_map.114
  52.3 1.8 %collective-permute-start.15 = (bf16[256,256]{1,0:T(8,128)(2,1)S(1)}, bf16[256,256]{1,0:T(8,128)(2,1)S(1)}, u32[]{:S(2)}, u32[]{:S(2)}) collective-permute-start(bf16[256,256]{1,0:T(8,128)(2,1)S(1)} %get-tuple-element.35), channel_id=1, source_target_pairs={{0,4},{1,5},{2,6},{3,7},{4,0},{5,1},{6,2},{7,3},{8,12},{9,13},{10,... | collective-permute-start | bytes 393224 | tf_op jit(solution)/shard_map/ppermute | solution.py:52
  54.2 2.9 %collective-permute-start.16 = (bf16[256,256]{1,0:T(8,128)(2,1)S(1)}, bf16[256,256]{1,0:T(8,128)(2,1)S(1)}, u32[]{:S(2)}, u32[]{:S(2)}) collective-permute-start(bf16[256,256]{1,0:T(8,128)(2,1)S(1)} %get-tuple-element.33.refs_10_), channel_id=1, source_target_pairs={{0,6},{1,7},{2,4},{3,5},{4,2},{5,3},{6,0},{7,1},{8,14},{9,15},{10,... | collective-permute-start | bytes 393224 | tf_op jit(solution)/shard_map/ppermute | solution.py:52
  57.1 0.0 collective-permute-done.10.refs_6_
  57.1 0.0 collective-permute-start.17
  57.1 0.0 collective-permute-done.11.refs_7_
  57.1 0.0 collective-permute-done.12.refs_8_
  57.1 0.0 copy-done.5
  57.1 2.5 %shard_map.115 = bf16[256,512]{1,0:T(8,128)(2,1)} custom-call(bf16[256,512]{1,0:T(8,128)(2,1)S(1)} %copy-done.2, bf16[256,128]{1,0:T(8,128)(2,1)S(1)} %constant_dynamic-slice_fusion.3.refs_1_, bf16[256,128]{1,0:T(8,128)(2,1)S(1)} %constant_dynamic-slice_fusion.2.refs_5_.refs_2_, f32[256,8]{1,0:T(8,128)S(1)} %copy.12.refs_2_.refs_3_, f32[1,8]{1,0:T(1,128)S(1)} %bitcast.3, ...), custom_call_target="tpu_custom_call" | custom-call | flops 3000000000 | bytes 10500000 | tf_op jit(solution)/shard_map/pallas_call | solution.py:76
  59.6 4.0 %collective-permute-done.15.refs_1_ = bf16[256,256]{1,0:T(8,128)(2,1)S(1)} collective-permute-done((bf16[256,256]{1,0:T(8,128)(2,1)S(1)}, bf16[256,256]{1,0:T(8,128)(2,1)S(1)}, u32[]{:S(2)}, u32[]{:S(2)}) %collective-permute-start.15) | collective-permute-done | bytes 131104 | tf_op jit(solution)/shard_map/ppermute | solution.py:52
  63.7 0.0 collective-permute-done.16.refs_2_
  63.7 0.6 collective-permute-done.17.refs_3_
  64.3 0.7 %shard_map.116 = bf16[256,256]{1,0:T(8,128)(2,1)} custom-call(bf16[256,256]{1,0:T(8,128)(2,1)S(1)} %get-tuple-element.34.refs_0_, bf16[256,256]{1,0:T(8,128)(2,1)S(1)} %collective-permute-done.15.refs_1_, bf16[256,256]{1,0:T(8,128)(2,1)S(1)} %collective-permute-done.16.refs_2_, bf16[256,256]{1,0:T(8,128)(2,1)S(1)} %collective-permute-done.17.refs_3_), custom_call_target="tpu_custom_call" | custom-call | flops 1300000000 | bytes 4550000 | tf_op jit(solution)/shard_map/pallas_call | solution.py:76
  (4 shorter events, 0.1 us)
Async XLA Ops:
  0.6 15.3 %copy-start = (bf16[256,1024]{1,0:T(8,128)(2,1)S(1)}, bf16[256,1024]{1,0:T(8,128)(2,1)}, u32[]{:S(2)}) copy-start(bf16[256,1024]{1,0:T(8,128)(2,1)} %param.10) | copy-start | bytes 1572868
  0.6 15.3 %copy-start.2 = (bf16[256,512]{1,0:T(8,128)(2,1)S(1)}, bf16[256,512]{1,0:T(8,128)(2,1)}, u32[]{:S(2)}) copy-start(bf16[256,512]{1,0:T(8,128)(2,1)} %refs_0_.7) | copy-start | bytes 786436
  1.7 9.2 %collective-permute-start.2 = (bf16[256,128]{1,0:T(8,128)(2,1)S(1)}, bf16[256,128]{1,0:T(8,128)(2,1)S(1)}, u32[]{:S(2)}, u32[]{:S(2)}) collective-permute-start(bf16[256,128]{1,0:T(8,128)(2,1)S(1)} %get-tuple-element.39.refs_1_), channel_id=1, source_target_pairs={{0,36},{1,37},{2,38},{3,39},{4,32},{5,33},{6,34},{7,35},{8,44},{9,... | collective-permute-start | bytes 196616 | tf_op jit(solution)/shard_map/ppermute | solution.py:44
  9.0 0.9 %copy-start.3 = (bf16[256,256]{1,0:T(8,128)(2,1)S(1)}, bf16[256,256]{1,0:T(8,128)(2,1)}, u32[]{:S(2)}) copy-start(bf16[256,256]{1,0:T(8,128)(2,1)} %refs_0_.6) | copy-start | bytes 393220
  10.9 9.6 %copy-start.1 = (bf16[8192,256]{1,0:T(8,128)(2,1)S(1)}, bf16[8192,256]{1,0:T(8,128)(2,1)}, u32[]{:S(2)}) copy-start(bf16[8192,256]{1,0:T(8,128)(2,1)} %param.17) | copy-start | bytes 12582916
  10.9 6.4 %collective-permute-start.3 = (bf16[512,128]{1,0:T(8,128)(2,1)S(1)}, bf16[512,128]{1,0:T(8,128)(2,1)S(1)}, u32[]{:S(2)}, u32[]{:S(2)}) collective-permute-start(bf16[512,128]{1,0:T(8,128)(2,1)S(1)} %shard_map.106), channel_id=1, source_target_pairs={{0,64},{32,96},{64,128},{96,160},{128,192},{160,224},{192,0},{224,... | collective-permute-start | bytes 393224 | tf_op jit(solution)/shard_map/ppermute | solution.py:37
  12.6 7.2 %collective-permute-start.4 = (bf16[512,128]{1,0:T(8,128)(2,1)S(1)}, bf16[512,128]{1,0:T(8,128)(2,1)S(1)}, u32[]{:S(2)}, u32[]{:S(2)}) collective-permute-start(bf16[512,128]{1,0:T(8,128)(2,1)S(1)} %shard_map.106), channel_id=1, source_target_pairs={{0,128},{32,160},{64,192},{96,224},{128,0},{160,32},{192,64},{224,... | collective-permute-start | bytes 393224 | tf_op jit(solution)/shard_map/ppermute | solution.py:37
  13.5 6.8 %collective-permute-start.5 = (bf16[512,128]{1,0:T(8,128)(2,1)S(1)}, bf16[512,128]{1,0:T(8,128)(2,1)S(1)}, u32[]{:S(2)}, u32[]{:S(2)}) collective-permute-start(bf16[512,128]{1,0:T(8,128)(2,1)S(1)} %shard_map.106), channel_id=1, source_target_pairs={{0,192},{32,224},{64,0},{96,32},{128,64},{160,96},{192,128},{224,1... | collective-permute-start | bytes 393224 | tf_op jit(solution)/shard_map/ppermute | solution.py:37
  20.4 1.9 %collective-permute-start.6 = (bf16[1792,128]{1,0:T(8,128)(2,1)S(1)}, bf16[1792,128]{1,0:T(8,128)(2,1)S(1)}, u32[]{:S(2)}, u32[]{:S(2)}) collective-permute-start(bf16[1792,128]{1,0:T(8,128)(2,1)S(1)} %shard_map.108.refs_1_), channel_id=1, source_target_pairs={{0,1},{1,0},{2,3},{3,2},{4,5},{5,4},{6,7},{7,6},{8,9},{9,8},{10,11... | collective-permute-start | bytes 1376264 | tf_op jit(solution)/shard_map/ppermute | solution.py:28
  20.5 1.8 %copy-start.4 = (bf16[256,256]{1,0:T(8,128)(2,1)S(1)}, bf16[256,256]{1,0:T(8,128)(2,1)}, u32[]{:S(2)}) copy-start(bf16[256,256]{1,0:T(8,128)(2,1)} %refs_0_.6) | copy-start | bytes 393220
  20.8 4.7 %collective-permute-start.1 = (bf16[16,256,256]{2,1,0:T(8,128)(2,1)S(1)}, bf16[16,256,256]{2,1,0:T(8,128)(2,1)S(1)}, u32[]{:S(2)}, u32[]{:S(2)}) collective-permute-start(bf16[16,256,256]{2,1,0:T(8,128)(2,1)S(1)} %get-tuple-element.20), channel_id=1, source_target_pairs={{0,1},{1,0},{2,3},{3,2},{4,5},{5,4},{6,7},{7,6},{8,9},{9,8},{10,11... | collective-permute-start | bytes 6291464 | tf_op jit(solution)/shard_map/ppermute | solution.py:28
  24.1 1.4 %collective-permute-start.7 = (bf16[256,256]{1,0:T(8,128)(2,1)S(1)}, bf16[256,256]{1,0:T(8,128)(2,1)S(1)}, u32[]{:S(2)}, u32[]{:S(2)}) collective-permute-start(bf16[256,256]{1,0:T(8,128)(2,1)S(1)} %shard_map.109.refs_2_), channel_id=1, source_target_pairs={{0,1},{1,0},{2,3},{3,2},{4,5},{5,4},{6,7},{7,6},{8,9},{9,8},{10,11... | collective-permute-start | bytes 393224 | tf_op jit(solution)/shard_map/ppermute | solution.py:28
  26.2 14.1 %collective-permute-start.8 = (bf16[2,2,256,256]{3,2,1,0:T(8,128)(2,1)S(1)}, bf16[2,2,256,256]{3,2,1,0:T(8,128)(2,1)S(1)}, u32[]{:S(2)}, u32[]{:S(2)}) collective-permute-start(bf16[2,2,256,256]{3,2,1,0:T(8,128)(2,1)S(1)} %get-tuple-element.24.refs_4_), channel_id=1, source_target_pairs={{0,8},{1,9},{2,10},{3,11},{4,12},{5,13},{6,14},{7,15},{8,0},{9,1},... | collective-permute-start | bytes 1572872 | tf_op jit(solution)/shard_map/ppermute | solution.py:48
  27.8 15.0 %collective-permute-start.9 = (bf16[2,2,256,256]{3,2,1,0:T(8,128)(2,1)S(1)}, bf16[2,2,256,256]{3,2,1,0:T(8,128)(2,1)S(1)}, u32[]{:S(2)}, u32[]{:S(2)}) collective-permute-start(bf16[2,2,256,256]{3,2,1,0:T(8,128)(2,1)S(1)} %get-tuple-element.27), channel_id=1, source_target_pairs={{0,24},{1,25},{2,26},{3,27},{4,28},{5,29},{6,30},{7,31},{8,16},{9,... | collective-permute-start | bytes 1572872 | tf_op jit(solution)/shard_map/ppermute | solution.py:48
  29.9 15.3 %collective-permute-start = (bf16[528,128]{1,0:T(8,128)(2,1)S(1)}, bf16[528,128]{1,0:T(8,128)(2,1)S(1)}, u32[]{:S(2)}, u32[]{:S(2)}) collective-permute-start(bf16[528,128]{1,0:T(8,128)(2,1)S(1)} %shard_map.104.refs_4_.refs_0_), channel_id=1, source_target_pairs={{0,32},{32,0},{64,96},{96,64},{128,160},{160,128},{192,224},{224,1... | collective-permute-start | bytes 405512 | tf_op jit(solution)/shard_map/ppermute | solution.py:32
  43.0 14.1 %copy-start.5 = (f32[8]{0:T(128)S(1)}, f32[8]{0:T(128)}, u32[]{:S(2)}) copy-start(f32[8]{0:T(128)} %param.13) | copy-start | bytes 100
  43.0 8.6 %collective-permute-start.13 = (bf16[2,256,256]{2,1,0:T(8,128)(2,1)S(1)}, bf16[2,256,256]{2,1,0:T(8,128)(2,1)S(1)}, u32[]{:S(2)}, u32[]{:S(2)}) collective-permute-start(bf16[2,256,256]{2,1,0:T(8,128)(2,1)S(1)} %get-tuple-element.28.refs_2_), channel_id=1, source_target_pairs={{0,24},{1,25},{2,26},{3,27},{4,28},{5,29},{6,30},{7,31},{8,16},{9,... | collective-permute-start | bytes 786440 | tf_op jit(solution)/shard_map/ppermute | solution.py:48
  45.2 7.0 %collective-permute-start.14 = (bf16[2,256,256]{2,1,0:T(8,128)(2,1)S(1)}, bf16[2,256,256]{2,1,0:T(8,128)(2,1)S(1)}, u32[]{:S(2)}, u32[]{:S(2)}) collective-permute-start(bf16[2,256,256]{2,1,0:T(8,128)(2,1)S(1)} %get-tuple-element.29.refs_3_), channel_id=1, source_target_pairs={{0,8},{1,9},{2,10},{3,11},{4,12},{5,13},{6,14},{7,15},{8,0},{9,1},... | collective-permute-start | bytes 786440 | tf_op jit(solution)/shard_map/ppermute | solution.py:48
  45.3 11.8 %collective-permute-start.10 = (bf16[528,128]{1,0:T(8,128)(2,1)S(1)}, bf16[528,128]{1,0:T(8,128)(2,1)S(1)}, u32[]{:S(2)}, u32[]{:S(2)}) collective-permute-start(bf16[528,128]{1,0:T(8,128)(2,1)S(1)} %shard_map.113), channel_id=1, source_target_pairs={{0,64},{32,96},{64,128},{96,160},{128,192},{160,224},{192,0},{224,... | collective-permute-start | bytes 405512 | tf_op jit(solution)/shard_map/ppermute | solution.py:37
  46.7 10.4 %collective-permute-start.11 = (bf16[528,128]{1,0:T(8,128)(2,1)S(1)}, bf16[528,128]{1,0:T(8,128)(2,1)S(1)}, u32[]{:S(2)}, u32[]{:S(2)}) collective-permute-start(bf16[528,128]{1,0:T(8,128)(2,1)S(1)} %shard_map.113), channel_id=1, source_target_pairs={{0,128},{32,160},{64,192},{96,224},{128,0},{160,32},{192,64},{224,... | collective-permute-start | bytes 405512 | tf_op jit(solution)/shard_map/ppermute | solution.py:37
  48.3 8.8 %collective-permute-start.12 = (bf16[528,128]{1,0:T(8,128)(2,1)S(1)}, bf16[528,128]{1,0:T(8,128)(2,1)S(1)}, u32[]{:S(2)}, u32[]{:S(2)}) collective-permute-start(bf16[528,128]{1,0:T(8,128)(2,1)S(1)} %shard_map.113), channel_id=1, source_target_pairs={{0,192},{32,224},{64,0},{96,32},{128,64},{160,96},{192,128},{224,1... | collective-permute-start | bytes 405512 | tf_op jit(solution)/shard_map/ppermute | solution.py:37
  52.3 11.3 %collective-permute-start.15 = (bf16[256,256]{1,0:T(8,128)(2,1)S(1)}, bf16[256,256]{1,0:T(8,128)(2,1)S(1)}, u32[]{:S(2)}, u32[]{:S(2)}) collective-permute-start(bf16[256,256]{1,0:T(8,128)(2,1)S(1)} %get-tuple-element.35), channel_id=1, source_target_pairs={{0,4},{1,5},{2,6},{3,7},{4,0},{5,1},{6,2},{7,3},{8,12},{9,13},{10,... | collective-permute-start | bytes 393224 | tf_op jit(solution)/shard_map/ppermute | solution.py:52
  54.2 9.5 %collective-permute-start.16 = (bf16[256,256]{1,0:T(8,128)(2,1)S(1)}, bf16[256,256]{1,0:T(8,128)(2,1)S(1)}, u32[]{:S(2)}, u32[]{:S(2)}) collective-permute-start(bf16[256,256]{1,0:T(8,128)(2,1)S(1)} %get-tuple-element.33.refs_10_), channel_id=1, source_target_pairs={{0,6},{1,7},{2,4},{3,5},{4,2},{5,3},{6,0},{7,1},{8,14},{9,15},{10,... | collective-permute-start | bytes 393224 | tf_op jit(solution)/shard_map/ppermute | solution.py:52
  57.1 7.2 %collective-permute-start.17 = (bf16[256,256]{1,0:T(8,128)(2,1)S(1)}, bf16[256,256]{1,0:T(8,128)(2,1)S(1)}, u32[]{:S(2)}, u32[]{:S(2)}) collective-permute-start(bf16[256,256]{1,0:T(8,128)(2,1)S(1)} %get-tuple-element.32.refs_9_), channel_id=1, source_target_pairs={{0,2},{1,3},{2,0},{3,1},{4,6},{5,7},{6,4},{7,5},{8,10},{9,11},{10,... | collective-permute-start | bytes 393224 | tf_op jit(solution)/shard_map/ppermute | solution.py:52

commit v8 on v7

--- a/solution.py
+++ b/solution.py
@@ -176,9 +176,8 @@
 
 def project_body(offsets):
     def body(s, own, mate, here, there, *outs):
-        each = len(offsets) // len(outs)
         for i, r in enumerate(offsets):
-            outs[i // each][(i % each) // 2, i % 2] = (
+            outs[i // 2][i % 2] = (
                 jnp.dot(own[s[5 + r]], here[...], preferred_element_type=f32)
                 + jnp.dot(mate[s[5 + r]], there[...], preferred_element_type=f32)
             ).astype(bf16)
@@ -192,8 +191,11 @@
         (kept1, arrived1, outs[:half]),
         (kept2, arrived2, outs[half:]),
     ):
-        for i, out in enumerate(pieces):
-            out[...] = (kept[i].astype(f32) + arrived[i].astype(f32)).astype(bf16)
+        if half == 1:
+            pieces[0][...] = (kept[...].astype(f32) + arrived[...].astype(f32)).astype(bf16)
+        else:
+            for i, out in enumerate(pieces):
+                out[...] = (kept[i].astype(f32) + arrived[i].astype(f32)).astype(bf16)
 
 
 def running_sums(decay):
@@ -416,34 +418,41 @@
         return call(
             project_body(offsets),
             [whole(mate.shape)] * 2 + [whole(attended.shape)] * 2,
-            [shape((2, 2, ROWS, length), bf16)] * 2,
+            [shape((2, ROWS, length), bf16)] * (len(offsets) // 2),
             [own_weight, mate, attended, attended_there],
             after=after,
             us=1.3,
         )
 
-    sent1, sent2 = project([4, 5, 8, 9, 14, 15, 10, 11])
-    kept1, kept2 = project([0, 1, 12, 13, 2, 3, 6, 7], [sent1, out_rows])
-    arrived1, arrived2 = swap_x(sent1, 1), swap_x(sent2, 3)
-
-    def add_split(blocks, out):
+    sent1, sent3 = project([5, 9, 15, 11])
+    sent0, sent2 = project([4, 8, 14, 10], [sent1])
+    kept1, kept3, kept0, kept2 = project([1, 13, 3, 7, 0, 12, 2, 6], [sent0, out_rows])
+
+    def add_split(blocks, pieces):
+        out = shape((ROWS, length), bf16)
         return call(
-            add_split_body, [whole(block.shape) for block in blocks], [out] * 4, blocks
+            add_split_body, [whole(block.shape) for block in blocks], [out] * pieces, blocks
         )
 
-    pair_rows = shape((2, ROWS, length), bf16)
-    kept1, sent1, kept2, sent2 = add_split((kept1, arrived1, kept2, arrived2), pair_rows)
-    arrived1, arrived2 = swap_x(sent1, 3), swap_x(sent2, 1)
+    def halve(kept, sent, kept_too, sent_too):
+        kept, sent, kept_too, sent_too = add_split(
+            (kept, swap_x(sent, 1), kept_too, swap_x(sent_too, 3)), 4
+        )
+        return kept, sent, kept_too, sent_too
+
+    kept1, sent1, kept3, sent3 = halve(kept1, sent1, kept3, sent3)
+    kept0, sent0, kept2, sent2 = halve(kept0, sent0, kept2, sent2)
+    z1, z3 = add_split((kept1, swap_x(sent1, 3), kept3, swap_x(sent3, 1)), 2)
+    z0, z2 = add_split((kept0, swap_x(sent0, 3), kept2, swap_x(sent2, 1)), 2)
     (joined,) = call(
         pair_body(heads),
         [whole(closing.shape)] * 2,
         [state_shape],
         (closing, partner),
-        after=[sent1, sent2],
+        after=[sent0, sent2],
     )
     earlier = [shift_y(joined, d) for d in (2, 1, 3)]
-    z0, z1, z2, z3 = add_split((kept1, arrived1, kept2, arrived2), shape((ROWS, length), bf16))
-    arrived = [z0] + [swap_zl(z, b) for b, z in ((2, z2), (3, z3), (1, z1))]
+    arrived = [z0] + [swap_zl(z, b) for b, z in ((3, z3), (1, z1), (2, z2))]
     (attn_out,) = call(
         sum_body(4),
         [whole((ROWS, length))] * 4,

time: 65.3 us -> 65 us (level); the launches traced: 65 us -> 64.1 us
  waiting for transfers between devices: 18.8 us -> 14.6 us
  starting transfers between devices: 32.6 us -> 35.7 us
    ppermute x4 -> x8, waiting for transfers between devices: 8.49 us -> 4.78 us  [swap_x(): return lax.ppermute(block, 'tp', [(t, t ^ 8 * offset) for t in range(TP)])]
    ppermute x4 -> x8, starting transfers between devices: 5.86 us -> 8.96 us  [swap_x(): return lax.ppermute(block, 'tp', [(t, t ^ 8 * offset) for t in range(TP)])]
    pallas_call x13 -> x16, Pallas kernels: 9.06 us -> 9.23 us  [call(): pl.pallas_call(ordered, in_specs=list(in_specs) + [pl.BlockSpec(memory_sp...]
  transfers between devices with their start and end apart: 18 -> 22, of which waited for: 11 -> 10; matrix products, arithmetic and copies ran while one was open for 3% -> 3% of each run, Pallas kernels for 12% -> 12%
where the time goes in v8:
time: 65 us; the launch traced here: 64.1 us
  starting transfers between devices  35.7 us (55%)
  waiting for transfers between devices  14.6 us (22%)
  Pallas kernels  9.23 us (14%)
  local copies, waits for them, and re-layouts  2.61 us (4%)
  other arithmetic  1.05 us (2%)
  between operations  0.89 us (1%)
    ppermute x6, starting transfers between devices, shift_y(): return lax.ppermute(block, 'section', route)  10.7 us
    pallas_call x16, Pallas kernels, call(): pl.pallas_call(ordered, in_specs=list(in_specs) + [pl.BlockSpec(memory_sp...  9.23 us
    ppermute x8, starting transfers between devices, swap_x(): return lax.ppermute(block, 'tp', [(t, t ^ 8 * offset) for t in range(TP)])  8.96 us
    ppermute x1, starting transfers between devices, swap_zh_near(): return lax.ppermute(block, ('section', 'tp'), route)  6.39 us
    ppermute x8, waiting for transfers between devices, swap_x(): return lax.ppermute(block, 'tp', [(t, t ^ 8 * offset) for t in range(TP)])  4.78 us
    ppermute x3, starting transfers between devices, swap_zl(): return lax.ppermute(block, 'tp', [(t, t ^ 2 * offset) for t in range(TP)])  4.58 us
    ppermute x1, starting transfers between devices, swap_zh(): return lax.ppermute(block, 'section', [(s, s ^ 1) for s in range(SECTIONS)])  4.26 us
    ppermute x3, waiting for transfers between devices, swap_zl(): return lax.ppermute(block, 'tp', [(t, t ^ 2 * offset) for t in range(TP)])  4.12 us
  transfers between devices with their start and end apart: 22, of which 10 were waited for; matrix products, arithmetic and copies ran while one was open for 3% of the time, Pallas kernels for 12%

profile of v8, /device:TPU:8, one launch (start us, length us, event | category | flops | bytes accessed | tf_op | source)
XLA Modules:
  0.0 64.1 jit_solution(15243242669331866032)
XLA Ops:
  0.6 0.0 copy-start
  0.7 1.1 %broadcast_select_fusion = (bf16[256,128]{1,0:T(8,128)(2,1)S(1)}, bf16[256,128]{1,0:T(8,128)(2,1)S(1)}, bf16[256,128]{1,0:T(8,128)(2,1)S(1)}, bf16[256,128]{1,0:T(8,128)(2,1)S(1)}) fusion(pred[]{:T(512)S(6)} %eq.5, bf16[256,1024]{1,0:T(8,128)(2,1)} %param.16, s32[]{:T(128)S(6)} %select_n.34, bf16[256,1024]{1,0:T(8,128)(2,1)} %param.15, s32[]{:T(128)S(6)} %select_n.37), kind=kLoop, calls=%fused_computation.1 | loop fusion | flops 65536 | bytes 524297 | tf_op jit(solution)/shard_map/jit(_where)/select_n | solution.py:353
  1.7 6.4 %collective-permute-start.2 = (bf16[256,128]{1,0:T(8,128)(2,1)S(1)}, bf16[256,128]{1,0:T(8,128)(2,1)S(1)}, u32[]{:S(2)}, u32[]{:S(2)}) collective-permute-start(bf16[256,128]{1,0:T(8,128)(2,1)S(1)} %get-tuple-element.55.refs_1_), channel_id=1, source_target_pairs={{0,36},{1,37},{2,38},{3,39},{4,32},{5,33},{6,34},{7,35},{8,44},{9,... | collective-permute-start | bytes 196616 | tf_op jit(solution)/shard_map/ppermute | solution.py:44
  8.1 0.8 %copy.12.refs_2_.refs_3_ = f32[256,8]{1,0:T(8,128)S(1)} copy(f32[256,8]{0,1:T(8,128)} %param.12) | data formatting | bytes 16384 | tf_op args[3]
  9.0 0.0 copy-start.3
  9.0 0.9 %copy-done.3 = bf16[256,256]{1,0:T(8,128)(2,1)S(1)} copy-done((bf16[256,256]{1,0:T(8,128)(2,1)S(1)}, bf16[256,256]{1,0:T(8,128)(2,1)}, u32[]{:S(2)}) %copy-start.3) | copy-done | bytes 131096
  9.9 0.5 shard_map.107
  10.4 0.6 collective-permute-done.2.refs_1_.refs_0_
  10.9 1.7 %collective-permute-start.3 = (bf16[512,128]{1,0:T(8,128)(2,1)S(1)}, bf16[512,128]{1,0:T(8,128)(2,1)S(1)}, u32[]{:S(2)}, u32[]{:S(2)}) collective-permute-start(bf16[512,128]{1,0:T(8,128)(2,1)S(1)} %shard_map.106), channel_id=1, source_target_pairs={{0,64},{32,96},{64,128},{96,160},{128,192},{160,224},{192,0},{224,... | collective-permute-start | bytes 393224 | tf_op jit(solution)/shard_map/ppermute | solution.py:37
  12.6 0.9 %collective-permute-start.4 = (bf16[512,128]{1,0:T(8,128)(2,1)S(1)}, bf16[512,128]{1,0:T(8,128)(2,1)S(1)}, u32[]{:S(2)}, u32[]{:S(2)}) collective-permute-start(bf16[512,128]{1,0:T(8,128)(2,1)S(1)} %shard_map.106), channel_id=1, source_target_pairs={{0,128},{32,160},{64,192},{96,224},{128,0},{160,32},{192,64},{224,... | collective-permute-start | bytes 393224 | tf_op jit(solution)/shard_map/ppermute | solution.py:37
  13.5 2.4 %collective-permute-start.5 = (bf16[512,128]{1,0:T(8,128)(2,1)S(1)}, bf16[512,128]{1,0:T(8,128)(2,1)S(1)}, u32[]{:S(2)}, u32[]{:S(2)}) collective-permute-start(bf16[512,128]{1,0:T(8,128)(2,1)S(1)} %shard_map.106), channel_id=1, source_target_pairs={{0,192},{32,224},{64,0},{96,32},{128,64},{160,96},{192,128},{224,1... | collective-permute-start | bytes 393224 | tf_op jit(solution)/shard_map/ppermute | solution.py:37
  16.0 1.4 %shard_map.104.refs_4_.refs_0_ = bf16[528,128]{1,0:T(8,128)(2,1)S(1)} custom-call(bf16[256,512]{1,0:T(8,128)(2,1)S(1)} %copy-done.2, bf16[256,128]{1,0:T(8,128)(2,1)S(1)} %constant_dynamic-slice_fusion.3.refs_1_, f32[256,8]{1,0:T(8,128)S(1)} %copy.12.refs_2_.refs_3_), custom_call_target="tpu_custom_call" | custom-call | flops 300000000 | bytes 1050000 | tf_op jit(solution)/shard_map/pallas_call | solution.py:76
  17.4 0.0 collective-permute-done.3.refs_1_
  17.4 2.4 %collective-permute-done.4.refs_2_ = bf16[512,128]{1,0:T(8,128)(2,1)S(1)} collective-permute-done((bf16[512,128]{1,0:T(8,128)(2,1)S(1)}, bf16[512,128]{1,0:T(8,128)(2,1)S(1)}, u32[]{:S(2)}, u32[]{:S(2)}) %collective-permute-start.4) | collective-permute-done | bytes 131104 | tf_op jit(solution)/shard_map/ppermute | solution.py:37
  19.8 0.6 collective-permute-done.5.refs_3_
  20.4 0.1 collective-permute-start.6
  20.5 0.0 copy-start.4
  20.5 0.3 shard_map.105
  20.8 0.6 collective-permute-start.1
  21.4 0.9 %collective-permute-done.6.refs_2_ = bf16[1792,128]{1,0:T(8,128)(2,1)S(1)} collective-permute-done((bf16[1792,128]{1,0:T(8,128)(2,1)S(1)}, bf16[1792,128]{1,0:T(8,128)(2,1)S(1)}, u32[]{:S(2)}, u32[]{:S(2)}) %collective-permute-start.6) | collective-permute-done | bytes 458784 | tf_op jit(solution)/shard_map/ppermute | solution.py:28
  22.3 1.8 %shard_map.109.refs_2_ = bf16[256,256]{1,0:T(8,128)(2,1)S(1)} custom-call(bf16[256,256]{1,0:T(8,128)(2,1)S(1)} %copy-done.4, bf16[1792,128]{1,0:T(8,128)(2,1)S(1)} %shard_map.108.refs_1_, bf16[1792,128]{1,0:T(8,128)(2,1)S(1)} %collective-permute-done.6.refs_2_, f32[512,128]{1,0:T(8,128)S(1)} %get-tuple-element.29.refs_5_.refs_3_, ...), custom_call_target="tpu_custom_call" | custom-call | flops 40000000000 | bytes 140000000 | tf_op jit(solution)/shard_map/pallas_call | solution.py:76
  24.1 0.2 collective-permute-start.7
  24.3 1.2 %collective-permute-done.7.refs_3_ = bf16[256,256]{1,0:T(8,128)(2,1)S(1)} collective-permute-done((bf16[256,256]{1,0:T(8,128)(2,1)S(1)}, bf16[256,256]{1,0:T(8,128)(2,1)S(1)}, u32[]{:S(2)}, u32[]{:S(2)}) %collective-permute-start.7) | collective-permute-done | bytes 131104 | tf_op jit(solution)/shard_map/ppermute | solution.py:28
  25.5 0.0 collective-permute-done.1.refs_1_
  25.5 0.4 shard_map.110
  26.0 0.4 shard_map.111
  26.4 1.6 %collective-permute-start.8 = (bf16[2,256,256]{2,1,0:T(8,128)(2,1)S(1)}, bf16[2,256,256]{2,1,0:T(8,128)(2,1)S(1)}, u32[]{:S(2)}, u32[]{:S(2)}) collective-permute-start(bf16[2,256,256]{2,1,0:T(8,128)(2,1)S(1)} %get-tuple-element.33.refs_4_), channel_id=1, source_target_pairs={{0,8},{1,9},{2,10},{3,11},{4,12},{5,13},{6,14},{7,15},{8,0},{9,1},... | collective-permute-start | bytes 786440 | tf_op jit(solution)/shard_map/ppermute | solution.py:48
  28.0 2.1 %collective-permute-start.9 = (bf16[2,256,256]{2,1,0:T(8,128)(2,1)S(1)}, bf16[2,256,256]{2,1,0:T(8,128)(2,1)S(1)}, u32[]{:S(2)}, u32[]{:S(2)}) collective-permute-start(bf16[2,256,256]{2,1,0:T(8,128)(2,1)S(1)} %get-tuple-element.36), channel_id=1, source_target_pairs={{0,24},{1,25},{2,26},{3,27},{4,28},{5,29},{6,30},{7,31},{8,16},{9,... | collective-permute-start | bytes 786440 | tf_op jit(solution)/shard_map/ppermute | solution.py:48
  30.1 4.3 %collective-permute-start = (bf16[528,128]{1,0:T(8,128)(2,1)S(1)}, bf16[528,128]{1,0:T(8,128)(2,1)S(1)}, u32[]{:S(2)}, u32[]{:S(2)}) collective-permute-start(bf16[528,128]{1,0:T(8,128)(2,1)S(1)} %shard_map.104.refs_4_.refs_0_), channel_id=1, source_target_pairs={{0,32},{32,0},{64,96},{96,64},{128,160},{160,128},{192,224},{224,1... | collective-permute-start | bytes 405512 | tf_op jit(solution)/shard_map/ppermute | solution.py:32
  34.4 0.6 collective-permute-start.13
  34.9 0.6 collective-permute-start.14
  35.6 0.8 %constant_dynamic-slice_fusion.2.refs_5_.refs_2_ = bf16[256,128]{1,0:T(8,128)(2,1)S(1)} fusion(bf16[256,1024]{1,0:T(8,128)(2,1)} %param.11, s32[]{:T(128)S(6)} %select_n.34), kind=kLoop, calls=%fused_computation.4 | loop fusion | bytes 131076 | tf_op jit(solution)/shard_map/dynamic_slice | solution.py:347
  36.4 0.7 %shard_map.112 = (bf16[2,256,256]{2,1,0:T(8,128)(2,1)S(1)}, bf16[2,256,256]{2,1,0:T(8,128)(2,1)S(1)}, bf16[2,256,256]{2,1,0:T(8,128)(2,1)S(1)}, bf16[2,256,256]{2,1,0:T(8,128)(2,1)S(1)}) custom-call(bf16[16,256,256]{2,1,0:T(8,128)(2,1)S(1)} %get-tuple-element.27.refs_0_, bf16[16,256,256]{2,1,0:T(8,128)(2,1)S(1)} %collective-permute-done.1.refs_1_, ...), custom_call_target="tpu_custom_call" | custom-call | flops 1300000000 | bytes 4550000 | tf_op jit(solution)/shard_map/pallas_call | solution.py:76
  37.1 0.0 collective-permute-done.8.refs_1_
  37.1 0.2 collective-permute-done.9.refs_3_
  37.3 0.1 shard_map.113
  37.5 2.8 %collective-permute-start.17 = (bf16[256,256]{1,0:T(8,128)(2,1)S(1)}, bf16[256,256]{1,0:T(8,128)(2,1)S(1)}, u32[]{:S(2)}, u32[]{:S(2)}) collective-permute-start(bf16[256,256]{1,0:T(8,128)(2,1)S(1)} %get-tuple-element.37.refs_2_), channel_id=1, source_target_pairs={{0,24},{1,25},{2,26},{3,27},{4,28},{5,29},{6,30},{7,31},{8,16},{9,... | collective-permute-start | bytes 393224 | tf_op jit(solution)/shard_map/ppermute | solution.py:48
  40.3 0.0 collective-permute-start.18
  40.3 2.4 %collective-permute-done.13.refs_1_ = bf16[2,256,256]{2,1,0:T(8,128)(2,1)S(1)} collective-permute-done((bf16[2,256,256]{2,1,0:T(8,128)(2,1)S(1)}, bf16[2,256,256]{2,1,0:T(8,128)(2,1)S(1)}, u32[]{:S(2)}, u32[]{:S(2)}) %collective-permute-start.13) | collective-permute-done | bytes 262176 | tf_op jit(solution)/shard_map/ppermute | solution.py:48
  42.7 2.2 %collective-permute-done.14.refs_3_ = bf16[2,256,256]{2,1,0:T(8,128)(2,1)S(1)} collective-permute-done((bf16[2,256,256]{2,1,0:T(8,128)(2,1)S(1)}, bf16[2,256,256]{2,1,0:T(8,128)(2,1)S(1)}, u32[]{:S(2)}, u32[]{:S(2)}) %collective-permute-start.14) | collective-permute-done | bytes 262176 | tf_op jit(solution)/shard_map/ppermute | solution.py:48
  44.9 0.1 shard_map.115
  45.0 1.2 %collective-permute-start.15 = (bf16[256,256]{1,0:T(8,128)(2,1)S(1)}, bf16[256,256]{1,0:T(8,128)(2,1)S(1)}, u32[]{:S(2)}, u32[]{:S(2)}) collective-permute-start(bf16[256,256]{1,0:T(8,128)(2,1)S(1)} %get-tuple-element.43), channel_id=1, source_target_pairs={{0,24},{1,25},{2,26},{3,27},{4,28},{5,29},{6,30},{7,31},{8,16},{9,... | collective-permute-start | bytes 393224 | tf_op jit(solution)/shard_map/ppermute | solution.py:48
  46.2 0.0 collective-permute-start.16
  46.2 0.0 collective-permute-done.refs_1_.refs_5_
  46.3 0.0 copy-start.5
  46.3 1.6 %collective-permute-start.10 = (bf16[528,128]{1,0:T(8,128)(2,1)S(1)}, bf16[528,128]{1,0:T(8,128)(2,1)S(1)}, u32[]{:S(2)}, u32[]{:S(2)}) collective-permute-start(bf16[528,128]{1,0:T(8,128)(2,1)S(1)} %shard_map.114), channel_id=1, source_target_pairs={{0,64},{32,96},{64,128},{96,160},{128,192},{160,224},{192,0},{224,... | collective-permute-start | bytes 405512 | tf_op jit(solution)/shard_map/ppermute | solution.py:37
  47.8 0.0 collective-permute-done.17.refs_1_
  47.9 1.9 %collective-permute-start.11 = (bf16[528,128]{1,0:T(8,128)(2,1)S(1)}, bf16[528,128]{1,0:T(8,128)(2,1)S(1)}, u32[]{:S(2)}, u32[]{:S(2)}) collective-permute-start(bf16[528,128]{1,0:T(8,128)(2,1)S(1)} %shard_map.114), channel_id=1, source_target_pairs={{0,128},{32,160},{64,192},{96,224},{128,0},{160,32},{192,64},{224,... | collective-permute-start | bytes 405512 | tf_op jit(solution)/shard_map/ppermute | solution.py:37
  49.8 0.0 collective-permute-done.18.refs_3_
  49.8 2.2 %collective-permute-start.12 = (bf16[528,128]{1,0:T(8,128)(2,1)S(1)}, bf16[528,128]{1,0:T(8,128)(2,1)S(1)}, u32[]{:S(2)}, u32[]{:S(2)}) collective-permute-start(bf16[528,128]{1,0:T(8,128)(2,1)S(1)} %shard_map.114), channel_id=1, source_target_pairs={{0,192},{32,224},{64,0},{96,32},{128,64},{160,96},{192,128},{224,1... | collective-permute-start | bytes 405512 | tf_op jit(solution)/shard_map/ppermute | solution.py:37
  52.0 0.1 shard_map.118
  52.0 0.0 collective-permute-done.15.refs_1_
  52.0 2.6 %collective-permute-start.21 = (bf16[256,256]{1,0:T(8,128)(2,1)S(1)}, bf16[256,256]{1,0:T(8,128)(2,1)S(1)}, u32[]{:S(2)}, u32[]{:S(2)}) collective-permute-start(bf16[256,256]{1,0:T(8,128)(2,1)S(1)} %get-tuple-element.51), channel_id=1, source_target_pairs={{0,4},{1,5},{2,6},{3,7},{4,0},{5,1},{6,2},{7,3},{8,12},{9,13},{10,... | collective-permute-start | bytes 393224 | tf_op jit(solution)/shard_map/ppermute | solution.py:52
  54.6 0.0 collective-permute-done.16.refs_3_
  54.6 0.1 shard_map.116
  54.6 2.0 %collective-permute-start.19 = (bf16[256,256]{1,0:T(8,128)(2,1)S(1)}, bf16[256,256]{1,0:T(8,128)(2,1)S(1)}, u32[]{:S(2)}, u32[]{:S(2)}) collective-permute-start(bf16[256,256]{1,0:T(8,128)(2,1)S(1)} %get-tuple-element.47.refs_10_), channel_id=1, source_target_pairs={{0,6},{1,7},{2,4},{3,5},{4,2},{5,3},{6,0},{7,1},{8,14},{9,15},{10,... | collective-permute-start | bytes 393224 | tf_op jit(solution)/shard_map/ppermute | solution.py:52
  56.7 0.0 collective-permute-done.10.refs_6_
  56.7 0.0 collective-permute-start.20
  56.7 0.0 collective-permute-done.12.refs_8_
  56.7 2.5 %shard_map.117 = bf16[256,512]{1,0:T(8,128)(2,1)} custom-call(bf16[256,512]{1,0:T(8,128)(2,1)S(1)} %copy-done.2, bf16[256,128]{1,0:T(8,128)(2,1)S(1)} %constant_dynamic-slice_fusion.3.refs_1_, bf16[256,128]{1,0:T(8,128)(2,1)S(1)} %constant_dynamic-slice_fusion.2.refs_5_.refs_2_, f32[256,8]{1,0:T(8,128)S(1)} %copy.12.refs_2_.refs_3_, f32[1,8]{1,0:T(1,128)S(1)} %bitcast.3, ...), custom_call_target="tpu_custom_call" | custom-call | flops 3000000000 | bytes 10500000 | tf_op jit(solution)/shard_map/pallas_call | solution.py:76
  59.2 3.0 %collective-permute-done.21.refs_3_ = bf16[256,256]{1,0:T(8,128)(2,1)S(1)} collective-permute-done((bf16[256,256]{1,0:T(8,128)(2,1)S(1)}, bf16[256,256]{1,0:T(8,128)(2,1)S(1)}, u32[]{:S(2)}, u32[]{:S(2)}) %collective-permute-start.21) | collective-permute-done | bytes 131104 | tf_op jit(solution)/shard_map/ppermute | solution.py:52
  62.2 0.0 collective-permute-done.19.refs_1_
  62.2 1.1 %collective-permute-done.20.refs_2_ = bf16[256,256]{1,0:T(8,128)(2,1)S(1)} collective-permute-done((bf16[256,256]{1,0:T(8,128)(2,1)S(1)}, bf16[256,256]{1,0:T(8,128)(2,1)S(1)}, u32[]{:S(2)}, u32[]{:S(2)}) %collective-permute-start.20) | collective-permute-done | bytes 131104 | tf_op jit(solution)/shard_map/ppermute | solution.py:52
  63.3 0.7 %shard_map.119 = bf16[256,256]{1,0:T(8,128)(2,1)} custom-call(bf16[256,256]{1,0:T(8,128)(2,1)S(1)} %get-tuple-element.50.refs_0_, bf16[256,256]{1,0:T(8,128)(2,1)S(1)} %collective-permute-done.19.refs_1_, bf16[256,256]{1,0:T(8,128)(2,1)S(1)} %collective-permute-done.20.refs_2_, bf16[256,256]{1,0:T(8,128)(2,1)S(1)} %collective-permute-done.21.refs_3_), custom_call_target="tpu_custom_call" | custom-call | flops 1300000000 | bytes 4550000 | tf_op jit(solution)/shard_map/pallas_call | solution.py:76
  (12 shorter events, 0.1 us)
Async XLA Ops:
  0.6 15.3 %copy-start = (bf16[256,1024]{1,0:T(8,128)(2,1)S(1)}, bf16[256,1024]{1,0:T(8,128)(2,1)}, u32[]{:S(2)}) copy-start(bf16[256,1024]{1,0:T(8,128)(2,1)} %param.10) | copy-start | bytes 1572868
  0.6 15.3 %copy-start.2 = (bf16[256,512]{1,0:T(8,128)(2,1)S(1)}, bf16[256,512]{1,0:T(8,128)(2,1)}, u32[]{:S(2)}) copy-start(bf16[256,512]{1,0:T(8,128)(2,1)} %refs_0_.7) | copy-start | bytes 786436
  1.7 9.2 %collective-permute-start.2 = (bf16[256,128]{1,0:T(8,128)(2,1)S(1)}, bf16[256,128]{1,0:T(8,128)(2,1)S(1)}, u32[]{:S(2)}, u32[]{:S(2)}) collective-permute-start(bf16[256,128]{1,0:T(8,128)(2,1)S(1)} %get-tuple-element.55.refs_1_), channel_id=1, source_target_pairs={{0,36},{1,37},{2,38},{3,39},{4,32},{5,33},{6,34},{7,35},{8,44},{9,... | collective-permute-start | bytes 196616 | tf_op jit(solution)/shard_map/ppermute | solution.py:44
  9.0 0.9 %copy-start.3 = (bf16[256,256]{1,0:T(8,128)(2,1)S(1)}, bf16[256,256]{1,0:T(8,128)(2,1)}, u32[]{:S(2)}) copy-start(bf16[256,256]{1,0:T(8,128)(2,1)} %refs_0_.6) | copy-start | bytes 393220
  10.9 9.6 %copy-start.1 = (bf16[8192,256]{1,0:T(8,128)(2,1)S(1)}, bf16[8192,256]{1,0:T(8,128)(2,1)}, u32[]{:S(2)}) copy-start(bf16[8192,256]{1,0:T(8,128)(2,1)} %param.17) | copy-start | bytes 12582916
  10.9 6.4 %collective-permute-start.3 = (bf16[512,128]{1,0:T(8,128)(2,1)S(1)}, bf16[512,128]{1,0:T(8,128)(2,1)S(1)}, u32[]{:S(2)}, u32[]{:S(2)}) collective-permute-start(bf16[512,128]{1,0:T(8,128)(2,1)S(1)} %shard_map.106), channel_id=1, source_target_pairs={{0,64},{32,96},{64,128},{96,160},{128,192},{160,224},{192,0},{224,... | collective-permute-start | bytes 393224 | tf_op jit(solution)/shard_map/ppermute | solution.py:37
  12.6 7.2 %collective-permute-start.4 = (bf16[512,128]{1,0:T(8,128)(2,1)S(1)}, bf16[512,128]{1,0:T(8,128)(2,1)S(1)}, u32[]{:S(2)}, u32[]{:S(2)}) collective-permute-start(bf16[512,128]{1,0:T(8,128)(2,1)S(1)} %shard_map.106), channel_id=1, source_target_pairs={{0,128},{32,160},{64,192},{96,224},{128,0},{160,32},{192,64},{224,... | collective-permute-start | bytes 393224 | tf_op jit(solution)/shard_map/ppermute | solution.py:37
  13.5 6.8 %collective-permute-start.5 = (bf16[512,128]{1,0:T(8,128)(2,1)S(1)}, bf16[512,128]{1,0:T(8,128)(2,1)S(1)}, u32[]{:S(2)}, u32[]{:S(2)}) collective-permute-start(bf16[512,128]{1,0:T(8,128)(2,1)S(1)} %shard_map.106), channel_id=1, source_target_pairs={{0,192},{32,224},{64,0},{96,32},{128,64},{160,96},{192,128},{224,1... | collective-permute-start | bytes 393224 | tf_op jit(solution)/shard_map/ppermute | solution.py:37
  20.4 1.9 %collective-permute-start.6 = (bf16[1792,128]{1,0:T(8,128)(2,1)S(1)}, bf16[1792,128]{1,0:T(8,128)(2,1)S(1)}, u32[]{:S(2)}, u32[]{:S(2)}) collective-permute-start(bf16[1792,128]{1,0:T(8,128)(2,1)S(1)} %shard_map.108.refs_1_), channel_id=1, source_target_pairs={{0,1},{1,0},{2,3},{3,2},{4,5},{5,4},{6,7},{7,6},{8,9},{9,8},{10,11... | collective-permute-start | bytes 1376264 | tf_op jit(solution)/shard_map/ppermute | solution.py:28
  20.5 1.8 %copy-start.4 = (bf16[256,256]{1,0:T(8,128)(2,1)S(1)}, bf16[256,256]{1,0:T(8,128)(2,1)}, u32[]{:S(2)}) copy-start(bf16[256,256]{1,0:T(8,128)(2,1)} %refs_0_.6) | copy-start | bytes 393220
  20.8 4.7 %collective-permute-start.1 = (bf16[16,256,256]{2,1,0:T(8,128)(2,1)S(1)}, bf16[16,256,256]{2,1,0:T(8,128)(2,1)S(1)}, u32[]{:S(2)}, u32[]{:S(2)}) collective-permute-start(bf16[16,256,256]{2,1,0:T(8,128)(2,1)S(1)} %get-tuple-element.28), channel_id=1, source_target_pairs={{0,1},{1,0},{2,3},{3,2},{4,5},{5,4},{6,7},{7,6},{8,9},{9,8},{10,11... | collective-permute-start | bytes 6291464 | tf_op jit(solution)/shard_map/ppermute | solution.py:28
  24.1 1.4 %collective-permute-start.7 = (bf16[256,256]{1,0:T(8,128)(2,1)S(1)}, bf16[256,256]{1,0:T(8,128)(2,1)S(1)}, u32[]{:S(2)}, u32[]{:S(2)}) collective-permute-start(bf16[256,256]{1,0:T(8,128)(2,1)S(1)} %shard_map.109.refs_2_), channel_id=1, source_target_pairs={{0,1},{1,0},{2,3},{3,2},{4,5},{5,4},{6,7},{7,6},{8,9},{9,8},{10,11... | collective-permute-start | bytes 393224 | tf_op jit(solution)/shard_map/ppermute | solution.py:28
  26.4 10.7 %collective-permute-start.8 = (bf16[2,256,256]{2,1,0:T(8,128)(2,1)S(1)}, bf16[2,256,256]{2,1,0:T(8,128)(2,1)S(1)}, u32[]{:S(2)}, u32[]{:S(2)}) collective-permute-start(bf16[2,256,256]{2,1,0:T(8,128)(2,1)S(1)} %get-tuple-element.33.refs_4_), channel_id=1, source_target_pairs={{0,8},{1,9},{2,10},{3,11},{4,12},{5,13},{6,14},{7,15},{8,0},{9,1},... | collective-permute-start | bytes 786440 | tf_op jit(solution)/shard_map/ppermute | solution.py:48
  28.0 9.3 %collective-permute-start.9 = (bf16[2,256,256]{2,1,0:T(8,128)(2,1)S(1)}, bf16[2,256,256]{2,1,0:T(8,128)(2,1)S(1)}, u32[]{:S(2)}, u32[]{:S(2)}) collective-permute-start(bf16[2,256,256]{2,1,0:T(8,128)(2,1)S(1)} %get-tuple-element.36), channel_id=1, source_target_pairs={{0,24},{1,25},{2,26},{3,27},{4,28},{5,29},{6,30},{7,31},{8,16},{9,... | collective-permute-start | bytes 786440 | tf_op jit(solution)/shard_map/ppermute | solution.py:48
  30.1 16.1 %collective-permute-start = (bf16[528,128]{1,0:T(8,128)(2,1)S(1)}, bf16[528,128]{1,0:T(8,128)(2,1)S(1)}, u32[]{:S(2)}, u32[]{:S(2)}) collective-permute-start(bf16[528,128]{1,0:T(8,128)(2,1)S(1)} %shard_map.104.refs_4_.refs_0_), channel_id=1, source_target_pairs={{0,32},{32,0},{64,96},{96,64},{128,160},{160,128},{192,224},{224,1... | collective-permute-start | bytes 405512 | tf_op jit(solution)/shard_map/ppermute | solution.py:32
  34.4 8.3 %collective-permute-start.13 = (bf16[2,256,256]{2,1,0:T(8,128)(2,1)S(1)}, bf16[2,256,256]{2,1,0:T(8,128)(2,1)S(1)}, u32[]{:S(2)}, u32[]{:S(2)}) collective-permute-start(bf16[2,256,256]{2,1,0:T(8,128)(2,1)S(1)} %get-tuple-element.32.refs_4_), channel_id=1, source_target_pairs={{0,8},{1,9},{2,10},{3,11},{4,12},{5,13},{6,14},{7,15},{8,0},{9,1},... | collective-permute-start | bytes 786440 | tf_op jit(solution)/shard_map/ppermute | solution.py:48
  34.9 9.9 %collective-permute-start.14 = (bf16[2,256,256]{2,1,0:T(8,128)(2,1)S(1)}, bf16[2,256,256]{2,1,0:T(8,128)(2,1)S(1)}, u32[]{:S(2)}, u32[]{:S(2)}) collective-permute-start(bf16[2,256,256]{2,1,0:T(8,128)(2,1)S(1)} %get-tuple-element.41), channel_id=1, source_target_pairs={{0,24},{1,25},{2,26},{3,27},{4,28},{5,29},{6,30},{7,31},{8,16},{9,... | collective-permute-start | bytes 786440 | tf_op jit(solution)/shard_map/ppermute | solution.py:48
  37.5 10.4 %collective-permute-start.17 = (bf16[256,256]{1,0:T(8,128)(2,1)S(1)}, bf16[256,256]{1,0:T(8,128)(2,1)S(1)}, u32[]{:S(2)}, u32[]{:S(2)}) collective-permute-start(bf16[256,256]{1,0:T(8,128)(2,1)S(1)} %get-tuple-element.37.refs_2_), channel_id=1, source_target_pairs={{0,24},{1,25},{2,26},{3,27},{4,28},{5,29},{6,30},{7,31},{8,16},{9,... | collective-permute-start | bytes 393224 | tf_op jit(solution)/shard_map/ppermute | solution.py:48
  40.3 9.5 %collective-permute-start.18 = (bf16[256,256]{1,0:T(8,128)(2,1)S(1)}, bf16[256,256]{1,0:T(8,128)(2,1)S(1)}, u32[]{:S(2)}, u32[]{:S(2)}) collective-permute-start(bf16[256,256]{1,0:T(8,128)(2,1)S(1)} %get-tuple-element.38.refs_3_), channel_id=1, source_target_pairs={{0,8},{1,9},{2,10},{3,11},{4,12},{5,13},{6,14},{7,15},{8,0},{9,1},... | collective-permute-start | bytes 393224 | tf_op jit(solution)/shard_map/ppermute | solution.py:48
  45.0 7.0 %collective-permute-start.15 = (bf16[256,256]{1,0:T(8,128)(2,1)S(1)}, bf16[256,256]{1,0:T(8,128)(2,1)S(1)}, u32[]{:S(2)}, u32[]{:S(2)}) collective-permute-start(bf16[256,256]{1,0:T(8,128)(2,1)S(1)} %get-tuple-element.43), channel_id=1, source_target_pairs={{0,24},{1,25},{2,26},{3,27},{4,28},{5,29},{6,30},{7,31},{8,16},{9,... | collective-permute-start | bytes 393224 | tf_op jit(solution)/shard_map/ppermute | solution.py:48
  46.2 8.4 %collective-permute-start.16 = (bf16[256,256]{1,0:T(8,128)(2,1)S(1)}, bf16[256,256]{1,0:T(8,128)(2,1)S(1)}, u32[]{:S(2)}, u32[]{:S(2)}) collective-permute-start(bf16[256,256]{1,0:T(8,128)(2,1)S(1)} %get-tuple-element.45), channel_id=1, source_target_pairs={{0,8},{1,9},{2,10},{3,11},{4,12},{5,13},{6,14},{7,15},{8,0},{9,1},... | collective-permute-start | bytes 393224 | tf_op jit(solution)/shard_map/ppermute | solution.py:48
  46.3 10.4 %copy-start.5 = (f32[8]{0:T(128)S(1)}, f32[8]{0:T(128)}, u32[]{:S(2)}) copy-start(f32[8]{0:T(128)} %param.13) | copy-start | bytes 100
  46.3 10.4 %collective-permute-start.10 = (bf16[528,128]{1,0:T(8,128)(2,1)S(1)}, bf16[528,128]{1,0:T(8,128)(2,1)S(1)}, u32[]{:S(2)}, u32[]{:S(2)}) collective-permute-start(bf16[528,128]{1,0:T(8,128)(2,1)S(1)} %shard_map.114), channel_id=1, source_target_pairs={{0,64},{32,96},{64,128},{96,160},{128,192},{160,224},{192,0},{224,... | collective-permute-start | bytes 405512 | tf_op jit(solution)/shard_map/ppermute | solution.py:37
  47.9 8.8 %collective-permute-start.11 = (bf16[528,128]{1,0:T(8,128)(2,1)S(1)}, bf16[528,128]{1,0:T(8,128)(2,1)S(1)}, u32[]{:S(2)}, u32[]{:S(2)}) collective-permute-start(bf16[528,128]{1,0:T(8,128)(2,1)S(1)} %shard_map.114), channel_id=1, source_target_pairs={{0,128},{32,160},{64,192},{96,224},{128,0},{160,32},{192,64},{224,... | collective-permute-start | bytes 405512 | tf_op jit(solution)/shard_map/ppermute | solution.py:37
  49.8 6.9 %collective-permute-start.12 = (bf16[528,128]{1,0:T(8,128)(2,1)S(1)}, bf16[528,128]{1,0:T(8,128)(2,1)S(1)}, u32[]{:S(2)}, u32[]{:S(2)}) collective-permute-start(bf16[528,128]{1,0:T(8,128)(2,1)S(1)} %shard_map.114), channel_id=1, source_target_pairs={{0,192},{32,224},{64,0},{96,32},{128,64},{160,96},{192,128},{224,1... | collective-permute-start | bytes 405512 | tf_op jit(solution)/shard_map/ppermute | solution.py:37
  52.0 10.2 %collective-permute-start.21 = (bf16[256,256]{1,0:T(8,128)(2,1)S(1)}, bf16[256,256]{1,0:T(8,128)(2,1)S(1)}, u32[]{:S(2)}, u32[]{:S(2)}) collective-permute-start(bf16[256,256]{1,0:T(8,128)(2,1)S(1)} %get-tuple-element.51), channel_id=1, source_target_pairs={{0,4},{1,5},{2,6},{3,7},{4,0},{5,1},{6,2},{7,3},{8,12},{9,13},{10,... | collective-permute-start | bytes 393224 | tf_op jit(solution)/shard_map/ppermute | solution.py:52
  54.6 7.5 %collective-permute-start.19 = (bf16[256,256]{1,0:T(8,128)(2,1)S(1)}, bf16[256,256]{1,0:T(8,128)(2,1)S(1)}, u32[]{:S(2)}, u32[]{:S(2)}) collective-permute-start(bf16[256,256]{1,0:T(8,128)(2,1)S(1)} %get-tuple-element.47.refs_10_), channel_id=1, source_target_pairs={{0,6},{1,7},{2,4},{3,5},{4,2},{5,3},{6,0},{7,1},{8,14},{9,15},{10,... | collective-permute-start | bytes 393224 | tf_op jit(solution)/shard_map/ppermute | solution.py:52
  56.7 6.7 %collective-permute-start.20 = (bf16[256,256]{1,0:T(8,128)(2,1)S(1)}, bf16[256,256]{1,0:T(8,128)(2,1)S(1)}, u32[]{:S(2)}, u32[]{:S(2)}) collective-permute-start(bf16[256,256]{1,0:T(8,128)(2,1)S(1)} %get-tuple-element.46.refs_9_), channel_id=1, source_target_pairs={{0,2},{1,3},{2,0},{3,1},{4,6},{5,7},{6,4},{7,5},{8,10},{9,11},{10,... | collective-permute-start | bytes 393224 | tf_op jit(solution)/shard_map/ppermute | solution.py:52

commit v9 on v7

--- a/solution.py
+++ b/solution.py
@@ -398,7 +398,7 @@
         [whole(head_block)] + [whole(pair.shape)] * 3,
         [shape((7 * length, HEAD_DIM), bf16)],
         (arrived_pair, fetched[1], fetched[0], fetched[2]),
-        after=[closing, near_part[0]],
+        after=[closing, near_part[0], own_weight],
     )
     others_there = swap_core(others)
     (attended,) = call(

time: 65.3 us -> 65.5 us (level)
    ppermute x6, waiting for transfers between devices: 2.98 us -> 0.02 us  [shift_y(): return lax.ppermute(block, 'section', route)]
    ppermute x1, waiting for transfers between devices: 0.57 us -> 2.79 us  [swap_zh_near(): return lax.ppermute(block, ('section', 'tp'), route)]
  transfers between devices with their start and end apart: 18 -> 18, of which waited for: 11 -> 9; matrix products, arithmetic and copies ran while one was open for 3% -> 2% of each run, Pallas kernels for 12% -> 12%
where the time goes in v9:
time: 65.5 us; the launch traced here: 64.9 us
  starting transfers between devices  32.2 us (49%)
  waiting for transfers between devices  18.5 us (28%)
  Pallas kernels  9.07 us (14%)
  local copies, waits for them, and re-layouts  3.2 us (5%)
  other arithmetic  1.06 us (2%)
  between operations  0.89 us (1%)
    ppermute x6, starting transfers between devices, shift_y(): return lax.ppermute(block, 'section', route)  10.1 us
    pallas_call x13, Pallas kernels, call(): pl.pallas_call(ordered, in_specs=list(in_specs) + [pl.BlockSpec(memory_sp...  9.07 us
    ppermute x4, waiting for transfers between devices, swap_x(): return lax.ppermute(block, 'tp', [(t, t ^ 8 * offset) for t in range(TP)])  8.58 us
    ppermute x1, starting transfers between devices, swap_zh_near(): return lax.ppermute(block, ('section', 'tp'), route)  6.39 us
    ppermute x4, starting transfers between devices, swap_x(): return lax.ppermute(block, 'tp', [(t, t ^ 8 * offset) for t in range(TP)])  5.85 us
    ppermute x3, waiting for transfers between devices, swap_zl(): return lax.ppermute(block, 'tp', [(t, t ^ 2 * offset) for t in range(TP)])  4.62 us
    ppermute x3, starting transfers between devices, swap_zl(): return lax.ppermute(block, 'tp', [(t, t ^ 2 * offset) for t in range(TP)])  4.57 us
    ppermute x1, starting transfers between devices, swap_zh(): return lax.ppermute(block, 'section', [(s, s ^ 1) for s in range(SECTIONS)])  4.48 us
  transfers between devices with their start and end apart: 18, of which 9 were waited for; matrix products, arithmetic and copies ran while one was open for 2% of the time, Pallas kernels for 12%

profile of v9, /device:TPU:8, one launch (start us, length us, event | category | flops | bytes accessed | tf_op | source)
XLA Modules:
  0.0 64.9 jit_solution(14916293719682624892)
XLA Ops:
  0.6 0.0 copy-start
  0.6 0.0 copy-start.5
  0.7 0.0 copy-start.3
  0.7 0.0 copy-start.2
  0.7 1.1 %broadcast_select_fusion = (bf16[256,128]{1,0:T(8,128)(2,1)S(1)}, bf16[256,128]{1,0:T(8,128)(2,1)S(1)}, bf16[256,128]{1,0:T(8,128)(2,1)S(1)}, bf16[256,128]{1,0:T(8,128)(2,1)S(1)}) fusion(pred[]{:T(512)S(6)} %eq.5, bf16[256,1024]{1,0:T(8,128)(2,1)} %param.16, s32[]{:T(128)S(6)} %select_n.34, bf16[256,1024]{1,0:T(8,128)(2,1)} %param.15, s32[]{:T(128)S(6)} %select_n.37), kind=kLoop, calls=%fused_computation.1 | loop fusion | flops 65536 | bytes 524297 | tf_op jit(solution)/shard_map/jit(_where)/select_n | solution.py:351
  1.8 6.4 %collective-permute-start.2 = (bf16[256,128]{1,0:T(8,128)(2,1)S(1)}, bf16[256,128]{1,0:T(8,128)(2,1)S(1)}, u32[]{:S(2)}, u32[]{:S(2)}) collective-permute-start(bf16[256,128]{1,0:T(8,128)(2,1)S(1)} %get-tuple-element.39.refs_1_), channel_id=1, source_target_pairs={{0,36},{1,37},{2,38},{3,39},{4,32},{5,33},{6,34},{7,35},{8,44},{9,... | collective-permute-start | bytes 196616 | tf_op jit(solution)/shard_map/ppermute | solution.py:44
  8.2 2.8 %collective-permute-done.2.refs_1_.refs_0_ = bf16[256,128]{1,0:T(8,128)(2,1)S(1)} collective-permute-done((bf16[256,128]{1,0:T(8,128)(2,1)S(1)}, bf16[256,128]{1,0:T(8,128)(2,1)S(1)}, u32[]{:S(2)}, u32[]{:S(2)}) %collective-permute-start.2) | collective-permute-done | bytes 65568 | tf_op jit(solution)/shard_map/ppermute | solution.py:44
  11.0 1.7 %collective-permute-start.3 = (bf16[512,128]{1,0:T(8,128)(2,1)S(1)}, bf16[512,128]{1,0:T(8,128)(2,1)S(1)}, u32[]{:S(2)}, u32[]{:S(2)}) collective-permute-start(bf16[512,128]{1,0:T(8,128)(2,1)S(1)} %shard_map.106), channel_id=1, source_target_pairs={{0,64},{32,96},{64,128},{96,160},{128,192},{160,224},{192,0},{224,... | collective-permute-start | bytes 393224 | tf_op jit(solution)/shard_map/ppermute | solution.py:37
  12.6 0.9 %collective-permute-start.4 = (bf16[512,128]{1,0:T(8,128)(2,1)S(1)}, bf16[512,128]{1,0:T(8,128)(2,1)S(1)}, u32[]{:S(2)}, u32[]{:S(2)}) collective-permute-start(bf16[512,128]{1,0:T(8,128)(2,1)S(1)} %shard_map.106), channel_id=1, source_target_pairs={{0,128},{32,160},{64,192},{96,224},{128,0},{160,32},{192,64},{224,... | collective-permute-start | bytes 393224 | tf_op jit(solution)/shard_map/ppermute | solution.py:37
  13.6 2.4 %collective-permute-start.5 = (bf16[512,128]{1,0:T(8,128)(2,1)S(1)}, bf16[512,128]{1,0:T(8,128)(2,1)S(1)}, u32[]{:S(2)}, u32[]{:S(2)}) collective-permute-start(bf16[512,128]{1,0:T(8,128)(2,1)S(1)} %shard_map.106), channel_id=1, source_target_pairs={{0,192},{32,224},{64,0},{96,32},{128,64},{160,96},{192,128},{224,1... | collective-permute-start | bytes 393224 | tf_op jit(solution)/shard_map/ppermute | solution.py:37
  16.0 0.0 copy-done
  16.0 0.0 copy-done.5
  16.0 0.1 copy.12.refs_2_.refs_3_
  16.1 0.0 copy-done.3
  16.1 0.5 shard_map.107
  16.6 0.0 copy-done.2
  16.6 1.4 %shard_map.104.refs_4_.refs_0_ = bf16[528,128]{1,0:T(8,128)(2,1)S(1)} custom-call(bf16[256,512]{1,0:T(8,128)(2,1)S(1)} %copy-done.2, bf16[256,128]{1,0:T(8,128)(2,1)S(1)} %constant_dynamic-slice_fusion.3.refs_1_, f32[256,8]{1,0:T(8,128)S(1)} %copy.12.refs_2_.refs_3_), custom_call_target="tpu_custom_call" | custom-call | flops 300000000 | bytes 1050000 | tf_op jit(solution)/shard_map/pallas_call | solution.py:76
  18.0 0.0 copy-start.1
  18.0 2.2 %copy-done.1 = bf16[8192,256]{1,0:T(8,128)(2,1)S(1)} copy-done((bf16[8192,256]{1,0:T(8,128)(2,1)S(1)}, bf16[8192,256]{1,0:T(8,128)(2,1)}, u32[]{:S(2)}) %copy-start.1) | copy-done | bytes 4194328
  20.2 0.3 shard_map.105
  20.5 0.0 collective-permute-done.3.refs_1_
  20.5 0.0 collective-permute-done.4.refs_2_
  20.5 0.0 collective-permute-done.5.refs_3_
  20.6 0.1 collective-permute-start.6
  20.7 0.5 collective-permute-start.1
  21.2 1.3 %collective-permute-done.6.refs_2_ = bf16[1792,128]{1,0:T(8,128)(2,1)S(1)} collective-permute-done((bf16[1792,128]{1,0:T(8,128)(2,1)S(1)}, bf16[1792,128]{1,0:T(8,128)(2,1)S(1)}, u32[]{:S(2)}, u32[]{:S(2)}) %collective-permute-start.6) | collective-permute-done | bytes 458784 | tf_op jit(solution)/shard_map/ppermute | solution.py:28
  22.5 1.8 %shard_map.109.refs_2_ = bf16[256,256]{1,0:T(8,128)(2,1)S(1)} custom-call(bf16[256,256]{1,0:T(8,128)(2,1)S(1)} %copy-done.3, bf16[1792,128]{1,0:T(8,128)(2,1)S(1)} %shard_map.108.refs_1_, bf16[1792,128]{1,0:T(8,128)(2,1)S(1)} %collective-permute-done.6.refs_2_, f32[512,128]{1,0:T(8,128)S(1)} %get-tuple-element.21.refs_5_.refs_3_, ...), custom_call_target="tpu_custom_call" | custom-call | flops 40000000000 | bytes 140000000 | tf_op jit(solution)/shard_map/pallas_call | solution.py:76
  24.3 0.2 collective-permute-start.7
  24.5 1.2 %collective-permute-done.7.refs_3_ = bf16[256,256]{1,0:T(8,128)(2,1)S(1)} collective-permute-done((bf16[256,256]{1,0:T(8,128)(2,1)S(1)}, bf16[256,256]{1,0:T(8,128)(2,1)S(1)}, u32[]{:S(2)}, u32[]{:S(2)}) %collective-permute-start.7) | collective-permute-done | bytes 131104 | tf_op jit(solution)/shard_map/ppermute | solution.py:28
  25.8 0.0 collective-permute-done.1.refs_1_
  25.8 0.7 %shard_map.110 = (bf16[2,2,256,256]{3,2,1,0:T(8,128)(2,1)S(1)}, bf16[2,2,256,256]{3,2,1,0:T(8,128)(2,1)S(1)}) custom-call(bf16[16,256,256]{2,1,0:T(8,128)(2,1)S(1)} %get-tuple-element.19.refs_6_.refs_0_, bf16[16,256,256]{2,1,0:T(8,128)(2,1)S(1)} %collective-permute-done.1.refs_1_, bf16[256,256]{1,0:T(8,128)(2,1)S(1)} %shard_map.109.refs_2_, ...), custom_call_target="tpu_custom_call" | custom-call | flops 1300000000 | bytes 4550000 | tf_op jit(solution)/shard_map/pallas_call | solution.py:76
  26.5 1.6 %collective-permute-start.8 = (bf16[2,2,256,256]{3,2,1,0:T(8,128)(2,1)S(1)}, bf16[2,2,256,256]{3,2,1,0:T(8,128)(2,1)S(1)}, u32[]{:S(2)}, u32[]{:S(2)}) collective-permute-start(bf16[2,2,256,256]{3,2,1,0:T(8,128)(2,1)S(1)} %get-tuple-element.24.refs_4_), channel_id=1, source_target_pairs={{0,8},{1,9},{2,10},{3,11},{4,12},{5,13},{6,14},{7,15},{8,0},{9,1},... | collective-permute-start | bytes 1572872 | tf_op jit(solution)/shard_map/ppermute | solution.py:48
  28.0 2.1 %collective-permute-start.9 = (bf16[2,2,256,256]{3,2,1,0:T(8,128)(2,1)S(1)}, bf16[2,2,256,256]{3,2,1,0:T(8,128)(2,1)S(1)}, u32[]{:S(2)}, u32[]{:S(2)}) collective-permute-start(bf16[2,2,256,256]{3,2,1,0:T(8,128)(2,1)S(1)} %get-tuple-element.27), channel_id=1, source_target_pairs={{0,24},{1,25},{2,26},{3,27},{4,28},{5,29},{6,30},{7,31},{8,16},{9,... | collective-permute-start | bytes 1572872 | tf_op jit(solution)/shard_map/ppermute | solution.py:48
  30.1 4.5 %collective-permute-start = (bf16[528,128]{1,0:T(8,128)(2,1)S(1)}, bf16[528,128]{1,0:T(8,128)(2,1)S(1)}, u32[]{:S(2)}, u32[]{:S(2)}) collective-permute-start(bf16[528,128]{1,0:T(8,128)(2,1)S(1)} %shard_map.104.refs_4_.refs_0_), channel_id=1, source_target_pairs={{0,32},{32,0},{64,96},{96,64},{128,160},{160,128},{192,224},{224,1... | collective-permute-start | bytes 405512 | tf_op jit(solution)/shard_map/ppermute | solution.py:32
  34.6 0.8 %constant_dynamic-slice_fusion.2.refs_5_.refs_2_ = bf16[256,128]{1,0:T(8,128)(2,1)S(1)} fusion(bf16[256,1024]{1,0:T(8,128)(2,1)} %param.11, s32[]{:T(128)S(6)} %select_n.34), kind=kLoop, calls=%fused_computation.4 | loop fusion | bytes 131076 | tf_op jit(solution)/shard_map/dynamic_slice | solution.py:345
  35.5 0.7 %shard_map.111 = (bf16[2,2,256,256]{3,2,1,0:T(8,128)(2,1)S(1)}, bf16[2,2,256,256]{3,2,1,0:T(8,128)(2,1)S(1)}) custom-call(bf16[16,256,256]{2,1,0:T(8,128)(2,1)S(1)} %get-tuple-element.19.refs_6_.refs_0_, bf16[16,256,256]{2,1,0:T(8,128)(2,1)S(1)} %collective-permute-done.1.refs_1_, bf16[256,256]{1,0:T(8,128)(2,1)S(1)} %shard_map.109.refs_2_, ...), custom_call_target="tpu_custom_call" | custom-call | flops 1300000000 | bytes 4550000 | tf_op jit(solution)/shard_map/pallas_call | solution.py:76
  36.2 4.4 %collective-permute-done.8.refs_1_ = bf16[2,2,256,256]{3,2,1,0:T(8,128)(2,1)S(1)} collective-permute-done((bf16[2,2,256,256]{3,2,1,0:T(8,128)(2,1)S(1)}, bf16[2,2,256,256]{3,2,1,0:T(8,128)(2,1)S(1)}, u32[]{:S(2)}, u32[]{:S(2)}) %collective-permute-start.8) | collective-permute-done | bytes 524320 | tf_op jit(solution)/shard_map/ppermute | solution.py:48
  40.5 2.4 %collective-permute-done.9.refs_3_ = bf16[2,2,256,256]{3,2,1,0:T(8,128)(2,1)S(1)} collective-permute-done((bf16[2,2,256,256]{3,2,1,0:T(8,128)(2,1)S(1)}, bf16[2,2,256,256]{3,2,1,0:T(8,128)(2,1)S(1)}, u32[]{:S(2)}, u32[]{:S(2)}) %collective-permute-start.9) | collective-permute-done | bytes 524320 | tf_op jit(solution)/shard_map/ppermute | solution.py:48
  43.0 0.2 shard_map.112
  43.2 0.0 copy-start.4
  43.2 2.2 %collective-permute-start.13 = (bf16[2,256,256]{2,1,0:T(8,128)(2,1)S(1)}, bf16[2,256,256]{2,1,0:T(8,128)(2,1)S(1)}, u32[]{:S(2)}, u32[]{:S(2)}) collective-permute-start(bf16[2,256,256]{2,1,0:T(8,128)(2,1)S(1)} %get-tuple-element.28.refs_2_), channel_id=1, source_target_pairs={{0,24},{1,25},{2,26},{3,27},{4,28},{5,29},{6,30},{7,31},{8,16},{9,... | collective-permute-start | bytes 786440 | tf_op jit(solution)/shard_map/ppermute | solution.py:48
  45.4 0.0 collective-permute-start.14
  45.4 0.0 collective-permute-done.refs_1_.refs_5_
  45.5 0.9 %collective-permute-start.10 = (bf16[528,128]{1,0:T(8,128)(2,1)S(1)}, bf16[528,128]{1,0:T(8,128)(2,1)S(1)}, u32[]{:S(2)}, u32[]{:S(2)}) collective-permute-start(bf16[528,128]{1,0:T(8,128)(2,1)S(1)} %shard_map.113), channel_id=1, source_target_pairs={{0,64},{32,96},{64,128},{96,160},{128,192},{160,224},{192,0},{224,... | collective-permute-start | bytes 405512 | tf_op jit(solution)/shard_map/ppermute | solution.py:37
  46.3 2.5 %collective-permute-start.11 = (bf16[528,128]{1,0:T(8,128)(2,1)S(1)}, bf16[528,128]{1,0:T(8,128)(2,1)S(1)}, u32[]{:S(2)}, u32[]{:S(2)}) collective-permute-start(bf16[528,128]{1,0:T(8,128)(2,1)S(1)} %shard_map.113), channel_id=1, source_target_pairs={{0,128},{32,160},{64,192},{96,224},{128,0},{160,32},{192,64},{224,... | collective-permute-start | bytes 405512 | tf_op jit(solution)/shard_map/ppermute | solution.py:37
  48.9 1.6 %collective-permute-start.12 = (bf16[528,128]{1,0:T(8,128)(2,1)S(1)}, bf16[528,128]{1,0:T(8,128)(2,1)S(1)}, u32[]{:S(2)}, u32[]{:S(2)}) collective-permute-start(bf16[528,128]{1,0:T(8,128)(2,1)S(1)} %shard_map.113), channel_id=1, source_target_pairs={{0,192},{32,224},{64,0},{96,32},{128,64},{160,96},{192,128},{224,1... | collective-permute-start | bytes 405512 | tf_op jit(solution)/shard_map/ppermute | solution.py:37
  50.5 1.2 %collective-permute-done.13.refs_1_ = bf16[2,256,256]{2,1,0:T(8,128)(2,1)S(1)} collective-permute-done((bf16[2,256,256]{2,1,0:T(8,128)(2,1)S(1)}, bf16[2,256,256]{2,1,0:T(8,128)(2,1)S(1)}, u32[]{:S(2)}, u32[]{:S(2)}) %collective-permute-start.13) | collective-permute-done | bytes 262176 | tf_op jit(solution)/shard_map/ppermute | solution.py:48
  51.7 0.6 collective-permute-done.14.refs_3_
  52.3 0.1 shard_map.114
  52.5 2.3 %collective-permute-start.15 = (bf16[256,256]{1,0:T(8,128)(2,1)S(1)}, bf16[256,256]{1,0:T(8,128)(2,1)S(1)}, u32[]{:S(2)}, u32[]{:S(2)}) collective-permute-start(bf16[256,256]{1,0:T(8,128)(2,1)S(1)} %get-tuple-element.35), channel_id=1, source_target_pairs={{0,4},{1,5},{2,6},{3,7},{4,0},{5,1},{6,2},{7,3},{8,12},{9,13},{10,... | collective-permute-start | bytes 393224 | tf_op jit(solution)/shard_map/ppermute | solution.py:52
  54.7 2.3 %collective-permute-start.16 = (bf16[256,256]{1,0:T(8,128)(2,1)S(1)}, bf16[256,256]{1,0:T(8,128)(2,1)S(1)}, u32[]{:S(2)}, u32[]{:S(2)}) collective-permute-start(bf16[256,256]{1,0:T(8,128)(2,1)S(1)} %get-tuple-element.33.refs_10_), channel_id=1, source_target_pairs={{0,6},{1,7},{2,4},{3,5},{4,2},{5,3},{6,0},{7,1},{8,14},{9,15},{10,... | collective-permute-start | bytes 393224 | tf_op jit(solution)/shard_map/ppermute | solution.py:52
  57.0 0.0 collective-permute-done.10.refs_6_
  57.0 0.0 collective-permute-start.17
  57.0 0.0 collective-permute-done.11.refs_7_
  57.0 0.0 collective-permute-done.12.refs_8_
  57.0 0.0 copy-done.4
  57.1 2.5 %shard_map.115 = bf16[256,512]{1,0:T(8,128)(2,1)} custom-call(bf16[256,512]{1,0:T(8,128)(2,1)S(1)} %copy-done.2, bf16[256,128]{1,0:T(8,128)(2,1)S(1)} %constant_dynamic-slice_fusion.3.refs_1_, bf16[256,128]{1,0:T(8,128)(2,1)S(1)} %constant_dynamic-slice_fusion.2.refs_5_.refs_2_, f32[256,8]{1,0:T(8,128)S(1)} %copy.12.refs_2_.refs_3_, f32[1,8]{1,0:T(1,128)S(1)} %bitcast.3, ...), custom_call_target="tpu_custom_call" | custom-call | flops 3000000000 | bytes 10500000 | tf_op jit(solution)/shard_map/pallas_call | solution.py:76
  59.6 4.1 %collective-permute-done.15.refs_1_ = bf16[256,256]{1,0:T(8,128)(2,1)S(1)} collective-permute-done((bf16[256,256]{1,0:T(8,128)(2,1)S(1)}, bf16[256,256]{1,0:T(8,128)(2,1)S(1)}, u32[]{:S(2)}, u32[]{:S(2)}) %collective-permute-start.15) | collective-permute-done | bytes 131104 | tf_op jit(solution)/shard_map/ppermute | solution.py:52
  63.7 0.0 collective-permute-done.16.refs_2_
  63.7 0.5 collective-permute-done.17.refs_3_
  64.2 0.7 %shard_map.116 = bf16[256,256]{1,0:T(8,128)(2,1)} custom-call(bf16[256,256]{1,0:T(8,128)(2,1)S(1)} %get-tuple-element.34.refs_0_, bf16[256,256]{1,0:T(8,128)(2,1)S(1)} %collective-permute-done.15.refs_1_, bf16[256,256]{1,0:T(8,128)(2,1)S(1)} %collective-permute-done.16.refs_2_, bf16[256,256]{1,0:T(8,128)(2,1)S(1)} %collective-permute-done.17.refs_3_), custom_call_target="tpu_custom_call" | custom-call | flops 1300000000 | bytes 4550000 | tf_op jit(solution)/shard_map/pallas_call | solution.py:76
  (4 shorter events, 0.1 us)
Async XLA Ops:
  0.6 15.3 %copy-start = (bf16[256,1024]{1,0:T(8,128)(2,1)S(1)}, bf16[256,1024]{1,0:T(8,128)(2,1)}, u32[]{:S(2)}) copy-start(bf16[256,1024]{1,0:T(8,128)(2,1)} %param.10) | copy-start | bytes 1572868
  0.6 15.3 %copy-start.5 = (f32[256,8]{0,1:T(8,128)S(1)}, f32[256,8]{0,1:T(8,128)}, u32[]{:S(2)}) copy-start(f32[256,8]{0,1:T(8,128)} %param.12) | copy-start | bytes 24580
  0.7 15.5 %copy-start.3 = (bf16[256,256]{1,0:T(8,128)(2,1)S(1)}, bf16[256,256]{1,0:T(8,128)(2,1)}, u32[]{:S(2)}) copy-start(bf16[256,256]{1,0:T(8,128)(2,1)} %refs_0_.6) | copy-start | bytes 393220
  0.7 16.0 %copy-start.2 = (bf16[256,512]{1,0:T(8,128)(2,1)S(1)}, bf16[256,512]{1,0:T(8,128)(2,1)}, u32[]{:S(2)}) copy-start(bf16[256,512]{1,0:T(8,128)(2,1)} %refs_0_.7) | copy-start | bytes 786436
  1.8 9.2 %collective-permute-start.2 = (bf16[256,128]{1,0:T(8,128)(2,1)S(1)}, bf16[256,128]{1,0:T(8,128)(2,1)S(1)}, u32[]{:S(2)}, u32[]{:S(2)}) collective-permute-start(bf16[256,128]{1,0:T(8,128)(2,1)S(1)} %get-tuple-element.39.refs_1_), channel_id=1, source_target_pairs={{0,36},{1,37},{2,38},{3,39},{4,32},{5,33},{6,34},{7,35},{8,44},{9,... | collective-permute-start | bytes 196616 | tf_op jit(solution)/shard_map/ppermute | solution.py:44
  11.0 9.6 %collective-permute-start.3 = (bf16[512,128]{1,0:T(8,128)(2,1)S(1)}, bf16[512,128]{1,0:T(8,128)(2,1)S(1)}, u32[]{:S(2)}, u32[]{:S(2)}) collective-permute-start(bf16[512,128]{1,0:T(8,128)(2,1)S(1)} %shard_map.106), channel_id=1, source_target_pairs={{0,64},{32,96},{64,128},{96,160},{128,192},{160,224},{192,0},{224,... | collective-permute-start | bytes 393224 | tf_op jit(solution)/shard_map/ppermute | solution.py:37
  12.6 7.9 %collective-permute-start.4 = (bf16[512,128]{1,0:T(8,128)(2,1)S(1)}, bf16[512,128]{1,0:T(8,128)(2,1)S(1)}, u32[]{:S(2)}, u32[]{:S(2)}) collective-permute-start(bf16[512,128]{1,0:T(8,128)(2,1)S(1)} %shard_map.106), channel_id=1, source_target_pairs={{0,128},{32,160},{64,192},{96,224},{128,0},{160,32},{192,64},{224,... | collective-permute-start | bytes 393224 | tf_op jit(solution)/shard_map/ppermute | solution.py:37
  13.6 7.0 %collective-permute-start.5 = (bf16[512,128]{1,0:T(8,128)(2,1)S(1)}, bf16[512,128]{1,0:T(8,128)(2,1)S(1)}, u32[]{:S(2)}, u32[]{:S(2)}) collective-permute-start(bf16[512,128]{1,0:T(8,128)(2,1)S(1)} %shard_map.106), channel_id=1, source_target_pairs={{0,192},{32,224},{64,0},{96,32},{128,64},{160,96},{192,128},{224,1... | collective-permute-start | bytes 393224 | tf_op jit(solution)/shard_map/ppermute | solution.py:37
  18.0 2.2 %copy-start.1 = (bf16[8192,256]{1,0:T(8,128)(2,1)S(1)}, bf16[8192,256]{1,0:T(8,128)(2,1)}, u32[]{:S(2)}) copy-start(bf16[8192,256]{1,0:T(8,128)(2,1)} %param.17) | copy-start | bytes 12582916
  20.6 1.9 %collective-permute-start.6 = (bf16[1792,128]{1,0:T(8,128)(2,1)S(1)}, bf16[1792,128]{1,0:T(8,128)(2,1)S(1)}, u32[]{:S(2)}, u32[]{:S(2)}) collective-permute-start(bf16[1792,128]{1,0:T(8,128)(2,1)S(1)} %shard_map.108.refs_1_), channel_id=1, source_target_pairs={{0,1},{1,0},{2,3},{3,2},{4,5},{5,4},{6,7},{7,6},{8,9},{9,8},{10,11... | collective-permute-start | bytes 1376264 | tf_op jit(solution)/shard_map/ppermute | solution.py:28
  20.7 5.1 %collective-permute-start.1 = (bf16[16,256,256]{2,1,0:T(8,128)(2,1)S(1)}, bf16[16,256,256]{2,1,0:T(8,128)(2,1)S(1)}, u32[]{:S(2)}, u32[]{:S(2)}) collective-permute-start(bf16[16,256,256]{2,1,0:T(8,128)(2,1)S(1)} %get-tuple-element.20), channel_id=1, source_target_pairs={{0,1},{1,0},{2,3},{3,2},{4,5},{5,4},{6,7},{7,6},{8,9},{9,8},{10,11... | collective-permute-start | bytes 6291464 | tf_op jit(solution)/shard_map/ppermute | solution.py:28
  24.3 1.4 %collective-permute-start.7 = (bf16[256,256]{1,0:T(8,128)(2,1)S(1)}, bf16[256,256]{1,0:T(8,128)(2,1)S(1)}, u32[]{:S(2)}, u32[]{:S(2)}) collective-permute-start(bf16[256,256]{1,0:T(8,128)(2,1)S(1)} %shard_map.109.refs_2_), channel_id=1, source_target_pairs={{0,1},{1,0},{2,3},{3,2},{4,5},{5,4},{6,7},{7,6},{8,9},{9,8},{10,11... | collective-permute-start | bytes 393224 | tf_op jit(solution)/shard_map/ppermute | solution.py:28
  26.5 14.1 %collective-permute-start.8 = (bf16[2,2,256,256]{3,2,1,0:T(8,128)(2,1)S(1)}, bf16[2,2,256,256]{3,2,1,0:T(8,128)(2,1)S(1)}, u32[]{:S(2)}, u32[]{:S(2)}) collective-permute-start(bf16[2,2,256,256]{3,2,1,0:T(8,128)(2,1)S(1)} %get-tuple-element.24.refs_4_), channel_id=1, source_target_pairs={{0,8},{1,9},{2,10},{3,11},{4,12},{5,13},{6,14},{7,15},{8,0},{9,1},... | collective-permute-start | bytes 1572872 | tf_op jit(solution)/shard_map/ppermute | solution.py:48
  28.0 14.9 %collective-permute-start.9 = (bf16[2,2,256,256]{3,2,1,0:T(8,128)(2,1)S(1)}, bf16[2,2,256,256]{3,2,1,0:T(8,128)(2,1)S(1)}, u32[]{:S(2)}, u32[]{:S(2)}) collective-permute-start(bf16[2,2,256,256]{3,2,1,0:T(8,128)(2,1)S(1)} %get-tuple-element.27), channel_id=1, source_target_pairs={{0,24},{1,25},{2,26},{3,27},{4,28},{5,29},{6,30},{7,31},{8,16},{9,... | collective-permute-start | bytes 1572872 | tf_op jit(solution)/shard_map/ppermute | solution.py:48
  30.1 15.3 %collective-permute-start = (bf16[528,128]{1,0:T(8,128)(2,1)S(1)}, bf16[528,128]{1,0:T(8,128)(2,1)S(1)}, u32[]{:S(2)}, u32[]{:S(2)}) collective-permute-start(bf16[528,128]{1,0:T(8,128)(2,1)S(1)} %shard_map.104.refs_4_.refs_0_), channel_id=1, source_target_pairs={{0,32},{32,0},{64,96},{96,64},{128,160},{160,128},{192,224},{224,1... | collective-permute-start | bytes 405512 | tf_op jit(solution)/shard_map/ppermute | solution.py:32
  43.2 13.9 %copy-start.4 = (f32[8]{0:T(128)S(1)}, f32[8]{0:T(128)}, u32[]{:S(2)}) copy-start(f32[8]{0:T(128)} %param.13) | copy-start | bytes 100
  43.2 8.5 %collective-permute-start.13 = (bf16[2,256,256]{2,1,0:T(8,128)(2,1)S(1)}, bf16[2,256,256]{2,1,0:T(8,128)(2,1)S(1)}, u32[]{:S(2)}, u32[]{:S(2)}) collective-permute-start(bf16[2,256,256]{2,1,0:T(8,128)(2,1)S(1)} %get-tuple-element.28.refs_2_), channel_id=1, source_target_pairs={{0,24},{1,25},{2,26},{3,27},{4,28},{5,29},{6,30},{7,31},{8,16},{9,... | collective-permute-start | bytes 786440 | tf_op jit(solution)/shard_map/ppermute | solution.py:48
  45.4 6.9 %collective-permute-start.14 = (bf16[2,256,256]{2,1,0:T(8,128)(2,1)S(1)}, bf16[2,256,256]{2,1,0:T(8,128)(2,1)S(1)}, u32[]{:S(2)}, u32[]{:S(2)}) collective-permute-start(bf16[2,256,256]{2,1,0:T(8,128)(2,1)S(1)} %get-tuple-element.29.refs_3_), channel_id=1, source_target_pairs={{0,8},{1,9},{2,10},{3,11},{4,12},{5,13},{6,14},{7,15},{8,0},{9,1},... | collective-permute-start | bytes 786440 | tf_op jit(solution)/shard_map/ppermute | solution.py:48
  45.5 11.6 %collective-permute-start.10 = (bf16[528,128]{1,0:T(8,128)(2,1)S(1)}, bf16[528,128]{1,0:T(8,128)(2,1)S(1)}, u32[]{:S(2)}, u32[]{:S(2)}) collective-permute-start(bf16[528,128]{1,0:T(8,128)(2,1)S(1)} %shard_map.113), channel_id=1, source_target_pairs={{0,64},{32,96},{64,128},{96,160},{128,192},{160,224},{192,0},{224,... | collective-permute-start | bytes 405512 | tf_op jit(solution)/shard_map/ppermute | solution.py:37
  46.3 10.7 %collective-permute-start.11 = (bf16[528,128]{1,0:T(8,128)(2,1)S(1)}, bf16[528,128]{1,0:T(8,128)(2,1)S(1)}, u32[]{:S(2)}, u32[]{:S(2)}) collective-permute-start(bf16[528,128]{1,0:T(8,128)(2,1)S(1)} %shard_map.113), channel_id=1, source_target_pairs={{0,128},{32,160},{64,192},{96,224},{128,0},{160,32},{192,64},{224,... | collective-permute-start | bytes 405512 | tf_op jit(solution)/shard_map/ppermute | solution.py:37
  48.9 8.2 %collective-permute-start.12 = (bf16[528,128]{1,0:T(8,128)(2,1)S(1)}, bf16[528,128]{1,0:T(8,128)(2,1)S(1)}, u32[]{:S(2)}, u32[]{:S(2)}) collective-permute-start(bf16[528,128]{1,0:T(8,128)(2,1)S(1)} %shard_map.113), channel_id=1, source_target_pairs={{0,192},{32,224},{64,0},{96,32},{128,64},{160,96},{192,128},{224,1... | collective-permute-start | bytes 405512 | tf_op jit(solution)/shard_map/ppermute | solution.py:37
  52.5 11.2 %collective-permute-start.15 = (bf16[256,256]{1,0:T(8,128)(2,1)S(1)}, bf16[256,256]{1,0:T(8,128)(2,1)S(1)}, u32[]{:S(2)}, u32[]{:S(2)}) collective-permute-start(bf16[256,256]{1,0:T(8,128)(2,1)S(1)} %get-tuple-element.35), channel_id=1, source_target_pairs={{0,4},{1,5},{2,6},{3,7},{4,0},{5,1},{6,2},{7,3},{8,12},{9,13},{10,... | collective-permute-start | bytes 393224 | tf_op jit(solution)/shard_map/ppermute | solution.py:52
  54.7 9.0 %collective-permute-start.16 = (bf16[256,256]{1,0:T(8,128)(2,1)S(1)}, bf16[256,256]{1,0:T(8,128)(2,1)S(1)}, u32[]{:S(2)}, u32[]{:S(2)}) collective-permute-start(bf16[256,256]{1,0:T(8,128)(2,1)S(1)} %get-tuple-element.33.refs_10_), channel_id=1, source_target_pairs={{0,6},{1,7},{2,4},{3,5},{4,2},{5,3},{6,0},{7,1},{8,14},{9,15},{10,... | collective-permute-start | bytes 393224 | tf_op jit(solution)/shard_map/ppermute | solution.py:52
  57.0 7.2 %collective-permute-start.17 = (bf16[256,256]{1,0:T(8,128)(2,1)S(1)}, bf16[256,256]{1,0:T(8,128)(2,1)S(1)}, u32[]{:S(2)}, u32[]{:S(2)}) collective-permute-start(bf16[256,256]{1,0:T(8,128)(2,1)S(1)} %get-tuple-element.32.refs_9_), channel_id=1, source_target_pairs={{0,2},{1,3},{2,0},{3,1},{4,6},{5,7},{6,4},{7,5},{8,10},{9,11},{10,... | collective-permute-start | bytes 393224 | tf_op jit(solution)/shard_map/ppermute | solution.py:52
